TPU v7x, 32 devices: a whole 2x2x4 slice. The times are simulated.
32 devices in a mesh: dp: 4 (over x, core), ctx: 8 (over z, y).
Axes of the slice: x: 2, y: 2, z: 4, core: 2. Of those that a mesh axis runs over, the one named last changes fastest.
Arguments:
- inputs: float32 [8, 2048, 960], P('dp', 'ctx'), may hold values from -6 to 6
- cotangent: float32 [8, 2048, 960], P('dp', 'ctx'), may hold values from -6 to 6
- weights: bfloat16 [10240, 960], P(('dp', 'ctx')), as said below
- gains: float32 [2, 960], replicated, may hold values from 0.25 to 1.75
- first_moment: float32 [10240, 960], P(('dp', 'ctx')), as said below
- second_moment: float32 [10240, 960], P(('dp', 'ctx')), as said below
- gain_first: float32 [2, 960], replicated, as said below
- gain_second: float32 [2, 960], replicated, as said below
Outputs:
- output: float32 [8, 2048, 960], P('dp', 'ctx')
- input_grad: float32 [8, 2048, 960], P('dp', 'ctx')
- weight_grad: float32 [10240, 960], P(('dp', 'ctx'))
- weight_second: float32 [10240, 960], P(('dp', 'ctx'))
- weight_new: float32 [10240, 960], P(('dp', 'ctx'))
- gain_grad: float32 [2, 960], replicated
- gain_second_new: float32 [2, 960], replicated
- gain_new: float32 [2, 960], replicated
Inputs may be any that keep to these rules, and one draw needn't show every extreme that they name: `weights`: independent entries; each of the seven matrices has its own scale of order its fan-in to the minus one half. `first_moment`: both signs, independent entries. `second_moment`: positive entries. `gain_first`: both signs, independent entries. `gain_second`: positive entries.
All inputs are finite; a program needn't handle non-finite values.
Results may differ from a plain program's by a relative error of at most 0.019.
Values may be sent and summed in bfloat16 or wider, within the bound.
No kernel may reach another device: no remote copies, remote signals or barrier semaphores. Data moves between devices by JAX's collectives and lax.ppermute only.
A program may use at most 176 MiB of HBM per device.

v0:
```python
import jax
import jax.numpy as jnp
from jax import lax
from jax.sharding import PartitionSpec as P

HEADS = 15
KV = 5
HD = 64
FF = 2560
MICRO = 2
STEP = 10


SCALE_QK = 0.125
THETA = 10000.0
EPSILON = 1e-05
BETA_ONE = 0.9
BETA_TWO = 0.95
ADAM_EPS = 1e-08
DECAY = 0.1
RATE = 0.02
GAIN_RATE = 0.2


def places(row_index, local_rows, ctx_count):
    half_rows = local_rows // 2
    owner_index = row_index // local_rows
    inner_index = row_index % local_rows
    return jnp.where(
        inner_index < half_rows,
        owner_index * half_rows + inner_index,
        (2 * ctx_count - 1 - owner_index) * half_rows + inner_index - half_rows,
    )


def rotate(values, positions_in, sign):
    half_width = values.shape[-1] // 2
    frequency = THETA ** (-jnp.arange(half_width, dtype=jnp.float32) * 2.0 / values.shape[-1])
    angles = positions_in.astype(jnp.float32)[:, None] * frequency[None, :]
    cosine = jnp.cos(angles)[:, None, :]
    sine_part = sign * jnp.sin(angles)[:, None, :]
    first_half = values[..., :half_width]
    second_half = values[..., half_width:]
    return jnp.concatenate(
        [
            first_half * cosine - second_half * sine_part,
            second_half * cosine + first_half * sine_part,
        ],
        axis=-1,
    )


def normalize(values):
    return values * lax.rsqrt(jnp.mean(values * values, axis=-1, keepdims=True) + EPSILON)


def norm_back(values, grad_in, gain_row):
    inv_scale = lax.rsqrt(jnp.mean(values * values, axis=-1, keepdims=True) + EPSILON)
    unit_rows = values * inv_scale
    grad_unit = grad_in * gain_row
    grad_values = inv_scale * (
        grad_unit - unit_rows * jnp.mean(grad_unit * unit_rows, axis=-1, keepdims=True)
    )
    return (grad_values, jnp.sum(grad_in * unit_rows, axis=0))


def matmul_n(left, right):
    return jnp.dot(left, right, preferred_element_type=jnp.float32)


def matmul_t(left, right):
    return lax.dot_general(
        left, right, (((1,), (1,)), ((), ())), preferred_element_type=jnp.float32
    )


def matmul_c(left, right):
    return lax.dot_general(
        left, right, (((0,), (0,)), ((), ())), preferred_element_type=jnp.float32
    )


def weight_terms(lefts, rights):
    return jnp.concatenate([matmul_c(lefts[member], rights[member]) for member in range(4)], axis=0)


def adam_update(param, grad, first, second, rate, decay, step_number):
    first_new = BETA_ONE * first + (1.0 - BETA_ONE) * grad
    second_new = BETA_TWO * second + (1.0 - BETA_TWO) * grad * grad
    fix_one = 1.0 - BETA_ONE**step_number
    fix_two = 1.0 - BETA_TWO**step_number
    update = first_new / fix_one / (jnp.sqrt(second_new / fix_two) + ADAM_EPS)
    return (first_new, second_new, param - rate * (update + decay * param))


def shards(inputs, cotangent, weights, gains, first_moment, second_moment, gain_first, gain_second):
    ctx_count = lax.axis_size("ctx")
    ctx_index = lax.axis_index("ctx")
    local_rows = inputs.shape[1]
    model_width = inputs.shape[2]
    q_cols = HEADS * HD
    kv_cols = KV * HD
    group_size = HEADS // KV
    cut_o = q_cols + 2 * kv_cols
    cut_g = cut_o + q_cols
    cut_d = cut_g + 2 * FF
    local_index = jnp.arange(local_rows, dtype=jnp.int32)
    pos_here = places(ctx_index * local_rows + local_index, local_rows, ctx_count)

    def to_heads(flat_rows):
        return flat_rows.reshape(local_rows, KV, group_size, HD).transpose(1, 2, 0, 3)

    def from_heads(split_rows):
        return split_rows.transpose(2, 0, 1, 3).reshape(local_rows, q_cols)

    outputs_list = []
    grads_list = []
    lefts_all = []
    rights_all = []
    gain_terms = jnp.zeros((2, model_width), jnp.float32)
    for micro_index in range(MICRO):
        gathered = lax.all_gather(weights, ("dp", "ctx"), axis=0, tiled=True)
        tokens_in = inputs[micro_index]
        cot_in = cotangent[micro_index]
        a_one = (normalize(tokens_in) * gains[0]).astype(jnp.bfloat16)
        qkv = matmul_t(a_one, gathered[:cut_o])
        q_rot = rotate(qkv[:, :q_cols].reshape(local_rows, HEADS, HD), pos_here, 1.0).astype(
            jnp.bfloat16
        )
        key_rot = rotate(
            qkv[:, q_cols : q_cols + kv_cols].reshape(local_rows, KV, HD), pos_here, 1.0
        )
        key_rot = key_rot.astype(jnp.bfloat16).reshape(local_rows, kv_cols)
        value_rows = qkv[:, q_cols + kv_cols :].astype(jnp.bfloat16)
        queries = to_heads(q_rot.reshape(local_rows, q_cols))

        def scores_of(key_piece):
            piece_rows = key_piece.shape[0]
            key_pos = places(jnp.arange(piece_rows, dtype=jnp.int32), local_rows, ctx_count)
            raw_scores = (
                jnp.einsum(
                    "kgqd,pkd->kgqp",
                    queries,
                    key_piece.reshape(piece_rows, KV, HD),
                    preferred_element_type=jnp.float32,
                )
                * SCALE_QK
            )
            visible = key_pos[None, None, None, :] <= pos_here[None, None, :, None]
            return (jnp.where(visible, raw_scores, -1e30), visible)

        running_max = jnp.full((KV, group_size, local_rows), -1e30, jnp.float32)
        attend_key_piece = lax.all_gather(key_rot, "ctx", axis=0, tiled=True)
        value_piece = lax.all_gather(value_rows, "ctx", axis=0, tiled=True)
        masked, attend_visible = scores_of(attend_key_piece)
        new_max = jnp.maximum(running_max, jnp.max(masked, axis=-1))
        expos = jnp.where(attend_visible, jnp.exp(masked - new_max[..., None]), 0.0)
        running_sum = jnp.sum(expos, axis=-1)
        weighted = jnp.einsum(
            "kgqp,pkd->kgqd",
            expos.astype(jnp.bfloat16),
            value_piece.reshape(value_piece.shape[0], KV, HD),
            preferred_element_type=jnp.float32,
        )
        running_max, running_sum, weighted = (new_max, running_sum, weighted)
        mixed = weighted / running_sum[..., None]
        log_total = running_max + jnp.log(running_sum)
        attn_low = from_heads(mixed).astype(jnp.bfloat16)
        resid = tokens_in + matmul_n(attn_low, gathered[cut_o:cut_g])
        a_two = (normalize(resid) * gains[1]).astype(jnp.bfloat16)
        gate_up = matmul_t(a_two, gathered[cut_g:cut_d])
        gate_pre = gate_up[:, :FF]
        up_pre = gate_up[:, FF:]
        gate_sigma = jax.nn.sigmoid(gate_pre)
        gate_act = gate_pre * gate_sigma
        hidden_act = (gate_act * up_pre).astype(jnp.bfloat16)
        result = resid + matmul_n(hidden_act, gathered[cut_d:])
        dy_low = cot_in.astype(jnp.bfloat16)
        d_hidden = matmul_t(dy_low, gathered[cut_d:])
        d_gate = d_hidden * up_pre * gate_sigma * (1.0 + gate_pre * (1.0 - gate_sigma))
        d_up = d_hidden * gate_act
        d_gu = jnp.concatenate([d_gate, d_up], axis=1).astype(jnp.bfloat16)
        d_two = matmul_n(d_gu, gathered[cut_g:cut_d])
        d_norm_two, d_gain_two = norm_back(resid, d_two, gains[1])
        d_resid = cot_in + d_norm_two
        d_resid_low = d_resid.astype(jnp.bfloat16)
        d_attn = matmul_t(d_resid_low, gathered[cut_o:cut_g]).astype(jnp.bfloat16)
        d_heads = to_heads(d_attn)
        row_delta = jnp.sum(d_heads.astype(jnp.float32) * mixed, axis=-1)

        def score_grads(key_piece, value_piece):
            piece_rows = key_piece.shape[0]
            masked, visible = scores_of(key_piece)
            probability = jnp.where(visible, jnp.exp(masked - log_total[..., None]), 0.0)
            d_prob = jnp.einsum(
                "kgqd,pkd->kgqp",
                d_heads,
                value_piece.reshape(piece_rows, KV, HD),
                preferred_element_type=jnp.float32,
            )
            d_score = (probability * (d_prob - row_delta[..., None])).astype(jnp.bfloat16)
            return (probability, d_score)

        back_key_piece = lax.all_gather(key_rot, "ctx", axis=0, tiled=True)
        back_value_piece = lax.all_gather(value_rows, "ctx", axis=0, tiled=True)
        back_piece_rows = back_key_piece.shape[0]
        back_probability, back_d_score = score_grads(back_key_piece, back_value_piece)
        d_q = SCALE_QK * jnp.einsum(
            "kgqp,pkd->kgqd",
            back_d_score,
            back_key_piece.reshape(back_piece_rows, KV, HD),
            preferred_element_type=jnp.float32,
        )
        joined_rows = jnp.concatenate([key_rot, value_rows], axis=1)
        joined_piece = lax.all_gather(joined_rows, "ctx", axis=0, tiled=True)
        kv_piece_rows = joined_piece.shape[0]
        kv_key_piece = joined_piece[:, :kv_cols]
        kv_value_piece = joined_piece[:, kv_cols:]
        kv_probability, kv_d_score = score_grads(kv_key_piece, kv_value_piece)
        key_part = SCALE_QK * jnp.einsum(
            "kgqp,kgqd->pkd", kv_d_score, queries, preferred_element_type=jnp.float32
        )
        value_part = jnp.einsum(
            "kgqp,kgqd->pkd",
            kv_probability.astype(jnp.bfloat16),
            d_heads,
            preferred_element_type=jnp.float32,
        )
        kv_terms = jnp.concatenate(
            [key_part.reshape(kv_piece_rows, kv_cols), value_part.reshape(kv_piece_rows, kv_cols)],
            axis=1,
        )
        d_kv = lax.psum_scatter(
            kv_terms.astype(jnp.bfloat16), "ctx", scatter_dimension=0, tiled=True
        ).astype(jnp.float32)
        d_k = d_kv[:, :kv_cols]
        d_v = d_kv[:, kv_cols:]
        dq_pre = rotate(from_heads(d_q).reshape(local_rows, HEADS, HD), pos_here, -1.0).reshape(
            local_rows, q_cols
        )
        dk_pre = rotate(d_k.reshape(local_rows, KV, HD), pos_here, -1.0).reshape(
            local_rows, kv_cols
        )
        d_qkv = jnp.concatenate([dq_pre, dk_pre, d_v], axis=1).astype(jnp.bfloat16)
        d_one = matmul_n(d_qkv, gathered[:cut_o])
        d_norm_one, d_gain_one = norm_back(tokens_in, d_one, gains[0])
        d_tokens = d_resid + d_norm_one
        lefts = (d_qkv, attn_low, d_gu, hidden_act)
        rights = (a_one, d_resid_low, a_two, dy_low)
        result, d_tokens, lefts, rights, gain_part = (
            result,
            d_tokens,
            lefts,
            rights,
            jnp.stack([d_gain_one, d_gain_two], axis=0),
        )
        outputs_list.append(result)
        grads_list.append(d_tokens)
        gain_terms = gain_terms + gain_part
        lefts_all.append(lefts)
        rights_all.append(rights)
    lefts_joined = [
        jnp.concatenate([entry[member] for entry in lefts_all], axis=0) for member in range(4)
    ]
    rights_joined = [
        jnp.concatenate([entry[member] for entry in rights_all], axis=0) for member in range(4)
    ]
    weight_share = lax.psum_scatter(
        weight_terms(lefts_joined, rights_joined), ("dp", "ctx"), scatter_dimension=0, tiled=True
    )
    gain_grad = lax.psum(gain_terms, ("dp", "ctx"))
    weight_first, weight_second, weight_new = adam_update(
        weights.astype(jnp.float32), weight_share, first_moment, second_moment, RATE, DECAY, STEP
    )
    gain_first_new, gain_second_new, gain_new = adam_update(
        gains, gain_grad, gain_first, gain_second, GAIN_RATE, 0.0, STEP
    )
    return (
        jnp.stack(outputs_list, axis=0),
        jnp.stack(grads_list, axis=0),
        weight_share,
        weight_second,
        weight_new,
        gain_grad,
        gain_second_new,
        gain_new,
    )


def solution(mesh):
    placed = (
        P("dp", "ctx", None),
        P("dp", "ctx", None),
        P(("dp", "ctx"), None),
        P(),
        P(("dp", "ctx"), None),
        P(("dp", "ctx"), None),
        P(),
        P(),
    )
    return jax.shard_map(
        shards,
        mesh=mesh,
        in_specs=placed,
        out_specs=(
            P("dp", "ctx", None),
            P("dp", "ctx", None),
            P(("dp", "ctx"), None),
            P(("dp", "ctx"), None),
            P(("dp", "ctx"), None),
            P(),
            P(),
            P(),
        ),
        check_vma=False,
    )
```

profile of v0, /device:TPU:0, one launch (start us, length us, event | category | flops | bytes accessed | tf_op | source)
XLA Modules:
  0.0 1577.5 jit_solution(17241494769161515159)
XLA Ops:
  12.2 136.0 %all-gather.8.cloned.1.call-done = bf16[10240,960]{1,0:T(8,128)(2,1)} async-done(((bf16[320,960]{1,0:T(8,128)(2,1)}), bf16[10240,960]{1,0:T(8,128)(2,1)}) %all-gather.8.cloned.1.call-update) | async-done | bytes 19660816 | tf_op jit(solution)/shard_map/all_gather | solution.py:122
  171.1 26.7 %all-gather.10.cloned.1.call-done = bf16[2048,320]{0,1:T(8,128)(2,1)} async-done(((bf16[256,320]{0,1:T(8,128)(2,1)}), bf16[2048,320]{0,1:T(8,128)(2,1)}) %all-gather.10.cloned.1.call-update) | async-done | bytes 1310736 | tf_op jit(solution)/shard_map/all_gather | solution.py:153
  197.8 14.5 fusion.6
  212.4 29.1 %all-gather.14.cloned.1.call-done = bf16[2048,320]{0,1:T(8,128)(2,1)} async-done(((bf16[256,320]{0,1:T(8,128)(2,1)}), bf16[2048,320]{0,1:T(8,128)(2,1)}) %all-gather.14.cloned.1.call-update) | async-done | bytes 1310736 | tf_op jit(solution)/shard_map/all_gather | solution.py:153
  241.4 29.5 %fusion = (f32[5,3,256]{2,1,0:T(4,128)S(1)}, f32[5,3,256]{2,1,0:T(4,128)S(1)}, f32[5,3,256,2048]{3,2,1,0:T(8,128)}) fusion(f32[5,3,256,2048]{3,2,1,0:T(8,128)} %get-tuple-element.99, f32[5,3,256]{2,1,0:T(4,128)S(1)} %broadcast_maximum_fusion.1, pred[256,2048]{1,0:T(8,128)(4,1)S(1)} %broadcast_compare_fusion, bf16[2048,5,64,1]{0,2,3,1:T(8,128)(2,1)} %bitcast.276, ...), kind=kOutput, calls=%fused_computation.10 | convolution fusion | flops 1070522880 | bytes 65287168 | tf_op jit(solution)/shard_map/kgqd,pkd->kgqp/dot_general | solution.py:141
  271.6 12.7 all-gather.12.cloned.1.call-done
  284.3 15.8 %fusion.137 = (bf16[256,5,3,64]{0,3,2,1:T(8,128)(2,1)}, f32[5,3,256,64]{2,3,1,0:T(8,128)}) fusion(f32[256,5,3]{0,2,1:T(4,128)S(1)} %bitcast.262, bf16[2048,5,64,1]{0,2,3,1:T(8,128)(2,1)} %bitcast.278, f32[5,3,256,2048]{3,2,1,0:T(8,128)} %get-tuple-element.99, f32[5,3,256]{2,1,0:T(4,128)S(1)} %broadcast_maximum_fusion.1, ...), kind=kOutput, calls=%fused_computation.155 | convolution fusion | flops 1046446080 | bytes 34797568 | tf_op jit(solution)/shard_map/kgqp,pkd->kgqd/dot_general | solution.py:159
  303.4 15.2 fusion.2
  319.2 8.0 all-gather.16.cloned.1.call-done
  327.2 15.5 fusion.135
  345.6 6.1 fusion.30
  351.7 6.3 multiply_convert_fusion.7
  358.0 8.9 multiply_reduce_fusion.2
  367.0 5.9 fusion.28
  372.9 6.5 multiply_convert_fusion.5
  379.4 8.7 multiply_reduce_fusion
  398.6 12.7 fusion.151
  411.3 14.2 fusion.61
  425.5 18.1 %fusion.64 = bf16[5,64,2048]{2,1,0:T(8,128)(2,1)} fusion(f32[5,3,256,2048]{3,2,1,0:T(8,128)} %fusion.151, bf16[5,3,256,64]{2,3,1,0:T(8,128)(2,1)} %bitcast.250, bf16[2048,5,64,1]{0,2,3,1:T(8,128)(2,1)S(1)} %bitcast.221, f32[5,3,256]{2,1,0:T(4,128)S(1)} %multiply_reduce_fusion.8, f32[5,3,256]{2,1,0:T(4,128)S(1)} %copy-done.63, ...), kind=kOutput, calls=%fused_computation.62 | convolution fusion | flops 2070609920 | bytes 35616768 | tf_op jit(solution)/shard_map/kgqp,kgqd->pkd/dot_general | solution.py:220
  448.8 13.0 fusion.149
  461.8 14.3 fusion.58
  476.1 18.1 %fusion.65 = bf16[5,64,2048]{2,1,0:T(8,128)(2,1)} fusion(f32[5,3,256,2048]{3,2,1,0:T(8,128)} %fusion.149, bf16[5,3,256,64]{2,3,1,0:T(8,128)(2,1)} %bitcast.254, bf16[2048,5,64,1]{0,2,3,1:T(8,128)(2,1)S(1)} %bitcast.222, f32[5,3,256]{2,1,0:T(4,128)S(1)} %multiply_reduce_fusion.5, f32[5,3,256]{2,1,0:T(4,128)S(1)} %copy-done.64, ...), kind=kOutput, calls=%fused_computation.63 | convolution fusion | flops 2070609920 | bytes 35616768 | tf_op jit(solution)/shard_map/kgqp,kgqd->pkd/dot_general | solution.py:220
  497.3 19.8 %fusion.101 = f32[5,3,256,64]{2,3,1,0:T(8,128)S(1)} fusion(bf16[2048,5,64,1]{0,2,3,1:T(8,128)(2,1)} %bitcast.277, f32[5,3,256,2048]{3,2,1,0:T(8,128)} %get-tuple-element.100, bf16[5,3,256,64]{2,3,1,0:T(8,128)(2,1)} %bitcast.255, bf16[2048,5,64,1]{0,2,3,1:T(8,128)(2,1)} %bitcast.281, f32[5,3,256]{2,1,0:T(4,128)S(1)} %multiply_reduce_fusion.5, ...), kind=kOutput, calls=%fused_computation.116 | convolution fusion | flops 2068561920 | bytes 36108288 | tf_op jit(solution)/shard_map/kgqp,pkd->kgqd/dot_general | solution.py:208
  517.2 19.5 %fusion.102 = f32[5,3,256,64]{2,3,1,0:T(8,128)S(1)} fusion(bf16[2048,5,64,1]{0,2,3,1:T(8,128)(2,1)} %bitcast.275, f32[5,3,256,2048]{3,2,1,0:T(8,128)} %get-tuple-element.99, bf16[5,3,256,64]{2,3,1,0:T(8,128)(2,1)S(1)} %bitcast.252, bf16[2048,5,64,1]{0,2,3,1:T(8,128)(2,1)} %bitcast.279, f32[5,3,256]{2,1,0:T(4,128)S(1)} %multiply_reduce_fusion.8, ...), kind=kOutput, calls=%fused_computation.117 | convolution fusion | flops 2068561920 | bytes 36108288 | tf_op jit(solution)/shard_map/kgqp,pkd->kgqd/dot_general | solution.py:208
  541.6 5.3 fusion.72
  546.9 26.1 %fusion.32 = f32[5120,960]{0,1:T(8,128)} fusion(bf16[256,2560]{1,0:T(8,128)(2,1)S(1)} %copy-done.85, bf16[256,2560]{1,0:T(8,128)(2,1)S(1)} %copy-done.84, bf16[256,2560]{1,0:T(8,128)(2,1)S(1)} %copy-done.82, bf16[256,2560]{1,0:T(8,128)(2,1)S(1)} %copy-done.80, bf16[256,960]{0,1:T(8,128)(2,1)S(1)} %copy-done.87, bf16[256,960]{0,1:T(8,128)(2,1)S(1)} %copy-done.31), kind=kOutput, calls=%fused_computation.38 | convolution fusion | flops 5056102400 | bytes 25886720 | tf_op jit(solution)/shard_map/dot_general | solution.py:78
  574.3 15.2 reduce-scatter.8.cloned.1.call-done
  596.1 41.1 %concatenate.127 = f32[10240,960]{0,1:T(8,128)} concatenate(f32[1600,960]{0,1:T(8,128)} %fusion.86, f32[960,960]{0,1:T(8,128)} %fusion.122, f32[5120,960]{0,1:T(8,128)} %fusion.32, f32[2560,960]{0,1:T(8,128)} %fusion.72), dimensions={0} | concatenate | bytes 78643200 | tf_op jit(solution)/shard_map/concatenate | solution.py:84
  637.1 40.9 %copy.40 = f32[10240,960]{1,0:T(8,128)} copy(f32[10240,960]{0,1:T(8,128)} %concatenate.127) | data formatting | bytes 78643200
  685.2 5.2 fusion.106
  705.1 49.8 %psum.7 = f32[2,960]{1,0:T(2,128)S(1)} all-reduce(f32[2,960]{1,0:T(2,128)S(1)} %maximum_add_fusion), channel_id=1, replica_groups=mesh['dp'=4,'ctx'=8] {'dp','ctx'}, use_global_device_ids=true, to_apply=%region_21.22 | all-reduce | flops 1920 | bytes 15360 | tf_op jit(solution)/shard_map/psum | solution.py:271
  759.6 799.1 %reduce-scatter.10.cloned.1.call-done = f32[320,960]{1,0:T(8,128)} async-done(((f32[10240,960]{1,0:T(8,128)}), f32[320,960]{1,0:T(8,128)}) %reduce-scatter.10.cloned.1.call-update) | async-done | bytes 1228816
  (274 shorter events, 104.3 us)
Async XLA Ops:
  7.2 141.0 %all-gather.8.cloned.1.call-start = ((), (), s32[]{:S(2)}) async-start(), calls=%async_computation.3 | async-start | bytes 21626880 | tf_op jit(solution)/shard_map/all_gather | solution.py:122
  7.9 189.9 %all-gather.10.cloned.1.call-start = ((), (), s32[]{:S(2)}) async-start(), calls=%async_computation.4 | async-start | bytes 1474560 | tf_op jit(solution)/shard_map/all_gather | solution.py:153
  9.7 141.4 %copy-start.65 = (f32[256]{0:T(256)}, f32[256]{0:T(256)S(1)}, u32[]{:S(2)}) copy-start(f32[256]{0:T(256)S(1)} %get-tuple-element.112) | copy-start | bytes 3076
  9.7 141.4 %copy-start.67 = (f32[256]{0:T(256)}, f32[256]{0:T(256)S(1)}, u32[]{:S(2)}) copy-start(f32[256]{0:T(256)S(1)} %get-tuple-element.113) | copy-start | bytes 3076
  11.1 140.0 %copy-start.59 = (f32[1,960]{1,0:T(1,128)}, f32[1,960]{1,0:T(1,128)S(1)}, u32[]{:S(2)}) copy-start(f32[1,960]{1,0:T(1,128)S(1)} %get-tuple-element.93) | copy-start | bytes 11524
  11.9 156.4 %copy-start.24 = (f32[256,32]{0,1:T(8,128)}, f32[256,32]{0,1:T(8,128)S(1)}, u32[]{:S(2)}) copy-start(f32[256,32]{0,1:T(8,128)S(1)} %get-tuple-element.97) | copy-start | bytes 98308
  12.1 139.0 %copy-start.28 = (bf16[256,960]{0,1:T(8,128)(2,1)}, bf16[256,960]{0,1:T(8,128)(2,1)S(1)}, u32[]{:S(2)}) copy-start(bf16[256,960]{0,1:T(8,128)(2,1)S(1)} %get-tuple-element.61) | copy-start | bytes 1474564
  12.2 140.1 %copy-start.26 = (bf16[256,960]{0,1:T(8,128)(2,1)}, bf16[256,960]{0,1:T(8,128)(2,1)S(1)}, u32[]{:S(2)}) copy-start(bf16[256,960]{0,1:T(8,128)(2,1)S(1)} %get-tuple-element.60) | copy-start | bytes 1474564
  157.2 84.2 %all-gather.14.cloned.1.call-start = ((), (), s32[]{:S(2)}) async-start(), calls=%async_computation.6 | async-start | bytes 1474560 | tf_op jit(solution)/shard_map/all_gather | solution.py:153
  158.0 126.3 %all-gather.12.cloned.1.call-start = ((), (), s32[]{:S(2)}) async-start(), calls=%async_computation.5 | async-start | bytes 1474560 | tf_op jit(solution)/shard_map/all_gather | solution.py:154
  159.7 167.4 %all-gather.16.cloned.1.call-start = ((), (), s32[]{:S(2)}) async-start(), calls=%async_computation.7 | async-start | bytes 1474560 | tf_op jit(solution)/shard_map/all_gather | solution.py:154
  161.5 235.1 %all-gather.18.cloned.1.call-start = ((), (), s32[]{:S(2)}) async-start(), calls=%async_computation.8 | async-start | bytes 2949120 | tf_op jit(solution)/shard_map/all_gather | solution.py:215
  163.3 283.4 %all-gather.20.cloned.1.call-start = ((), (), s32[]{:S(2)}) async-start(), calls=%async_computation.10 | async-start | bytes 2949120 | tf_op jit(solution)/shard_map/all_gather | solution.py:215
  170.8 402.4 %reduce-scatter.6.cloned.1.call-start = ((), (), s32[]{:S(2)}) async-start(), calls=%async_computation.9 | async-start | bytes 2949120 | tf_op jit(solution)/shard_map/reduce_scatter | solution.py:233
  197.8 43.6 %copy-start.13 = (bf16[256,15,32]{0,2,1:T(8,128)(2,1)S(1)}, bf16[256,15,32]{0,2,1:T(8,128)(2,1)}, u32[]{:S(2)}) copy-start(bf16[256,15,32]{0,2,1:T(8,128)(2,1)} %get-tuple-element.88) | copy-start | bytes 737284
  197.8 43.6 %copy-start.15 = (bf16[256,15,32]{0,2,1:T(8,128)(2,1)S(1)}, bf16[256,15,32]{0,2,1:T(8,128)(2,1)}, u32[]{:S(2)}) copy-start(bf16[256,15,32]{0,2,1:T(8,128)(2,1)} %get-tuple-element.89) | copy-start | bytes 737284
  302.8 85.4 %copy-start.5 = (f32[256,960]{0,1:T(8,128)}, f32[256,960]{0,1:T(8,128)S(1)}, u32[]{:S(2)}) copy-start(f32[256,960]{0,1:T(8,128)S(1)} %get-tuple-element.106) | copy-start | bytes 2949124
  345.3 42.8 %copy-start.19 = (f32[256,960]{0,1:T(8,128)}, f32[256,960]{0,1:T(8,128)S(1)}, u32[]{:S(2)}) copy-start(f32[256,960]{0,1:T(8,128)S(1)} %get-tuple-element.108) | copy-start | bytes 2949124
  398.6 12.7 copy-start.41
  446.6 142.8 %reduce-scatter.8.cloned.1.call-start = ((), (), s32[]{:S(2)}) async-start(), calls=%async_computation.11 | async-start | bytes 2949120 | tf_op jit(solution)/shard_map/reduce_scatter | solution.py:233
  448.8 13.0 copy-start.44
  448.8 13.0 copy-start.64
  497.3 19.9 %copy-start.42 = (bf16[256,960]{0,1:T(8,128)(2,1)S(1)}, bf16[256,960]{0,1:T(8,128)(2,1)}, u32[]{:S(2)}) copy-start(bf16[256,960]{0,1:T(8,128)(2,1)} %copy-done.40) | copy-start | bytes 1474564
  497.3 1061.4 %reduce-scatter.10.cloned.1.call-start = ((), (), s32[]{:S(2)}) async-start(), calls=%async_computation.12 | async-start | bytes 43253760
  517.2 19.5 %copy-start.25 = (f32[256,32]{0,1:T(8,128)S(1)}, f32[256,32]{0,1:T(8,128)}, u32[]{:S(2)}) copy-start(f32[256,32]{0,1:T(8,128)} %copy-done.24) | copy-start | bytes 98308
  517.2 19.5 %copy-start.49 = (f32[256,32]{0,1:T(8,128)S(1)}, f32[256,32]{0,1:T(8,128)}, u32[]{:S(2)}) copy-start(f32[256,32]{0,1:T(8,128)} %get-tuple-element.95) | copy-start | bytes 98308
  537.1 53.6 %copy-start.36 = (bf16[256,15,64]{0,2,1:T(8,128)(2,1)}, bf16[256,15,64]{0,2,1:T(8,128)(2,1)S(1)}, u32[]{:S(2)}) copy-start(bf16[256,15,64]{0,2,1:T(8,128)(2,1)S(1)} %pad_maximum_fusion.4) | copy-start | bytes 1474564
  538.3 52.4 %copy-start.38 = (bf16[256,15,64]{0,2,1:T(8,128)(2,1)}, bf16[256,15,64]{0,2,1:T(8,128)(2,1)S(1)}, u32[]{:S(2)}) copy-start(bf16[256,15,64]{0,2,1:T(8,128)(2,1)S(1)} %pad_maximum_fusion.5) | copy-start | bytes 1474564
  573.1 18.3 %copy-start.27 = (bf16[256,960]{0,1:T(8,128)(2,1)S(1)}, bf16[256,960]{0,1:T(8,128)(2,1)}, u32[]{:S(2)}) copy-start(bf16[256,960]{0,1:T(8,128)(2,1)} %copy-done.26) | copy-start | bytes 1474564
  573.1 18.3 %copy-start.29 = (bf16[256,960]{0,1:T(8,128)(2,1)S(1)}, bf16[256,960]{0,1:T(8,128)(2,1)}, u32[]{:S(2)}) copy-start(bf16[256,960]{0,1:T(8,128)(2,1)} %copy-done.28) | copy-start | bytes 1474564
  574.3 21.8 %copy-start.50 = (bf16[256,320]{0,1:T(8,128)(2,1)}, bf16[256,320]{0,1:T(8,128)(2,1)S(1)}, u32[]{:S(2)}) copy-start(bf16[256,320]{0,1:T(8,128)(2,1)S(1)} %get-tuple-element.81) | copy-start | bytes 491524
  757.5 804.1 %copy-start.2 = (f32[320,960]{0,1:T(8,128)S(1)}, f32[320,960]{0,1:T(8,128)}, u32[]{:S(2)}) copy-start(f32[320,960]{0,1:T(8,128)} %copy.24) | copy-start | bytes 3686404
  (67 other events, 254.1 us)
Sparse Core Ops, SparseCore 0:
  10.9 137.2 all-gather.7
  157.4 40.4 all-gather.9
  200.5 40.9 all-gather.13
  243.3 40.9 all-gather.11
  286.2 40.9 all-gather.15
  329.1 55.5 all-gather.17
  386.7 55.0 all-gather.19
  446.7 69.3 reduce-scatter.5
  519.7 69.7 reduce-scatter.7
  678.1 880.5 reduce-scatter.9
where the time goes:
time: 1580 us
  waiting for transfers between devices  1030 us (65%)
  matrix products  321 us (20%)
  local copies, waits for them, and re-layouts  117 us (7%)
  blocking collectives  49.8 us (3%)
  other arithmetic  45.9 us (3%)
    unnamed x11, waiting for transfers between devices  800 us
    all_gather x1, waiting for transfers between devices, shards(): gathered = lax.all_gather(weights, ('dp', 'ctx'), axis=0, tiled=True)  136 us
    dot_general x4, matrix products, scores_of(): jnp.einsum('kgqd,pkd->kgqp', queries, key_piece.reshape(piece_rows, KV, H...  69.7 us
    unnamed x183, local copies, waits for them, and re-layouts  61.3 us
    all_gather x2, waiting for transfers between devices, shards(): attend_key_piece = lax.all_gather(key_rot, 'ctx', axis=0, tiled=True)  55.8 us
    psum x1, blocking collectives, shards(): gain_grad = lax.psum(gain_terms, ('dp', 'ctx'))  49.8 us
    dot_general x8, matrix products, matmul_n(): return jnp.dot(left, right, preferred_element_type=jnp.float32)  41.1 us
    concatenate x1, local copies, waits for them, and re-layouts, weight_terms(): jnp.concatenate([matmul_c(lefts[member], rights[member]) for member in ra...  41.1 us
  transfers between devices with their start and end apart: 10, of which 7 were waited for; matrix products, arithmetic and copies ran while one was open for 23% of the time, Pallas kernels for 0%

commit v1 on v0

--- a/solution.py
+++ b/solution.py
@@ -80,8 +80,72 @@
     )
 
 
-def weight_terms(lefts, rights):
-    return jnp.concatenate([matmul_c(lefts[member], rights[member]) for member in range(4)], axis=0)
+def axis_bits():
+    dp_bits = lax.axis_size("dp").bit_length() - 1
+    ctx_bits = lax.axis_size("ctx").bit_length() - 1
+    low_ctx = ctx_bits // 2
+    core = [("dp", 0)]
+    along_x = [("dp", bit) for bit in range(1, dp_bits)]
+    along_y = [("ctx", bit) for bit in range(low_ctx)]
+    along_z = [("ctx", bit) for bit in range(low_ctx, ctx_bits)]
+    return core, along_x, along_y, along_z
+
+
+def swap(values, where):
+    axis, bit = where
+    size = lax.axis_size(axis)
+    return lax.ppermute(values, axis, [(i, i ^ (1 << bit)) for i in range(size)])
+
+
+def my_bit(where):
+    axis, bit = where
+    return (lax.axis_index(axis) >> bit) & 1
+
+
+def halve(values, bits, where, last):
+    dim = bits.index(where)
+    mine = my_bit(where)
+    away = lax.dynamic_index_in_dim(values, 1 - mine, dim, keepdims=False)
+    keep = lax.dynamic_index_in_dim(values, mine, dim, keepdims=False)
+    total = keep.astype(jnp.float32) + swap(away, where).astype(jnp.float32)
+    rest = [b for b in bits if b != where]
+    return (total if last else total.astype(jnp.bfloat16)), rest
+
+
+def scatter_sum(terms):
+    core, along_x, along_y, along_z = axis_bits()
+    dp_count, ctx_count = lax.axis_size("dp"), lax.axis_size("ctx")
+    everything = jnp.concatenate(terms, axis=0)
+    rows = everything.shape[0] // (dp_count * ctx_count)
+    width = everything.shape[1]
+    first = -(-rows // 48) * 16
+    cuts = [(0, first), (first, 2 * first), (2 * first, rows)]
+    bits = [("dp", b) for b in reversed(range(dp_count.bit_length() - 1))]
+    bits += [("ctx", b) for b in reversed(range(ctx_count.bit_length() - 1))]
+    values, rest = halve(
+        everything.reshape([2] * len(bits) + [rows, width]), bits, core[0], False
+    )
+    orders = [
+        along_x + along_y + along_z,
+        along_y + along_z + along_x,
+        along_z + along_x + along_y,
+    ]
+    done = []
+    states = [(values[..., low:high, :], rest) for low, high in cuts]
+    for step in range(len(orders[0])):
+        last = step == len(orders[0]) - 1
+        states = [
+            halve(part, left, orders[member][step], last)
+            for member, (part, left) in enumerate(states)
+        ]
+    return jnp.concatenate([part for part, _ in states], axis=0)
+
+
+def butterfly_sum(values):
+    core, along_x, along_y, along_z = axis_bits()
+    for where in core + along_x + along_y + along_z:
+        values = values + swap(values, where)
+    return values
 
 
 def adam_update(param, grad, first, second, rate, decay, step_number):
@@ -118,8 +182,8 @@
     lefts_all = []
     rights_all = []
     gain_terms = jnp.zeros((2, model_width), jnp.float32)
+    gathered = lax.all_gather(weights, ("dp", "ctx"), axis=0, tiled=True)
     for micro_index in range(MICRO):
-        gathered = lax.all_gather(weights, ("dp", "ctx"), axis=0, tiled=True)
         tokens_in = inputs[micro_index]
         cot_in = cotangent[micro_index]
         a_one = (normalize(tokens_in) * gains[0]).astype(jnp.bfloat16)
@@ -150,8 +214,10 @@
             return (jnp.where(visible, raw_scores, -1e30), visible)
 
         running_max = jnp.full((KV, group_size, local_rows), -1e30, jnp.float32)
-        attend_key_piece = lax.all_gather(key_rot, "ctx", axis=0, tiled=True)
-        value_piece = lax.all_gather(value_rows, "ctx", axis=0, tiled=True)
+        joined_rows = jnp.concatenate([key_rot, value_rows], axis=1)
+        joined_piece = lax.all_gather(joined_rows, "ctx", axis=0, tiled=True)
+        attend_key_piece = joined_piece[:, :kv_cols]
+        value_piece = joined_piece[:, kv_cols:]
         masked, attend_visible = scores_of(attend_key_piece)
         new_max = jnp.maximum(running_max, jnp.max(masked, axis=-1))
         expos = jnp.where(attend_visible, jnp.exp(masked - new_max[..., None]), 0.0)
@@ -201,22 +267,14 @@
             d_score = (probability * (d_prob - row_delta[..., None])).astype(jnp.bfloat16)
             return (probability, d_score)
 
-        back_key_piece = lax.all_gather(key_rot, "ctx", axis=0, tiled=True)
-        back_value_piece = lax.all_gather(value_rows, "ctx", axis=0, tiled=True)
-        back_piece_rows = back_key_piece.shape[0]
-        back_probability, back_d_score = score_grads(back_key_piece, back_value_piece)
+        kv_piece_rows = joined_piece.shape[0]
+        kv_probability, kv_d_score = score_grads(attend_key_piece, value_piece)
         d_q = SCALE_QK * jnp.einsum(
             "kgqp,pkd->kgqd",
-            back_d_score,
-            back_key_piece.reshape(back_piece_rows, KV, HD),
+            kv_d_score,
+            attend_key_piece.reshape(kv_piece_rows, KV, HD),
             preferred_element_type=jnp.float32,
         )
-        joined_rows = jnp.concatenate([key_rot, value_rows], axis=1)
-        joined_piece = lax.all_gather(joined_rows, "ctx", axis=0, tiled=True)
-        kv_piece_rows = joined_piece.shape[0]
-        kv_key_piece = joined_piece[:, :kv_cols]
-        kv_value_piece = joined_piece[:, kv_cols:]
-        kv_probability, kv_d_score = score_grads(kv_key_piece, kv_value_piece)
         key_part = SCALE_QK * jnp.einsum(
             "kgqp,kgqd->pkd", kv_d_score, queries, preferred_element_type=jnp.float32
         )
@@ -265,10 +323,13 @@
     rights_joined = [
         jnp.concatenate([entry[member] for entry in rights_all], axis=0) for member in range(4)
     ]
-    weight_share = lax.psum_scatter(
-        weight_terms(lefts_joined, rights_joined), ("dp", "ctx"), scatter_dimension=0, tiled=True
-    )
-    gain_grad = lax.psum(gain_terms, ("dp", "ctx"))
+    weight_share = scatter_sum(
+        [
+            matmul_c(lefts_joined[member], rights_joined[member]).astype(jnp.bfloat16)
+            for member in range(4)
+        ]
+    )
+    gain_grad = butterfly_sum(gain_terms)
     weight_first, weight_second, weight_new = adam_update(
         weights.astype(jnp.float32), weight_share, first_moment, second_moment, RATE, DECAY, STEP
     )

time: 1580 us -> 829 us (0.52)
  waiting for transfers between devices: 1030 us -> 387 us
  matrix products: 321 us -> 255 us
  blocking collectives: 49.8 us -> 0 us
  local copies, waits for them, and re-layouts: 117 us -> 91.6 us
  starting transfers between devices: 0.7 us -> 17.3 us
    unnamed x11 -> x5, waiting for transfers between devices: 800 us -> 0.75 us
    ppermute x0 -> x18, waiting for transfers between devices: none -> 103 us  [swap(): return lax.ppermute(values, axis, [(i, i ^ 1 << bit) for i in range(size)])]
    all_gather x2, waiting for transfers between devices: 0.04 us -> 89.8 us  [shards(): joined_piece = lax.all_gather(joined_rows, 'ctx', axis=0, tiled=True)]
    all_gather x4 -> x0, waiting for transfers between devices: 76.5 us -> none  [the longest x2 55.8 us: shards(): attend_key_piece = lax.all_gather(key_rot, 'ctx', axis=0, tiled=True)]
    unnamed x183 -> x177, local copies, waits for them, and re-layouts: 61.3 us -> 5.99 us
    psum x1 -> x0, blocking collectives: 49.8 us -> none  [shards(): gain_grad = lax.psum(gain_terms, ('dp', 'ctx'))]
    dot_general x4 -> x2, matrix products: 69.7 us -> 26.6 us  [scores_of(): jnp.einsum('kgqd,pkd->kgqp', queries, key_piece.reshape(piece_rows, KV, H...]
    reduce_scatter x2, waiting for transfers between devices: 15.2 us -> 56 us  [shards(): lax.psum_scatter(kv_terms.astype(jnp.bfloat16), 'ctx', scatter_dimension=...]
  transfers between devices with their start and end apart: 10 -> 23, of which waited for: 7 -> 17; matrix products, arithmetic and copies ran while one was open for 23% -> 18% of each run, Pallas kernels for 0% -> 0%
where the time goes in v1:
time: 829 us; the launch traced here: 824 us
  waiting for transfers between devices  387 us (47%)
  matrix products  255 us (31%)
  local copies, waits for them, and re-layouts  91.6 us (11%)
  other arithmetic  57.5 us (7%)
  starting transfers between devices  17.3 us (2%)
  between operations  15.5 us (2%)
    all_gather x1, waiting for transfers between devices, shards(): gathered = lax.all_gather(weights, ('dp', 'ctx'), axis=0, tiled=True)  137 us
    ppermute x18, waiting for transfers between devices, swap(): return lax.ppermute(values, axis, [(i, i ^ 1 << bit) for i in range(size)])  103 us
    all_gather x2, waiting for transfers between devices, shards(): joined_piece = lax.all_gather(joined_rows, 'ctx', axis=0, tiled=True)  89.8 us
    concatenate x2, local copies, waits for them, and re-layouts, scatter_sum(): everything = jnp.concatenate(terms, axis=0)  56.8 us
    reduce_scatter x2, waiting for transfers between devices, shards(): lax.psum_scatter(kv_terms.astype(jnp.bfloat16), 'ctx', scatter_dimension=...  56 us
    dot_general x2, matrix products, score_grads(): jnp.einsum('kgqd,pkd->kgqp', d_heads, value_piece.reshape(piece_rows, KV,...  42.3 us
    dot_general x8, matrix products, matmul_n(): return jnp.dot(left, right, preferred_element_type=jnp.float32)  41.2 us
    dot_general x8, matrix products, matmul_t(): lax.dot_general(left, right, (((1,), (1,)), ((), ())), preferred_element_...  36 us
  transfers between devices with their start and end apart: 23, of which 17 were waited for; matrix products, arithmetic and copies ran while one was open for 18% of the time, Pallas kernels for 0%

profile of v1, /device:TPU:0, one launch (start us, length us, event | category | flops | bytes accessed | tf_op | source)
XLA Modules:
  0.0 823.6 jit_solution(12146945210968247376)
XLA Ops:
  10.9 137.3 %all-gather.4.cloned.1.call-done = bf16[10240,960]{1,0:T(8,128)(2,1)} async-done(((bf16[320,960]{1,0:T(8,128)(2,1)}), bf16[10240,960]{1,0:T(8,128)(2,1)}) %all-gather.4.cloned.1.call-update) | async-done | bytes 19660816 | tf_op jit(solution)/shard_map/all_gather | solution.py:185
  163.8 48.8 %all-gather.8.cloned.1.call-done = bf16[2048,640]{0,1:T(8,128)(2,1)} async-done(((bf16[256,640]{0,1:T(8,128)(2,1)}), bf16[2048,640]{0,1:T(8,128)(2,1)}) %all-gather.8.cloned.1.call-update) | async-done | bytes 2621456 | tf_op jit(solution)/shard_map/all_gather | solution.py:218
  215.5 13.6 %fusion.188 = (f32[5,3,256]{2,1,0:T(4,128)S(1)}, f32[5,3,256,2048]{3,2,1,0:T(8,128)}) fusion(bf16[2048,5,64,1]{0,2,3,1:T(8,128)(2,1)S(1)} %bitcast.261, bf16[256,5,3,32]{0,3,2,1:T(8,128)(2,1)S(1)} %bitcast.284, bf16[256,5,3,32]{0,3,2,1:T(8,128)(2,1)S(1)} %bitcast.286, pred[256,2048]{1,0:T(8,128)(4,1)S(1)} %broadcast_compare_fusion), kind=kOutput, calls=%fused_computation.317 | convolution fusion | flops 1031205120 | bytes 33799168 | tf_op jit(solution)/shard_map/kgqd,pkd->kgqp/dot_general | solution.py:205
  229.1 41.1 %all-gather.6.cloned.1.call-done = bf16[2048,640]{0,1:T(8,128)(2,1)} async-done(((bf16[256,640]{0,1:T(8,128)(2,1)}), bf16[2048,640]{0,1:T(8,128)(2,1)}) %all-gather.6.cloned.1.call-update) | async-done | bytes 2621456 | tf_op jit(solution)/shard_map/all_gather | solution.py:218
  273.2 13.0 %fusion.189 = (f32[5,3,256]{2,1,0:T(4,128)S(1)}, f32[5,3,256,2048]{3,2,1,0:T(8,128)}) fusion(bf16[2048,5,64,1]{0,2,3,1:T(8,128)(2,1)S(1)} %bitcast.263, bf16[256,5,3,32]{0,3,2,1:T(8,128)(2,1)S(1)} %bitcast.282, bf16[256,5,3,32]{0,3,2,1:T(8,128)(2,1)S(1)} %bitcast.280, pred[256,2048]{1,0:T(8,128)(4,1)S(1)} %broadcast_compare_fusion), kind=kOutput, calls=%fused_computation.318 | convolution fusion | flops 1031205120 | bytes 33799168 | tf_op jit(solution)/shard_map/kgqd,pkd->kgqp/dot_general | solution.py:205
  286.2 24.6 %fusion = (f32[5,3,256]{2,1,0:T(4,128)S(1)}, f32[5,3,256]{2,1,0:T(4,128)S(1)}) fusion(f32[5,3,256,2048]{3,2,1,0:T(8,128)} %get-tuple-element.91, f32[5,3,256]{2,1,0:T(4,128)S(1)} %broadcast_maximum_fusion.1, pred[256,2048]{1,0:T(8,128)(4,1)S(1)} %broadcast_compare_fusion, f32[5,3,256,2048]{3,2,1,0:T(8,128)} %get-tuple-element.89, ...), kind=kLoop, calls=%fused_computation.8 | loop fusion | flops 47178240 | bytes 63500288 | tf_op jit(solution)/shard_map/reduce_sum | solution.py:224
  312.1 14.1 %fusion.128 = (bf16[256,5,3,64]{0,3,2,1:T(8,128)(2,1)S(1)}, f32[5,3,256,64]{2,3,1,0:T(8,128)}) fusion(f32[256,5,3]{0,2,1:T(4,128)S(1)} %bitcast.303, bf16[2048,5,64,1]{0,2,3,1:T(8,128)(2,1)} %bitcast.274, f32[5,3,256,2048]{3,2,1,0:T(8,128)} %get-tuple-element.89, f32[5,3,256]{2,1,0:T(4,128)S(1)} %broadcast_maximum_fusion, ...), kind=kOutput, calls=%fused_computation.162 | convolution fusion | flops 1030717440 | bytes 34797568 | tf_op jit(solution)/shard_map/kgqp,pkd->kgqd/dot_general | solution.py:225
  329.8 14.4 %fusion.130 = (bf16[256,5,3,64]{0,3,2,1:T(8,128)(2,1)}, f32[5,3,256,64]{2,3,1,0:T(8,128)}) fusion(f32[256,5,3]{0,2,1:T(4,128)S(1)} %bitcast.302, bf16[2048,5,64,1]{0,2,3,1:T(8,128)(2,1)} %bitcast.272, f32[5,3,256,2048]{3,2,1,0:T(8,128)} %get-tuple-element.91, f32[5,3,256]{2,1,0:T(4,128)S(1)} %broadcast_maximum_fusion.1, ...), kind=kOutput, calls=%fused_computation.167 | convolution fusion | flops 1030717440 | bytes 34797568 | tf_op jit(solution)/shard_map/kgqp,pkd->kgqd/dot_general | solution.py:225
  359.6 8.8 %multiply_reduce_fusion.2 = (f32[960]{0:T(1024)}, f32[256]{0:T(256)S(1)}, bf16[256,960]{0,1:T(8,128)(2,1)S(1)}, f32[256,960]{0,1:T(8,128)S(1)}) fusion(f32[256,960]{0,1:T(8,128)S(1)} %get-tuple-element.97, f32[256]{0:T(256)S(1)} %add_rsqrt_fusion.2, f32[960]{0:T(1024)S(1)} %bitcast.309, f32[256,960]{0,1:T(8,128)S(1)} %copy-done.19, ...), kind=kOutput, calls=%fused_computation.173 | convolution fusion | flops 2524035840 | bytes 16558592 | tf_op jit(solution)/shard_map/dot_general | solution.py:68
  374.7 6.5 multiply_convert_fusion.3
  381.2 8.1 multiply_reduce_fusion
  394.1 12.6 %fusion.51 = bf16[5,64,2048]{2,1,0:T(8,128)(2,1)S(1)} fusion(bf16[5,3,256,64]{2,3,1,0:T(8,128)(2,1)S(1)} %bitcast.300, f32[5,3,256,2048]{3,2,1,0:T(8,128)} %get-tuple-element.89, f32[5,3,256]{2,1,0:T(4,128)S(1)} %copy-done.65, pred[256,2048]{1,0:T(8,128)(4,1)S(1)} %broadcast_compare_fusion), kind=kOutput, calls=%fused_computation.61 | convolution fusion | flops 1030881280 | bytes 33799168 | tf_op jit(solution)/shard_map/kgqp,kgqd->pkd/dot_general | solution.py:281
  406.7 21.1 %multiply_convert_fusion = bf16[5,3,256,2048]{3,2,1,0:T(8,128)(2,1)} fusion(f32[5,3,256,2048]{3,2,1,0:T(8,128)} %get-tuple-element.89, bf16[5,3,256,64]{2,3,1,0:T(8,128)(2,1)S(1)} %bitcast.301, bf16[2048,5,64,1]{0,2,3,1:T(8,128)(2,1)S(1)} %bitcast.275, f32[5,3,256]{2,1,0:T(4,128)S(1)} %multiply_reduce_fusion.5, f32[5,3,256]{2,1,0:T(4,128)S(1)} %copy-done.65, ...), kind=kOutput, calls=%fused_computation | convolution fusion | flops 1045954560 | bytes 49543168 | tf_op jit(solution)/shard_map/kgqd,pkd->kgqp/dot_general | solution.py:261
  427.8 8.4 %fusion.60 = bf16[5,64,2048]{2,1,0:T(8,128)(2,1)S(1)} fusion(bf16[5,3,256,2048]{3,2,1,0:T(8,128)(2,1)} %multiply_convert_fusion, bf16[256,5,3,32]{0,3,2,1:T(8,128)(2,1)S(1)} %bitcast.285, bf16[256,5,3,32]{0,3,2,1:T(8,128)(2,1)S(1)} %bitcast.287), kind=kOutput, calls=%fused_computation.66 | convolution fusion | flops 1008926720 | bytes 17530880 | tf_op jit(solution)/shard_map/kgqp,kgqd->pkd/dot_general | solution.py:278
  440.6 21.2 %multiply_convert_fusion.1 = bf16[5,3,256,2048]{3,2,1,0:T(8,128)(2,1)} fusion(f32[5,3,256,2048]{3,2,1,0:T(8,128)} %get-tuple-element.91, bf16[5,3,256,64]{2,3,1,0:T(8,128)(2,1)S(1)} %bitcast.297, bf16[2048,5,64,1]{0,2,3,1:T(8,128)(2,1)S(1)} %bitcast.273, f32[5,3,256]{2,1,0:T(4,128)S(1)} %multiply_reduce_fusion.8, f32[5,3,256]{2,1,0:T(4,128)S(1)} %copy-done.64, ...), kind=kOutput, calls=%fused_computation.2 | convolution fusion | flops 1045954560 | bytes 49543168 | tf_op jit(solution)/shard_map/kgqd,pkd->kgqp/dot_general | solution.py:261
  461.8 8.5 %fusion.58 = bf16[5,64,2048]{2,1,0:T(8,128)(2,1)S(1)} fusion(bf16[5,3,256,2048]{3,2,1,0:T(8,128)(2,1)} %multiply_convert_fusion.1, bf16[256,5,3,32]{0,3,2,1:T(8,128)(2,1)S(1)} %bitcast.283, bf16[256,5,3,32]{0,3,2,1:T(8,128)(2,1)S(1)} %bitcast.281), kind=kOutput, calls=%fused_computation.64 | convolution fusion | flops 1008926720 | bytes 17530880 | tf_op jit(solution)/shard_map/kgqp,kgqd->pkd/dot_general | solution.py:278
  470.4 12.6 %fusion.54 = bf16[5,64,2048]{2,1,0:T(8,128)(2,1)S(1)} fusion(bf16[5,3,256,64]{2,3,1,0:T(8,128)(2,1)S(1)} %bitcast.298, f32[5,3,256,2048]{3,2,1,0:T(8,128)} %get-tuple-element.91, f32[5,3,256]{2,1,0:T(4,128)S(1)} %copy-done.64, pred[256,2048]{1,0:T(8,128)(4,1)S(1)} %broadcast_compare_fusion), kind=kOutput, calls=%fused_computation.62 | convolution fusion | flops 1030881280 | bytes 33799168 | tf_op jit(solution)/shard_map/kgqp,kgqd->pkd/dot_general | solution.py:281
  486.1 8.4 %convolution_multiply_fusion = f32[5,3,256,64]{2,3,1,0:T(8,128)S(1)} fusion(bf16[5,3,256,2048]{3,2,1,0:T(8,128)(2,1)} %multiply_convert_fusion, bf16[2048,5,64,1]{0,2,3,1:T(8,128)(2,1)S(1)} %bitcast.262), kind=kOutput, calls=%fused_computation.139 | convolution fusion | flops 1006878720 | bytes 18022400 | tf_op jit(solution)/shard_map/kgqp,pkd->kgqd/dot_general | solution.py:272
  494.6 8.6 %convolution_multiply_fusion.1 = f32[5,3,256,64]{2,3,1,0:T(8,128)S(1)} fusion(bf16[5,3,256,2048]{3,2,1,0:T(8,128)(2,1)} %multiply_convert_fusion.1, bf16[2048,5,64,1]{0,2,3,1:T(8,128)(2,1)S(1)} %bitcast.264), kind=kOutput, calls=%fused_computation.140 | convolution fusion | flops 1006878720 | bytes 18022400 | tf_op jit(solution)/shard_map/kgqp,pkd->kgqd/dot_general | solution.py:272
  511.7 11.6 %convolution_convert_fusion = bf16[5120,960]{0,1:T(8,128)(2,1)} fusion(bf16[256,2560]{1,0:T(8,128)(2,1)} %get-tuple-element.37, bf16[256,2560]{1,0:T(8,128)(2,1)} %copy-done.80, bf16[256,2560]{1,0:T(8,128)(2,1)} %copy-done.79, bf16[256,2560]{1,0:T(8,128)(2,1)} %copy-done.78, bf16[256,960]{0,1:T(8,128)(2,1)S(1)} %copy-done.82, ...), kind=kOutput, calls=%fused_computation.25 | convolution fusion | flops 5061017600 | bytes 16056320 | tf_op jit(solution)/shard_map/dot_general | solution.py:78
  524.4 56.0 %reduce-scatter.3.cloned.1.call-done = bf16[256,640]{0,1:T(8,128)(2,1)} async-done(((bf16[2048,640]{0,1:T(8,128)(2,1)}), bf16[256,640]{0,1:T(8,128)(2,1)}) %reduce-scatter.3.cloned.1.call-update) | async-done | bytes 327696 | tf_op jit(solution)/shard_map/reduce_scatter | solution.py:291
  585.9 28.8 %concatenate.130 = bf16[10240,960]{0,1:T(8,128)(2,1)} concatenate(bf16[1600,960]{0,1:T(8,128)(2,1)} %convolution_convert_fusion.2, bf16[960,960]{0,1:T(8,128)(2,1)S(1)} %convolution_convert_fusion.3, bf16[5120,960]{0,1:T(8,128)(2,1)} %convolution_convert_fusion, bf16[2560,960]{0,1:T(8,128)(2,1)} %convolution_convert_fusion.1), dimensions={0} | concatenate | bytes 39321600 | tf_op jit(solution)/shard_map/concatenate | solution.py:118
  614.7 28.0 %copy.18 = bf16[10240,960]{1,0:T(8,128)(2,1)} copy(bf16[10240,960]{0,1:T(8,128)(2,1)} %concatenate.130) | data formatting | bytes 39321600 | tf_op jit(solution)/shard_map/concatenate | solution.py:118
  642.8 9.7 %dynamic-slice_bitcast_fusion = bf16[2,2,2,2,320,960]{5,4,3,2,1,0:T(8,128)(2,1)} fusion(bf16[2,2,2,2,2,320,960]{6,5,4,3,2,1,0:T(8,128)(2,1)} %bitcast.257, s32[]{:T(128)S(6)} %select_n.167), kind=kLoop, calls=%fused_computation.24 | loop fusion | bytes 19660804 | tf_op jit(solution)/shard_map/jit(dynamic_index_in_dim)/squeeze | solution.py:108
  672.9 8.1 fusion.6
  695.9 24.1 %collective-permute-done.9 = bf16[2,2,2,96,960]{4,3,2,1,0:T(8,128)(2,1)S(1)} collective-permute-done((bf16[2,2,2,96,960]{4,3,2,1,0:T(8,128)(2,1)}, bf16[2,2,2,96,960]{4,3,2,1,0:T(8,128)(2,1)S(1)}, u32[]{:S(2)}, u32[]{:S(2)}) %collective-permute-start.9) | collective-permute-done | bytes 1474592 | tf_op jit(solution)/shard_map/ppermute | solution.py:97
  722.8 6.8 collective-permute-done.15
  732.2 6.5 collective-permute-done.16
  742.5 15.1 %collective-permute-done.10 = bf16[2,2,96,960]{3,2,1,0:T(8,128)(2,1)S(1)} collective-permute-done((bf16[2,2,96,960]{3,2,1,0:T(8,128)(2,1)S(1)}, bf16[2,2,96,960]{3,2,1,0:T(8,128)(2,1)S(1)}, u32[]{:S(2)}, u32[]{:S(2)}) %collective-permute-start.10) | collective-permute-done | bytes 737312 | tf_op jit(solution)/shard_map/ppermute | solution.py:97
  769.3 7.9 collective-permute-done.6
  786.4 13.7 %collective-permute-done.7 = bf16[2,112,960]{2,1,0:T(8,128)(2,1)S(1)} collective-permute-done((bf16[2,112,960]{2,1,0:T(8,128)(2,1)S(1)}, bf16[2,112,960]{2,1,0:T(8,128)(2,1)S(1)}, u32[]{:S(2)}, u32[]{:S(2)}) %collective-permute-start.7) | collective-permute-done | bytes 430112 | tf_op jit(solution)/shard_map/ppermute | solution.py:97
  807.9 6.6 collective-permute-done.4
  (323 shorter events, 153.4 us)
Async XLA Ops:
  7.2 141.0 %all-gather.4.cloned.1.call-start = ((), (), s32[]{:S(2)}) async-start(), calls=%async_computation.2 | async-start | bytes 21626880 | tf_op jit(solution)/shard_map/all_gather | solution.py:185
  7.9 204.6 %all-gather.8.cloned.1.call-start = ((), (), s32[]{:S(2)}) async-start(), calls=%async_computation.4 | async-start | bytes 2949120 | tf_op jit(solution)/shard_map/all_gather | solution.py:218
  9.7 138.4 %copy-start.66 = (f32[256]{0:T(256)}, f32[256]{0:T(256)S(1)}, u32[]{:S(2)}) copy-start(f32[256]{0:T(256)S(1)} %get-tuple-element.103) | copy-start | bytes 3076
  9.7 138.4 %copy-start.68 = (f32[256]{0:T(256)}, f32[256]{0:T(256)S(1)}, u32[]{:S(2)}) copy-start(f32[256]{0:T(256)S(1)} %get-tuple-element.104) | copy-start | bytes 3076
  9.8 138.4 %copy-start.59 = (f32[1,960]{1,0:T(1,128)}, f32[1,960]{1,0:T(1,128)S(1)}, u32[]{:S(2)}) copy-start(f32[1,960]{1,0:T(1,128)S(1)} %get-tuple-element.83) | copy-start | bytes 11524
  10.6 151.6 %copy-start.32 = (f32[256,32]{0,1:T(8,128)}, f32[256,32]{0,1:T(8,128)S(1)}, u32[]{:S(2)}) copy-start(f32[256,32]{0,1:T(8,128)S(1)} %get-tuple-element.87) | copy-start | bytes 98308
  10.8 140.3 %copy-start.36 = (bf16[256,960]{0,1:T(8,128)(2,1)}, bf16[256,960]{0,1:T(8,128)(2,1)S(1)}, u32[]{:S(2)}) copy-start(bf16[256,960]{0,1:T(8,128)(2,1)S(1)} %get-tuple-element.51) | copy-start | bytes 1474564
  10.8 141.4 %copy-start.34 = (bf16[256,960]{0,1:T(8,128)(2,1)}, bf16[256,960]{0,1:T(8,128)(2,1)S(1)}, u32[]{:S(2)}) copy-start(bf16[256,960]{0,1:T(8,128)(2,1)S(1)} %get-tuple-element.50) | copy-start | bytes 1474564
  157.3 112.9 %all-gather.6.cloned.1.call-start = ((), (), s32[]{:S(2)}) async-start(), calls=%async_computation.3 | async-start | bytes 2949120 | tf_op jit(solution)/shard_map/all_gather | solution.py:218
  159.2 364.1 %reduce-scatter.5.cloned.1.call-start = ((), (), s32[]{:S(2)}) async-start(), calls=%async_computation.6 | async-start | bytes 2949120 | tf_op jit(solution)/shard_map/reduce_scatter | solution.py:291
  163.7 51.8 %copy-start.28 = (bf16[256,15,32]{0,2,1:T(8,128)(2,1)}, bf16[256,15,32]{0,2,1:T(8,128)(2,1)S(1)}, u32[]{:S(2)}) copy-start(bf16[256,15,32]{0,2,1:T(8,128)(2,1)S(1)} %get-tuple-element.78) | copy-start | bytes 737284
  163.7 109.5 %copy-start.24 = (bf16[256,15,32]{0,2,1:T(8,128)(2,1)}, bf16[256,15,32]{0,2,1:T(8,128)(2,1)S(1)}, u32[]{:S(2)}) copy-start(bf16[256,15,32]{0,2,1:T(8,128)(2,1)S(1)} %get-tuple-element.58) | copy-start | bytes 737284
  163.7 109.5 %copy-start.26 = (bf16[256,15,32]{0,2,1:T(8,128)(2,1)}, bf16[256,15,32]{0,2,1:T(8,128)(2,1)S(1)}, u32[]{:S(2)}) copy-start(bf16[256,15,32]{0,2,1:T(8,128)(2,1)S(1)} %get-tuple-element.59) | copy-start | bytes 737284
  437.9 142.5 %reduce-scatter.3.cloned.1.call-start = ((), (), s32[]{:S(2)}) async-start(), calls=%async_computation.5 | async-start | bytes 2949120 | tf_op jit(solution)/shard_map/reduce_scatter | solution.py:291
  652.5 20.3 %collective-permute-start = (bf16[2,2,2,2,320,960]{5,4,3,2,1,0:T(8,128)(2,1)}, bf16[2,2,2,2,320,960]{5,4,3,2,1,0:T(8,128)(2,1)}, u32[]{:S(2)}, u32[]{:S(2)}) collective-permute-start(bf16[2,2,2,2,320,960]{5,4,3,2,1,0:T(8,128)(2,1)} %dynamic-slice_bitcast_fusion), channel_id=1, source_target_pairs={{0,8},{8,0},{16,24},{24,16},{1,9},{9,1},{17,25},{25,17},{2,10},{10... | collective-permute-start | bytes 29491208 | tf_op jit(solution)/shard_map/ppermute | solution.py:97
  672.3 17.0 %collective-permute-start.13 = (f32[2,960]{1,0:T(2,128)S(1)}, f32[2,960]{1,0:T(2,128)S(1)}, u32[]{:S(2)}, u32[]{:S(2)}) collective-permute-start(f32[2,960]{1,0:T(2,128)S(1)} %maximum_add_fusion), channel_id=1, source_target_pairs={{0,8},{8,0},{16,24},{24,16},{1,9},{9,1},{17,25},{25,17},{2,10},{10... | collective-permute-start | bytes 23048 | tf_op jit(solution)/shard_map/ppermute | solution.py:97
  683.5 36.5 %collective-permute-start.9 = (bf16[2,2,2,96,960]{4,3,2,1,0:T(8,128)(2,1)}, bf16[2,2,2,96,960]{4,3,2,1,0:T(8,128)(2,1)S(1)}, u32[]{:S(2)}, u32[]{:S(2)}) collective-permute-start(bf16[2,2,2,96,960]{4,3,2,1,0:T(8,128)(2,1)} %dynamic-slice_bitcast_fusion.2), channel_id=1, source_target_pairs={{0,2},{1,3},{2,0},{3,1},{4,6},{5,7},{6,4},{7,5},{8,10},{9,11},{10,... | collective-permute-start | bytes 4423688 | tf_op jit(solution)/shard_map/ppermute | solution.py:97
  687.7 53.8 %collective-permute-start.5 = (bf16[2,2,2,112,960]{4,3,2,1,0:T(8,128)(2,1)S(1)}, bf16[2,2,2,112,960]{4,3,2,1,0:T(8,128)(2,1)S(1)}, u32[]{:S(2)}, u32[]{:S(2)}) collective-permute-start(bf16[2,2,2,112,960]{4,3,2,1,0:T(8,128)(2,1)S(1)} %dynamic-slice_bitcast_fusion.1), channel_id=1, source_target_pairs={{0,1},{1,0},{2,3},{3,2},{4,5},{5,4},{6,7},{7,6},{8,9},{9,8},{10,11... | collective-permute-start | bytes 5160968 | tf_op jit(solution)/shard_map/ppermute | solution.py:97
  689.3 3.7 collective-permute-start.14
  693.0 36.6 %collective-permute-start.15 = (f32[2,960]{1,0:T(2,128)S(1)}, f32[2,960]{1,0:T(2,128)S(1)}, u32[]{:S(2)}, u32[]{:S(2)}) collective-permute-start(f32[2,960]{1,0:T(2,128)S(1)} %fusion.219), channel_id=1, source_target_pairs={{0,1},{1,0},{2,3},{3,2},{4,5},{5,4},{6,7},{7,6},{8,9},{9,8},{10,11... | collective-permute-start | bytes 23048 | tf_op jit(solution)/shard_map/ppermute | solution.py:97
  694.3 65.2 %collective-permute-start.1 = (bf16[2,2,2,112,960]{4,3,0,1,2:T(8,128)(2,1)S(1)}, bf16[2,2,2,112,960]{4,3,0,1,2:T(8,128)(2,1)S(1)}, u32[]{:S(2)}, u32[]{:S(2)}) collective-permute-start(bf16[2,2,2,112,960]{4,3,0,1,2:T(8,128)(2,1)S(1)} %bitcast.271), channel_id=1, source_target_pairs={{0,16},{8,24},{16,0},{24,8},{1,17},{9,25},{17,1},{25,9},{2,18},{10... | collective-permute-start | bytes 5160968 | tf_op jit(solution)/shard_map/ppermute | solution.py:97
  720.8 36.8 %collective-permute-start.10 = (bf16[2,2,96,960]{3,2,1,0:T(8,128)(2,1)S(1)}, bf16[2,2,96,960]{3,2,1,0:T(8,128)(2,1)S(1)}, u32[]{:S(2)}, u32[]{:S(2)}) collective-permute-start(bf16[2,2,96,960]{3,2,1,0:T(8,128)(2,1)S(1)} %dynamic-slice_bitcast_fusion.5), channel_id=1, source_target_pairs={{0,4},{1,5},{2,6},{3,7},{4,0},{5,1},{6,2},{7,3},{8,12},{9,13},{10,... | collective-permute-start | bytes 2211848 | tf_op jit(solution)/shard_map/ppermute | solution.py:97
  729.6 9.1 %collective-permute-start.16 = (f32[2,960]{1,0:T(2,128)S(1)}, f32[2,960]{1,0:T(2,128)S(1)}, u32[]{:S(2)}, u32[]{:S(2)}) collective-permute-start(f32[2,960]{1,0:T(2,128)S(1)} %add.441), channel_id=1, source_target_pairs={{0,2},{1,3},{2,0},{3,1},{4,6},{5,7},{6,4},{7,5},{8,10},{9,11},{10,... | collective-permute-start | bytes 23048 | tf_op jit(solution)/shard_map/ppermute | solution.py:97
  738.7 22.9 %collective-permute-start.17 = (f32[2,960]{1,0:T(2,128)S(1)}, f32[2,960]{1,0:T(2,128)S(1)}, u32[]{:S(2)}, u32[]{:S(2)}) collective-permute-start(f32[2,960]{1,0:T(2,128)S(1)} %add.442), channel_id=1, source_target_pairs={{0,4},{1,5},{2,6},{3,7},{4,0},{5,1},{6,2},{7,3},{8,12},{9,13},{10,... | collective-permute-start | bytes 23048 | tf_op jit(solution)/shard_map/ppermute | solution.py:97
  742.4 34.8 %collective-permute-start.6 = (bf16[2,2,112,960]{3,2,1,0:T(8,128)(2,1)S(1)}, bf16[2,2,112,960]{3,2,1,0:T(8,128)(2,1)S(1)}, u32[]{:S(2)}, u32[]{:S(2)}) collective-permute-start(bf16[2,2,112,960]{3,2,1,0:T(8,128)(2,1)S(1)} %dynamic-slice_bitcast_fusion.3), channel_id=1, source_target_pairs={{0,2},{1,3},{2,0},{3,1},{4,6},{5,7},{6,4},{7,5},{8,10},{9,11},{10,... | collective-permute-start | bytes 2580488 | tf_op jit(solution)/shard_map/ppermute | solution.py:97
  758.0 10.6 %collective-permute-start.11 = (bf16[2,96,960]{2,1,0:T(8,128)(2,1)S(1)}, bf16[2,96,960]{2,1,0:T(8,128)(2,1)S(1)}, u32[]{:S(2)}, u32[]{:S(2)}) collective-permute-start(bf16[2,96,960]{2,1,0:T(8,128)(2,1)S(1)} %dynamic-slice_bitcast_fusion.8), channel_id=1, source_target_pairs={{0,16},{8,24},{16,0},{24,8},{1,17},{9,25},{17,1},{25,9},{2,18},{10... | collective-permute-start | bytes 1105928 | tf_op jit(solution)/shard_map/ppermute | solution.py:97
  760.5 23.4 %collective-permute-start.2 = (bf16[2,2,112,960]{3,2,0,1:T(8,128)(2,1)S(1)}, bf16[2,2,112,960]{3,2,0,1:T(8,128)(2,1)S(1)}, u32[]{:S(2)}, u32[]{:S(2)}) collective-permute-start(bf16[2,2,112,960]{3,2,0,1:T(8,128)(2,1)S(1)} %dynamic-slice_bitcast_fusion.4), channel_id=1, source_target_pairs={{0,1},{1,0},{2,3},{3,2},{4,5},{5,4},{6,7},{7,6},{8,9},{9,8},{10,11... | collective-permute-start | bytes 2580488 | tf_op jit(solution)/shard_map/ppermute | solution.py:97
  768.8 17.5 %collective-permute-start.12 = (bf16[96,960]{1,0:T(8,128)(2,1)S(1)}, bf16[96,960]{1,0:T(8,128)(2,1)S(1)}, u32[]{:S(2)}, u32[]{:S(2)}) collective-permute-start(bf16[96,960]{1,0:T(8,128)(2,1)S(1)} %dynamic-slice_bitcast_fusion.11), channel_id=1, source_target_pairs={{0,1},{1,0},{2,3},{3,2},{4,5},{5,4},{6,7},{7,6},{8,9},{9,8},{10,11... | collective-permute-start | bytes 552968 | tf_op jit(solution)/shard_map/ppermute | solution.py:97
  777.6 22.5 %collective-permute-start.7 = (bf16[2,112,960]{2,1,0:T(8,128)(2,1)S(1)}, bf16[2,112,960]{2,1,0:T(8,128)(2,1)S(1)}, u32[]{:S(2)}, u32[]{:S(2)}) collective-permute-start(bf16[2,112,960]{2,1,0:T(8,128)(2,1)S(1)} %dynamic-slice_bitcast_fusion.6), channel_id=1, source_target_pairs={{0,4},{1,5},{2,6},{3,7},{4,0},{5,1},{6,2},{7,3},{8,12},{9,13},{10,... | collective-permute-start | bytes 1290248 | tf_op jit(solution)/shard_map/ppermute | solution.py:97
  784.3 18.7 %collective-permute-start.3 = (bf16[2,112,960]{2,1,0:T(8,128)(2,1)S(1)}, bf16[2,112,960]{2,1,0:T(8,128)(2,1)S(1)}, u32[]{:S(2)}, u32[]{:S(2)}) collective-permute-start(bf16[2,112,960]{2,1,0:T(8,128)(2,1)S(1)} %dynamic-slice_bitcast_fusion.7), channel_id=1, source_target_pairs={{0,2},{1,3},{2,0},{3,1},{4,6},{5,7},{6,4},{7,5},{8,10},{9,11},{10,... | collective-permute-start | bytes 1290248 | tf_op jit(solution)/shard_map/ppermute | solution.py:97
  800.3 7.5 collective-permute-start.8
  803.2 11.3 %collective-permute-start.4 = (bf16[112,960]{1,0:T(8,128)(2,1)S(1)}, bf16[112,960]{1,0:T(8,128)(2,1)S(1)}, u32[]{:S(2)}, u32[]{:S(2)}) collective-permute-start(bf16[112,960]{1,0:T(8,128)(2,1)S(1)} %dynamic-slice_bitcast_fusion.10), channel_id=1, source_target_pairs={{0,4},{1,5},{2,6},{3,7},{4,0},{5,1},{6,2},{7,3},{8,12},{9,13},{10,... | collective-permute-start | bytes 645128 | tf_op jit(solution)/shard_map/ppermute | solution.py:97
  (81 other events, 725.2 us)
Sparse Core Ops, SparseCore 0:
  10.9 137.2 all-gather.3
  157.4 55.0 all-gather.7
  215.1 55.0 all-gather.5
  438.0 68.9 reduce-scatter.4
  510.4 69.9 reduce-scatter.2

commit v2 on v1

v2 whole, which is shorter than its diff:
```python
import jax
import jax.numpy as jnp
import numpy as np
from jax import lax
from jax.experimental import pallas as pl
from jax.experimental.pallas import tpu as pltpu
from jax.sharding import PartitionSpec as P

HEADS = 15
KV = 5
HD = 64
FF = 2560
STEP = 10


SCALE_QK = 0.125
THETA = 10000.0
EPSILON = 1e-05
BETA_ONE = 0.9
BETA_TWO = 0.95
ADAM_EPS = 1e-08
DECAY = 0.1
RATE = 0.02
GAIN_RATE = 0.2
GROUP = HEADS // KV
KEY_TILE = 256
HIDDEN = -1e30
VMEM_BYTES = 48 * 1024 * 1024


def places(row_index, local_rows, ctx_count):
    half_rows = local_rows // 2
    owner_index = row_index // local_rows
    inner_index = row_index % local_rows
    return jnp.where(
        inner_index < half_rows,
        owner_index * half_rows + inner_index,
        (2 * ctx_count - 1 - owner_index) * half_rows + inner_index - half_rows,
    )


def angle_tables(positions_in, sign):
    half_width = HD // 2
    frequency = THETA ** (-jnp.arange(half_width, dtype=jnp.float32) * 2.0 / HD)
    angles = frequency[:, None] * positions_in.astype(jnp.float32)[None, :]
    return jnp.cos(angles), sign * jnp.sin(angles)


def rotate(values, tables):
    cosine, sine_part = tables
    heads = values.reshape(-1, HD, values.shape[-1])
    first_half = heads[:, : HD // 2]
    second_half = heads[:, HD // 2 :]
    return jnp.concatenate(
        [
            first_half * cosine - second_half * sine_part,
            second_half * cosine + first_half * sine_part,
        ],
        axis=1,
    ).reshape(values.shape)


def normalize(values):
    return values * lax.rsqrt(jnp.mean(values * values, axis=-1, keepdims=True) + EPSILON)


def norm_back(values, grad_in, gain_row):
    inv_scale = lax.rsqrt(jnp.mean(values * values, axis=-1, keepdims=True) + EPSILON)
    unit_rows = values * inv_scale
    grad_unit = grad_in * gain_row
    grad_values = inv_scale * (
        grad_unit - unit_rows * jnp.mean(grad_unit * unit_rows, axis=-1, keepdims=True)
    )
    return (grad_values, jnp.sum(grad_in * unit_rows, axis=0))


def matmul_n(left, right):
    return jnp.dot(left, right, preferred_element_type=jnp.float32)


def matmul_t(left, right):
    return lax.dot_general(
        left, right, (((1,), (1,)), ((), ())), preferred_element_type=jnp.float32
    )


def matmul_c(left, right):
    return lax.dot_general(
        left, right, (((0,), (0,)), ((), ())), preferred_element_type=jnp.float32
    )


def axis_bits():
    dp_bits = lax.axis_size("dp").bit_length() - 1
    ctx_bits = lax.axis_size("ctx").bit_length() - 1
    low_ctx = ctx_bits // 2
    core = [("dp", 0)]
    along_x = [("dp", bit) for bit in range(1, dp_bits)]
    along_y = [("ctx", bit) for bit in range(low_ctx)]
    along_z = [("ctx", bit) for bit in range(low_ctx, ctx_bits)]
    return core, along_x, along_y, along_z


def swap(values, where):
    axis, bit = where
    size = lax.axis_size(axis)
    return lax.ppermute(values, axis, [(i, i ^ (1 << bit)) for i in range(size)])


def my_bit(where):
    axis, bit = where
    return (lax.axis_index(axis) >> bit) & 1


def rel_offsets(order, axis_sizes):
    dp_count, ctx_count = axis_sizes
    offsets = np.zeros((1,), np.int64)
    for axis, bit in order:
        step = (1 << bit) * (ctx_count if axis == "dp" else 1)
        offsets = np.concatenate([offsets, offsets ^ step])
    return offsets


def spread(values, order):
    values = values[None]
    for where in order:
        values = jnp.concatenate([values, swap(values, where)], axis=0)
    return values


def collect(values, order):
    kept, arrived = values, None
    for where in order:
        half = kept.shape[0] // 2
        if arrived is None:
            away, kept_next = kept[half:], kept[:half]
            arrived = swap(away, where)
        else:
            away = add_low(kept[half:], arrived[half:])
            kept_next = add_low(kept[:half], arrived[:half])
            arrived = swap(away, where)
        kept = kept_next
    return kept[0].astype(jnp.float32) + arrived[0].astype(jnp.float32)


def add_low(left, right):
    return (left.astype(jnp.float32) + right.astype(jnp.float32)).astype(jnp.bfloat16)


def row_groups(rows):
    first = -(-rows // 48) * 16
    return [(0, first), (first, 2 * first), (2 * first, rows)]


def sum_orders():
    core, along_x, along_y, along_z = axis_bits()
    return [
        along_x + along_y + along_z,
        along_y + along_z + along_x,
        along_z + along_x + along_y,
    ]


def lookup(slot, offsets):
    total = jnp.int32(0)
    for bit in range(len(offsets).bit_length() - 1):
        total = total + ((slot >> bit) & 1) * int(offsets[1 << bit])
    return total


def find(offset, offsets):
    total = jnp.int32(0)
    for bit in range(len(offsets).bit_length() - 1):
        place = int(offsets[1 << bit]).bit_length() - 1
        total = total + (((offset >> place) & 1) << bit)
    return total


def gather_weights(weights):
    rows, width = weights.shape
    sizes = (lax.axis_size("dp"), lax.axis_size("ctx"))
    count = sizes[0] * sizes[1]
    core = axis_bits()[0][0]
    me = lax.axis_index("dp") * sizes[1] + lax.axis_index("ctx")
    groups = row_groups(rows)
    orders = [list(reversed(order)) for order in sum_orders()]
    mine = [spread(weights[low:high], order) for (low, high), order in zip(groups, orders)]
    other = [swap(part, core) for part in mine]
    tables = [rel_offsets(order, sizes) for order in orders]

    def body(me_ref, *refs):
        out_ref = refs[-1]
        bit = (me_ref[0] // sizes[1]) & 1
        for (low, high), own, far in zip(groups, refs[:3], refs[3:6]):
            out_ref[0, bit, 0, low:high] = own[0]
            out_ref[0, 1 - bit, 0, low:high] = far[0]

    def place(step, me_ref):
        target = step_offset(step) ^ me_ref[0]
        return (target // (2 * sizes[1]), 0, target % sizes[1], 0, 0)

    def step_offset(step):
        return lookup(step, tables[0])

    in_specs = [
        pl.BlockSpec(
            (1, high - low, width),
            lambda step, me_ref, table=table: (find(step_offset(step), table), 0, 0),
        )
        for (low, high), table in zip(groups, tables)
    ] * 2
    placed = pl.pallas_call(
        body,
        grid_spec=pltpu.PrefetchScalarGridSpec(
            num_scalar_prefetch=1,
            grid=(count // 2,),
            in_specs=in_specs,
            out_specs=pl.BlockSpec((1, 2, 1, rows, width), place),
        ),
        out_shape=jax.ShapeDtypeStruct((sizes[0] // 2, 2, sizes[1], rows, width), weights.dtype),
        compiler_params=pltpu.CompilerParams(vmem_limit_bytes=VMEM_BYTES),
    )(me.reshape(1).astype(jnp.int32), *mine, *other)
    return placed.reshape(count * rows, width)


def scatter_sum(terms):
    sizes = (lax.axis_size("dp"), lax.axis_size("ctx"))
    count = sizes[0] * sizes[1]
    core = axis_bits()[0][0]
    me = (lax.axis_index("dp") * sizes[1] + lax.axis_index("ctx")).reshape(1).astype(jnp.int32)
    blocks, rows, width = terms[0].shape
    groups = row_groups(rows)
    orders = sum_orders()
    tables = [rel_offsets(list(reversed(order)), sizes) for order in orders]

    def sources(flip):
        def chosen(member):
            def index(step, me_ref):
                target = lookup(step, tables[0]) ^ me_ref[0] ^ flip
                return (jnp.where(target // blocks == member, target % blocks, 0), 0, 0)

            return pl.BlockSpec((1, rows, width), index)

        return [chosen(member) for member in range(len(terms))]

    def holder(step, me_ref, flip):
        return (lookup(step, tables[0]) ^ me_ref[0] ^ flip) // blocks

    def pick_body(me_ref, *refs):
        held = holder(pl.program_id(0), me_ref, sizes[1])
        for member in range(len(terms)):

            @pl.when(held == member)
            def _(member=member):
                refs[-1][...] = refs[member][...]

    away = pl.pallas_call(
        pick_body,
        grid_spec=pltpu.PrefetchScalarGridSpec(
            num_scalar_prefetch=1,
            grid=(count // 2,),
            in_specs=sources(sizes[1]),
            out_specs=pl.BlockSpec((1, rows, width), lambda step, me_ref: (step, 0, 0)),
        ),
        out_shape=jax.ShapeDtypeStruct((count // 2, rows, width), jnp.bfloat16),
        compiler_params=pltpu.CompilerParams(vmem_limit_bytes=VMEM_BYTES),
    )(me, *terms)
    arrived = swap(away, core)

    def merge_body(me_ref, *refs):
        held = holder(pl.program_id(0), me_ref, 0)
        outs = refs[-3:]
        far = refs[-4]
        for member in range(len(terms)):

            @pl.when(held == member)
            def _(member=member):
                for (low, high), out in zip(groups, outs):
                    out[0] = (
                        refs[member][0, low:high].astype(jnp.float32)
                        + far[0, low:high].astype(jnp.float32)
                    ).astype(jnp.bfloat16)

    parts = pl.pallas_call(
        merge_body,
        grid_spec=pltpu.PrefetchScalarGridSpec(
            num_scalar_prefetch=1,
            grid=(count // 2,),
            in_specs=sources(0)
            + [pl.BlockSpec((1, rows, width), lambda step, me_ref: (step, 0, 0))],
            out_specs=[
                pl.BlockSpec(
                    (1, high - low, width),
                    lambda step, me_ref, table=table: (
                        find(lookup(step, tables[0]), table),
                        0,
                        0,
                    ),
                )
                for (low, high), table in zip(groups, tables)
            ],
        ),
        out_shape=[
            jax.ShapeDtypeStruct((count // 2, high - low, width), jnp.bfloat16)
            for low, high in groups
        ],
        compiler_params=pltpu.CompilerParams(vmem_limit_bytes=VMEM_BYTES),
    )(me, *terms, arrived)
    return jnp.concatenate([collect(part, order) for part, order in zip(parts, orders)], axis=0)


def butterfly_sum(values):
    core, along_x, along_y, along_z = axis_bits()
    for where in core + along_x + along_y + along_z:
        values = values + swap(values, where)
    return values


def turned(values):
    return jnp.transpose(values)


def attend_body(queries_ref, key_ref, value_ref, key_pos_ref, query_pos_ref, out_ref, total_ref, work):
    low_cols = queries_ref.shape[-1] // 2
    queries = queries_ref[0, 0]
    pieces = []
    largest = jnp.full((1, queries.shape[1]), HIDDEN, jnp.float32)
    largest_high = jnp.full((1, low_cols), HIDDEN, jnp.float32)
    keys_per_half = key_ref.shape[-1]
    for half in range(2):
        picked = queries if half == 0 else queries_ref[0, 0, :, low_cols:]
        places_of = query_pos_ref[...] if half == 0 else query_pos_ref[:, low_cols:]
        for start in range(0, keys_per_half, KEY_TILE):
            keys = turned(key_ref[0, half, :, start : start + KEY_TILE])
            scores = matmul_n(keys, picked)
            seen = key_pos_ref[half, start : start + KEY_TILE] <= places_of
            scores = jnp.where(seen, scores, HIDDEN)
            if half == 0:
                work[start : start + KEY_TILE] = scores
                largest = jnp.maximum(largest, jnp.max(scores, axis=0, keepdims=True))
            else:
                work[keys_per_half + start : keys_per_half + start + KEY_TILE, low_cols:] = scores
                largest_high = jnp.maximum(largest_high, jnp.max(scores, axis=0, keepdims=True))
    low_max = largest[:, :low_cols]
    high_max = jnp.maximum(largest[:, low_cols:], largest_high)
    largest = jnp.concatenate([low_max, high_max], axis=1)
    total = jnp.zeros_like(largest)
    mixed = jnp.zeros((HD, queries.shape[1]), jnp.float32)
    total_high = jnp.zeros_like(largest_high)
    mixed_high = jnp.zeros((HD, low_cols), jnp.float32)
    for half in range(2):
        for start in range(0, keys_per_half, KEY_TILE):
            values = value_ref[0, half, :, start : start + KEY_TILE]
            row = half * keys_per_half + start
            if half == 0:
                expos = jnp.exp(work[row : row + KEY_TILE] - largest)
                total = total + jnp.sum(expos, axis=0, keepdims=True)
                mixed = mixed + matmul_n(values, expos.astype(jnp.bfloat16))
            else:
                expos = jnp.exp(work[row : row + KEY_TILE, low_cols:] - high_max)
                total_high = total_high + jnp.sum(expos, axis=0, keepdims=True)
                mixed_high = mixed_high + matmul_n(values, expos.astype(jnp.bfloat16))
    total = jnp.concatenate([total[:, :low_cols], total[:, low_cols:] + total_high], axis=1)
    mixed = jnp.concatenate([mixed[:, :low_cols], mixed[:, low_cols:] + mixed_high], axis=1)
    out_ref[0, 0] = (mixed / total).astype(jnp.bfloat16)
    total_ref[0, 0] = largest + jnp.log(total)


def attend_back_body(
    queries_ref,
    key_ref,
    value_ref,
    key_pos_ref,
    query_pos_ref,
    out_ref,
    total_ref,
    d_out_ref,
    d_queries_ref,
    d_pair_ref,
):
    low_cols = queries_ref.shape[-1] // 2
    keys_per_half = key_ref.shape[-1]
    delta = jnp.sum(
        d_out_ref[0, 0].astype(jnp.float32) * out_ref[0, 0].astype(jnp.float32),
        axis=0,
        keepdims=True,
    )
    totals = total_ref[0, 0]
    d_queries = []
    for half in range(2):
        if half == 0:
            queries, d_out = queries_ref[0, 0], d_out_ref[0, 0]
            places_of, log_total, row_delta = query_pos_ref[...], totals, delta
        else:
            queries, d_out = queries_ref[0, 0, :, low_cols:], d_out_ref[0, 0, :, low_cols:]
            places_of = query_pos_ref[:, low_cols:]
            log_total, row_delta = totals[:, low_cols:], delta[:, low_cols:]
        part = jnp.zeros((HD, queries.shape[1]), jnp.float32)
        for start in range(0, keys_per_half, KEY_TILE):
            keys_flat = key_ref[0, half, :, start : start + KEY_TILE]
            scores = matmul_n(turned(keys_flat), queries)
            seen = key_pos_ref[half, start : start + KEY_TILE] <= places_of
            probs = jnp.where(seen, jnp.exp(scores - log_total), 0.0)
            values = turned(value_ref[0, half, :, start : start + KEY_TILE])
            d_probs = matmul_n(values, d_out)
            d_scores = (probs * (d_probs - row_delta)).astype(jnp.bfloat16)
            part = part + matmul_n(keys_flat, d_scores)
            d_pair_ref[0, half, 0, start : start + KEY_TILE, :HD] = matmul_t(
                d_scores, queries
            ).astype(jnp.bfloat16)
            d_pair_ref[0, half, 0, start : start + KEY_TILE, HD:] = matmul_t(
                probs.astype(jnp.bfloat16), d_out
            ).astype(jnp.bfloat16)
        d_queries.append(part)
    d_queries_ref[0, 0, :, :low_cols] = d_queries[0][:, :low_cols]
    d_queries_ref[0, 0, :, low_cols:] = d_queries[0][:, low_cols:] + d_queries[1]


def attention_specs(cols, keys_per_half):
    packed = pl.BlockSpec((1, 1, HD, cols), lambda seq, head: (seq, head, 0, 0))
    return packed, [
        packed,
        pl.BlockSpec((1, 2, HD, keys_per_half), lambda seq, head: (seq, 0, head, 0)),
        pl.BlockSpec((1, 2, HD, keys_per_half), lambda seq, head: (seq, 0, KV + head, 0)),
        pl.BlockSpec((2, keys_per_half, 1), lambda seq, head: (0, 0, 0)),
        pl.BlockSpec((1, cols), lambda seq, head: (0, 0)),
    ]


def attend(queries, pairs, key_pos, query_pos):
    seqs, _, _, cols = queries.shape
    keys_per_half = pairs.shape[-1]
    packed, specs = attention_specs(cols, keys_per_half)
    work = seqs * HEADS * keys_per_half * cols // GROUP * 3
    return pl.pallas_call(
        attend_body,
        grid=(seqs, KV),
        in_specs=specs,
        out_specs=[packed, pl.BlockSpec((1, 1, 1, cols), lambda seq, head: (seq, head, 0, 0))],
        out_shape=[
            jax.ShapeDtypeStruct(queries.shape, jnp.bfloat16),
            jax.ShapeDtypeStruct((seqs, KV, 1, cols), jnp.float32),
        ],
        scratch_shapes=[pltpu.VMEM((2 * keys_per_half, cols), jnp.float32)],
        cost_estimate=pl.CostEstimate(
            flops=work * HD, bytes_accessed=8 * 1024 * 1024, transcendentals=work
        ),
        compiler_params=pltpu.CompilerParams(vmem_limit_bytes=VMEM_BYTES),
    )(queries, pairs, pairs, key_pos, query_pos)


def attend_back(queries, pairs, key_pos, query_pos, mixed, log_total, d_mixed):
    seqs, _, _, cols = queries.shape
    keys_per_half = pairs.shape[-1]
    packed, specs = attention_specs(cols, keys_per_half)
    work = seqs * HEADS * keys_per_half * cols // GROUP * 3
    return pl.pallas_call(
        attend_back_body,
        grid=(seqs, KV),
        in_specs=specs
        + [
            packed,
            pl.BlockSpec((1, 1, 1, cols), lambda seq, head: (seq, head, 0, 0)),
            packed,
        ],
        out_specs=[
            packed,
            pl.BlockSpec(
                (1, 2, 1, keys_per_half, 2 * HD), lambda seq, head: (seq, 0, head, 0, 0)
            ),
        ],
        out_shape=[
            jax.ShapeDtypeStruct(queries.shape, jnp.float32),
            jax.ShapeDtypeStruct((seqs, 2, KV, keys_per_half, 2 * HD), jnp.bfloat16),
        ],
        cost_estimate=pl.CostEstimate(
            flops=work * HD * 3, bytes_accessed=16 * 1024 * 1024, transcendentals=work
        ),
        compiler_params=pltpu.CompilerParams(vmem_limit_bytes=VMEM_BYTES),
    )(queries, pairs, pairs, key_pos, query_pos, mixed, log_total, d_mixed)


def feed_body(
    a_two_ref, dy_ref, gate_ref, up_ref, down_ref, out_ref, d_two_ref, d_gate_ref, d_up_ref, d_down_ref
):
    @pl.when(pl.program_id(0) == 0)
    def _():
        out_ref[...] = jnp.zeros_like(out_ref)
        d_two_ref[...] = jnp.zeros_like(d_two_ref)

    a_two, dy_low = a_two_ref[...], dy_ref[...]
    gate_rows, up_rows, down_rows = gate_ref[...], up_ref[...], down_ref[...]
    gate_pre = matmul_t(gate_rows, a_two)
    up_pre = matmul_t(up_rows, a_two)
    d_hidden = matmul_t(down_rows, dy_low)
    sigma = jax.nn.sigmoid(gate_pre)
    gate_act = gate_pre * sigma
    hidden = (gate_act * up_pre).astype(jnp.bfloat16)
    d_gate = (d_hidden * up_pre * sigma * (1.0 + gate_pre * (1.0 - sigma))).astype(jnp.bfloat16)
    d_up = (d_hidden * gate_act).astype(jnp.bfloat16)
    out_ref[...] += matmul_c(hidden, down_rows)
    d_two_ref[...] += matmul_c(d_gate, gate_rows) + matmul_c(d_up, up_rows)
    d_gate_ref[0] = matmul_n(d_gate, a_two).astype(jnp.bfloat16)
    d_up_ref[0] = matmul_n(d_up, a_two).astype(jnp.bfloat16)
    d_down_ref[0] = matmul_n(hidden, dy_low).astype(jnp.bfloat16)


def feed_forward(a_two, dy_low, gathered, rows, cut_g):
    tokens, width = a_two.shape
    blocks = FF // rows
    first = cut_g // rows
    whole = pl.BlockSpec((tokens, width), lambda step: (0, 0))
    grads = pl.BlockSpec((1, rows, width), lambda step: (step, 0, 0))
    return pl.pallas_call(
        feed_body,
        grid=(blocks,),
        in_specs=[whole, whole]
        + [
            pl.BlockSpec((rows, width), lambda step, start=first + member * blocks: (start + step, 0))
            for member in range(3)
        ],
        out_specs=[whole, whole, grads, grads, grads],
        out_shape=[jax.ShapeDtypeStruct((tokens, width), jnp.float32)] * 2
        + [jax.ShapeDtypeStruct((blocks, rows, width), jnp.bfloat16)] * 3,
        cost_estimate=pl.CostEstimate(
            flops=18 * tokens * width * FF, bytes_accessed=12 * FF * width, transcendentals=FF * tokens
        ),
        compiler_params=pltpu.CompilerParams(vmem_limit_bytes=VMEM_BYTES),
    )(a_two, dy_low, gathered, gathered, gathered)


def adam_update(param, grad, first, second, rate, decay, step_number):
    first_new = BETA_ONE * first + (1.0 - BETA_ONE) * grad
    second_new = BETA_TWO * second + (1.0 - BETA_TWO) * grad * grad
    fix_one = 1.0 - BETA_ONE**step_number
    fix_two = 1.0 - BETA_TWO**step_number
    update = first_new / fix_one / (jnp.sqrt(second_new / fix_two) + ADAM_EPS)
    return (first_new, second_new, param - rate * (update + decay * param))


def shards(inputs, cotangent, weights, gains, first_moment, second_moment, gain_first, gain_second):
    sizes = (lax.axis_size("dp"), lax.axis_size("ctx"))
    ctx_count = sizes[1]
    ctx_index = lax.axis_index("ctx")
    seqs, local_rows, model_width = inputs.shape
    half_rows = local_rows // 2
    tokens = seqs * local_rows
    weight_rows = weights.shape[0]
    q_cols = HEADS * HD
    kv_cols = KV * HD
    cut_o = q_cols + 2 * kv_cols
    cut_g = cut_o + q_cols
    along_y, along_z = axis_bits()[2:]
    ctx_order = list(reversed(along_z)) + along_y
    local_index = jnp.arange(local_rows, dtype=jnp.int32)
    pos_here = places(ctx_index * local_rows + local_index, local_rows, ctx_count)
    pos_tokens = jnp.tile(pos_here, seqs)
    turn, turn_back = angle_tables(pos_tokens, 1.0), angle_tables(pos_tokens, -1.0)

    def pack(flat):
        return (
            flat.reshape(KV, GROUP, HD, seqs, 2, half_rows)
            .transpose(3, 0, 2, 4, 1, 5)
            .reshape(seqs, KV, HD, 2 * GROUP * half_rows)
        )

    def unpack(packed):
        return (
            packed.reshape(seqs, KV, HD, 2, GROUP, half_rows)
            .transpose(1, 4, 2, 0, 3, 5)
            .reshape(q_cols, tokens)
        )

    owners = ctx_index ^ jnp.asarray(rel_offsets(ctx_order, sizes), jnp.int32)
    inner = jnp.arange(half_rows, dtype=jnp.int32)
    key_pos = jnp.stack(
        [
            (owners[:, None] * half_rows + inner[None, :]).reshape(-1, 1),
            ((2 * ctx_count - 1 - owners[:, None]) * half_rows + inner[None, :]).reshape(-1, 1),
        ]
    )
    query_pos = jnp.broadcast_to(
        pos_here.reshape(2, 1, half_rows), (2, GROUP, half_rows)
    ).reshape(1, 2 * GROUP * half_rows)

    gathered = gather_weights(weights)
    tokens_in = inputs.reshape(tokens, model_width)
    cot_in = cotangent.reshape(tokens, model_width)
    a_one = (normalize(tokens_in) * gains[0]).astype(jnp.bfloat16)
    qkv = matmul_t(gathered[:cut_o], a_one)
    q_rot = (rotate(qkv[:q_cols], turn).astype(jnp.bfloat16) * SCALE_QK).astype(jnp.bfloat16)
    key_rot = rotate(qkv[q_cols : q_cols + kv_cols], turn).astype(jnp.bfloat16)
    value_rows = qkv[q_cols + kv_cols :].astype(jnp.bfloat16)
    queries = pack(q_rot)
    joined = jnp.concatenate([key_rot, value_rows], axis=0).reshape(2 * kv_cols, seqs, local_rows)

    def lay(slots):
        return (
            slots.reshape(ctx_count, 2 * kv_cols, 2, half_rows)
            .transpose(2, 1, 0, 3)
            .reshape(2, 2 * kv_cols, ctx_count * half_rows)
        )

    pairs = jnp.stack([lay(spread(joined[:, seq], ctx_order)) for seq in range(seqs)])
    mixed, log_total = attend(queries, pairs, key_pos, query_pos)
    attn_low = unpack(mixed)
    resid = tokens_in + matmul_c(attn_low, gathered[cut_o:cut_g])
    a_two = (normalize(resid) * gains[1]).astype(jnp.bfloat16)
    dy_low = cot_in.astype(jnp.bfloat16)
    fed, d_two, d_gate, d_up, d_down = feed_forward(a_two, dy_low, gathered, weight_rows, cut_g)
    result = resid + fed
    d_norm_two, d_gain_two = norm_back(resid, d_two, gains[1])
    d_resid = cot_in + d_norm_two
    d_resid_low = d_resid.astype(jnp.bfloat16)
    d_attn = matmul_t(gathered[cut_o:cut_g], d_resid_low).astype(jnp.bfloat16)
    d_queries, d_pairs = attend_back(
        queries, pairs, key_pos, query_pos, mixed, log_total, pack(d_attn)
    )
    d_pair_slots = d_pairs.reshape(seqs, 2, KV, ctx_count, half_rows, 2 * HD).transpose(
        0, 3, 1, 2, 4, 5
    )
    d_own = jnp.stack(
        [collect(d_pair_slots[seq], list(reversed(ctx_order))) for seq in range(seqs)]
    )
    d_own = d_own.transpose(2, 4, 0, 1, 3).reshape(KV, 2 * HD, tokens)
    d_k = d_own[:, :HD].reshape(kv_cols, tokens)
    d_v = d_own[:, HD:].reshape(kv_cols, tokens)
    d_qkv = jnp.concatenate(
        [
            rotate(unpack(d_queries) * SCALE_QK, turn_back).astype(jnp.bfloat16),
            rotate(d_k, turn_back).astype(jnp.bfloat16),
            d_v.astype(jnp.bfloat16),
        ],
        axis=0,
    )
    d_one = matmul_c(d_qkv, gathered[:cut_o])
    d_norm_one, d_gain_one = norm_back(tokens_in, d_one, gains[0])
    d_tokens = d_resid + d_norm_one
    d_first = jnp.concatenate(
        [
            matmul_n(d_qkv, a_one).astype(jnp.bfloat16),
            matmul_n(attn_low, d_resid_low).astype(jnp.bfloat16),
        ],
        axis=0,
    ).reshape(-1, weight_rows, model_width)
    weight_share = scatter_sum([d_first, d_gate, d_up, d_down])
    gain_grad = butterfly_sum(jnp.stack([d_gain_one, d_gain_two], axis=0))
    weight_first, weight_second, weight_new = adam_update(
        weights.astype(jnp.float32), weight_share, first_moment, second_moment, RATE, DECAY, STEP
    )
    gain_first_new, gain_second_new, gain_new = adam_update(
        gains, gain_grad, gain_first, gain_second, GAIN_RATE, 0.0, STEP
    )
    return (
        result.reshape(inputs.shape),
        d_tokens.reshape(inputs.shape),
        weight_share,
        weight_second,
        weight_new,
        gain_grad,
        gain_second_new,
        gain_new,
    )


def solution(mesh):
    placed = (
        P("dp", "ctx", None),
        P("dp", "ctx", None),
        P(("dp", "ctx"), None),
        P(),
        P(("dp", "ctx"), None),
        P(("dp", "ctx"), None),
        P(),
        P(),
    )
    return jax.shard_map(
        shards,
        mesh=mesh,
        in_specs=placed,
        out_specs=(
            P("dp", "ctx", None),
            P("dp", "ctx", None),
            P(("dp", "ctx"), None),
            P(("dp", "ctx"), None),
            P(("dp", "ctx"), None),
            P(),
            P(),
            P(),
        ),
        check_vma=False,
    )
```

time: 829 us -> 783 us (0.945)
  matrix products: 255 us -> 21.1 us
  Pallas kernels: 0 us -> 150 us
  local copies, waits for them, and re-layouts: 91.6 us -> 135 us
  starting transfers between devices: 17.3 us -> 43.8 us
  waiting for transfers between devices: 387 us -> 373 us
  between operations: 15.5 us -> 2.14 us
    ppermute x18 -> x45, waiting for transfers between devices: 103 us -> 373 us  [swap(): return lax.ppermute(values, axis, [(i, i ^ 1 << bit) for i in range(size)])]
    all_gather x3 -> x0, waiting for transfers between devices: 227 us -> none  [the longest x1 137 us: shards(): gathered = lax.all_gather(weights, ('dp', 'ctx'), axis=0, tiled=True)]
    dot_general x12 -> x0, matrix products: 157 us -> none  [the longest x2 42.3 us: score_grads(): jnp.einsum('kgqd,pkd->kgqp', d_heads, value_piece.reshape(piece_rows, KV,...]
    pallas_call x0 -> x6, Pallas kernels: none -> 150 us  [the longest x1 41.7 us: attend_back(): pl.pallas_call(attend_back_body, grid=(seqs, KV), in_specs=specs + [packe...]
    reduce_scatter x2 -> x0, waiting for transfers between devices: 56 us -> none  [shards(): lax.psum_scatter(kv_terms.astype(jnp.bfloat16), 'ctx', scatter_dimension=...]
    concatenate x2 -> x6, local copies, waits for them, and re-layouts: 56.8 us -> 12.1 us  [the longest x1 7.88 us: shards(): jnp.concatenate([matmul_n(d_qkv, a_one).astype(jnp.bfloat16), matmul_n(at...]
    dot_general x8 -> x2, matrix products: 41.2 us -> 4.98 us  [matmul_n(): return jnp.dot(left, right, preferred_element_type=jnp.float32)]
    unnamed x177 -> x133, local copies, waits for them, and re-layouts: 5.99 us -> 42 us
  transfers between devices with their start and end apart: 23 -> 45, of which waited for: 17 -> 31; matrix products, arithmetic and copies ran while one was open for 18% -> 13% of each run, Pallas kernels for 0% -> 0%
where the time goes in v2:
time: 783 us; the launch traced here: 777 us
  waiting for transfers between devices  373 us (48%)
  Pallas kernels  150 us (19%)
  local copies, waits for them, and re-layouts  135 us (17%)
  other arithmetic  52.4 us (7%)
  starting transfers between devices  43.8 us (6%)
  matrix products  21.1 us (3%)
    ppermute x45, waiting for transfers between devices, swap(): return lax.ppermute(values, axis, [(i, i ^ 1 << bit) for i in range(size)])  373 us
    ppermute x45, starting transfers between devices, swap(): return lax.ppermute(values, axis, [(i, i ^ 1 << bit) for i in range(size)])  43.8 us
    unnamed x133, local copies, waits for them, and re-layouts  42 us
    pallas_call x1, Pallas kernels, attend_back(): pl.pallas_call(attend_back_body, grid=(seqs, KV), in_specs=specs + [packe...  41.7 us
    pallas_call x1, Pallas kernels, feed_forward(): pl.pallas_call(feed_body, grid=(blocks,), in_specs=[whole, whole] + [pl.B...  36.5 us
    pallas_call x1, Pallas kernels, attend(): pl.pallas_call(attend_body, grid=(seqs, KV), in_specs=specs, out_specs=[p...  22.6 us
    convert_element_type x12, other arithmetic, add_low(): (left.astype(jnp.float32) + right.astype(jnp.float32)).astype(jnp.bfloat16)  19.2 us
    pallas_call x1, Pallas kernels, gather_weights(): pl.pallas_call(body, grid_spec=pltpu.PrefetchScalarGridSpec(num_scalar_pr...  19.1 us
  transfers between devices with their start and end apart: 45, of which 31 were waited for; matrix products, arithmetic and copies ran while one was open for 13% of the time, Pallas kernels for 0%

profile of v2, /device:TPU:0, one launch (start us, length us, event | category | flops | bytes accessed | tf_op | source)
XLA Modules:
  0.0 776.6 jit_solution(16544699978810511357)
XLA Ops:
  4.7 5.6 collective-permute-done.4
  13.4 29.3 %collective-permute-done = bf16[1,112,960]{2,1,0:T(8,128)(2,1)S(1)} collective-permute-done((bf16[1,112,960]{2,1,0:T(8,128)(2,1)S(1)}, bf16[1,112,960]{2,1,0:T(8,128)(2,1)S(1)}, u32[]{:S(2)}, u32[]{:S(2)}) %collective-permute-start) | collective-permute-done | bytes 215072 | tf_op jit(solution)/shard_map/ppermute | solution.py:107
  46.6 9.7 %collective-permute-done.1 = bf16[2,112,960]{2,1,0:T(8,128)(2,1)S(1)} collective-permute-done((bf16[2,112,960]{2,1,0:T(8,128)(2,1)S(1)}, bf16[2,112,960]{2,1,0:T(8,128)(2,1)S(1)}, u32[]{:S(2)}, u32[]{:S(2)}) %collective-permute-start.1) | collective-permute-done | bytes 430112 | tf_op jit(solution)/shard_map/ppermute | solution.py:107
  59.5 6.3 collective-permute-done.9
  69.7 12.7 %collective-permute-done.6 = bf16[4,112,960]{2,1,0:T(8,128)(2,1)S(1)} collective-permute-done((bf16[4,112,960]{2,1,0:T(8,128)(2,1)S(1)}, bf16[4,112,960]{2,1,0:T(8,128)(2,1)S(1)}, u32[]{:S(2)}, u32[]{:S(2)}) %collective-permute-start.6) | collective-permute-done | bytes 860192 | tf_op jit(solution)/shard_map/ppermute | solution.py:107
  87.6 14.4 %collective-permute-done.10 = bf16[4,96,960]{2,1,0:T(8,128)(2,1)S(1)} collective-permute-done((bf16[4,96,960]{2,1,0:T(8,128)(2,1)S(1)}, bf16[4,96,960]{2,1,0:T(8,128)(2,1)S(1)}, u32[]{:S(2)}, u32[]{:S(2)}) %collective-permute-start.10) | collective-permute-done | bytes 737312 | tf_op jit(solution)/shard_map/ppermute | solution.py:107
  107.3 15.9 %collective-permute-done.7 = bf16[8,112,960]{2,1,0:T(8,128)(2,1)S(1)} collective-permute-done((bf16[8,112,960]{2,1,0:T(8,128)(2,1)S(1)}, bf16[8,112,960]{2,1,0:T(8,128)(2,1)S(1)}, u32[]{:S(2)}, u32[]{:S(2)}) %collective-permute-start.7) | collective-permute-done | bytes 1720352 | tf_op jit(solution)/shard_map/ppermute | solution.py:107
  126.8 8.9 %collective-permute-done.11 = bf16[8,96,960]{2,1,0:T(8,128)(2,1)S(1)} collective-permute-done((bf16[8,96,960]{2,1,0:T(8,128)(2,1)S(1)}, bf16[8,96,960]{2,1,0:T(8,128)(2,1)S(1)}, u32[]{:S(2)}, u32[]{:S(2)}) %collective-permute-start.11) | collective-permute-done | bytes 1474592 | tf_op jit(solution)/shard_map/ppermute | solution.py:107
  146.1 19.1 %shard_map.152 = bf16[2,2,8,320,960]{4,3,2,1,0:T(8,128)(2,1)} custom-call(s32[1]{0:T(128)} %bitcast.1.me_ref, bf16[16,112,960]{2,1,0:T(8,128)(2,1)} %constant_dynamic-update-slice_fusion.refs_0_, bf16[16,112,960]{2,1,0:T(8,128)(2,1)} %constant_dynamic-update-slice_fusion.5.refs_1_, bf16[16,96,960]{2,1,0:T(8,128)(2,1)S(1)} %constant_dynamic-update-slice_fusion.10.refs_2_, ...), custom_call_target="tpu_custom_call" | custom-call | tf_op jit(solution)/shard_map/pallas_call | solution.py:212
  179.2 22.1 %collective-permute-done.18 = bf16[1,640,256]{2,1,0:T(8,128)(2,1)S(1)} collective-permute-done((bf16[1,640,256]{2,1,0:T(8,128)(2,1)S(1)}, bf16[1,640,256]{2,1,0:T(8,128)(2,1)S(1)}, u32[]{:S(2)}, u32[]{:S(2)}) %collective-permute-start.18) | collective-permute-done | bytes 327712 | tf_op jit(solution)/shard_map/ppermute | solution.py:107
  201.4 6.7 collective-permute-done.15
  208.3 13.9 %collective-permute-done.19 = bf16[2,640,256]{2,1,0:T(8,128)(2,1)S(1)} collective-permute-done((bf16[2,640,256]{2,1,0:T(8,128)(2,1)S(1)}, bf16[2,640,256]{2,1,0:T(8,128)(2,1)S(1)}, u32[]{:S(2)}, u32[]{:S(2)}) %collective-permute-start.19) | collective-permute-done | bytes 655392 | tf_op jit(solution)/shard_map/ppermute | solution.py:107
  223.9 12.2 %collective-permute-done.16 = bf16[2,640,256]{2,1,0:T(8,128)(2,1)S(1)} collective-permute-done((bf16[2,640,256]{2,1,0:T(8,128)(2,1)S(1)}, bf16[2,640,256]{2,1,0:T(8,128)(2,1)S(1)}, u32[]{:S(2)}, u32[]{:S(2)}) %collective-permute-start.16) | collective-permute-done | bytes 655392 | tf_op jit(solution)/shard_map/ppermute | solution.py:107
  274.6 7.8 %collective-permute-done.17 = bf16[4,640,256]{2,1,0:T(8,128)(2,1)} collective-permute-done((bf16[4,640,256]{2,1,0:T(8,128)(2,1)}, bf16[4,640,256]{2,1,0:T(8,128)(2,1)}, u32[]{:S(2)}, u32[]{:S(2)}) %collective-permute-start.17) | collective-permute-done | bytes 1310752 | tf_op jit(solution)/shard_map/ppermute | solution.py:107
  303.4 22.6 %shard_map.153 = (bf16[2,5,64,768]{3,2,1,0:T(8,128)(2,1)S(1)}, f32[2,5,1,768]{3,2,1,0:T(1,128)S(1)}) custom-call(bf16[2,5,64,768]{3,2,1,0:T(8,128)(2,1)S(1)} %copy-done.1, bf16[2,2,640,1024]{3,2,1,0:T(8,128)(2,1)} %copy-done.37, bf16[2,2,640,1024]{3,2,1,0:T(8,128)(2,1)} %copy-done.37, s32[2,1024,1]{2,1,0:T(8,128)S(1)} %pad_add_fusion.key_pos_ref, ...), custom_call_target="tpu_custom_call" | custom-call | flops 1509949440 | bytes 8388608 | tf_op jit(solution)/shard_map/pallas_call | solution.py:435
  338.4 36.5 %shard_map.154 = (f32[512,960]{1,0:T(8,128)S(1)}, f32[512,960]{1,0:T(8,128)}, bf16[8,320,960]{2,1,0:T(8,128)(2,1)}, bf16[8,320,960]{2,1,0:T(8,128)(2,1)}, bf16[8,320,960]{2,1,0:T(8,128)(2,1)}) custom-call(bf16[512,960]{1,0:T(8,128)(2,1)S(1)} %multiply_convert_fusion.a_two_ref, bf16[512,960]{1,0:T(8,128)(2,1)S(1)} %bitcast_convert_fusion.dy_ref, ...), custom_call_target="tpu_custom_call" | custom-call | flops 22649241600 | bytes 29491200 | tf_op jit(solution)/shard_map/pallas_call | solution.py:514
  392.8 41.7 %shard_map.155 = (f32[2,5,64,768]{3,2,1,0:T(8,128)S(1)}, bf16[2,2,5,1024,128]{4,3,2,1,0:T(8,128)(2,1)}) custom-call(bf16[2,5,64,768]{3,2,1,0:T(8,128)(2,1)S(1)} %copy-done.2, bf16[2,2,640,1024]{3,2,1,0:T(8,128)(2,1)} %copy-done.37, bf16[2,2,640,1024]{3,2,1,0:T(8,128)(2,1)} %copy-done.37, s32[2,1024,1]{2,1,0:T(8,128)S(1)} %pad_add_fusion.key_pos_ref, ...), custom_call_target="tpu_custom_call" | custom-call | flops 4529848320 | bytes 16777216 | tf_op jit(solution)/shard_map/pallas_call | solution.py:457
  445.0 29.2 %collective-permute-done.21 = bf16[4,2,5,128,128]{4,3,1,0,2:T(8,128)(2,1)} collective-permute-done((bf16[4,2,5,128,128]{4,3,1,0,2:T(8,128)(2,1)}, bf16[4,2,5,128,128]{4,3,1,0,2:T(8,128)(2,1)}, u32[]{:S(2)}, u32[]{:S(2)}) %collective-permute-start.21) | collective-permute-done | bytes 1310752 | tf_op jit(solution)/shard_map/ppermute | solution.py:107
  474.2 26.1 %collective-permute-done.24 = bf16[4,2,5,128,128]{4,3,1,0,2:T(8,128)(2,1)} collective-permute-done((bf16[4,2,5,128,128]{4,3,1,0,2:T(8,128)(2,1)}, bf16[4,2,5,128,128]{4,3,1,0,2:T(8,128)(2,1)}, u32[]{:S(2)}, u32[]{:S(2)}) %collective-permute-start.24) | collective-permute-done | bytes 1310752 | tf_op jit(solution)/shard_map/ppermute | solution.py:107
  518.9 7.9 %collective-permute-done.22 = bf16[2,2,5,128,128]{4,3,1,0,2:T(8,128)(2,1)} collective-permute-done((bf16[2,2,5,128,128]{4,3,1,0,2:T(8,128)(2,1)}, bf16[2,2,5,128,128]{4,3,1,0,2:T(8,128)(2,1)}, u32[]{:S(2)}, u32[]{:S(2)}) %collective-permute-start.22) | collective-permute-done | bytes 655392 | tf_op jit(solution)/shard_map/ppermute | solution.py:107
  528.0 12.3 %collective-permute-done.25 = bf16[2,2,5,128,128]{4,3,1,0,2:T(8,128)(2,1)S(1)} collective-permute-done((bf16[2,2,5,128,128]{4,3,1,0,2:T(8,128)(2,1)}, bf16[2,2,5,128,128]{4,3,1,0,2:T(8,128)(2,1)S(1)}, u32[]{:S(2)}, u32[]{:S(2)}) %collective-permute-start.25) | collective-permute-done | bytes 655392 | tf_op jit(solution)/shard_map/ppermute | solution.py:107
  541.5 9.2 %collective-permute-done.23 = bf16[1,2,5,128,128]{4,3,1,0,2:T(8,128)(2,1)S(1)} collective-permute-done((bf16[1,2,5,128,128]{4,3,1,0,2:T(8,128)(2,1)S(1)}, bf16[1,2,5,128,128]{4,3,1,0,2:T(8,128)(2,1)S(1)}, u32[]{:S(2)}, u32[]{:S(2)}) %collective-permute-start.23) | collective-permute-done | bytes 327712 | tf_op jit(solution)/shard_map/ppermute | solution.py:107
  567.3 7.9 %copy.162 = bf16[2560,960]{1,0:T(8,128)(2,1)} copy(bf16[2560,960]{0,1:T(8,128)(2,1)} %pad_maximum_fusion) | data formatting | bytes 9830400 | tf_op jit(solution)/shard_map/concatenate | solution.py:639
  577.7 13.4 %shard_map.156 = bf16[16,320,960]{2,1,0:T(8,128)(2,1)} custom-call(s32[1]{0:T(128)} %bitcast.1.me_ref, bf16[8,320,960]{2,1,0:T(8,128)(2,1)S(1)} %bitcast.120, bf16[8,320,960]{2,1,0:T(8,128)(2,1)} %get-tuple-element.26.refs_1_, bf16[8,320,960]{2,1,0:T(8,128)(2,1)} %get-tuple-element.27.refs_2_, bf16[8,320,960]{2,1,0:T(8,128)(2,1)} %get-tuple-element.28.refs_3_), custom_call_target="tpu_custom_call" | custom-call | tf_op jit(solution)/shard_map/pallas_call | solution.py:257
  591.1 16.4 %collective-permute-done.27.refs_4_ = bf16[16,320,960]{2,1,0:T(8,128)(2,1)S(1)} collective-permute-done((bf16[16,320,960]{2,1,0:T(8,128)(2,1)}, bf16[16,320,960]{2,1,0:T(8,128)(2,1)S(1)}, u32[]{:S(2)}, u32[]{:S(2)}) %collective-permute-start.27) | collective-permute-done | bytes 9830432 | tf_op jit(solution)/shard_map/ppermute | solution.py:107
  611.3 16.4 %shard_map.157 = (bf16[16,112,960]{2,1,0:T(8,128)(2,1)}, bf16[16,112,960]{2,1,0:T(8,128)(2,1)}, bf16[16,96,960]{2,1,0:T(8,128)(2,1)S(1)}) custom-call(s32[1]{0:T(128)} %bitcast.1.me_ref, bf16[8,320,960]{2,1,0:T(8,128)(2,1)} %bitcast.119, bf16[8,320,960]{2,1,0:T(8,128)(2,1)} %get-tuple-element.26.refs_1_, bf16[8,320,960]{2,1,0:T(8,128)(2,1)} %get-tuple-element.27.refs_2_, ...), custom_call_target="tpu_custom_call" | custom-call | tf_op jit(solution)/shard_map/pallas_call | solution.py:284
  633.5 5.7 multiply_reduce_fusion.1
  645.8 27.4 %collective-permute-done.41 = f32[2,960]{1,0:T(2,128)S(1)} collective-permute-done((f32[2,960]{1,0:T(2,128)S(1)}, f32[2,960]{1,0:T(2,128)S(1)}, u32[]{:S(2)}, u32[]{:S(2)}) %collective-permute-start.41) | collective-permute-done | bytes 7712 | tf_op jit(solution)/shard_map/ppermute | solution.py:107
  674.1 9.5 %collective-permute-done.42 = f32[2,960]{1,0:T(2,128)S(1)} collective-permute-done((f32[2,960]{1,0:T(2,128)S(1)}, f32[2,960]{1,0:T(2,128)S(1)}, u32[]{:S(2)}, u32[]{:S(2)}) %collective-permute-start.42) | collective-permute-done | bytes 7712 | tf_op jit(solution)/shard_map/ppermute | solution.py:107
  701.7 24.3 %collective-permute-done.37 = bf16[4,96,960]{2,1,0:T(8,128)(2,1)} collective-permute-done((bf16[4,96,960]{2,1,0:T(8,128)(2,1)}, bf16[4,96,960]{2,1,0:T(8,128)(2,1)}, u32[]{:S(2)}, u32[]{:S(2)}) %collective-permute-start.37) | collective-permute-done | bytes 737312 | tf_op jit(solution)/shard_map/ppermute | solution.py:107
  730.3 8.1 %collective-permute-done.38 = bf16[2,96,960]{2,1,0:T(8,128)(2,1)S(1)} collective-permute-done((bf16[2,96,960]{2,1,0:T(8,128)(2,1)S(1)}, bf16[2,96,960]{2,1,0:T(8,128)(2,1)S(1)}, u32[]{:S(2)}, u32[]{:S(2)}) %collective-permute-start.38) | collective-permute-done | bytes 368672 | tf_op jit(solution)/shard_map/ppermute | solution.py:107
  750.1 17.5 %collective-permute-done.34 = bf16[2,112,960]{2,1,0:T(8,128)(2,1)S(1)} collective-permute-done((bf16[2,112,960]{2,1,0:T(8,128)(2,1)S(1)}, bf16[2,112,960]{2,1,0:T(8,128)(2,1)S(1)}, u32[]{:S(2)}, u32[]{:S(2)}) %collective-permute-start.34) | collective-permute-done | bytes 430112 | tf_op jit(solution)/shard_map/ppermute | solution.py:107
  (327 shorter events, 257.8 us)
Async XLA Ops:
  10.4 33.1 %collective-permute-start.5 = (bf16[2,112,960]{2,1,0:T(8,128)(2,1)S(1)}, bf16[2,112,960]{2,1,0:T(8,128)(2,1)S(1)}, u32[]{:S(2)}, u32[]{:S(2)}) collective-permute-start(bf16[2,112,960]{2,1,0:T(8,128)(2,1)S(1)} %pad_maximum_fusion.21), channel_id=1, source_target_pairs={{0,4},{1,5},{2,6},{3,7},{4,0},{5,1},{6,2},{7,3},{8,12},{9,13},{10,... | collective-permute-start | bytes 1290248 | tf_op jit(solution)/shard_map/ppermute | solution.py:107
  13.3 29.4 %collective-permute-start = (bf16[1,112,960]{2,1,0:T(8,128)(2,1)S(1)}, bf16[1,112,960]{2,1,0:T(8,128)(2,1)S(1)}, u32[]{:S(2)}, u32[]{:S(2)}) collective-permute-start(bf16[1,112,960]{2,1,0:T(8,128)(2,1)S(1)} %get-tuple-element.117), channel_id=1, source_target_pairs={{0,4},{1,5},{2,6},{3,7},{4,0},{5,1},{6,2},{7,3},{8,12},{9,13},{10,... | collective-permute-start | bytes 645128 | tf_op jit(solution)/shard_map/ppermute | solution.py:107
  43.5 38.8 %collective-permute-start.6 = (bf16[4,112,960]{2,1,0:T(8,128)(2,1)S(1)}, bf16[4,112,960]{2,1,0:T(8,128)(2,1)S(1)}, u32[]{:S(2)}, u32[]{:S(2)}) collective-permute-start(bf16[4,112,960]{2,1,0:T(8,128)(2,1)S(1)} %pad_maximum_fusion.11), channel_id=1, source_target_pairs={{0,2},{1,3},{2,0},{3,1},{4,6},{5,7},{6,4},{7,5},{8,10},{9,11},{10,... | collective-permute-start | bytes 2580488 | tf_op jit(solution)/shard_map/ppermute | solution.py:107
  56.4 28.7 %collective-permute-start.2 = (bf16[4,112,960]{2,1,0:T(8,128)(2,1)S(1)}, bf16[4,112,960]{2,1,0:T(8,128)(2,1)S(1)}, u32[]{:S(2)}, u32[]{:S(2)}) collective-permute-start(bf16[4,112,960]{2,1,0:T(8,128)(2,1)S(1)} %pad_maximum_fusion.10), channel_id=1, source_target_pairs={{0,1},{1,0},{2,3},{3,2},{4,5},{5,4},{6,7},{7,6},{8,9},{9,8},{10,11... | collective-permute-start | bytes 2580488 | tf_op jit(solution)/shard_map/ppermute | solution.py:107
  65.9 36.1 %collective-permute-start.10 = (bf16[4,96,960]{2,1,0:T(8,128)(2,1)S(1)}, bf16[4,96,960]{2,1,0:T(8,128)(2,1)S(1)}, u32[]{:S(2)}, u32[]{:S(2)}) collective-permute-start(bf16[4,96,960]{2,1,0:T(8,128)(2,1)S(1)} %pad_maximum_fusion.12), channel_id=1, source_target_pairs={{0,4},{1,5},{2,6},{3,7},{4,0},{5,1},{6,2},{7,3},{8,12},{9,13},{10,... | collective-permute-start | bytes 2211848 | tf_op jit(solution)/shard_map/ppermute | solution.py:107
  82.6 40.7 %collective-permute-start.7 = (bf16[8,112,960]{2,1,0:T(8,128)(2,1)S(1)}, bf16[8,112,960]{2,1,0:T(8,128)(2,1)S(1)}, u32[]{:S(2)}, u32[]{:S(2)}) collective-permute-start(bf16[8,112,960]{2,1,0:T(8,128)(2,1)S(1)} %pad_maximum_fusion.2), channel_id=1, source_target_pairs={{0,1},{1,0},{2,3},{3,2},{4,5},{5,4},{6,7},{7,6},{8,9},{9,8},{10,11... | collective-permute-start | bytes 5160968 | tf_op jit(solution)/shard_map/ppermute | solution.py:107
  85.2 39.7 %collective-permute-start.3 = (bf16[8,112,960]{2,1,0:T(8,128)(2,1)S(1)}, bf16[8,112,960]{2,1,0:T(8,128)(2,1)S(1)}, u32[]{:S(2)}, u32[]{:S(2)}) collective-permute-start(bf16[8,112,960]{2,1,0:T(8,128)(2,1)S(1)} %pad_maximum_fusion.1), channel_id=1, source_target_pairs={{0,16},{8,24},{16,0},{24,8},{1,17},{9,25},{17,1},{25,9},{2,18},{10... | collective-permute-start | bytes 5160968 | tf_op jit(solution)/shard_map/ppermute | solution.py:107
  102.1 33.5 %collective-permute-start.11 = (bf16[8,96,960]{2,1,0:T(8,128)(2,1)S(1)}, bf16[8,96,960]{2,1,0:T(8,128)(2,1)S(1)}, u32[]{:S(2)}, u32[]{:S(2)}) collective-permute-start(bf16[8,96,960]{2,1,0:T(8,128)(2,1)S(1)} %pad_maximum_fusion.4), channel_id=1, source_target_pairs={{0,2},{1,3},{2,0},{3,1},{4,6},{5,7},{6,4},{7,5},{8,10},{9,11},{10,... | collective-permute-start | bytes 4423688 | tf_op jit(solution)/shard_map/ppermute | solution.py:107
  124.7 21.4 %collective-permute-start.13 = (bf16[16,112,960]{2,1,0:T(8,128)(2,1)}, bf16[16,112,960]{2,1,0:T(8,128)(2,1)}, u32[]{:S(2)}, u32[]{:S(2)}) collective-permute-start(bf16[16,112,960]{2,1,0:T(8,128)(2,1)} %constant_dynamic-update-slice_fusion.5.refs_1_), channel_id=1, source_target_pairs={{0,8},{8,0},{16,24},{24,16},{1,9},{9,1},{17,25},{25,17},{2,10},{10... | collective-permute-start | bytes 10321928 | tf_op jit(solution)/shard_map/ppermute | solution.py:107
  126.4 19.7 %collective-permute-start.12 = (bf16[16,112,960]{2,1,0:T(8,128)(2,1)}, bf16[16,112,960]{2,1,0:T(8,128)(2,1)}, u32[]{:S(2)}, u32[]{:S(2)}) collective-permute-start(bf16[16,112,960]{2,1,0:T(8,128)(2,1)} %constant_dynamic-update-slice_fusion.refs_0_), channel_id=1, source_target_pairs={{0,8},{8,0},{16,24},{24,16},{1,9},{9,1},{17,25},{25,17},{2,10},{10... | collective-permute-start | bytes 10321928 | tf_op jit(solution)/shard_map/ppermute | solution.py:107
  175.9 25.3 %collective-permute-start.18 = (bf16[1,640,256]{2,1,0:T(8,128)(2,1)S(1)}, bf16[1,640,256]{2,1,0:T(8,128)(2,1)S(1)}, u32[]{:S(2)}, u32[]{:S(2)}) collective-permute-start(bf16[1,640,256]{2,1,0:T(8,128)(2,1)S(1)} %bitcast.147), channel_id=1, source_target_pairs={{0,4},{1,5},{2,6},{3,7},{4,0},{5,1},{6,2},{7,3},{8,12},{9,13},{10,... | collective-permute-start | bytes 983048 | tf_op jit(solution)/shard_map/ppermute | solution.py:107
  177.1 31.1 %collective-permute-start.15 = (bf16[1,640,256]{2,1,0:T(8,128)(2,1)S(1)}, bf16[1,640,256]{2,1,0:T(8,128)(2,1)S(1)}, u32[]{:S(2)}, u32[]{:S(2)}) collective-permute-start(bf16[1,640,256]{2,1,0:T(8,128)(2,1)S(1)} %bitcast.144), channel_id=1, source_target_pairs={{0,4},{1,5},{2,6},{3,7},{4,0},{5,1},{6,2},{7,3},{8,12},{9,13},{10,... | collective-permute-start | bytes 983048 | tf_op jit(solution)/shard_map/ppermute | solution.py:107
  201.3 20.8 %collective-permute-start.19 = (bf16[2,640,256]{2,1,0:T(8,128)(2,1)S(1)}, bf16[2,640,256]{2,1,0:T(8,128)(2,1)S(1)}, u32[]{:S(2)}, u32[]{:S(2)}) collective-permute-start(bf16[2,640,256]{2,1,0:T(8,128)(2,1)S(1)} %pad_maximum_fusion.18), channel_id=1, source_target_pairs={{0,2},{1,3},{2,0},{3,1},{4,6},{5,7},{6,4},{7,5},{8,10},{9,11},{10,... | collective-permute-start | bytes 1966088 | tf_op jit(solution)/shard_map/ppermute | solution.py:107
  208.2 27.9 %collective-permute-start.16 = (bf16[2,640,256]{2,1,0:T(8,128)(2,1)S(1)}, bf16[2,640,256]{2,1,0:T(8,128)(2,1)S(1)}, u32[]{:S(2)}, u32[]{:S(2)}) collective-permute-start(bf16[2,640,256]{2,1,0:T(8,128)(2,1)S(1)} %pad_maximum_fusion.17), channel_id=1, source_target_pairs={{0,2},{1,3},{2,0},{3,1},{4,6},{5,7},{6,4},{7,5},{8,10},{9,11},{10,... | collective-permute-start | bytes 1966088 | tf_op jit(solution)/shard_map/ppermute | solution.py:107
  223.5 35.7 %collective-permute-start.20 = (bf16[4,640,256]{2,1,0:T(8,128)(2,1)}, bf16[4,640,256]{2,1,0:T(8,128)(2,1)}, u32[]{:S(2)}, u32[]{:S(2)}) collective-permute-start(bf16[4,640,256]{2,1,0:T(8,128)(2,1)} %pad_maximum_fusion.6), channel_id=1, source_target_pairs={{0,1},{1,0},{2,3},{3,2},{4,5},{5,4},{6,7},{7,6},{8,9},{9,8},{10,11... | collective-permute-start | bytes 3932168 | tf_op jit(solution)/shard_map/ppermute | solution.py:107
  237.4 45.1 %collective-permute-start.17 = (bf16[4,640,256]{2,1,0:T(8,128)(2,1)}, bf16[4,640,256]{2,1,0:T(8,128)(2,1)}, u32[]{:S(2)}, u32[]{:S(2)}) collective-permute-start(bf16[4,640,256]{2,1,0:T(8,128)(2,1)} %pad_maximum_fusion.5), channel_id=1, source_target_pairs={{0,1},{1,0},{2,3},{3,2},{4,5},{5,4},{6,7},{7,6},{8,9},{9,8},{10,11... | collective-permute-start | bytes 3932168 | tf_op jit(solution)/shard_map/ppermute | solution.py:107
  442.2 32.0 %collective-permute-start.21 = (bf16[4,2,5,128,128]{4,3,1,0,2:T(8,128)(2,1)}, bf16[4,2,5,128,128]{4,3,1,0,2:T(8,128)(2,1)}, u32[]{:S(2)}, u32[]{:S(2)}) collective-permute-start(bf16[4,2,5,128,128]{4,3,1,0,2:T(8,128)(2,1)} %get-tuple-element.92), channel_id=1, source_target_pairs={{0,1},{1,0},{2,3},{3,2},{4,5},{5,4},{6,7},{7,6},{8,9},{9,8},{10,11... | collective-permute-start | bytes 3932168 | tf_op jit(solution)/shard_map/ppermute | solution.py:107
  442.6 57.7 %collective-permute-start.24 = (bf16[4,2,5,128,128]{4,3,1,0,2:T(8,128)(2,1)}, bf16[4,2,5,128,128]{4,3,1,0,2:T(8,128)(2,1)}, u32[]{:S(2)}, u32[]{:S(2)}) collective-permute-start(bf16[4,2,5,128,128]{4,3,1,0,2:T(8,128)(2,1)} %get-tuple-element.93), channel_id=1, source_target_pairs={{0,1},{1,0},{2,3},{3,2},{4,5},{5,4},{6,7},{7,6},{8,9},{9,8},{10,11... | collective-permute-start | bytes 3932168 | tf_op jit(solution)/shard_map/ppermute | solution.py:107
  505.3 21.5 %collective-permute-start.22 = (bf16[2,2,5,128,128]{4,3,1,0,2:T(8,128)(2,1)}, bf16[2,2,5,128,128]{4,3,1,0,2:T(8,128)(2,1)}, u32[]{:S(2)}, u32[]{:S(2)}) collective-permute-start(bf16[2,2,5,128,128]{4,3,1,0,2:T(8,128)(2,1)} %get-tuple-element.83), channel_id=1, source_target_pairs={{0,2},{1,3},{2,0},{3,1},{4,6},{5,7},{6,4},{7,5},{8,10},{9,11},{10,... | collective-permute-start | bytes 1966088 | tf_op jit(solution)/shard_map/ppermute | solution.py:107
  515.2 25.1 %collective-permute-start.25 = (bf16[2,2,5,128,128]{4,3,1,0,2:T(8,128)(2,1)}, bf16[2,2,5,128,128]{4,3,1,0,2:T(8,128)(2,1)S(1)}, u32[]{:S(2)}, u32[]{:S(2)}) collective-permute-start(bf16[2,2,5,128,128]{4,3,1,0,2:T(8,128)(2,1)} %get-tuple-element.90), channel_id=1, source_target_pairs={{0,2},{1,3},{2,0},{3,1},{4,6},{5,7},{6,4},{7,5},{8,10},{9,11},{10,... | collective-permute-start | bytes 1966088 | tf_op jit(solution)/shard_map/ppermute | solution.py:107
  527.9 22.8 %collective-permute-start.23 = (bf16[1,2,5,128,128]{4,3,1,0,2:T(8,128)(2,1)S(1)}, bf16[1,2,5,128,128]{4,3,1,0,2:T(8,128)(2,1)S(1)}, u32[]{:S(2)}, u32[]{:S(2)}) collective-permute-start(bf16[1,2,5,128,128]{4,3,1,0,2:T(8,128)(2,1)S(1)} %add_convert_fusion.18), channel_id=1, source_target_pairs={{0,4},{1,5},{2,6},{3,7},{4,0},{5,1},{6,2},{7,3},{8,12},{9,13},{10,... | collective-permute-start | bytes 983048 | tf_op jit(solution)/shard_map/ppermute | solution.py:107
  630.6 59.3 %collective-permute-start.28 = (bf16[8,112,960]{2,1,0:T(8,128)(2,1)}, bf16[8,112,960]{2,1,0:T(8,128)(2,1)}, u32[]{:S(2)}, u32[]{:S(2)}) collective-permute-start(bf16[8,112,960]{2,1,0:T(8,128)(2,1)} %slice.318), channel_id=1, source_target_pairs={{0,16},{8,24},{16,0},{24,8},{1,17},{9,25},{17,1},{25,9},{2,18},{10... | collective-permute-start | bytes 5160968 | tf_op jit(solution)/shard_map/ppermute | solution.py:107
  633.5 52.0 %collective-permute-start.36 = (bf16[8,96,960]{2,1,0:T(8,128)(2,1)}, bf16[8,96,960]{2,1,0:T(8,128)(2,1)}, u32[]{:S(2)}, u32[]{:S(2)}) collective-permute-start(bf16[8,96,960]{2,1,0:T(8,128)(2,1)} %slice.344), channel_id=1, source_target_pairs={{0,2},{1,3},{2,0},{3,1},{4,6},{5,7},{6,4},{7,5},{8,10},{9,11},{10,... | collective-permute-start | bytes 4423688 | tf_op jit(solution)/shard_map/ppermute | solution.py:107
  640.8 57.5 %collective-permute-start.32 = (bf16[8,112,960]{2,1,0:T(8,128)(2,1)}, bf16[8,112,960]{2,1,0:T(8,128)(2,1)}, u32[]{:S(2)}, u32[]{:S(2)}) collective-permute-start(bf16[8,112,960]{2,1,0:T(8,128)(2,1)} %slice.331), channel_id=1, source_target_pairs={{0,1},{1,0},{2,3},{3,2},{4,5},{5,4},{6,7},{7,6},{8,9},{9,8},{10,11... | collective-permute-start | bytes 5160968 | tf_op jit(solution)/shard_map/ppermute | solution.py:107
  641.7 31.4 %collective-permute-start.41 = (f32[2,960]{1,0:T(2,128)S(1)}, f32[2,960]{1,0:T(2,128)S(1)}, u32[]{:S(2)}, u32[]{:S(2)}) collective-permute-start(f32[2,960]{1,0:T(2,128)S(1)} %fusion.27), channel_id=1, source_target_pairs={{0,16},{8,24},{16,0},{24,8},{1,17},{9,25},{17,1},{25,9},{2,18},{10... | collective-permute-start | bytes 23048 | tf_op jit(solution)/shard_map/ppermute | solution.py:107
  688.9 37.2 %collective-permute-start.37 = (bf16[4,96,960]{2,1,0:T(8,128)(2,1)}, bf16[4,96,960]{2,1,0:T(8,128)(2,1)}, u32[]{:S(2)}, u32[]{:S(2)}) collective-permute-start(bf16[4,96,960]{2,1,0:T(8,128)(2,1)} %get-tuple-element.95), channel_id=1, source_target_pairs={{0,4},{1,5},{2,6},{3,7},{4,0},{5,1},{6,2},{7,3},{8,12},{9,13},{10,... | collective-permute-start | bytes 2211848 | tf_op jit(solution)/shard_map/ppermute | solution.py:107
  693.3 35.4 %collective-permute-start.29 = (bf16[4,112,960]{2,1,0:T(8,128)(2,1)}, bf16[4,112,960]{2,1,0:T(8,128)(2,1)}, u32[]{:S(2)}, u32[]{:S(2)}) collective-permute-start(bf16[4,112,960]{2,1,0:T(8,128)(2,1)} %get-tuple-element.87), channel_id=1, source_target_pairs={{0,1},{1,0},{2,3},{3,2},{4,5},{5,4},{6,7},{7,6},{8,9},{9,8},{10,11... | collective-permute-start | bytes 2580488 | tf_op jit(solution)/shard_map/ppermute | solution.py:107
  695.8 32.3 %collective-permute-start.44 = (f32[2,960]{1,0:T(2,128)S(1)}, f32[2,960]{1,0:T(2,128)S(1)}, u32[]{:S(2)}, u32[]{:S(2)}) collective-permute-start(f32[2,960]{1,0:T(2,128)S(1)} %add.396), channel_id=1, source_target_pairs={{0,4},{1,5},{2,6},{3,7},{4,0},{5,1},{6,2},{7,3},{8,12},{9,13},{10,... | collective-permute-start | bytes 23048 | tf_op jit(solution)/shard_map/ppermute | solution.py:107
  701.1 40.3 %collective-permute-start.33 = (bf16[4,112,960]{2,1,0:T(8,128)(2,1)S(1)}, bf16[4,112,960]{2,1,0:T(8,128)(2,1)S(1)}, u32[]{:S(2)}, u32[]{:S(2)}) collective-permute-start(bf16[4,112,960]{2,1,0:T(8,128)(2,1)S(1)} %get-tuple-element.89), channel_id=1, source_target_pairs={{0,2},{1,3},{2,0},{3,1},{4,6},{5,7},{6,4},{7,5},{8,10},{9,11},{10,... | collective-permute-start | bytes 2580488 | tf_op jit(solution)/shard_map/ppermute | solution.py:107
  730.2 19.7 %collective-permute-start.30 = (bf16[2,112,960]{2,1,0:T(8,128)(2,1)S(1)}, bf16[2,112,960]{2,1,0:T(8,128)(2,1)S(1)}, u32[]{:S(2)}, u32[]{:S(2)}) collective-permute-start(bf16[2,112,960]{2,1,0:T(8,128)(2,1)S(1)} %get-tuple-element.105), channel_id=1, source_target_pairs={{0,2},{1,3},{2,0},{3,1},{4,6},{5,7},{6,4},{7,5},{8,10},{9,11},{10,... | collective-permute-start | bytes 1290248 | tf_op jit(solution)/shard_map/ppermute | solution.py:107
  741.7 25.8 %collective-permute-start.34 = (bf16[2,112,960]{2,1,0:T(8,128)(2,1)S(1)}, bf16[2,112,960]{2,1,0:T(8,128)(2,1)S(1)}, u32[]{:S(2)}, u32[]{:S(2)}) collective-permute-start(bf16[2,112,960]{2,1,0:T(8,128)(2,1)S(1)} %get-tuple-element.107), channel_id=1, source_target_pairs={{0,4},{1,5},{2,6},{3,7},{4,0},{5,1},{6,2},{7,3},{8,12},{9,13},{10,... | collective-permute-start | bytes 1290248 | tf_op jit(solution)/shard_map/ppermute | solution.py:107
  750.0 21.4 %collective-permute-start.31 = (bf16[1,112,960]{2,1,0:T(8,128)(2,1)S(1)}, bf16[1,112,960]{2,1,0:T(8,128)(2,1)S(1)}, u32[]{:S(2)}, u32[]{:S(2)}) collective-permute-start(bf16[1,112,960]{2,1,0:T(8,128)(2,1)S(1)} %add_convert_fusion.22), channel_id=1, source_target_pairs={{0,4},{1,5},{2,6},{3,7},{4,0},{5,1},{6,2},{7,3},{8,12},{9,13},{10,... | collective-permute-start | bytes 645128 | tf_op jit(solution)/shard_map/ppermute | solution.py:107
  (70 other events, 747.9 us)

commit v3 on v2

v3 whole, which is shorter than its diff:
```python
import jax
import jax.numpy as jnp
import numpy as np
from jax import lax
from jax.experimental import pallas as pl
from jax.experimental.pallas import tpu as pltpu
from jax.sharding import Mesh
from jax.sharding import PartitionSpec as P

HEADS = 15
KV = 5
HD = 64
FF = 2560
STEP = 10


SCALE_QK = 0.125
THETA = 10000.0
EPSILON = 1e-05
BETA_ONE = 0.9
BETA_TWO = 0.95
ADAM_EPS = 1e-08
DECAY = 0.1
RATE = 0.02
GAIN_RATE = 0.2
GROUP = HEADS // KV
KEY_TILE = 256
HIDDEN = -1e30
VMEM_BYTES = 48 * 1024 * 1024


def places(row_index, local_rows, ctx_count):
    half_rows = local_rows // 2
    owner_index = row_index // local_rows
    inner_index = row_index % local_rows
    return jnp.where(
        inner_index < half_rows,
        owner_index * half_rows + inner_index,
        (2 * ctx_count - 1 - owner_index) * half_rows + inner_index - half_rows,
    )


def angle_tables(positions_in, sign):
    half_width = HD // 2
    frequency = THETA ** (-jnp.arange(half_width, dtype=jnp.float32) * 2.0 / HD)
    angles = frequency[:, None] * positions_in.astype(jnp.float32)[None, :]
    return jnp.cos(angles), sign * jnp.sin(angles)


def rotate(values, tables):
    cosine, sine_part = tables
    heads = values.reshape(-1, HD, values.shape[-1])
    first_half = heads[:, : HD // 2]
    second_half = heads[:, HD // 2 :]
    return jnp.concatenate(
        [
            first_half * cosine - second_half * sine_part,
            second_half * cosine + first_half * sine_part,
        ],
        axis=1,
    ).reshape(values.shape)


def normalize(values):
    return values * lax.rsqrt(jnp.mean(values * values, axis=-1, keepdims=True) + EPSILON)


def norm_back(values, grad_in, gain_row):
    inv_scale = lax.rsqrt(jnp.mean(values * values, axis=-1, keepdims=True) + EPSILON)
    unit_rows = values * inv_scale
    grad_unit = grad_in * gain_row
    grad_values = inv_scale * (
        grad_unit - unit_rows * jnp.mean(grad_unit * unit_rows, axis=-1, keepdims=True)
    )
    return (grad_values, jnp.sum(grad_in * unit_rows, axis=0))


def matmul_n(left, right):
    return jnp.dot(left, right, preferred_element_type=jnp.float32)


def matmul_t(left, right):
    return lax.dot_general(
        left, right, (((1,), (1,)), ((), ())), preferred_element_type=jnp.float32
    )


def matmul_c(left, right):
    return lax.dot_general(
        left, right, (((0,), (0,)), ((), ())), preferred_element_type=jnp.float32
    )


def bit_groups():
    x_bits = lax.axis_size("x").bit_length() - 1
    ctx_bits = lax.axis_size("ctx").bit_length() - 1
    low_ctx = ctx_bits // 2
    along_x = [("x", bit) for bit in range(x_bits)]
    along_y = [("ctx", bit) for bit in range(low_ctx)]
    along_z = [("ctx", bit) for bit in range(low_ctx, ctx_bits)]
    return along_x, along_y, along_z


def swap_by(values, axis, offset):
    size = lax.axis_size(axis)
    return lax.ppermute(values, axis, [(i, i ^ offset) for i in range(size)])


def swap(values, where):
    return swap_by(values, where[0], 1 << where[1])


def add_low(left, right):
    return (left.astype(jnp.float32) + right.astype(jnp.float32)).astype(jnp.bfloat16)


def rel_offsets(order):
    strides = {"x": 2 * lax.axis_size("ctx"), "ctx": 1}
    offsets = np.zeros((1,), np.int64)
    for axis, bit in order:
        offsets = np.concatenate([offsets, offsets ^ (strides[axis] << bit)])
    return offsets


def lookup(slot, offsets):
    total = jnp.int32(0)
    for bit in range(len(offsets).bit_length() - 1):
        total = total + ((slot >> bit) & 1) * int(offsets[1 << bit])
    return total


def find(offset, offsets):
    total = jnp.int32(0)
    for bit in range(len(offsets).bit_length() - 1):
        place = int(offsets[1 << bit]).bit_length() - 1
        total = total + (((offset >> place) & 1) << bit)
    return total


def collect(values, order):
    kept, arrived = values, None
    for where in order:
        half = kept.shape[0] // 2
        if arrived is None:
            away, kept_next = kept[half:], kept[:half]
        else:
            away = add_low(kept[half:], arrived[half:])
            kept_next = add_low(kept[:half], arrived[:half])
        arrived = swap(away, where)
        kept = kept_next
    return kept[0].astype(jnp.float32) + arrived[0].astype(jnp.float32)


def scatter_whole(terms):
    ctx_count = lax.axis_size("ctx")
    count = 2 * lax.axis_size("x") * ctx_count
    along_x, along_y, along_z = bit_groups()
    core = ("core", 0)
    me = device_index().reshape(1)
    blocks, rows, width = terms[0].shape
    first = -(-rows // 48) * 16
    groups = [(0, first), (first, 2 * first), (2 * first, rows)]
    orders = [
        along_x + along_y + along_z,
        along_y + along_z + along_x,
        along_z + along_x + along_y,
    ]
    tables = [rel_offsets(list(reversed(order))) for order in orders]

    def target(step, me_ref, flip):
        return lookup(step, tables[0]) ^ me_ref[0] ^ flip

    def sources(flip):
        def chosen(member):
            def index(step, me_ref):
                spot = target(step, me_ref, flip)
                return (jnp.where(spot // blocks == member, spot % blocks, 0), 0, 0)

            return pl.BlockSpec((1, rows, width), index)

        return [chosen(member) for member in range(len(terms))]

    def pick_body(me_ref, *refs):
        held = target(pl.program_id(0), me_ref, ctx_count) // blocks
        for member in range(len(terms)):

            @pl.when(held == member)
            def _(member=member):
                refs[-1][...] = refs[member][...]

    away = pl.pallas_call(
        pick_body,
        grid_spec=pltpu.PrefetchScalarGridSpec(
            num_scalar_prefetch=1,
            grid=(count // 2,),
            in_specs=sources(ctx_count),
            out_specs=pl.BlockSpec((1, rows, width), lambda step, me_ref: (step, 0, 0)),
        ),
        out_shape=jax.ShapeDtypeStruct((count // 2, rows, width), jnp.bfloat16),
        compiler_params=pltpu.CompilerParams(vmem_limit_bytes=VMEM_BYTES),
    )(me, *terms)
    arrived = swap(away, core)

    def merge_body(me_ref, *refs):
        held = target(pl.program_id(0), me_ref, 0) // blocks
        for member in range(len(terms)):

            @pl.when(held == member)
            def _(member=member):
                for (low, high), out in zip(groups, refs[-3:]):
                    out[0] = add_low(refs[member][0, low:high], refs[-4][0, low:high])

    parts = pl.pallas_call(
        merge_body,
        grid_spec=pltpu.PrefetchScalarGridSpec(
            num_scalar_prefetch=1,
            grid=(count // 2,),
            in_specs=sources(0)
            + [pl.BlockSpec((1, rows, width), lambda step, me_ref: (step, 0, 0))],
            out_specs=[
                pl.BlockSpec(
                    (1, high - low, width),
                    lambda step, me_ref, table=table: (
                        find(lookup(step, tables[0]), table),
                        0,
                        0,
                    ),
                )
                for (low, high), table in zip(groups, tables)
            ],
        ),
        out_shape=[
            jax.ShapeDtypeStruct((count // 2, high - low, width), jnp.bfloat16)
            for low, high in groups
        ],
        compiler_params=pltpu.CompilerParams(vmem_limit_bytes=VMEM_BYTES),
    )(me, *terms, arrived)
    return jnp.concatenate([collect(part, order) for part, order in zip(parts, orders)], axis=0)


def device_index():
    return (
        (lax.axis_index("x") * 2 + lax.axis_index("core")) * lax.axis_size("ctx")
        + lax.axis_index("ctx")
    ).astype(jnp.int32)


def splits_rows(rows):
    return lax.axis_size("x") == 2 and rows % 32 == 0


def reduce_ctx(keep, away):
    arrived = swap(away, ("core", 0))
    along_x, along_y, along_z = bit_groups()
    rows = keep.shape[2]
    first = -(-rows // 32) * 16
    sums = []
    plain = along_y + along_z
    ctx_bits = len(plain)
    for low, high, order in ((0, first, plain), (first, rows, along_z + along_y)):
        shape = (keep.shape[0],) + (2,) * ctx_bits + (high - low, keep.shape[3])
        held = keep[:, :, low:high].reshape(shape)
        come = arrived[:, :, low:high].reshape(shape)
        left = list(reversed(range(ctx_bits)))
        for where in order:
            dim = 1 + left.index(where[1])
            left.remove(where[1])
            sent = add_low(
                lax.index_in_dim(held, 1, dim, False), lax.index_in_dim(come, 1, dim, False)
            )
            held = add_low(
                lax.index_in_dim(held, 0, dim, False), lax.index_in_dim(come, 0, dim, False)
            )
            come = swap(sent, where)
        sums.append(add_low(held, come))
    return jnp.concatenate(sums, axis=1)


def turned(values):
    return jnp.transpose(values)


def load_packed(ref, aligned):
    if not aligned:
        return ref[0, 0]
    half = ref.shape[1] // 2
    return jnp.concatenate(
        [
            ref[head * HD : (head + 1) * HD, side * half : (side + 1) * half]
            for side in range(2)
            for head in range(GROUP)
        ],
        axis=1,
    )


def store_packed(ref, values, aligned):
    if not aligned:
        ref[0, 0] = values
        return
    half = ref.shape[1] // 2
    for side in range(2):
        for head in range(GROUP):
            start = (side * GROUP + head) * half
            ref[head * HD : (head + 1) * HD, side * half : (side + 1) * half] = values[
                :, start : start + half
            ]


def load_tile(refs, side, tile):
    length = refs[0].shape[1] // 2
    if length >= KEY_TILE:
        start = side * length + tile * KEY_TILE
        return refs[0][:, start : start + KEY_TILE]
    many = KEY_TILE // length
    return jnp.concatenate(
        [
            ref[:, side * length : (side + 1) * length]
            for ref in refs[tile * many : (tile + 1) * many]
        ],
        axis=1,
    )


def attend_body(count, aligned, queries_ref, key_pos_ref, query_pos_ref, *refs):
    key_refs, value_refs = refs[:count], refs[count : 2 * count]
    out_ref, total_ref, work = refs[2 * count :]
    queries = load_packed(queries_ref, aligned)
    low_cols = queries.shape[1] // 2
    queries_high = queries[:, low_cols:]
    tiles = key_pos_ref.shape[1] // KEY_TILE
    largest = jnp.full((1, queries.shape[1]), HIDDEN, jnp.float32)
    largest_high = jnp.full((1, low_cols), HIDDEN, jnp.float32)
    for side in range(2):
        for tile in range(tiles):
            keys = turned(load_tile(key_refs, side, tile))
            row = (side * tiles + tile) * KEY_TILE
            key_places = key_pos_ref[side, tile * KEY_TILE : (tile + 1) * KEY_TILE]
            if side == 0:
                scores = matmul_n(keys, queries)
                scores = jnp.where(key_places <= query_pos_ref[...], scores, HIDDEN)
                work[row : row + KEY_TILE] = scores
                largest = jnp.maximum(largest, jnp.max(scores, axis=0, keepdims=True))
            else:
                scores = matmul_n(keys, queries_high)
                scores = jnp.where(key_places <= query_pos_ref[:, low_cols:], scores, HIDDEN)
                work[row : row + KEY_TILE, low_cols:] = scores
                largest_high = jnp.maximum(largest_high, jnp.max(scores, axis=0, keepdims=True))
    high_max = jnp.maximum(largest[:, low_cols:], largest_high)
    largest = jnp.concatenate([largest[:, :low_cols], high_max], axis=1)
    total = jnp.zeros_like(largest)
    mixed = jnp.zeros((HD, queries.shape[1]), jnp.float32)
    total_high = jnp.zeros_like(largest_high)
    mixed_high = jnp.zeros((HD, low_cols), jnp.float32)
    for side in range(2):
        for tile in range(tiles):
            values = load_tile(value_refs, side, tile)
            row = (side * tiles + tile) * KEY_TILE
            if side == 0:
                expos = jnp.exp(work[row : row + KEY_TILE] - largest)
                total = total + jnp.sum(expos, axis=0, keepdims=True)
                mixed = mixed + matmul_n(values, expos.astype(jnp.bfloat16))
            else:
                expos = jnp.exp(work[row : row + KEY_TILE, low_cols:] - high_max)
                total_high = total_high + jnp.sum(expos, axis=0, keepdims=True)
                mixed_high = mixed_high + matmul_n(values, expos.astype(jnp.bfloat16))
    total = jnp.concatenate([total[:, :low_cols], total[:, low_cols:] + total_high], axis=1)
    mixed = jnp.concatenate([mixed[:, :low_cols], mixed[:, low_cols:] + mixed_high], axis=1)
    store_packed(out_ref, (mixed / total).astype(jnp.bfloat16), aligned)
    total_ref[0, 0] = largest + jnp.log(total)


def attend_back_body(
    count, aligned, queries_ref, key_pos_ref, query_pos_ref, *refs
):
    key_refs, value_refs = refs[:count], refs[count : 2 * count]
    out_ref, total_ref, d_out_ref, cosine_ref, sine_ref = refs[2 * count : 2 * count + 5]
    d_queries_ref, pair_refs = refs[2 * count + 5], refs[2 * count + 6 :]
    all_queries, all_d_out = load_packed(queries_ref, aligned), load_packed(d_out_ref, aligned)
    low_cols = all_queries.shape[1] // 2
    tiles = key_pos_ref.shape[1] // KEY_TILE
    delta = jnp.sum(
        all_d_out.astype(jnp.float32) * load_packed(out_ref, aligned).astype(jnp.float32),
        axis=0,
        keepdims=True,
    )
    totals = total_ref[0, 0]
    parts = []
    for side in range(2):
        if side == 0:
            queries, d_out = all_queries, all_d_out
            query_places, log_total, row_delta = query_pos_ref[...], totals, delta
        else:
            queries, d_out = all_queries[:, low_cols:], all_d_out[:, low_cols:]
            query_places = query_pos_ref[:, low_cols:]
            log_total, row_delta = totals[:, low_cols:], delta[:, low_cols:]
        part = jnp.zeros((HD, queries.shape[1]), jnp.float32)
        for tile in range(tiles):
            keys_flat = load_tile(key_refs, side, tile)
            scores = matmul_n(turned(keys_flat), queries)
            seen = key_pos_ref[side, tile * KEY_TILE : (tile + 1) * KEY_TILE] <= query_places
            probs = jnp.where(seen, jnp.exp(scores - log_total), 0.0)
            d_probs = matmul_n(turned(load_tile(value_refs, side, tile)), d_out)
            d_scores = (probs * (d_probs - row_delta)).astype(jnp.bfloat16)
            part = part + matmul_n(keys_flat, d_scores)
            d_key = matmul_t(d_scores, queries).astype(jnp.bfloat16)
            d_value = matmul_t(probs.astype(jnp.bfloat16), d_out).astype(jnp.bfloat16)
            if aligned:
                length = key_refs[0].shape[1] // 2
                near = pair_refs[0].shape[0]
                for piece in range(KEY_TILE // length):
                    slot = tile * (KEY_TILE // length) + piece
                    ref = pair_refs[slot // near]
                    rows = slice(piece * length, (piece + 1) * length)
                    ref[slot % near, 0, side, :, :HD] = d_key[rows]
                    ref[slot % near, 0, side, :, HD:] = d_value[rows]
            else:
                rows = slice(tile * KEY_TILE, (tile + 1) * KEY_TILE)
                pair_refs[0][side, 0, rows, :HD] = d_key
                pair_refs[0][side, 0, rows, HD:] = d_value
        parts.append(part)
    d_queries = jnp.concatenate(
        [parts[0][:, :low_cols], parts[0][:, low_cols:] + parts[1]], axis=1
    )
    cosine, sine_part = cosine_ref[...], sine_ref[...]
    first_half, second_half = d_queries[: HD // 2], d_queries[HD // 2 :]
    turned_back = jnp.concatenate(
        [
            first_half * cosine + second_half * sine_part,
            second_half * cosine - first_half * sine_part,
        ],
        axis=0,
    )
    store_packed(d_queries_ref, (turned_back * SCALE_QK).astype(jnp.bfloat16), aligned)


def head_specs(count, aligned, cols, keys, local_rows, seq):
    if aligned:
        packed = pl.BlockSpec((GROUP * HD, local_rows), lambda head: (head, seq))
    else:
        packed = pl.BlockSpec((1, 1, HD, cols), lambda head: (seq, head, 0, 0))
    specs = [
        packed,
        pl.BlockSpec((2, keys, 1), lambda head: (0, 0, 0)),
        pl.BlockSpec((1, cols), lambda head: (0, 0)),
    ]
    specs += [pl.BlockSpec((HD, 2 * keys // count), lambda head: (head, seq))] * count
    specs += [pl.BlockSpec((HD, 2 * keys // count), lambda head: (KV + head, seq))] * count
    return packed, specs


def attend(queries, pairs, key_pos, query_pos, local_rows, seq):
    aligned = queries.ndim == 2
    cols, keys, count = query_pos.shape[1], key_pos.shape[1], len(pairs)
    _, specs = head_specs(count, aligned, cols, keys, local_rows, seq)
    work = HEADS * keys * cols // GROUP * 3 // 2
    if aligned:
        out_spec = pl.BlockSpec((GROUP * HD, local_rows), lambda head: (head, 0))
        out_shape = jax.ShapeDtypeStruct((HEADS * HD, local_rows), jnp.bfloat16)
    else:
        out_spec = pl.BlockSpec((1, 1, HD, cols), lambda head: (0, head, 0, 0))
        out_shape = jax.ShapeDtypeStruct((1, KV, HD, cols), jnp.bfloat16)
    return pl.pallas_call(
        lambda *refs: attend_body(count, aligned, *refs),
        grid=(KV,),
        in_specs=specs,
        out_specs=[out_spec, pl.BlockSpec((1, 1, 1, cols), lambda head: (0, head, 0, 0))],
        out_shape=[out_shape, jax.ShapeDtypeStruct((1, KV, 1, cols), jnp.float32)],
        scratch_shapes=[pltpu.VMEM((2 * keys, cols), jnp.float32)],
        cost_estimate=pl.CostEstimate(
            flops=work * HD * 4, bytes_accessed=8 * 1024 * 1024, transcendentals=work
        ),
        compiler_params=pltpu.CompilerParams(vmem_limit_bytes=VMEM_BYTES),
    )(queries, key_pos, query_pos, *pairs, *pairs)


def attend_back(
    queries, pairs, key_pos, query_pos, mixed, log_total, d_mixed, tables, local_rows, seq, near
):
    aligned = queries.ndim == 2
    cols, keys, count = query_pos.shape[1], key_pos.shape[1], len(pairs)
    packed, specs = head_specs(count, aligned, cols, keys, local_rows, seq)
    work = HEADS * keys * cols // GROUP * 3 // 2
    if aligned:
        own = pl.BlockSpec((GROUP * HD, local_rows), lambda head: (head, 0))
        own_shape = jax.ShapeDtypeStruct((HEADS * HD, local_rows), jnp.bfloat16)
        length = keys // count
        pair_specs = [
            pl.BlockSpec((near, 1, 2, length, 2 * HD), lambda head: (0, head, 0, 0, 0))
        ] * (count // near)
        pair_shapes = [jax.ShapeDtypeStruct((near, KV, 2, length, 2 * HD), jnp.bfloat16)] * (
            count // near
        )
    else:
        own = pl.BlockSpec((1, 1, HD, cols), lambda head: (0, head, 0, 0))
        own_shape = jax.ShapeDtypeStruct((1, KV, HD, cols), jnp.bfloat16)
        pair_specs = [pl.BlockSpec((2, 1, keys, 2 * HD), lambda head: (0, head, 0, 0))]
        pair_shapes = [jax.ShapeDtypeStruct((2, KV, keys, 2 * HD), jnp.bfloat16)]
    table_spec = pl.BlockSpec((HD // 2, cols), lambda head: (0, 0))
    return pl.pallas_call(
        lambda *refs: attend_back_body(count, aligned, *refs),
        grid=(KV,),
        in_specs=specs
        + [
            own,
            pl.BlockSpec((1, 1, 1, cols), lambda head: (0, head, 0, 0)),
            packed,
            table_spec,
            table_spec,
        ],
        out_specs=[own] + pair_specs,
        out_shape=[own_shape] + pair_shapes,
        cost_estimate=pl.CostEstimate(
            flops=work * HD * 10, bytes_accessed=16 * 1024 * 1024, transcendentals=work
        ),
        compiler_params=pltpu.CompilerParams(vmem_limit_bytes=VMEM_BYTES),
    )(queries, key_pos, query_pos, *pairs, *pairs, mixed, log_total, d_mixed, *tables)


def put_rows(values, keep_ref, away_ref, member, core):
    half = values.shape[0] // 2
    for mine, low, far in ((0, 0, half), (1, half, 0)):

        @pl.when(core == mine)
        def _(low=low, far=far):
            keep_ref[member, 0] = values[low : low + half]
            away_ref[member, 0] = values[far : far + half]


def feed_body(
    parts, split, me_ref, a_two_ref, dy_ref, *refs
):
    weight_refs, (out_ref, d_two_ref), grad_refs = refs[:6], refs[6:8], refs[8:]
    core = me_ref[0]
    step = pl.program_id(0)

    @pl.when(step == 0)
    def _():
        out_ref[...] = jnp.zeros_like(out_ref)
        d_two_ref[...] = jnp.zeros_like(d_two_ref)

    def rows_of(member):
        wanted = feed_core(member, step, parts)
        return jnp.where(wanted == core, weight_refs[2 * member][...], weight_refs[2 * member + 1][...])

    a_two, dy_low = a_two_ref[...], dy_ref[...]
    gate_rows, up_rows, down_rows = rows_of(0), rows_of(1), rows_of(2)
    gate_pre = matmul_t(gate_rows, a_two)
    up_pre = matmul_t(up_rows, a_two)
    d_hidden = matmul_t(down_rows, dy_low)
    sigma = jax.nn.sigmoid(gate_pre)
    gate_act = gate_pre * sigma
    hidden = (gate_act * up_pre).astype(jnp.bfloat16)
    d_gate = (d_hidden * up_pre * sigma * (1.0 + gate_pre * (1.0 - sigma))).astype(jnp.bfloat16)
    d_up = (d_hidden * gate_act).astype(jnp.bfloat16)
    out_ref[...] += matmul_c(hidden, down_rows)
    d_two_ref[...] += matmul_c(d_gate, gate_rows) + matmul_c(d_up, up_rows)
    for member, (left, right) in enumerate(((d_gate, a_two), (d_up, a_two), (hidden, dy_low))):
        grad = matmul_n(left, right).astype(jnp.bfloat16)
        if split:
            put_rows(grad, grad_refs[0], grad_refs[1], member, core)
        else:
            grad_refs[member][0] = grad


def feed_core(member, step, parts):
    ctx_count, single = parts
    return (member + 1) % 2 if single else step // ctx_count


def feed_forward(a_two, dy_low, mine, far, rows):
    tokens, width = a_two.shape
    ctx_count = lax.axis_size("ctx")
    blocks = FF // rows
    single = blocks == ctx_count
    split = splits_rows(rows)
    parts = (ctx_count, single)
    whole = pl.BlockSpec((tokens, width), lambda step, me_ref: (0, 0))

    def weight_spec(member, own):
        def index(step, me_ref):
            matches = (feed_core(member, step, parts) == me_ref[0]) == own
            return (jnp.where(matches, step % ctx_count, 0), 0)

        return pl.BlockSpec((rows, width), index)

    places_x = [(member + 1) // 2 if single else member + 1 for member in range(3)]
    weight_specs = [weight_spec(member, own) for member in range(3) for own in (True, False)]
    weight_args = [held[places_x[member]] for member in range(3) for held in (mine, far)]
    if split:
        half = pl.BlockSpec(
            (3, 1, rows // 2, width), lambda step, me_ref: (0, step ^ me_ref[1], 0, 0)
        )
        grad_specs = [half, half]
        grad_shapes = [jax.ShapeDtypeStruct((3, blocks, rows // 2, width), jnp.bfloat16)] * 2
    else:
        grad_specs = [pl.BlockSpec((1, rows, width), lambda step, me_ref: (step, 0, 0))] * 3
        grad_shapes = [jax.ShapeDtypeStruct((blocks, rows, width), jnp.bfloat16)] * 3
    me = jnp.stack([lax.axis_index("core"), lax.axis_index("ctx")]).astype(jnp.int32)
    return pl.pallas_call(
        lambda *refs: feed_body(parts, split, *refs),
        grid_spec=pltpu.PrefetchScalarGridSpec(
            num_scalar_prefetch=1,
            grid=(blocks,),
            in_specs=[whole, whole] + weight_specs,
            out_specs=[whole, whole] + grad_specs,
        ),
        out_shape=[jax.ShapeDtypeStruct((tokens, width), jnp.float32)] * 2 + grad_shapes,
        cost_estimate=pl.CostEstimate(
            flops=18 * tokens * width * FF, bytes_accessed=12 * FF * width, transcendentals=FF * tokens
        ),
        compiler_params=pltpu.CompilerParams(vmem_limit_bytes=VMEM_BYTES),
    )(me, a_two, dy_low, *weight_args)


def first_grads(d_qkv, attn_low, a_one, d_resid_low, rows):
    tokens, width = a_one.shape
    split = splits_rows(rows)
    early = d_qkv.shape[0] // rows
    blocks = early + attn_low.shape[0] // rows

    def body(me_ref, qkv_ref, attn_ref, one_ref, resid_ref, *grad_refs):
        first = pl.program_id(0) < early
        left = jnp.where(first, qkv_ref[...], attn_ref[...])
        right = jnp.where(first, one_ref[...], resid_ref[...])
        grad = matmul_n(left, right).astype(jnp.bfloat16)
        if split:
            put_rows(grad, grad_refs[0], grad_refs[1], 0, me_ref[0])
        else:
            grad_refs[0][0] = grad

    whole = pl.BlockSpec((tokens, width), lambda step, me_ref: (0, 0))
    if split:
        half = pl.BlockSpec(
            (1, 1, rows // 2, width), lambda step, me_ref: (0, step ^ me_ref[1], 0, 0)
        )
        grad_specs = [half, half]
        grad_shapes = [jax.ShapeDtypeStruct((1, blocks, rows // 2, width), jnp.bfloat16)] * 2
    else:
        grad_specs = [pl.BlockSpec((1, rows, width), lambda step, me_ref: (step, 0, 0))]
        grad_shapes = [jax.ShapeDtypeStruct((blocks, rows, width), jnp.bfloat16)]
    me = jnp.stack([lax.axis_index("core"), lax.axis_index("ctx")]).astype(jnp.int32)
    return pl.pallas_call(
        body,
        grid_spec=pltpu.PrefetchScalarGridSpec(
            num_scalar_prefetch=1,
            grid=(blocks,),
            in_specs=[
                pl.BlockSpec((rows, tokens), lambda step, me_ref: (jnp.minimum(step, early - 1), 0)),
                pl.BlockSpec((rows, tokens), lambda step, me_ref: (jnp.maximum(step - early, 0), 0)),
                whole,
                whole,
            ],
            out_specs=grad_specs,
        ),
        out_shape=grad_shapes,
        cost_estimate=pl.CostEstimate(
            flops=2 * tokens * width * blocks * rows, bytes_accessed=2 * blocks * rows * width, transcendentals=0
        ),
        compiler_params=pltpu.CompilerParams(vmem_limit_bytes=VMEM_BYTES),
    )(me, d_qkv, attn_low, a_one, d_resid_low)


def adam_update(param, grad, first, second, rate, decay, step_number):
    first_new = BETA_ONE * first + (1.0 - BETA_ONE) * grad
    second_new = BETA_TWO * second + (1.0 - BETA_TWO) * grad * grad
    fix_one = 1.0 - BETA_ONE**step_number
    fix_two = 1.0 - BETA_TWO**step_number
    update = first_new / fix_one / (jnp.sqrt(second_new / fix_two) + ADAM_EPS)
    return (first_new, second_new, param - rate * (update + decay * param))


def shards(inputs, cotangent, weights, gains, first_moment, second_moment, gain_first, gain_second):
    ctx_count = lax.axis_size("ctx")
    x_count = lax.axis_size("x")
    ctx_index, core, x_index = lax.axis_index("ctx"), lax.axis_index("core"), lax.axis_index("x")
    seqs, local_rows, model_width = inputs.shape
    half_rows = local_rows // 2
    tokens = seqs * local_rows
    weight_rows = weights.shape[0]
    q_cols = HEADS * HD
    kv_cols = KV * HD
    cut_o = q_cols + 2 * kv_cols
    along_y, along_z = bit_groups()[1:]
    y_count, z_count = 1 << len(along_y), 1 << len(along_z)
    slot_offsets = [z * y_count + y for y in range(y_count) for z in range(z_count)]
    aligned = half_rows % 128 == 0
    local_index = jnp.arange(local_rows, dtype=jnp.int32)
    pos_here = places(ctx_index * local_rows + local_index, local_rows, ctx_count)
    cosine, sine_part = angle_tables(pos_here, 1.0)
    turn = (jnp.tile(cosine, (1, seqs)), jnp.tile(sine_part, (1, seqs)))
    turn_back = (turn[0], -turn[1])

    def pack(flat):
        if aligned:
            return flat
        return (
            flat.reshape(KV, GROUP, HD, -1, 2, half_rows)
            .transpose(3, 0, 2, 4, 1, 5)
            .reshape(-1, KV, HD, 2 * GROUP * half_rows)
        )

    def unpack(packed):
        if aligned:
            return packed
        return (
            packed.reshape(KV, HD, 2, GROUP, half_rows)
            .transpose(0, 3, 1, 2, 4)
            .reshape(q_cols, local_rows)
        )

    def by_columns(row):
        rows = row.shape[0]
        return jnp.broadcast_to(
            row.reshape(rows, 2, 1, half_rows), (rows, 2, GROUP, half_rows)
        ).reshape(rows, 2 * GROUP * half_rows)

    owners = ctx_index ^ jnp.asarray(slot_offsets, jnp.int32)
    inner = jnp.arange(half_rows, dtype=jnp.int32)
    key_pos = jnp.stack(
        [
            (owners[:, None] * half_rows + inner[None, :]).reshape(-1, 1),
            ((2 * ctx_count - 1 - owners[:, None]) * half_rows + inner[None, :]).reshape(-1, 1),
        ]
    )
    query_pos = by_columns(pos_here[None, :])
    packed_tables = (by_columns(cosine), by_columns(sine_part))

    held = lax.all_gather(weights, ("x", "ctx"), axis=0, tiled=True)
    held = held.reshape(x_count, ctx_count * weight_rows, model_width)
    mine = [held[x] for x in range(x_count)]
    far = [swap(part, ("core", 0)) for part in mine]
    first_rows = jnp.where(core == 0, mine[0], far[0])
    if first_rows.shape[0] < cut_o + q_cols:
        first_rows = jnp.concatenate([first_rows, jnp.where(core == 0, far[0], mine[0])], axis=0)
    qkv_rows, o_rows = first_rows[:cut_o], first_rows[cut_o : cut_o + q_cols]

    tokens_in = inputs.reshape(tokens, model_width)
    cot_in = cotangent.reshape(tokens, model_width)
    dy_low = cot_in.astype(jnp.bfloat16)
    a_one = (normalize(tokens_in) * gains[0]).astype(jnp.bfloat16)
    pair_rows = matmul_t(qkv_rows[q_cols:], a_one)
    joined = jnp.concatenate(
        [rotate(pair_rows[:kv_cols], turn).astype(jnp.bfloat16), pair_rows[kv_cols:].astype(jnp.bfloat16)],
        axis=0,
    )
    near = [joined] + [swap_by(joined, "ctx", z * y_count) for z in range(1, z_count)]
    pairs = list(near)
    for y in range(1, y_count):
        pairs += [swap_by(part, "ctx", y) for part in near]
    if not aligned:
        pairs = [
            jnp.stack(pairs)
            .reshape(ctx_count, 2 * kv_cols, seqs, 2, half_rows)
            .transpose(1, 2, 3, 0, 4)
            .reshape(2 * kv_cols, seqs * 2 * ctx_count * half_rows)
        ]
    q_rot = rotate(matmul_t(qkv_rows[:q_cols], a_one), turn).astype(jnp.bfloat16)
    queries = pack((q_rot * SCALE_QK).astype(jnp.bfloat16))
    attended = [
        attend(queries, pairs, key_pos, query_pos, local_rows, seq) for seq in range(seqs)
    ]
    attn_low = jnp.concatenate([unpack(mixed) for mixed, _ in attended], axis=1)
    resid = tokens_in + matmul_c(attn_low, o_rows)
    a_two = (normalize(resid) * gains[1]).astype(jnp.bfloat16)
    fed, d_two, *feed_grads = feed_forward(a_two, dy_low, mine, far, weight_rows)
    split = splits_rows(weight_rows)
    if split:
        feed_sums = reduce_ctx(*feed_grads)
    result = resid + fed
    d_norm_two, d_gain_two = norm_back(resid, d_two, gains[1])
    d_resid = cot_in + d_norm_two
    d_resid_low = d_resid.astype(jnp.bfloat16)
    d_attn = pack(matmul_t(o_rows, d_resid_low).astype(jnp.bfloat16))
    d_q, d_pair = [], []
    for seq in range(seqs):
        mixed, log_total = attended[seq]
        d_queries, *d_slots = attend_back(
            queries, pairs, key_pos, query_pos, mixed, log_total, d_attn, packed_tables,
            local_rows, seq, z_count,
        )
        d_q.append(unpack(d_queries))
        if not aligned:
            d_slots = (
                d_slots[0]
                .reshape(2, KV, ctx_count, half_rows, 2 * HD)
                .transpose(2, 1, 0, 3, 4)
                .reshape(y_count, z_count, KV, 2, half_rows, 2 * HD)
            )
            d_slots = [d_slots[y] for y in range(y_count)]
        line = d_slots[0].astype(jnp.float32)
        for y in range(1, y_count):
            line = line + swap_by(d_slots[y], "ctx", y).astype(jnp.float32)
        total = line[0]
        for z in range(1, z_count):
            total = total + swap_by(line[z].astype(jnp.bfloat16), "ctx", z * y_count).astype(jnp.float32)
        d_pair.append(total)
    d_own = jnp.stack(d_pair).transpose(1, 4, 0, 2, 3).reshape(KV, 2 * HD, tokens)
    d_qkv = jnp.concatenate(
        [
            jnp.concatenate(d_q, axis=1),
            rotate(d_own[:, :HD].reshape(kv_cols, tokens), turn_back).astype(jnp.bfloat16),
            d_own[:, HD:].reshape(kv_cols, tokens).astype(jnp.bfloat16),
        ],
        axis=0,
    )
    first_terms = first_grads(d_qkv, attn_low, a_one, d_resid_low, weight_rows)
    if split:
        first_sums = reduce_ctx(*first_terms)
        sums = [first_sums[0], feed_sums[0], feed_sums[1], feed_sums[2]]
        own_x = [jnp.where(x_index == 0, sums[core_of], sums[2 + core_of]) for core_of in range(2)]
        other_x = [jnp.where(x_index == 0, sums[2 + core_of], sums[core_of]) for core_of in range(2)]
        halves = [
            own.astype(jnp.float32) + swap(other, ("x", 0)).astype(jnp.float32)
            for own, other in zip(own_x, other_x)
        ]
        own_half = jnp.where(core == 0, halves[0], halves[1])
        other_half = jnp.where(core == 0, halves[1], halves[0]).astype(jnp.bfloat16)
        come = swap(other_half, ("core", 0)).astype(jnp.float32)
        weight_share = jnp.concatenate(
            [jnp.where(core == 0, own_half, come), jnp.where(core == 0, come, own_half)], axis=0
        )
    else:
        weight_share = scatter_whole([first_terms[0], *feed_grads])
    d_one = matmul_c(d_qkv, qkv_rows)
    d_norm_one, d_gain_one = norm_back(tokens_in, d_one, gains[0])
    d_tokens = d_resid + d_norm_one
    gain_parts = lax.all_gather(jnp.stack([d_gain_one, d_gain_two], axis=0), ("x", "core", "ctx"))
    gain_grad = jnp.sum(gain_parts, axis=0)
    weight_first, weight_second, weight_new = adam_update(
        weights.astype(jnp.float32), weight_share, first_moment, second_moment, RATE, DECAY, STEP
    )
    gain_first_new, gain_second_new, gain_new = adam_update(
        gains, gain_grad, gain_first, gain_second, GAIN_RATE, 0.0, STEP
    )
    return (
        result.reshape(inputs.shape),
        d_tokens.reshape(inputs.shape),
        weight_share,
        weight_second,
        weight_new,
        gain_grad,
        gain_second_new,
        gain_new,
    )


def solution(mesh):
    fine = Mesh(
        mesh.devices.reshape(mesh.shape["dp"] // 2, 2, mesh.shape["ctx"]), ("x", "core", "ctx")
    )
    rows = P(("x", "core"), "ctx", None)
    stacked = P(("x", "core", "ctx"), None)
    return jax.shard_map(
        shards,
        mesh=fine,
        in_specs=(rows, rows, stacked, P(), stacked, stacked, P(), P()),
        out_specs=(rows, rows, stacked, stacked, stacked, P(), P(), P()),
        check_vma=False,
    )
```

time: 783 us -> 785 us (level)
  blocking collectives: 0 us -> 68 us
  local copies, waits for them, and re-layouts: 135 us -> 87.6 us
  Pallas kernels: 150 us -> 121 us
  between operations: 2.14 us -> 15.6 us
    ppermute x45 -> x34, waiting for transfers between devices: 373 us -> 233 us  [swap_by(): return lax.ppermute(values, axis, [(i, i ^ offset) for i in range(size)])]
    all_gather x0 -> x1, waiting for transfers between devices: none -> 138 us  [shards(): held = lax.all_gather(weights, ('x', 'ctx'), axis=0, tiled=True)]
    all_gather x0 -> x1, blocking collectives: none -> 68 us  [shards(): lax.all_gather(jnp.stack([d_gain_one, d_gain_two], axis=0), ('x', 'core',...]
    slice x13 -> x18, local copies, waits for them, and re-layouts: 9.92 us -> 43.2 us  [the longest x3 21 us: shards(): mine = [held[x] for x in range(x_count)]]
    pallas_call x6, Pallas kernels: 150 us -> 121 us  [the longest x2 45.5 us: attend_back(): pl.pallas_call(lambda *refs: attend_back_body(count, aligned, *refs), gri...]
    unnamed x133 -> x132, local copies, waits for them, and re-layouts: 42 us -> 16.1 us
    reshape x9 -> x2, local copies, waits for them, and re-layouts: 17.8 us -> 0.11 us  [by_columns(): return jnp.broadcast_to(row.reshape(rows, 2, 1, half_rows), (rows, 2, GRO...]
    transpose x4 -> x1, local copies, waits for them, and re-layouts: 16.8 us -> 0.09 us  [shards(): jnp.stack(d_pair).transpose(1, 4, 0, 2, 3).reshape(KV, 2 * HD, tokens)]
  transfers between devices with their start and end apart: 45 -> 35, of which waited for: 31 -> 18; matrix products, arithmetic and copies ran while one was open for 13% -> 11% of each run, Pallas kernels for 0% -> 7%
where the time goes in v3:
time: 785 us; the launch traced here: 775 us
  waiting for transfers between devices  371 us (47%)
  Pallas kernels  121 us (15%)
  local copies, waits for them, and re-layouts  87.6 us (11%)
  blocking collectives  68 us (9%)
  other arithmetic  52.8 us (7%)
  starting transfers between devices  43.3 us (6%)
  matrix products  15.8 us (2%)
  between operations  15.6 us (2%)
    ppermute x34, waiting for transfers between devices, swap_by(): return lax.ppermute(values, axis, [(i, i ^ offset) for i in range(size)])  233 us
    all_gather x1, waiting for transfers between devices, shards(): held = lax.all_gather(weights, ('x', 'ctx'), axis=0, tiled=True)  138 us
    all_gather x1, blocking collectives, shards(): lax.all_gather(jnp.stack([d_gain_one, d_gain_two], axis=0), ('x', 'core',...  68 us
    pallas_call x2, Pallas kernels, attend_back(): pl.pallas_call(lambda *refs: attend_back_body(count, aligned, *refs), gri...  45.5 us
    ppermute x34, starting transfers between devices, swap_by(): return lax.ppermute(values, axis, [(i, i ^ offset) for i in range(size)])  43.2 us
    pallas_call x1, Pallas kernels, feed_forward(): pl.pallas_call(lambda *refs: feed_body(parts, split, *refs), grid_spec=pl...  43.1 us
    pallas_call x2, Pallas kernels, attend(): pl.pallas_call(lambda *refs: attend_body(count, aligned, *refs), grid=(KV...  25.5 us
    slice x3, local copies, waits for them, and re-layouts, shards(): mine = [held[x] for x in range(x_count)]  21 us
  transfers between devices with their start and end apart: 35, of which 18 were waited for; matrix products, arithmetic and copies ran while one was open for 11% of the time, Pallas kernels for 7%

profile of v3, /device:TPU:0, one launch (start us, length us, event | category | flops | bytes accessed | tf_op | source)
XLA Modules:
  0.0 775.4 jit_solution(14152461840738166969)
XLA Ops:
  7.9 137.8 %all-gather.4.cloned.1.call-done = bf16[5120,960]{1,0:T(8,128)(2,1)} async-done(((bf16[320,960]{1,0:T(8,128)(2,1)}), bf16[5120,960]{1,0:T(8,128)(2,1)}) %all-gather.4.cloned.1.call-update) | async-done | bytes 9830416 | tf_op jit(solution)/shard_map/all_gather | solution.py:729
  145.7 5.4 slice.353.refs_3_
  151.0 8.0 %copy.121 = bf16[2560,960]{0,1:T(8,128)(2,1)} copy(bf16[2560,960]{1,0:T(8,128)(2,1)} %slice.353.refs_3_) | data formatting | bytes 9830400 | tf_op jit(solution)/shard_map/slice | solution.py:731
  161.2 6.3 collective-permute-done
  167.5 7.8 %copy.122.refs_4_ = bf16[2560,960]{1,0:T(8,128)(2,1)} copy(bf16[2560,960]{0,1:T(8,128)(2,1)} %collective-permute-done) | data formatting | bytes 9830400 | tf_op jit(solution)/shard_map/ppermute | solution.py:106
  175.4 9.0 %fusion.65 = (bf16[2560,960]{1,0:T(8,128)(2,1)}, bf16[2560,960]{1,0:T(8,128)(2,1)}) fusion(bf16[5120,960]{1,0:T(8,128)(2,1)} %all-gather.4.cloned.1.call-done, bf16[2560,960]{1,0:T(8,128)(2,1)} %copy.122.refs_4_, pred[]{:T(512)S(6)} %eq.6), kind=kLoop, calls=%fused_computation.181 | loop fusion | flops 2457600 | bytes 24576000 | tf_op jit(solution)/shard_map/slice | solution.py:731
  184.4 7.7 copy.133
  228.4 8.1 %collective-permute-done.1.refs_4_.refs_12_ = bf16[640,512]{1,0:T(8,128)(2,1)S(1)} collective-permute-done((bf16[640,512]{1,0:T(8,128)(2,1)S(1)}, bf16[640,512]{1,0:T(8,128)(2,1)S(1)}, u32[]{:S(2)}, u32[]{:S(2)}) %collective-permute-start.1) | collective-permute-done | bytes 655392 | tf_op jit(solution)/shard_map/ppermute | solution.py:106
  238.0 15.0 %collective-permute-done.2.refs_5_.refs_13_ = bf16[640,512]{1,0:T(8,128)(2,1)S(1)} collective-permute-done((bf16[640,512]{1,0:T(8,128)(2,1)S(1)}, bf16[640,512]{1,0:T(8,128)(2,1)S(1)}, u32[]{:S(2)}, u32[]{:S(2)}) %collective-permute-start.2) | collective-permute-done | bytes 655392 | tf_op jit(solution)/shard_map/ppermute | solution.py:106
  257.7 13.3 %collective-permute-done.6.refs_9_.refs_17_ = bf16[640,512]{1,0:T(8,128)(2,1)S(1)} collective-permute-done((bf16[640,512]{1,0:T(8,128)(2,1)S(1)}, bf16[640,512]{1,0:T(8,128)(2,1)S(1)}, u32[]{:S(2)}, u32[]{:S(2)}) %collective-permute-start.6) | collective-permute-done | bytes 655392 | tf_op jit(solution)/shard_map/ppermute | solution.py:106
  271.0 12.2 %collective-permute-done.7.refs_10_.refs_18_ = bf16[640,512]{1,0:T(8,128)(2,1)S(1)} collective-permute-done((bf16[640,512]{1,0:T(8,128)(2,1)S(1)}, bf16[640,512]{1,0:T(8,128)(2,1)S(1)}, u32[]{:S(2)}, u32[]{:S(2)}) %collective-permute-start.7) | collective-permute-done | bytes 655392 | tf_op jit(solution)/shard_map/ppermute | solution.py:106
  283.2 12.9 %shard_map.152 = (bf16[960,256]{1,0:T(8,128)(2,1)S(1)}, f32[1,5,1,768]{3,2,1,0:T(1,128)S(1)}) custom-call(bf16[960,512]{1,0:T(8,128)(2,1)} %bitcast.190, s32[2,1024,1]{2,1,0:T(8,128)} %pad_add_fusion.refs_1_, s32[1,768]{1,0:T(1,128)S(1)} %broadcast_in_dim.9.refs_2_, bf16[640,512]{1,0:T(8,128)(2,1)S(1)} %pad_maximum_fusion.3.refs_3_.refs_11_, ...), custom_call_target="tpu_custom_call" | custom-call | flops 1509949440 | bytes 8388608 | tf_op jit(solution)/shard_map/pallas_call | solution.py:463
  297.0 12.5 %shard_map.153 = (bf16[960,256]{1,0:T(8,128)(2,1)S(1)}, f32[1,5,1,768]{3,2,1,0:T(1,128)S(1)}) custom-call(bf16[960,512]{1,0:T(8,128)(2,1)} %bitcast.191, s32[2,1024,1]{2,1,0:T(8,128)} %pad_add_fusion.refs_1_, s32[1,768]{1,0:T(1,128)S(1)} %broadcast_in_dim.9.refs_2_, bf16[640,512]{1,0:T(8,128)(2,1)S(1)} %pad_maximum_fusion.3.refs_3_.refs_11_, ...), custom_call_target="tpu_custom_call" | custom-call | flops 1509949440 | bytes 8388608 | tf_op jit(solution)/shard_map/pallas_call | solution.py:463
  315.5 7.9 %copy.135.refs_6_.refs_8_ = bf16[2560,960]{1,0:T(8,128)(2,1)} copy(bf16[2560,960]{0,1:T(8,128)(2,1)} %collective-permute-done.8) | data formatting | bytes 9830400 | tf_op jit(solution)/shard_map/ppermute | solution.py:106
  325.9 43.1 %shard_map.154 = (f32[512,960]{1,0:T(8,128)S(1)}, f32[512,960]{1,0:T(8,128)}, bf16[3,8,160,960]{3,2,1,0:T(8,128)(2,1)}, bf16[3,8,160,960]{3,2,1,0:T(8,128)(2,1)}) custom-call(s32[2]{0:T(128)S(1)} %pad_add_fusion.1.refs_0_.me_ref, bf16[512,960]{1,0:T(8,128)(2,1)S(1)} %copy-done.14, bf16[512,960]{1,0:T(8,128)(2,1)S(1)} %copy-done.11, ...), custom_call_target="tpu_custom_call" | custom-call | flops 22649241600 | bytes 29491200 | tf_op jit(solution)/shard_map/pallas_call | solution.py:600
  378.8 22.6 %shard_map.155 = (bf16[960,256]{1,0:T(8,128)(2,1)S(1)}, bf16[4,5,2,128,128]{4,3,2,1,0:T(8,128)(2,1)}, bf16[4,5,2,128,128]{4,3,2,1,0:T(8,128)(2,1)}) custom-call(bf16[960,512]{1,0:T(8,128)(2,1)} %bitcast.192, s32[2,1024,1]{2,1,0:T(8,128)} %pad_add_fusion.refs_1_, s32[1,768]{1,0:T(1,128)S(1)} %broadcast_in_dim.9.refs_2_, ...), custom_call_target="tpu_custom_call" | custom-call | flops 3774873600 | bytes 16777216 | tf_op jit(solution)/shard_map/pallas_call | solution.py:500
  403.0 22.8 %shard_map.156 = (bf16[960,256]{1,0:T(8,128)(2,1)S(1)}, bf16[4,5,2,128,128]{4,3,2,1,0:T(8,128)(2,1)}, bf16[4,5,2,128,128]{4,3,2,1,0:T(8,128)(2,1)}) custom-call(bf16[960,512]{1,0:T(8,128)(2,1)} %bitcast.193, s32[2,1024,1]{2,1,0:T(8,128)} %pad_add_fusion.refs_1_, s32[1,768]{1,0:T(1,128)S(1)} %broadcast_in_dim.9.refs_2_, ...), custom_call_target="tpu_custom_call" | custom-call | flops 3774873600 | bytes 16777216 | tf_op jit(solution)/shard_map/pallas_call | solution.py:500
  426.4 7.0 collective-permute-done.9
  439.3 19.4 %collective-permute-done.13 = bf16[4,5,2,128,128]{4,3,2,1,0:T(8,128)(2,1)S(1)} collective-permute-done((bf16[4,5,2,128,128]{4,3,2,1,0:T(8,128)(2,1)}, bf16[4,5,2,128,128]{4,3,2,1,0:T(8,128)(2,1)S(1)}, u32[]{:S(2)}, u32[]{:S(2)}) %collective-permute-start.13) | collective-permute-done | bytes 1310752 | tf_op jit(solution)/shard_map/ppermute | solution.py:106
  468.8 6.3 collective-permute-done.14
  475.1 12.3 %collective-permute-done.15 = bf16[5,2,128,128]{3,2,1,0:T(8,128)(2,1)} collective-permute-done((bf16[5,2,128,128]{3,2,1,0:T(8,128)(2,1)}, bf16[5,2,128,128]{3,2,1,0:T(8,128)(2,1)}, u32[]{:S(2)}, u32[]{:S(2)}) %collective-permute-start.15) | collective-permute-done | bytes 327712 | tf_op jit(solution)/shard_map/ppermute | solution.py:106
  494.9 7.0 shard_map.157
  501.9 6.0 fusion.66
  514.6 4.5 multiply_reduce_fusion.1
  548.8 32.4 %collective-permute-done.25 = bf16[3,2,2,80,960]{4,3,0,1,2:T(8,128)(2,1)S(1)} collective-permute-done((bf16[3,2,2,80,960]{4,3,0,1,2:T(8,128)(2,1)S(1)}, bf16[3,2,2,80,960]{4,3,0,1,2:T(8,128)(2,1)S(1)}, u32[]{:S(2)}, u32[]{:S(2)}) %collective-permute-start.25) | collective-permute-done | bytes 1843232 | tf_op jit(solution)/shard_map/ppermute | solution.py:106
  586.3 6.6 collective-permute-done.28
  594.2 5.9 collective-permute-done.19
  601.1 49.6 %collective-permute-done.20 = bf16[1,80,960]{2,1,0:T(8,128)(2,1)S(1)} collective-permute-done((bf16[1,80,960]{2,1,0:T(8,128)(2,1)S(1)}, bf16[1,80,960]{2,1,0:T(8,128)(2,1)S(1)}, u32[]{:S(2)}, u32[]{:S(2)}) %collective-permute-start.20) | collective-permute-done | bytes 153632 | tf_op jit(solution)/shard_map/ppermute | solution.py:106
  651.9 22.7 %collective-permute-done.27 = bf16[3,80,960]{2,1,0:T(8,128)(2,1)S(1)} collective-permute-done((bf16[3,80,960]{2,1,0:T(8,128)(2,1)S(1)}, bf16[3,80,960]{2,1,0:T(8,128)(2,1)S(1)}, u32[]{:S(2)}, u32[]{:S(2)}) %collective-permute-start.27) | collective-permute-done | bytes 460832 | tf_op jit(solution)/shard_map/ppermute | solution.py:106
  680.6 6.5 collective-permute-done.31
  687.1 6.1 collective-permute-done.32
  695.4 68.0 %all-gather.1 = f32[32,2,960]{2,1,0:T(2,128)S(1)} all-gather(f32[1,2,960]{2,1,0:T(2,128)S(1)} %maximum_bitcast_fusion.1), channel_id=2, replica_groups=mesh['x'=2,'core'=2,'ctx'=8] {'x','core','ctx'}, dimensions={0}, use_global_device_ids=true | all-gather | bytes 253440 | tf_op jit(solution)/shard_map/all_gather | solution.py:828
  (288 shorter events, 147.0 us)
Async XLA Ops:
  7.2 138.5 %all-gather.4.cloned.1.call-start = ((), (), s32[]{:S(2)}) async-start(), calls=%async_computation | async-start | bytes 11141120 | tf_op jit(solution)/shard_map/all_gather | solution.py:729
  192.1 123.4 %collective-permute-start.8 = (bf16[2560,960]{0,1:T(8,128)(2,1)}, bf16[2560,960]{0,1:T(8,128)(2,1)}, u32[]{:S(2)}, u32[]{:S(2)}) collective-permute-start(bf16[2560,960]{0,1:T(8,128)(2,1)} %copy.133), channel_id=1, source_target_pairs={{0,8},{8,0},{1,9},{9,1},{2,10},{10,2},{3,11},{11,3},{4,12},{12,4},... | collective-permute-start | bytes 14745608 | tf_op jit(solution)/shard_map/ppermute | solution.py:106
  206.2 30.3 %collective-permute-start.1 = (bf16[640,512]{1,0:T(8,128)(2,1)S(1)}, bf16[640,512]{1,0:T(8,128)(2,1)S(1)}, u32[]{:S(2)}, u32[]{:S(2)}) collective-permute-start(bf16[640,512]{1,0:T(8,128)(2,1)S(1)} %pad_maximum_fusion.3.refs_3_.refs_11_), channel_id=1, source_target_pairs={{0,2},{1,3},{2,0},{3,1},{4,6},{5,7},{6,4},{7,5},{8,10},{9,11},{10,... | collective-permute-start | bytes 1966088 | tf_op jit(solution)/shard_map/ppermute | solution.py:106
  206.3 46.7 %collective-permute-start.2 = (bf16[640,512]{1,0:T(8,128)(2,1)S(1)}, bf16[640,512]{1,0:T(8,128)(2,1)S(1)}, u32[]{:S(2)}, u32[]{:S(2)}) collective-permute-start(bf16[640,512]{1,0:T(8,128)(2,1)S(1)} %pad_maximum_fusion.3.refs_3_.refs_11_), channel_id=1, source_target_pairs={{0,4},{1,5},{2,6},{3,7},{4,0},{5,1},{6,2},{7,3},{8,12},{9,13},{10,... | collective-permute-start | bytes 1966088 | tf_op jit(solution)/shard_map/ppermute | solution.py:106
  208.3 46.2 %collective-permute-start.3 = (bf16[640,512]{1,0:T(8,128)(2,1)S(1)}, bf16[640,512]{1,0:T(8,128)(2,1)S(1)}, u32[]{:S(2)}, u32[]{:S(2)}) collective-permute-start(bf16[640,512]{1,0:T(8,128)(2,1)S(1)} %pad_maximum_fusion.3.refs_3_.refs_11_), channel_id=1, source_target_pairs={{0,6},{1,7},{2,4},{3,5},{4,2},{5,3},{6,0},{7,1},{8,14},{9,15},{10,... | collective-permute-start | bytes 1966088 | tf_op jit(solution)/shard_map/ppermute | solution.py:106
  225.3 32.5 %collective-permute-start.4 = (bf16[640,512]{1,0:T(8,128)(2,1)S(1)}, bf16[640,512]{1,0:T(8,128)(2,1)S(1)}, u32[]{:S(2)}, u32[]{:S(2)}) collective-permute-start(bf16[640,512]{1,0:T(8,128)(2,1)S(1)} %pad_maximum_fusion.3.refs_3_.refs_11_), channel_id=1, source_target_pairs={{0,1},{1,0},{2,3},{3,2},{4,5},{5,4},{6,7},{7,6},{8,9},{9,8},{10,11... | collective-permute-start | bytes 1966088 | tf_op jit(solution)/shard_map/ppermute | solution.py:106
  236.5 21.2 %collective-permute-start.5 = (bf16[640,512]{1,0:T(8,128)(2,1)S(1)}, bf16[640,512]{1,0:T(8,128)(2,1)S(1)}, u32[]{:S(2)}, u32[]{:S(2)}) collective-permute-start(bf16[640,512]{1,0:T(8,128)(2,1)S(1)} %collective-permute-done.1.refs_4_.refs_12_), channel_id=1, source_target_pairs={{0,1},{1,0},{2,3},{3,2},{4,5},{5,4},{6,7},{7,6},{8,9},{9,8},{10,11... | collective-permute-start | bytes 1966088 | tf_op jit(solution)/shard_map/ppermute | solution.py:106
  253.0 18.0 %collective-permute-start.6 = (bf16[640,512]{1,0:T(8,128)(2,1)S(1)}, bf16[640,512]{1,0:T(8,128)(2,1)S(1)}, u32[]{:S(2)}, u32[]{:S(2)}) collective-permute-start(bf16[640,512]{1,0:T(8,128)(2,1)S(1)} %collective-permute-done.2.refs_5_.refs_13_), channel_id=1, source_target_pairs={{0,1},{1,0},{2,3},{3,2},{4,5},{5,4},{6,7},{7,6},{8,9},{9,8},{10,11... | collective-permute-start | bytes 1966088 | tf_op jit(solution)/shard_map/ppermute | solution.py:106
  254.5 28.7 %collective-permute-start.7 = (bf16[640,512]{1,0:T(8,128)(2,1)S(1)}, bf16[640,512]{1,0:T(8,128)(2,1)S(1)}, u32[]{:S(2)}, u32[]{:S(2)}) collective-permute-start(bf16[640,512]{1,0:T(8,128)(2,1)S(1)} %collective-permute-done.3.refs_6_.refs_14_), channel_id=1, source_target_pairs={{0,1},{1,0},{2,3},{3,2},{4,5},{5,4},{6,7},{7,6},{8,9},{9,8},{10,11... | collective-permute-start | bytes 1966088 | tf_op jit(solution)/shard_map/ppermute | solution.py:106
  401.4 32.0 %collective-permute-start.9 = (bf16[4,5,2,128,128]{4,3,2,1,0:T(8,128)(2,1)}, bf16[4,5,2,128,128]{4,3,2,1,0:T(8,128)(2,1)S(1)}, u32[]{:S(2)}, u32[]{:S(2)}) collective-permute-start(bf16[4,5,2,128,128]{4,3,2,1,0:T(8,128)(2,1)} %get-tuple-element.33), channel_id=1, source_target_pairs={{0,1},{1,0},{2,3},{3,2},{4,5},{5,4},{6,7},{7,6},{8,9},{9,8},{10,11... | collective-permute-start | bytes 3932168 | tf_op jit(solution)/shard_map/ppermute | solution.py:106
  425.8 32.9 %collective-permute-start.13 = (bf16[4,5,2,128,128]{4,3,2,1,0:T(8,128)(2,1)}, bf16[4,5,2,128,128]{4,3,2,1,0:T(8,128)(2,1)S(1)}, u32[]{:S(2)}, u32[]{:S(2)}) collective-permute-start(bf16[4,5,2,128,128]{4,3,2,1,0:T(8,128)(2,1)} %get-tuple-element.35), channel_id=1, source_target_pairs={{0,1},{1,0},{2,3},{3,2},{4,5},{5,4},{6,7},{7,6},{8,9},{9,8},{10,11... | collective-permute-start | bytes 3932168 | tf_op jit(solution)/shard_map/ppermute | solution.py:106
  426.4 101.9 %collective-permute-start.24 = (bf16[3,8,160,960]{3,2,1,0:T(8,128)(2,1)}, bf16[3,8,160,960]{3,2,1,0:T(8,128)(2,1)}, u32[]{:S(2)}, u32[]{:S(2)}) collective-permute-start(bf16[3,8,160,960]{3,2,1,0:T(8,128)(2,1)} %get-tuple-element.39), channel_id=1, source_target_pairs={{0,8},{8,0},{1,9},{9,1},{2,10},{10,2},{3,11},{11,3},{4,12},{12,4},... | collective-permute-start | bytes 22118408 | tf_op jit(solution)/shard_map/ppermute | solution.py:106
  434.9 26.8 %collective-permute-start.10 = (bf16[5,2,128,128]{3,2,1,0:T(8,128)(2,1)S(1)}, bf16[5,2,128,128]{3,2,1,0:T(8,128)(2,1)S(1)}, u32[]{:S(2)}, u32[]{:S(2)}) collective-permute-start(bf16[5,2,128,128]{3,2,1,0:T(8,128)(2,1)S(1)} %get-tuple-element.131), channel_id=1, source_target_pairs={{0,2},{1,3},{2,0},{3,1},{4,6},{5,7},{6,4},{7,5},{8,10},{9,11},{10,... | collective-permute-start | bytes 983048 | tf_op jit(solution)/shard_map/ppermute | solution.py:106
  434.9 27.7 %collective-permute-start.11 = (bf16[5,2,128,128]{3,2,1,0:T(8,128)(2,1)S(1)}, bf16[5,2,128,128]{3,2,1,0:T(8,128)(2,1)S(1)}, u32[]{:S(2)}, u32[]{:S(2)}) collective-permute-start(bf16[5,2,128,128]{3,2,1,0:T(8,128)(2,1)S(1)} %get-tuple-element.133), channel_id=1, source_target_pairs={{0,4},{1,5},{2,6},{3,7},{4,0},{5,1},{6,2},{7,3},{8,12},{9,13},{10,... | collective-permute-start | bytes 983048 | tf_op jit(solution)/shard_map/ppermute | solution.py:106
  436.9 30.8 %collective-permute-start.12 = (bf16[5,2,128,128]{3,2,1,0:T(8,128)(2,1)}, bf16[5,2,128,128]{3,2,1,0:T(8,128)(2,1)}, u32[]{:S(2)}, u32[]{:S(2)}) collective-permute-start(bf16[5,2,128,128]{3,2,1,0:T(8,128)(2,1)} %get-tuple-element.132), channel_id=1, source_target_pairs={{0,6},{1,7},{2,4},{3,5},{4,2},{5,3},{6,0},{7,1},{8,14},{9,15},{10,... | collective-permute-start | bytes 983048 | tf_op jit(solution)/shard_map/ppermute | solution.py:106
  461.7 25.7 %collective-permute-start.15 = (bf16[5,2,128,128]{3,2,1,0:T(8,128)(2,1)}, bf16[5,2,128,128]{3,2,1,0:T(8,128)(2,1)}, u32[]{:S(2)}, u32[]{:S(2)}) collective-permute-start(bf16[5,2,128,128]{3,2,1,0:T(8,128)(2,1)} %get-tuple-element.136), channel_id=1, source_target_pairs={{0,4},{1,5},{2,6},{3,7},{4,0},{5,1},{6,2},{7,3},{8,12},{9,13},{10,... | collective-permute-start | bytes 983048 | tf_op jit(solution)/shard_map/ppermute | solution.py:106
  462.6 24.7 %collective-permute-start.16 = (bf16[5,2,128,128]{3,2,1,0:T(8,128)(2,1)}, bf16[5,2,128,128]{3,2,1,0:T(8,128)(2,1)}, u32[]{:S(2)}, u32[]{:S(2)}) collective-permute-start(bf16[5,2,128,128]{3,2,1,0:T(8,128)(2,1)} %get-tuple-element.135), channel_id=1, source_target_pairs={{0,6},{1,7},{2,4},{3,5},{4,2},{5,3},{6,0},{7,1},{8,14},{9,15},{10,... | collective-permute-start | bytes 983048 | tf_op jit(solution)/shard_map/ppermute | solution.py:106
  501.9 17.6 %collective-permute-start.17 = (bf16[1,8,160,960]{3,2,1,0:T(8,128)(2,1)}, bf16[1,8,160,960]{3,2,1,0:T(8,128)(2,1)}, u32[]{:S(2)}, u32[]{:S(2)}) collective-permute-start(bf16[1,8,160,960]{3,2,1,0:T(8,128)(2,1)} %get-tuple-element.37), channel_id=1, source_target_pairs={{0,8},{8,0},{1,9},{9,1},{2,10},{10,2},{3,11},{11,3},{4,12},{12,4},... | collective-permute-start | bytes 7372808 | tf_op jit(solution)/shard_map/ppermute | solution.py:106
  521.9 17.6 %collective-permute-start.18 = (bf16[1,2,2,80,960]{4,3,1,2,0:T(8,128)(2,1)S(1)}, bf16[1,2,2,80,960]{4,3,1,2,0:T(8,128)(2,1)S(1)}, u32[]{:S(2)}, u32[]{:S(2)}) collective-permute-start(bf16[1,2,2,80,960]{4,3,1,2,0:T(8,128)(2,1)S(1)} %fusion.27), channel_id=1, source_target_pairs={{0,1},{1,0},{2,3},{3,2},{4,5},{5,4},{6,7},{7,6},{8,9},{9,8},{10,11... | collective-permute-start | bytes 1843208 | tf_op jit(solution)/shard_map/ppermute | solution.py:106
  524.0 19.9 %collective-permute-start.21 = (bf16[1,2,2,80,960]{4,3,2,1,0:T(8,128)(2,1)S(1)}, bf16[1,2,2,80,960]{4,3,2,1,0:T(8,128)(2,1)S(1)}, u32[]{:S(2)}, u32[]{:S(2)}) collective-permute-start(bf16[1,2,2,80,960]{4,3,2,1,0:T(8,128)(2,1)S(1)} %get-tuple-element.111), channel_id=1, source_target_pairs={{0,2},{1,3},{2,0},{3,1},{4,6},{5,7},{6,4},{7,5},{8,10},{9,11},{10,... | collective-permute-start | bytes 1843208 | tf_op jit(solution)/shard_map/ppermute | solution.py:106
  533.9 47.3 %collective-permute-start.25 = (bf16[3,2,2,80,960]{4,3,0,1,2:T(8,128)(2,1)S(1)}, bf16[3,2,2,80,960]{4,3,0,1,2:T(8,128)(2,1)S(1)}, u32[]{:S(2)}, u32[]{:S(2)}) collective-permute-start(bf16[3,2,2,80,960]{4,3,0,1,2:T(8,128)(2,1)S(1)} %fusion.3), channel_id=1, source_target_pairs={{0,1},{1,0},{2,3},{3,2},{4,5},{5,4},{6,7},{7,6},{8,9},{9,8},{10,11... | collective-permute-start | bytes 5529608 | tf_op jit(solution)/shard_map/ppermute | solution.py:106
  536.0 56.9 %collective-permute-start.28 = (bf16[3,2,2,80,960]{4,3,0,2,1:T(8,128)(2,1)S(1)}, bf16[3,2,2,80,960]{4,3,0,2,1:T(8,128)(2,1)S(1)}, u32[]{:S(2)}, u32[]{:S(2)}) collective-permute-start(bf16[3,2,2,80,960]{4,3,0,2,1:T(8,128)(2,1)S(1)} %fusion.5), channel_id=1, source_target_pairs={{0,2},{1,3},{2,0},{3,1},{4,6},{5,7},{6,4},{7,5},{8,10},{9,11},{10,... | collective-permute-start | bytes 5529608 | tf_op jit(solution)/shard_map/ppermute | solution.py:106
  539.7 60.3 %collective-permute-start.19 = (bf16[1,2,80,960]{3,2,1,0:T(8,128)(2,1)S(1)}, bf16[1,2,80,960]{3,2,1,0:T(8,128)(2,1)S(1)}, u32[]{:S(2)}, u32[]{:S(2)}) collective-permute-start(bf16[1,2,80,960]{3,2,1,0:T(8,128)(2,1)S(1)} %get-tuple-element.124), channel_id=1, source_target_pairs={{0,2},{1,3},{2,0},{3,1},{4,6},{5,7},{6,4},{7,5},{8,10},{9,11},{10,... | collective-permute-start | bytes 921608 | tf_op jit(solution)/shard_map/ppermute | solution.py:106
  544.2 56.3 %collective-permute-start.22 = (bf16[1,2,80,960]{3,2,1,0:T(8,128)(2,1)S(1)}, bf16[1,2,80,960]{3,2,1,0:T(8,128)(2,1)S(1)}, u32[]{:S(2)}, u32[]{:S(2)}) collective-permute-start(bf16[1,2,80,960]{3,2,1,0:T(8,128)(2,1)S(1)} %get-tuple-element.130), channel_id=1, source_target_pairs={{0,4},{1,5},{2,6},{3,7},{4,0},{5,1},{6,2},{7,3},{8,12},{9,13},{10,... | collective-permute-start | bytes 921608 | tf_op jit(solution)/shard_map/ppermute | solution.py:106
  582.1 68.6 %collective-permute-start.26 = (bf16[3,2,80,960]{3,2,0,1:T(8,128)(2,1)S(1)}, bf16[3,2,80,960]{3,2,0,1:T(8,128)(2,1)S(1)}, u32[]{:S(2)}, u32[]{:S(2)}) collective-permute-start(bf16[3,2,80,960]{3,2,0,1:T(8,128)(2,1)S(1)} %get-tuple-element.93), channel_id=1, source_target_pairs={{0,2},{1,3},{2,0},{3,1},{4,6},{5,7},{6,4},{7,5},{8,10},{9,11},{10,... | collective-permute-start | bytes 2764808 | tf_op jit(solution)/shard_map/ppermute | solution.py:106
  593.8 57.1 %collective-permute-start.29 = (bf16[3,2,80,960]{3,2,0,1:T(8,128)(2,1)S(1)}, bf16[3,2,80,960]{3,2,0,1:T(8,128)(2,1)S(1)}, u32[]{:S(2)}, u32[]{:S(2)}) collective-permute-start(bf16[3,2,80,960]{3,2,0,1:T(8,128)(2,1)S(1)} %get-tuple-element.99), channel_id=1, source_target_pairs={{0,4},{1,5},{2,6},{3,7},{4,0},{5,1},{6,2},{7,3},{8,12},{9,13},{10,... | collective-permute-start | bytes 2764808 | tf_op jit(solution)/shard_map/ppermute | solution.py:106
  600.1 50.5 %collective-permute-start.20 = (bf16[1,80,960]{2,1,0:T(8,128)(2,1)S(1)}, bf16[1,80,960]{2,1,0:T(8,128)(2,1)S(1)}, u32[]{:S(2)}, u32[]{:S(2)}) collective-permute-start(bf16[1,80,960]{2,1,0:T(8,128)(2,1)S(1)} %fusion.52), channel_id=1, source_target_pairs={{0,4},{1,5},{2,6},{3,7},{4,0},{5,1},{6,2},{7,3},{8,12},{9,13},{10,... | collective-permute-start | bytes 460808 | tf_op jit(solution)/shard_map/ppermute | solution.py:106
  600.5 51.3 %collective-permute-start.23 = (bf16[1,80,960]{2,1,0:T(8,128)(2,1)S(1)}, bf16[1,80,960]{2,1,0:T(8,128)(2,1)S(1)}, u32[]{:S(2)}, u32[]{:S(2)}) collective-permute-start(bf16[1,80,960]{2,1,0:T(8,128)(2,1)S(1)} %fusion.54), channel_id=1, source_target_pairs={{0,1},{1,0},{2,3},{3,2},{4,5},{5,4},{6,7},{7,6},{8,9},{9,8},{10,11... | collective-permute-start | bytes 460808 | tf_op jit(solution)/shard_map/ppermute | solution.py:106
  650.9 23.7 %collective-permute-start.27 = (bf16[3,80,960]{2,1,0:T(8,128)(2,1)S(1)}, bf16[3,80,960]{2,1,0:T(8,128)(2,1)S(1)}, u32[]{:S(2)}, u32[]{:S(2)}) collective-permute-start(bf16[3,80,960]{2,1,0:T(8,128)(2,1)S(1)} %fusion.40), channel_id=1, source_target_pairs={{0,4},{1,5},{2,6},{3,7},{4,0},{5,1},{6,2},{7,3},{8,12},{9,13},{10,... | collective-permute-start | bytes 1382408 | tf_op jit(solution)/shard_map/ppermute | solution.py:106
  651.2 23.7 %collective-permute-start.30 = (bf16[3,80,960]{2,1,0:T(8,128)(2,1)S(1)}, bf16[3,80,960]{2,1,0:T(8,128)(2,1)S(1)}, u32[]{:S(2)}, u32[]{:S(2)}) collective-permute-start(bf16[3,80,960]{2,1,0:T(8,128)(2,1)S(1)} %fusion.42), channel_id=1, source_target_pairs={{0,1},{1,0},{2,3},{3,2},{4,5},{5,4},{6,7},{7,6},{8,9},{9,8},{10,11... | collective-permute-start | bytes 1382408 | tf_op jit(solution)/shard_map/ppermute | solution.py:106
  676.8 16.4 %collective-permute-start.32 = (bf16[160,960]{1,0:T(8,128)(2,1)}, bf16[160,960]{1,0:T(8,128)(2,1)}, u32[]{:S(2)}, u32[]{:S(2)}) collective-permute-start(bf16[160,960]{1,0:T(8,128)(2,1)} %get-tuple-element.137), channel_id=1, source_target_pairs={{0,16},{16,0},{1,17},{17,1},{2,18},{18,2},{3,19},{19,3},{4,20},{20... | collective-permute-start | bytes 921608 | tf_op jit(solution)/shard_map/ppermute | solution.py:106
  695.4 68.8 %collective-permute-start.33 = (bf16[160,960]{1,0:T(8,128)(2,1)}, bf16[160,960]{1,0:T(8,128)(2,1)S(1)}, u32[]{:S(2)}, u32[]{:S(2)}) collective-permute-start(bf16[160,960]{1,0:T(8,128)(2,1)} %get-tuple-element.81), channel_id=1, source_target_pairs={{0,8},{8,0},{1,9},{9,1},{2,10},{10,2},{3,11},{11,3},{4,12},{12,4},... | collective-permute-start | bytes 921608 | tf_op jit(solution)/shard_map/ppermute | solution.py:106
  (64 other events, 769.0 us)
Sparse Core Ops, SparseCore 0:
  10.7 134.9 all-gather.3

commit v4 on v3

--- a/solution.py
+++ b/solution.py
@@ -249,31 +249,135 @@
     return lax.axis_size("x") == 2 and rows % 32 == 0
 
 
-def reduce_ctx(keep, away):
+def spread(values, order):
+    values = values[None]
+    for where in order:
+        values = double(values, where)
+    return values
+
+
+def double(values, where):
+    return jnp.concatenate([values, swap(values, where)], axis=0)
+
+
+def ctx_orders():
+    along_x, along_y, along_z = bit_groups()
+    return [along_y + along_z, along_z + along_y]
+
+
+def row_cuts(rows):
+    first = -(-rows // 32) * 16
+    return [(0, first), (first, rows)]
+
+
+def step_ctx(held, come, left, where):
+    dim = 1 + left.index(where[1])
+    rest = [bit for bit in left if bit != where[1]]
+    pick = lambda values, side: lax.index_in_dim(values, side, dim, False)
+    sent = add_low(pick(held, 1), pick(come, 1))
+    return add_low(pick(held, 0), pick(come, 0)), sent, rest
+
+
+def reduce_start(keep, away):
     arrived = swap(away, ("core", 0))
-    along_x, along_y, along_z = bit_groups()
-    rows = keep.shape[2]
-    first = -(-rows // 32) * 16
-    sums = []
-    plain = along_y + along_z
-    ctx_bits = len(plain)
-    for low, high, order in ((0, first, plain), (first, rows, along_z + along_y)):
-        shape = (keep.shape[0],) + (2,) * ctx_bits + (high - low, keep.shape[3])
+    states = []
+    for (low, high), order in zip(row_cuts(keep.shape[2]), ctx_orders()):
+        shape = (keep.shape[0],) + (2,) * len(order) + (high - low, keep.shape[3])
         held = keep[:, :, low:high].reshape(shape)
         come = arrived[:, :, low:high].reshape(shape)
-        left = list(reversed(range(ctx_bits)))
-        for where in order:
-            dim = 1 + left.index(where[1])
-            left.remove(where[1])
-            sent = add_low(
-                lax.index_in_dim(held, 1, dim, False), lax.index_in_dim(come, 1, dim, False)
-            )
-            held = add_low(
-                lax.index_in_dim(held, 0, dim, False), lax.index_in_dim(come, 0, dim, False)
-            )
-            come = swap(sent, where)
+        left = list(reversed(range(len(order))))
+        states.append(step_ctx(held, come, left, order[0]))
+    return states
+
+
+def ride_parts(ride):
+    rounded = lax.reduce_precision(ride, 8, 7)
+    return rounded, lax.reduce_precision(ride - rounded, 8, 7)
+
+
+def with_ride(sent, parts):
+    extra = jnp.concatenate([*parts, jnp.zeros((12, parts[0].shape[1]), jnp.float32)])
+    return jnp.concatenate([sent.reshape(-1, sent.shape[-1]), extra.astype(jnp.bfloat16)], axis=0)
+
+
+def swap_with(sent, ride, where):
+    parts = ride_parts(ride)
+    come, other = off_ride(swap(with_ride(sent, parts), where), sent.shape)
+    return come, (parts[0] + parts[1]) + other
+
+
+def off_ride(come, shape):
+    parts = come[-16:].astype(jnp.float32)
+    return come[:-16].reshape(shape), parts[0:2] + parts[2:4]
+
+
+def reduce_finish(states, ride=None):
+    sums = []
+    for member, ((held, sent, left), order) in enumerate(zip(states, ctx_orders())):
+        for position, where in enumerate(order):
+            if ride is not None and member == 0:
+                come, ride = swap_with(sent, ride, where)
+            else:
+                come = swap(sent, where)
+            if position + 1 < len(order):
+                held, sent, left = step_ctx(held, come, left, order[position + 1])
         sums.append(add_low(held, come))
-    return jnp.concatenate(sums, axis=1)
+    return jnp.concatenate(sums, axis=1), ride
+
+
+def gather_halves(weights):
+    rows = weights.shape[0]
+    x_index, core = lax.axis_index("x"), lax.axis_index("core")
+    half = rows // 2
+    far = swap(weights, ("x", 0))
+    low = jnp.where(x_index == 0, weights, far)
+    high = jnp.where(x_index == 0, far, weights)
+    both = jnp.stack([low, high])
+    keep = jnp.where(core == 0, both[:, :half], both[:, half:])
+    come = swap(jnp.where(core == 0, both[:, half:], both[:, :half]), ("core", 0))
+    first = jnp.where(core == 0, keep, come)
+    second = jnp.where(core == 0, come, keep)
+    return first[0], jnp.stack([second[0], first[1], second[1]])
+
+
+def place_rows(own, far):
+    tables = [rel_offsets(list(reversed(order))) for order in ctx_orders()]
+    slots, width = own[0].shape[0], own[0].shape[2]
+    lengths = [part.shape[1] for part in own]
+    half = sum(lengths)
+
+    def body(me_ref, *refs):
+        out_ref = refs[-1]
+        for core in range(2):
+
+            @pl.when(me_ref[0] == core)
+            def _(core=core):
+                for source, base in ((0, core * half), (2, (1 - core) * half)):
+                    out_ref[0, base : base + lengths[0]] = refs[source][0]
+                    out_ref[0, base + lengths[0] : base + half] = refs[source + 1][0]
+
+    specs = [
+        pl.BlockSpec(
+            (1, length, width),
+            lambda step, me_ref, table=table: (find(step ^ me_ref[1], table), 0, 0),
+        )
+        for length, table in zip(lengths, tables)
+    ]
+    me = jnp.stack([lax.axis_index("core"), lax.axis_index("ctx")]).astype(jnp.int32)
+    return pl.pallas_call(
+        body,
+        grid_spec=pltpu.PrefetchScalarGridSpec(
+            num_scalar_prefetch=1,
+            grid=(slots,),
+            in_specs=specs * 2,
+            out_specs=pl.BlockSpec((1, 2 * half, width), lambda step, me_ref: (step, 0, 0)),
+        ),
+        out_shape=jax.ShapeDtypeStruct((slots, 2 * half, width), own[0].dtype),
+        cost_estimate=pl.CostEstimate(
+            flops=0, bytes_accessed=8 * slots * half * width, transcendentals=0
+        ),
+        compiler_params=pltpu.CompilerParams(vmem_limit_bytes=VMEM_BYTES),
+    )(me, *own, *far).reshape(slots * 2 * half, width)
 
 
 def turned(values):
@@ -468,7 +572,7 @@
         out_shape=[out_shape, jax.ShapeDtypeStruct((1, KV, 1, cols), jnp.float32)],
         scratch_shapes=[pltpu.VMEM((2 * keys, cols), jnp.float32)],
         cost_estimate=pl.CostEstimate(
-            flops=work * HD * 4, bytes_accessed=8 * 1024 * 1024, transcendentals=work
+            flops=work * HD, bytes_accessed=1024 * 1024, transcendentals=0
         ),
         compiler_params=pltpu.CompilerParams(vmem_limit_bytes=VMEM_BYTES),
     )(queries, key_pos, query_pos, *pairs, *pairs)
@@ -511,7 +615,7 @@
         out_specs=[own] + pair_specs,
         out_shape=[own_shape] + pair_shapes,
         cost_estimate=pl.CostEstimate(
-            flops=work * HD * 10, bytes_accessed=16 * 1024 * 1024, transcendentals=work
+            flops=work * HD, bytes_accessed=1024 * 1024, transcendentals=0
         ),
         compiler_params=pltpu.CompilerParams(vmem_limit_bytes=VMEM_BYTES),
     )(queries, key_pos, query_pos, *pairs, *pairs, mixed, log_total, d_mixed, *tables)
@@ -530,7 +634,12 @@
 def feed_body(
     parts, split, me_ref, a_two_ref, dy_ref, *refs
 ):
-    weight_refs, (out_ref, d_two_ref), grad_refs = refs[:6], refs[6:8], refs[8:]
+    count = 4 if split else 6
+    weight_refs, (out_ref, d_two_ref), grad_refs = (
+        refs[:count],
+        refs[count : count + 2],
+        refs[count + 2 :],
+    )
     core = me_ref[0]
     step = pl.program_id(0)
 
@@ -540,8 +649,14 @@
         d_two_ref[...] = jnp.zeros_like(d_two_ref)
 
     def rows_of(member):
+        if split:
+            own = jnp.concatenate([weight_refs[0][0, member], weight_refs[1][0, member]], axis=0)
+            far = jnp.concatenate([weight_refs[2][0, member], weight_refs[3][0, member]], axis=0)
+            return jnp.concatenate(
+                [jnp.where(core == 0, own, far), jnp.where(core == 0, far, own)], axis=0
+            )
         wanted = feed_core(member, step, parts)
-        return jnp.where(wanted == core, weight_refs[2 * member][...], weight_refs[2 * member + 1][...])
+        return jnp.where(wanted == core, weight_refs[2 * member][0], weight_refs[2 * member + 1][0])
 
     a_two, dy_low = a_two_ref[...], dy_ref[...]
     gate_rows, up_rows, down_rows = rows_of(0), rows_of(1), rows_of(2)
@@ -578,22 +693,30 @@
     whole = pl.BlockSpec((tokens, width), lambda step, me_ref: (0, 0))
 
     def weight_spec(member, own):
+        first = (member + 1) * blocks // ctx_count // 2 * ctx_count
+
         def index(step, me_ref):
             matches = (feed_core(member, step, parts) == me_ref[0]) == own
-            return (jnp.where(matches, step % ctx_count, 0), 0)
-
-        return pl.BlockSpec((rows, width), index)
-
-    places_x = [(member + 1) // 2 if single else member + 1 for member in range(3)]
-    weight_specs = [weight_spec(member, own) for member in range(3) for own in (True, False)]
-    weight_args = [held[places_x[member]] for member in range(3) for held in (mine, far)]
+            return (first + jnp.where(matches, step % ctx_count, 0), 0, 0)
+
+        return pl.BlockSpec((1, rows, width), index)
+
     if split:
-        half = pl.BlockSpec(
-            (3, 1, rows // 2, width), lambda step, me_ref: (0, step ^ me_ref[1], 0, 0)
-        )
+        tables = [rel_offsets(list(reversed(order))) for order in ctx_orders()]
+        weight_specs = [
+            pl.BlockSpec(
+                (1, 3, part.shape[2], width),
+                lambda step, me_ref, table=table: (find(step, table), 0, 0, 0),
+            )
+            for part, table in zip(mine, tables)
+        ] * 2
+        weight_args = [*mine, *far]
+        half = pl.BlockSpec((3, 1, rows // 2, width), lambda step, me_ref: (0, step, 0, 0))
         grad_specs = [half, half]
         grad_shapes = [jax.ShapeDtypeStruct((3, blocks, rows // 2, width), jnp.bfloat16)] * 2
     else:
+        weight_specs = [weight_spec(member, own) for member in range(3) for own in (True, False)]
+        weight_args = [mine, far] * 3
         grad_specs = [pl.BlockSpec((1, rows, width), lambda step, me_ref: (step, 0, 0))] * 3
         grad_shapes = [jax.ShapeDtypeStruct((blocks, rows, width), jnp.bfloat16)] * 3
     me = jnp.stack([lax.axis_index("core"), lax.axis_index("ctx")]).astype(jnp.int32)
@@ -726,17 +849,31 @@
     query_pos = by_columns(pos_here[None, :])
     packed_tables = (by_columns(cosine), by_columns(sine_part))
 
-    held = lax.all_gather(weights, ("x", "ctx"), axis=0, tiled=True)
-    held = held.reshape(x_count, ctx_count * weight_rows, model_width)
-    mine = [held[x] for x in range(x_count)]
-    far = [swap(part, ("core", 0)) for part in mine]
-    first_rows = jnp.where(core == 0, mine[0], far[0])
-    if first_rows.shape[0] < cut_o + q_cols:
-        first_rows = jnp.concatenate([first_rows, jnp.where(core == 0, far[0], mine[0])], axis=0)
+    split = splits_rows(weight_rows)
+    if split:
+        first_half, feed_half = gather_halves(weights)
+        cuts = row_cuts(weight_rows // 2)
+        backward = [list(reversed(order)) for order in ctx_orders()]
+        first_own = [spread(first_half[low:high], order) for (low, high), order in zip(cuts, backward)]
+        first_far = [swap(part, ("core", 0)) for part in first_own]
+        feed_half, first_own = lax.optimization_barrier((feed_half, first_own))
+        mine = [feed_half[None, :, low:high] for low, high in cuts]
+        mine = [double(part, order[0]) for part, order in zip(mine, backward)]
+        first_rows = place_rows(first_own, first_far)
+    else:
+        mine = lax.all_gather(weights, ("x", "ctx"), axis=0, tiled=True)
+        mine = mine.reshape(x_count * ctx_count, weight_rows, model_width)
+        far = swap(mine, ("core", 0))
+        sides = [
+            jnp.where(core == 0, mine[:ctx_count], far[:ctx_count]),
+            jnp.where(core == 0, far[:ctx_count], mine[:ctx_count]),
+        ]
+        first_rows = jnp.concatenate(sides).reshape(-1, model_width)
     qkv_rows, o_rows = first_rows[:cut_o], first_rows[cut_o : cut_o + q_cols]
 
-    tokens_in = inputs.reshape(tokens, model_width)
-    cot_in = cotangent.reshape(tokens, model_width)
+    tokens_in, cot_in = lax.optimization_barrier(
+        (inputs.reshape(tokens, model_width), cotangent.reshape(tokens, model_width))
+    )
     dy_low = cot_in.astype(jnp.bfloat16)
     a_one = (normalize(tokens_in) * gains[0]).astype(jnp.bfloat16)
     pair_rows = matmul_t(qkv_rows[q_cols:], a_one)
@@ -744,6 +881,10 @@
         [rotate(pair_rows[:kv_cols], turn).astype(jnp.bfloat16), pair_rows[kv_cols:].astype(jnp.bfloat16)],
         axis=0,
     )
+    if split:
+        joined, mine = lax.optimization_barrier((joined, mine))
+        for position in range(1, len(backward[0])):
+            mine = [double(part, order[position]) for part, order in zip(mine, backward)]
     near = [joined] + [swap_by(joined, "ctx", z * y_count) for z in range(1, z_count)]
     pairs = list(near)
     for y in range(1, y_count):
@@ -757,21 +898,28 @@
         ]
     q_rot = rotate(matmul_t(qkv_rows[:q_cols], a_one), turn).astype(jnp.bfloat16)
     queries = pack((q_rot * SCALE_QK).astype(jnp.bfloat16))
-    attended = [
-        attend(queries, pairs, key_pos, query_pos, local_rows, seq) for seq in range(seqs)
-    ]
+    attended = []
+    for seq in range(seqs):
+        attended.append(attend(queries, pairs, key_pos, query_pos, local_rows, seq))
+        if split and seq == 0:
+            attended, mine = lax.optimization_barrier((attended, mine))
+            far = [swap(part, ("core", 0)) for part in mine]
     attn_low = jnp.concatenate([unpack(mixed) for mixed, _ in attended], axis=1)
     resid = tokens_in + matmul_c(attn_low, o_rows)
     a_two = (normalize(resid) * gains[1]).astype(jnp.bfloat16)
     fed, d_two, *feed_grads = feed_forward(a_two, dy_low, mine, far, weight_rows)
-    split = splits_rows(weight_rows)
-    if split:
-        feed_sums = reduce_ctx(*feed_grads)
     result = resid + fed
     d_norm_two, d_gain_two = norm_back(resid, d_two, gains[1])
     d_resid = cot_in + d_norm_two
     d_resid_low = d_resid.astype(jnp.bfloat16)
     d_attn = pack(matmul_t(o_rows, d_resid_low).astype(jnp.bfloat16))
+    if split:
+        feed_states = reduce_start(*feed_grads)
+        feed_states = [list(state) for state in feed_states]
+        d_attn, sends = lax.optimization_barrier((d_attn, [state[1] for state in feed_states]))
+        for state, sent in zip(feed_states, sends):
+            state[1] = sent
+        feed_sums, _ = reduce_finish(feed_states)
     d_q, d_pair = [], []
     for seq in range(seqs):
         mixed, log_total = attended[seq]
@@ -795,6 +943,8 @@
         for z in range(1, z_count):
             total = total + swap_by(line[z].astype(jnp.bfloat16), "ctx", z * y_count).astype(jnp.float32)
         d_pair.append(total)
+    if split:
+        d_pair, feed_sums = lax.optimization_barrier((d_pair, feed_sums))
     d_own = jnp.stack(d_pair).transpose(1, 4, 0, 2, 3).reshape(KV, 2 * HD, tokens)
     d_qkv = jnp.concatenate(
         [
@@ -805,28 +955,28 @@
         axis=0,
     )
     first_terms = first_grads(d_qkv, attn_low, a_one, d_resid_low, weight_rows)
+    d_one = matmul_c(d_qkv, qkv_rows)
+    d_norm_one, d_gain_one = norm_back(tokens_in, d_one, gains[0])
+    d_tokens = d_resid + d_norm_one
+    gain_grad = jnp.stack([d_gain_one, d_gain_two], axis=0)
     if split:
-        first_sums = reduce_ctx(*first_terms)
+        first_sums, gain_grad = reduce_finish(reduce_start(*first_terms), gain_grad)
         sums = [first_sums[0], feed_sums[0], feed_sums[1], feed_sums[2]]
-        own_x = [jnp.where(x_index == 0, sums[core_of], sums[2 + core_of]) for core_of in range(2)]
-        other_x = [jnp.where(x_index == 0, sums[2 + core_of], sums[core_of]) for core_of in range(2)]
-        halves = [
-            own.astype(jnp.float32) + swap(other, ("x", 0)).astype(jnp.float32)
-            for own, other in zip(own_x, other_x)
-        ]
+        own_x = jnp.stack([jnp.where(x_index == 0, sums[c], sums[2 + c]) for c in range(2)])
+        other_x = jnp.stack([jnp.where(x_index == 0, sums[2 + c], sums[c]) for c in range(2)])
+        come, gain_grad = swap_with(other_x, gain_grad, ("x", 0))
+        halves = own_x.astype(jnp.float32) + come.astype(jnp.float32)
         own_half = jnp.where(core == 0, halves[0], halves[1])
         other_half = jnp.where(core == 0, halves[1], halves[0]).astype(jnp.bfloat16)
-        come = swap(other_half, ("core", 0)).astype(jnp.float32)
+        come, gain_grad = swap_with(other_half, gain_grad, ("core", 0))
+        come = come.astype(jnp.float32)
         weight_share = jnp.concatenate(
             [jnp.where(core == 0, own_half, come), jnp.where(core == 0, come, own_half)], axis=0
         )
     else:
         weight_share = scatter_whole([first_terms[0], *feed_grads])
-    d_one = matmul_c(d_qkv, qkv_rows)
-    d_norm_one, d_gain_one = norm_back(tokens_in, d_one, gains[0])
-    d_tokens = d_resid + d_norm_one
-    gain_parts = lax.all_gather(jnp.stack([d_gain_one, d_gain_two], axis=0), ("x", "core", "ctx"))
-    gain_grad = jnp.sum(gain_parts, axis=0)
+        for where in [("core", 0)] + sum(bit_groups(), []):
+            gain_grad = gain_grad + swap(gain_grad, where)
     weight_first, weight_second, weight_new = adam_update(
         weights.astype(jnp.float32), weight_share, first_moment, second_moment, RATE, DECAY, STEP
     )

time: 785 us -> 703 us (0.90)
  blocking collectives: 68 us -> 0 us
  local copies, waits for them, and re-layouts: 87.6 us -> 60.4 us
  waiting for transfers between devices: 371 us -> 385 us
  between operations: 15.6 us -> 2.54 us
  other arithmetic: 52.8 us -> 63.9 us
    ppermute x34 -> x49, waiting for transfers between devices: 233 us -> 385 us  [swap_by(): return lax.ppermute(values, axis, [(i, i ^ offset) for i in range(size)])]
    all_gather x1 -> x0, waiting for transfers between devices: 138 us -> none  [shards(): held = lax.all_gather(weights, ('x', 'ctx'), axis=0, tiled=True)]
    all_gather x1 -> x0, blocking collectives: 68 us -> none  [shards(): lax.all_gather(jnp.stack([d_gain_one, d_gain_two], axis=0), ('x', 'core',...]
    slice x14 -> x19, local copies, waits for them, and re-layouts: 39.9 us -> 21.2 us  [the longest x4 7.16 us: step_ctx(): pick = lambda values, side: lax.index_in_dim(values, side, dim, False)]
    concatenate x0 -> x18, other arithmetic: none -> 17.2 us  [the longest x12 15 us: double(): return jnp.concatenate([values, swap(values, where)], axis=0)]
    ppermute x2 -> x0, local copies, waits for them, and re-layouts: 15.8 us -> none  [swap_by(): return lax.ppermute(values, axis, [(i, i ^ offset) for i in range(size)])]
    unnamed x132 -> x171, local copies, waits for them, and re-layouts: 16.1 us -> 27.1 us
    slice x1 -> x0, other arithmetic: 9.03 us -> none  [shards(): mine = [held[x] for x in range(x_count)]]
  transfers between devices with their start and end apart: 35 -> 49, of which waited for: 18 -> 28; matrix products, arithmetic and copies ran while one was open for 11% -> 11% of each run, Pallas kernels for 7% -> 7%
where the time goes in v4:
time: 703 us; the launch traced here: 693 us
  waiting for transfers between devices  385 us (55%)
  Pallas kernels  127 us (18%)
  other arithmetic  63.9 us (9%)
  local copies, waits for them, and re-layouts  60.4 us (9%)
  starting transfers between devices  44.9 us (6%)
  matrix products  9.33 us (1%)
    ppermute x49, waiting for transfers between devices, swap_by(): return lax.ppermute(values, axis, [(i, i ^ offset) for i in range(size)])  385 us
    pallas_call x2, Pallas kernels, attend_back(): pl.pallas_call(lambda *refs: attend_back_body(count, aligned, *refs), gri...  45.6 us
    ppermute x49, starting transfers between devices, swap_by(): return lax.ppermute(values, axis, [(i, i ^ offset) for i in range(size)])  44.9 us
    pallas_call x1, Pallas kernels, feed_forward(): pl.pallas_call(lambda *refs: feed_body(parts, split, *refs), grid_spec=pl...  41.6 us
    unnamed x171, local copies, waits for them, and re-layouts  27.1 us
    pallas_call x2, Pallas kernels, attend(): pl.pallas_call(lambda *refs: attend_body(count, aligned, *refs), grid=(KV...  25.4 us
    concatenate x12, other arithmetic, double(): return jnp.concatenate([values, swap(values, where)], axis=0)  15 us
  transfers between devices with their start and end apart: 49, of which 28 were waited for; matrix products, arithmetic and copies ran while one was open for 11% of the time, Pallas kernels for 7%

profile of v4, /device:TPU:0, one launch (start us, length us, event | category | flops | bytes accessed | tf_op | source)
XLA Modules:
  0.0 692.7 jit_solution(6206358637366141974)
XLA Ops:
  3.6 14.9 %collective-permute-done = bf16[320,960]{1,0:T(8,128)(2,1)S(1)} collective-permute-done((bf16[320,960]{1,0:T(8,128)(2,1)}, bf16[320,960]{1,0:T(8,128)(2,1)S(1)}, u32[]{:S(2)}, u32[]{:S(2)}) %collective-permute-start) | collective-permute-done | bytes 614432 | tf_op jit(solution)/shard_map/ppermute | solution.py:106
  38.8 10.2 %collective-permute-done.3 = bf16[2,80,960]{2,1,0:T(8,128)(2,1)S(1)} collective-permute-done((bf16[2,80,960]{2,1,0:T(8,128)(2,1)S(1)}, bf16[2,80,960]{2,1,0:T(8,128)(2,1)S(1)}, u32[]{:S(2)}, u32[]{:S(2)}) %collective-permute-start.3) | collective-permute-done | bytes 307232 | tf_op jit(solution)/shard_map/ppermute | solution.py:106
  50.7 3.9 collective-permute-done.6
  54.9 9.5 %collective-permute-done.4 = bf16[4,80,960]{2,1,0:T(8,128)(2,1)S(1)} collective-permute-done((bf16[4,80,960]{2,1,0:T(8,128)(2,1)S(1)}, bf16[4,80,960]{2,1,0:T(8,128)(2,1)S(1)}, u32[]{:S(2)}, u32[]{:S(2)}) %collective-permute-start.4) | collective-permute-done | bytes 614432 | tf_op jit(solution)/shard_map/ppermute | solution.py:106
  64.6 4.0 collective-permute-done.7
  75.4 8.4 %collective-permute-done.11 = bf16[1,3,80,960]{3,2,1,0:T(8,128)(2,1)} collective-permute-done((bf16[1,3,80,960]{3,2,1,0:T(8,128)(2,1)}, bf16[1,3,80,960]{3,2,1,0:T(8,128)(2,1)}, u32[]{:S(2)}, u32[]{:S(2)}) %collective-permute-start.11) | collective-permute-done | bytes 460832 | tf_op jit(solution)/shard_map/ppermute | solution.py:106
  85.9 10.3 %collective-permute-done.10 = bf16[1,3,80,960]{3,2,1,0:T(8,128)(2,1)} collective-permute-done((bf16[1,3,80,960]{3,2,1,0:T(8,128)(2,1)S(1)}, bf16[1,3,80,960]{3,2,1,0:T(8,128)(2,1)}, u32[]{:S(2)}, u32[]{:S(2)}) %collective-permute-start.10) | collective-permute-done | bytes 460832 | tf_op jit(solution)/shard_map/ppermute | solution.py:106
  98.3 7.2 %shard_map.152 = bf16[8,320,960]{2,1,0:T(8,128)(2,1)} custom-call(s32[2]{0:T(128)S(1)} %pad_add_fusion.1.me_ref.refs_0_, bf16[8,80,960]{2,1,0:T(8,128)(2,1)S(1)} %pad_maximum_fusion.5.refs_0_, bf16[8,80,960]{2,1,0:T(8,128)(2,1)S(1)} %pad_maximum_fusion.6.refs_1_, bf16[8,80,960]{2,1,0:T(8,128)(2,1)} %collective-permute-done.8.refs_2_, ...), custom_call_target="tpu_custom_call" | custom-call | bytes 9830400 | tf_op jit(solution)/shard_map/pallas_call | solution.py:367
  114.2 40.8 %collective-permute-done.19 = bf16[2,3,80,960]{3,2,1,0:T(8,128)(2,1)S(1)} collective-permute-done((bf16[2,3,80,960]{3,2,1,0:T(8,128)(2,1)S(1)}, bf16[2,3,80,960]{3,2,1,0:T(8,128)(2,1)S(1)}, u32[]{:S(2)}, u32[]{:S(2)}) %collective-permute-start.19) | collective-permute-done | bytes 921632 | tf_op jit(solution)/shard_map/ppermute | solution.py:106
  167.6 4.3 fusion.72
  171.9 46.8 %collective-permute-done.14.refs_6_.refs_14_ = bf16[640,512]{1,0:T(8,128)(2,1)S(1)} collective-permute-done((bf16[640,512]{1,0:T(8,128)(2,1)S(1)}, bf16[640,512]{1,0:T(8,128)(2,1)S(1)}, u32[]{:S(2)}, u32[]{:S(2)}) %collective-permute-start.14) | collective-permute-done | bytes 655392 | tf_op jit(solution)/shard_map/ppermute | solution.py:106
  219.5 10.7 %collective-permute-done.13.refs_5_.refs_13_ = bf16[640,512]{1,0:T(8,128)(2,1)S(1)} collective-permute-done((bf16[640,512]{1,0:T(8,128)(2,1)S(1)}, bf16[640,512]{1,0:T(8,128)(2,1)S(1)}, u32[]{:S(2)}, u32[]{:S(2)}) %collective-permute-start.13) | collective-permute-done | bytes 655392 | tf_op jit(solution)/shard_map/ppermute | solution.py:106
  231.8 12.4 %collective-permute-done.12.refs_4_.refs_12_ = bf16[640,512]{1,0:T(8,128)(2,1)S(1)} collective-permute-done((bf16[640,512]{1,0:T(8,128)(2,1)S(1)}, bf16[640,512]{1,0:T(8,128)(2,1)S(1)}, u32[]{:S(2)}, u32[]{:S(2)}) %collective-permute-start.12) | collective-permute-done | bytes 655392 | tf_op jit(solution)/shard_map/ppermute | solution.py:106
  248.5 11.8 %collective-permute-done.16.refs_8_.refs_16_ = bf16[640,512]{1,0:T(8,128)(2,1)S(1)} collective-permute-done((bf16[640,512]{1,0:T(8,128)(2,1)S(1)}, bf16[640,512]{1,0:T(8,128)(2,1)S(1)}, u32[]{:S(2)}, u32[]{:S(2)}) %collective-permute-start.16) | collective-permute-done | bytes 655392 | tf_op jit(solution)/shard_map/ppermute | solution.py:106
  260.3 12.8 %shard_map.153 = (bf16[960,256]{1,0:T(8,128)(2,1)S(1)}, f32[1,5,1,768]{3,2,1,0:T(1,128)S(1)}) custom-call(bf16[960,512]{1,0:T(8,128)(2,1)} %bitcast.188, s32[2,1024,1]{2,1,0:T(8,128)} %pad_add_fusion.refs_1_, s32[1,768]{1,0:T(1,128)S(1)} %broadcast_in_dim.13.refs_2_, bf16[640,512]{1,0:T(8,128)(2,1)S(1)} %pad_maximum_fusion.18.refs_3_.refs_11_, ...), custom_call_target="tpu_custom_call" | custom-call | flops 377487360 | bytes 1048576 | tf_op jit(solution)/shard_map/pallas_call | solution.py:567
  275.7 4.5 pad_maximum_fusion.1.refs_4_
  280.9 12.6 %shard_map.154 = (bf16[960,256]{1,0:T(8,128)(2,1)S(1)}, f32[1,5,1,768]{3,2,1,0:T(1,128)S(1)}) custom-call(bf16[960,512]{1,0:T(8,128)(2,1)} %bitcast.189, s32[2,1024,1]{2,1,0:T(8,128)} %pad_add_fusion.refs_1_, s32[1,768]{1,0:T(1,128)S(1)} %broadcast_in_dim.13.refs_2_, bf16[640,512]{1,0:T(8,128)(2,1)S(1)} %pad_maximum_fusion.18.refs_3_.refs_11_, ...), custom_call_target="tpu_custom_call" | custom-call | flops 377487360 | bytes 1048576 | tf_op jit(solution)/shard_map/pallas_call | solution.py:567
  297.3 41.6 %shard_map.155 = (f32[512,960]{1,0:T(8,128)S(1)}, f32[512,960]{1,0:T(8,128)}, bf16[3,8,160,960]{3,2,1,0:T(8,128)(2,1)}, bf16[3,8,160,960]{3,2,1,0:T(8,128)(2,1)}) custom-call(s32[2]{0:T(128)S(1)} %pad_add_fusion.1.me_ref.refs_0_, bf16[512,960]{1,0:T(8,128)(2,1)S(1)} %multiply_convert_fusion.refs_1_, bf16[512,960]{1,0:T(8,128)(2,1)S(1)} %convert_element_type.750.refs_2_, ...), custom_call_target="tpu_custom_call" | custom-call | flops 22649241600 | bytes 29491200 | tf_op jit(solution)/shard_map/pallas_call | solution.py:723
  347.4 5.3 fusion.69
  371.4 22.6 %shard_map.157 = (bf16[960,256]{1,0:T(8,128)(2,1)S(1)}, bf16[4,5,2,128,128]{4,3,2,1,0:T(8,128)(2,1)}, bf16[4,5,2,128,128]{4,3,2,1,0:T(8,128)(2,1)}) custom-call(bf16[960,512]{1,0:T(8,128)(2,1)} %bitcast.190, s32[2,1024,1]{2,1,0:T(8,128)} %pad_add_fusion.refs_1_, s32[1,768]{1,0:T(1,128)S(1)} %broadcast_in_dim.13.refs_2_, ...), custom_call_target="tpu_custom_call" | custom-call | flops 377487360 | bytes 1048576 | tf_op jit(solution)/shard_map/pallas_call | solution.py:604
  402.9 23.0 %shard_map.156 = (bf16[960,256]{1,0:T(8,128)(2,1)S(1)}, bf16[4,5,2,128,128]{4,3,2,1,0:T(8,128)(2,1)}, bf16[4,5,2,128,128]{4,3,2,1,0:T(8,128)(2,1)}) custom-call(bf16[960,512]{1,0:T(8,128)(2,1)} %bitcast.191, s32[2,1024,1]{2,1,0:T(8,128)} %pad_add_fusion.refs_1_, s32[1,768]{1,0:T(1,128)S(1)} %broadcast_in_dim.13.refs_2_, ...), custom_call_target="tpu_custom_call" | custom-call | flops 377487360 | bytes 1048576 | tf_op jit(solution)/shard_map/pallas_call | solution.py:604
  434.8 34.0 %collective-permute-done.34 = bf16[3,2,2,80,960]{4,3,0,1,2:T(8,128)(2,1)} collective-permute-done((bf16[3,2,2,80,960]{4,3,0,1,2:T(8,128)(2,1)}, bf16[3,2,2,80,960]{4,3,0,1,2:T(8,128)(2,1)}, u32[]{:S(2)}, u32[]{:S(2)}) %collective-permute-start.34) | collective-permute-done | bytes 1843232 | tf_op jit(solution)/shard_map/ppermute | solution.py:106
  475.3 21.2 %collective-permute-done.26 = bf16[4,5,2,128,128]{4,3,2,1,0:T(8,128)(2,1)S(1)} collective-permute-done((bf16[4,5,2,128,128]{4,3,2,1,0:T(8,128)(2,1)}, bf16[4,5,2,128,128]{4,3,2,1,0:T(8,128)(2,1)S(1)}, u32[]{:S(2)}, u32[]{:S(2)}) %collective-permute-start.26) | collective-permute-done | bytes 1310752 | tf_op jit(solution)/shard_map/ppermute | solution.py:106
  504.8 61.8 %collective-permute-done.38 = bf16[3,2,80,960]{3,2,0,1:T(8,128)(2,1)S(1)} collective-permute-done((bf16[3,2,80,960]{3,2,0,1:T(8,128)(2,1)S(1)}, bf16[3,2,80,960]{3,2,0,1:T(8,128)(2,1)S(1)}, u32[]{:S(2)}, u32[]{:S(2)}) %collective-permute-start.38) | collective-permute-done | bytes 921632 | tf_op jit(solution)/shard_map/ppermute | solution.py:106
  567.2 13.5 %collective-permute-done.28 = bf16[5,2,128,128]{3,2,1,0:T(8,128)(2,1)S(1)} collective-permute-done((bf16[5,2,128,128]{3,2,1,0:T(8,128)(2,1)S(1)}, bf16[5,2,128,128]{3,2,1,0:T(8,128)(2,1)S(1)}, u32[]{:S(2)}, u32[]{:S(2)}) %collective-permute-start.28) | collective-permute-done | bytes 327712 | tf_op jit(solution)/shard_map/ppermute | solution.py:106
  580.8 10.1 %collective-permute-done.36 = bf16[3,80,960]{2,1,0:T(8,128)(2,1)S(1)} collective-permute-done((bf16[3,80,960]{2,1,0:T(8,128)(2,1)S(1)}, bf16[3,80,960]{2,1,0:T(8,128)(2,1)S(1)}, u32[]{:S(2)}, u32[]{:S(2)}) %collective-permute-start.36) | collective-permute-done | bytes 460832 | tf_op jit(solution)/shard_map/ppermute | solution.py:106
  599.2 7.2 %shard_map.158 = (bf16[1,8,160,960]{3,2,1,0:T(8,128)(2,1)}, bf16[1,8,160,960]{3,2,1,0:T(8,128)(2,1)}) custom-call(s32[2]{0:T(128)S(1)} %pad_add_fusion.1.me_ref.refs_0_, bf16[1600,512]{1,0:T(8,128)(2,1)S(1)} %pad_maximum_fusion.4.qkv_ref, bf16[960,512]{1,0:T(8,128)(2,1)S(1)} %copy-done.23, bf16[512,960]{1,0:T(8,128)(2,1)S(1)} %copy-done.17, ...), custom_call_target="tpu_custom_call" | custom-call | flops 2516582400 | bytes 4915200 | tf_op jit(solution)/shard_map/pallas_call | solution.py:766
  614.8 15.5 %collective-permute-done.44 = bf16[1,2,2,80,960]{4,3,2,1,0:T(8,128)(2,1)S(1)} collective-permute-done((bf16[1,2,2,80,960]{4,3,2,1,0:T(8,128)(2,1)S(1)}, bf16[1,2,2,80,960]{4,3,2,1,0:T(8,128)(2,1)S(1)}, u32[]{:S(2)}, u32[]{:S(2)}) %collective-permute-start.44) | collective-permute-done | bytes 614432 | tf_op jit(solution)/shard_map/ppermute | solution.py:106
  633.7 13.6 %collective-permute-done.45 = bf16[1,2,80,960]{3,2,1,0:T(8,128)(2,1)S(1)} collective-permute-done((bf16[1,2,80,960]{3,2,1,0:T(8,128)(2,1)S(1)}, bf16[1,2,80,960]{3,2,1,0:T(8,128)(2,1)S(1)}, u32[]{:S(2)}, u32[]{:S(2)}) %collective-permute-start.45) | collective-permute-done | bytes 307232 | tf_op jit(solution)/shard_map/ppermute | solution.py:106
  648.7 4.7 collective-permute-done.46
  653.4 5.0 collective-permute-done.43
  664.2 13.4 %collective-permute-done.47 = bf16[336,960]{1,0:T(8,128)(2,1)} collective-permute-done((bf16[336,960]{1,0:T(8,128)(2,1)}, bf16[336,960]{1,0:T(8,128)(2,1)}, u32[]{:S(2)}, u32[]{:S(2)}) %collective-permute-start.47) | collective-permute-done | bytes 645152 | tf_op jit(solution)/shard_map/ppermute | solution.py:106
  (392 shorter events, 172.6 us)
Async XLA Ops:
  0.6 17.9 %collective-permute-start = (bf16[320,960]{1,0:T(8,128)(2,1)}, bf16[320,960]{1,0:T(8,128)(2,1)S(1)}, u32[]{:S(2)}, u32[]{:S(2)}) collective-permute-start(bf16[320,960]{1,0:T(8,128)(2,1)} %param.11), channel_id=1, source_target_pairs={{0,16},{16,0},{1,17},{17,1},{2,18},{18,2},{3,19},{19,3},{4,20},{20... | collective-permute-start | bytes 1843208 | tf_op jit(solution)/shard_map/ppermute | solution.py:106
  64.5 33.8 %collective-permute-start.8 = (bf16[8,80,960]{2,1,0:T(8,128)(2,1)S(1)}, bf16[8,80,960]{2,1,0:T(8,128)(2,1)}, u32[]{:S(2)}, u32[]{:S(2)}) collective-permute-start(bf16[8,80,960]{2,1,0:T(8,128)(2,1)S(1)} %pad_maximum_fusion.5.refs_0_), channel_id=1, source_target_pairs={{0,8},{8,0},{1,9},{9,1},{2,10},{10,2},{3,11},{11,3},{4,12},{12,4},... | collective-permute-start | bytes 3686408 | tf_op jit(solution)/shard_map/ppermute | solution.py:106
  68.7 29.6 %collective-permute-start.9 = (bf16[8,80,960]{2,1,0:T(8,128)(2,1)S(1)}, bf16[8,80,960]{2,1,0:T(8,128)(2,1)}, u32[]{:S(2)}, u32[]{:S(2)}) collective-permute-start(bf16[8,80,960]{2,1,0:T(8,128)(2,1)S(1)} %pad_maximum_fusion.6.refs_1_), channel_id=1, source_target_pairs={{0,8},{8,0},{1,9},{9,1},{2,10},{10,2},{3,11},{11,3},{4,12},{12,4},... | collective-permute-start | bytes 3686408 | tf_op jit(solution)/shard_map/ppermute | solution.py:106
  71.3 24.9 %collective-permute-start.10 = (bf16[1,3,80,960]{3,2,1,0:T(8,128)(2,1)S(1)}, bf16[1,3,80,960]{3,2,1,0:T(8,128)(2,1)}, u32[]{:S(2)}, u32[]{:S(2)}) collective-permute-start(bf16[1,3,80,960]{3,2,1,0:T(8,128)(2,1)S(1)} %get-tuple-element.184), channel_id=1, source_target_pairs={{0,4},{1,5},{2,6},{3,7},{4,0},{5,1},{6,2},{7,3},{8,12},{9,13},{10,... | collective-permute-start | bytes 1382408 | tf_op jit(solution)/shard_map/ppermute | solution.py:106
  111.2 43.8 %collective-permute-start.19 = (bf16[2,3,80,960]{3,2,1,0:T(8,128)(2,1)S(1)}, bf16[2,3,80,960]{3,2,1,0:T(8,128)(2,1)S(1)}, u32[]{:S(2)}, u32[]{:S(2)}) collective-permute-start(bf16[2,3,80,960]{3,2,1,0:T(8,128)(2,1)S(1)} %copy-done.32), channel_id=1, source_target_pairs={{0,2},{1,3},{2,0},{3,1},{4,6},{5,7},{6,4},{7,5},{8,10},{9,11},{10,... | collective-permute-start | bytes 2764808 | tf_op jit(solution)/shard_map/ppermute | solution.py:106
  111.4 45.6 %collective-permute-start.21 = (bf16[2,3,80,960]{3,2,1,0:T(8,128)(2,1)S(1)}, bf16[2,3,80,960]{3,2,1,0:T(8,128)(2,1)S(1)}, u32[]{:S(2)}, u32[]{:S(2)}) collective-permute-start(bf16[2,3,80,960]{3,2,1,0:T(8,128)(2,1)S(1)} %copy-done.30), channel_id=1, source_target_pairs={{0,4},{1,5},{2,6},{3,7},{4,0},{5,1},{6,2},{7,3},{8,12},{9,13},{10,... | collective-permute-start | bytes 2764808 | tf_op jit(solution)/shard_map/ppermute | solution.py:106
  113.6 48.6 %collective-permute-start.15 = (bf16[640,512]{1,0:T(8,128)(2,1)S(1)}, bf16[640,512]{1,0:T(8,128)(2,1)S(1)}, u32[]{:S(2)}, u32[]{:S(2)}) collective-permute-start(bf16[640,512]{1,0:T(8,128)(2,1)S(1)} %pad_maximum_fusion.18.refs_3_.refs_11_), channel_id=1, source_target_pairs={{0,1},{1,0},{2,3},{3,2},{4,5},{5,4},{6,7},{7,6},{8,9},{9,8},{10,11... | collective-permute-start | bytes 1966088 | tf_op jit(solution)/shard_map/ppermute | solution.py:106
  156.5 116.6 %collective-permute-start.20 = (bf16[4,3,80,960]{3,2,1,0:T(8,128)(2,1)}, bf16[4,3,80,960]{3,2,1,0:T(8,128)(2,1)}, u32[]{:S(2)}, u32[]{:S(2)}) collective-permute-start(bf16[4,3,80,960]{3,2,1,0:T(8,128)(2,1)} %pad_maximum_fusion.2), channel_id=1, source_target_pairs={{0,1},{1,0},{2,3},{3,2},{4,5},{5,4},{6,7},{7,6},{8,9},{9,8},{10,11... | collective-permute-start | bytes 5529608 | tf_op jit(solution)/shard_map/ppermute | solution.py:106
  158.7 117.0 %collective-permute-start.22 = (bf16[4,3,80,960]{3,2,1,0:T(8,128)(2,1)}, bf16[4,3,80,960]{3,2,1,0:T(8,128)(2,1)}, u32[]{:S(2)}, u32[]{:S(2)}) collective-permute-start(bf16[4,3,80,960]{3,2,1,0:T(8,128)(2,1)} %pad_maximum_fusion.3), channel_id=1, source_target_pairs={{0,2},{1,3},{2,0},{3,1},{4,6},{5,7},{6,4},{7,5},{8,10},{9,11},{10,... | collective-permute-start | bytes 5529608 | tf_op jit(solution)/shard_map/ppermute | solution.py:106
  158.7 60.0 %collective-permute-start.14 = (bf16[640,512]{1,0:T(8,128)(2,1)S(1)}, bf16[640,512]{1,0:T(8,128)(2,1)S(1)}, u32[]{:S(2)}, u32[]{:S(2)}) collective-permute-start(bf16[640,512]{1,0:T(8,128)(2,1)S(1)} %pad_maximum_fusion.18.refs_3_.refs_11_), channel_id=1, source_target_pairs={{0,6},{1,7},{2,4},{3,5},{4,2},{5,3},{6,0},{7,1},{8,14},{9,15},{10,... | collective-permute-start | bytes 1966088 | tf_op jit(solution)/shard_map/ppermute | solution.py:106
  160.8 69.5 %collective-permute-start.13 = (bf16[640,512]{1,0:T(8,128)(2,1)S(1)}, bf16[640,512]{1,0:T(8,128)(2,1)S(1)}, u32[]{:S(2)}, u32[]{:S(2)}) collective-permute-start(bf16[640,512]{1,0:T(8,128)(2,1)S(1)} %pad_maximum_fusion.18.refs_3_.refs_11_), channel_id=1, source_target_pairs={{0,4},{1,5},{2,6},{3,7},{4,0},{5,1},{6,2},{7,3},{8,12},{9,13},{10,... | collective-permute-start | bytes 1966088 | tf_op jit(solution)/shard_map/ppermute | solution.py:106
  162.3 81.9 %collective-permute-start.12 = (bf16[640,512]{1,0:T(8,128)(2,1)S(1)}, bf16[640,512]{1,0:T(8,128)(2,1)S(1)}, u32[]{:S(2)}, u32[]{:S(2)}) collective-permute-start(bf16[640,512]{1,0:T(8,128)(2,1)S(1)} %pad_maximum_fusion.18.refs_3_.refs_11_), channel_id=1, source_target_pairs={{0,2},{1,3},{2,0},{3,1},{4,6},{5,7},{6,4},{7,5},{8,10},{9,11},{10,... | collective-permute-start | bytes 1966088 | tf_op jit(solution)/shard_map/ppermute | solution.py:106
  218.7 29.8 %collective-permute-start.18 = (bf16[640,512]{1,0:T(8,128)(2,1)S(1)}, bf16[640,512]{1,0:T(8,128)(2,1)S(1)}, u32[]{:S(2)}, u32[]{:S(2)}) collective-permute-start(bf16[640,512]{1,0:T(8,128)(2,1)S(1)} %collective-permute-done.14.refs_6_.refs_14_), channel_id=1, source_target_pairs={{0,1},{1,0},{2,3},{3,2},{4,5},{5,4},{6,7},{7,6},{8,9},{9,8},{10,11... | collective-permute-start | bytes 1966088 | tf_op jit(solution)/shard_map/ppermute | solution.py:106
  230.3 18.3 %collective-permute-start.17 = (bf16[640,512]{1,0:T(8,128)(2,1)S(1)}, bf16[640,512]{1,0:T(8,128)(2,1)S(1)}, u32[]{:S(2)}, u32[]{:S(2)}) collective-permute-start(bf16[640,512]{1,0:T(8,128)(2,1)S(1)} %collective-permute-done.13.refs_5_.refs_13_), channel_id=1, source_target_pairs={{0,1},{1,0},{2,3},{3,2},{4,5},{5,4},{6,7},{7,6},{8,9},{9,8},{10,11... | collective-permute-start | bytes 1966088 | tf_op jit(solution)/shard_map/ppermute | solution.py:106
  280.2 17.1 %collective-permute-start.24 = (bf16[8,3,80,960]{3,2,1,0:T(8,128)(2,1)}, bf16[8,3,80,960]{3,2,1,0:T(8,128)(2,1)}, u32[]{:S(2)}, u32[]{:S(2)}) collective-permute-start(bf16[8,3,80,960]{3,2,1,0:T(8,128)(2,1)} %pad_maximum_fusion.1.refs_4_), channel_id=1, source_target_pairs={{0,8},{8,0},{1,9},{9,1},{2,10},{10,2},{3,11},{11,3},{4,12},{12,4},... | collective-permute-start | bytes 11059208 | tf_op jit(solution)/shard_map/ppermute | solution.py:106
  340.3 19.2 %collective-permute-start.25 = (bf16[3,8,160,960]{3,2,1,0:T(8,128)(2,1)}, bf16[3,8,160,960]{3,2,1,0:T(8,128)(2,1)}, u32[]{:S(2)}, u32[]{:S(2)}) collective-permute-start(bf16[3,8,160,960]{3,2,1,0:T(8,128)(2,1)} %get-tuple-element.60), channel_id=1, source_target_pairs={{0,8},{8,0},{1,9},{9,1},{2,10},{10,2},{3,11},{11,3},{4,12},{12,4},... | collective-permute-start | bytes 22118408 | tf_op jit(solution)/shard_map/ppermute | solution.py:106
  394.8 34.5 %collective-permute-start.30 = (bf16[4,5,2,128,128]{4,3,2,1,0:T(8,128)(2,1)}, bf16[4,5,2,128,128]{4,3,2,1,0:T(8,128)(2,1)}, u32[]{:S(2)}, u32[]{:S(2)}) collective-permute-start(bf16[4,5,2,128,128]{4,3,2,1,0:T(8,128)(2,1)} %get-tuple-element.68), channel_id=1, source_target_pairs={{0,1},{1,0},{2,3},{3,2},{4,5},{5,4},{6,7},{7,6},{8,9},{9,8},{10,11... | collective-permute-start | bytes 3932168 | tf_op jit(solution)/shard_map/ppermute | solution.py:106
  395.1 73.7 %collective-permute-start.34 = (bf16[3,2,2,80,960]{4,3,0,1,2:T(8,128)(2,1)}, bf16[3,2,2,80,960]{4,3,0,1,2:T(8,128)(2,1)}, u32[]{:S(2)}, u32[]{:S(2)}) collective-permute-start(bf16[3,2,2,80,960]{4,3,0,1,2:T(8,128)(2,1)} %fusion), channel_id=1, source_target_pairs={{0,1},{1,0},{2,3},{3,2},{4,5},{5,4},{6,7},{7,6},{8,9},{9,8},{10,11... | collective-permute-start | bytes 5529608 | tf_op jit(solution)/shard_map/ppermute | solution.py:106
  396.9 74.7 %collective-permute-start.37 = (bf16[3,2,2,80,960]{4,3,0,2,1:T(8,128)(2,1)}, bf16[3,2,2,80,960]{4,3,0,2,1:T(8,128)(2,1)}, u32[]{:S(2)}, u32[]{:S(2)}) collective-permute-start(bf16[3,2,2,80,960]{4,3,0,2,1:T(8,128)(2,1)} %fusion.1), channel_id=1, source_target_pairs={{0,2},{1,3},{2,0},{3,1},{4,6},{5,7},{6,4},{7,5},{8,10},{9,11},{10,... | collective-permute-start | bytes 5529608 | tf_op jit(solution)/shard_map/ppermute | solution.py:106
  425.9 70.5 %collective-permute-start.26 = (bf16[4,5,2,128,128]{4,3,2,1,0:T(8,128)(2,1)}, bf16[4,5,2,128,128]{4,3,2,1,0:T(8,128)(2,1)S(1)}, u32[]{:S(2)}, u32[]{:S(2)}) collective-permute-start(bf16[4,5,2,128,128]{4,3,2,1,0:T(8,128)(2,1)} %get-tuple-element.66), channel_id=1, source_target_pairs={{0,1},{1,0},{2,3},{3,2},{4,5},{5,4},{6,7},{7,6},{8,9},{9,8},{10,11... | collective-permute-start | bytes 3932168 | tf_op jit(solution)/shard_map/ppermute | solution.py:106
  431.6 66.0 %collective-permute-start.31 = (bf16[5,2,128,128]{3,2,1,0:T(8,128)(2,1)S(1)}, bf16[5,2,128,128]{3,2,1,0:T(8,128)(2,1)S(1)}, u32[]{:S(2)}, u32[]{:S(2)}) collective-permute-start(bf16[5,2,128,128]{3,2,1,0:T(8,128)(2,1)S(1)} %get-tuple-element.173), channel_id=1, source_target_pairs={{0,2},{1,3},{2,0},{3,1},{4,6},{5,7},{6,4},{7,5},{8,10},{9,11},{10,... | collective-permute-start | bytes 983048 | tf_op jit(solution)/shard_map/ppermute | solution.py:106
  433.1 66.0 %collective-permute-start.33 = (bf16[5,2,128,128]{3,2,1,0:T(8,128)(2,1)S(1)}, bf16[5,2,128,128]{3,2,1,0:T(8,128)(2,1)S(1)}, u32[]{:S(2)}, u32[]{:S(2)}) collective-permute-start(bf16[5,2,128,128]{3,2,1,0:T(8,128)(2,1)S(1)} %get-tuple-element.174), channel_id=1, source_target_pairs={{0,6},{1,7},{2,4},{3,5},{4,2},{5,3},{6,0},{7,1},{8,14},{9,15},{10,... | collective-permute-start | bytes 983048 | tf_op jit(solution)/shard_map/ppermute | solution.py:106
  468.9 32.6 %collective-permute-start.32 = (bf16[5,2,128,128]{3,2,1,0:T(8,128)(2,1)S(1)}, bf16[5,2,128,128]{3,2,1,0:T(8,128)(2,1)S(1)}, u32[]{:S(2)}, u32[]{:S(2)}) collective-permute-start(bf16[5,2,128,128]{3,2,1,0:T(8,128)(2,1)S(1)} %get-tuple-element.175), channel_id=1, source_target_pairs={{0,4},{1,5},{2,6},{3,7},{4,0},{5,1},{6,2},{7,3},{8,12},{9,13},{10,... | collective-permute-start | bytes 983048 | tf_op jit(solution)/shard_map/ppermute | solution.py:106
  471.6 31.5 %collective-permute-start.35 = (bf16[3,2,80,960]{3,2,0,1:T(8,128)(2,1)S(1)}, bf16[3,2,80,960]{3,2,0,1:T(8,128)(2,1)S(1)}, u32[]{:S(2)}, u32[]{:S(2)}) collective-permute-start(bf16[3,2,80,960]{3,2,0,1:T(8,128)(2,1)S(1)} %get-tuple-element.135), channel_id=1, source_target_pairs={{0,2},{1,3},{2,0},{3,1},{4,6},{5,7},{6,4},{7,5},{8,10},{9,11},{10,... | collective-permute-start | bytes 2764808 | tf_op jit(solution)/shard_map/ppermute | solution.py:106
  496.5 70.2 %collective-permute-start.38 = (bf16[3,2,80,960]{3,2,0,1:T(8,128)(2,1)S(1)}, bf16[3,2,80,960]{3,2,0,1:T(8,128)(2,1)S(1)}, u32[]{:S(2)}, u32[]{:S(2)}) collective-permute-start(bf16[3,2,80,960]{3,2,0,1:T(8,128)(2,1)S(1)} %get-tuple-element.141), channel_id=1, source_target_pairs={{0,4},{1,5},{2,6},{3,7},{4,0},{5,1},{6,2},{7,3},{8,12},{9,13},{10,... | collective-permute-start | bytes 2764808 | tf_op jit(solution)/shard_map/ppermute | solution.py:106
  497.6 69.6 %collective-permute-start.27 = (bf16[5,2,128,128]{3,2,1,0:T(8,128)(2,1)S(1)}, bf16[5,2,128,128]{3,2,1,0:T(8,128)(2,1)S(1)}, u32[]{:S(2)}, u32[]{:S(2)}) collective-permute-start(bf16[5,2,128,128]{3,2,1,0:T(8,128)(2,1)S(1)} %get-tuple-element.176), channel_id=1, source_target_pairs={{0,2},{1,3},{2,0},{3,1},{4,6},{5,7},{6,4},{7,5},{8,10},{9,11},{10,... | collective-permute-start | bytes 983048 | tf_op jit(solution)/shard_map/ppermute | solution.py:106
  499.1 68.1 %collective-permute-start.29 = (bf16[5,2,128,128]{3,2,1,0:T(8,128)(2,1)S(1)}, bf16[5,2,128,128]{3,2,1,0:T(8,128)(2,1)S(1)}, u32[]{:S(2)}, u32[]{:S(2)}) collective-permute-start(bf16[5,2,128,128]{3,2,1,0:T(8,128)(2,1)S(1)} %get-tuple-element.177), channel_id=1, source_target_pairs={{0,6},{1,7},{2,4},{3,5},{4,2},{5,3},{6,0},{7,1},{8,14},{9,15},{10,... | collective-permute-start | bytes 983048 | tf_op jit(solution)/shard_map/ppermute | solution.py:106
  501.5 79.2 %collective-permute-start.28 = (bf16[5,2,128,128]{3,2,1,0:T(8,128)(2,1)S(1)}, bf16[5,2,128,128]{3,2,1,0:T(8,128)(2,1)S(1)}, u32[]{:S(2)}, u32[]{:S(2)}) collective-permute-start(bf16[5,2,128,128]{3,2,1,0:T(8,128)(2,1)S(1)} %get-tuple-element.178), channel_id=1, source_target_pairs={{0,4},{1,5},{2,6},{3,7},{4,0},{5,1},{6,2},{7,3},{8,12},{9,13},{10,... | collective-permute-start | bytes 983048 | tf_op jit(solution)/shard_map/ppermute | solution.py:106
  503.3 87.7 %collective-permute-start.36 = (bf16[3,80,960]{2,1,0:T(8,128)(2,1)S(1)}, bf16[3,80,960]{2,1,0:T(8,128)(2,1)S(1)}, u32[]{:S(2)}, u32[]{:S(2)}) collective-permute-start(bf16[3,80,960]{2,1,0:T(8,128)(2,1)S(1)} %fusion.26), channel_id=1, source_target_pairs={{0,4},{1,5},{2,6},{3,7},{4,0},{5,1},{6,2},{7,3},{8,12},{9,13},{10,... | collective-permute-start | bytes 1382408 | tf_op jit(solution)/shard_map/ppermute | solution.py:106
  566.8 24.4 %collective-permute-start.39 = (bf16[3,80,960]{2,1,0:T(8,128)(2,1)S(1)}, bf16[3,80,960]{2,1,0:T(8,128)(2,1)S(1)}, u32[]{:S(2)}, u32[]{:S(2)}) collective-permute-start(bf16[3,80,960]{2,1,0:T(8,128)(2,1)S(1)} %fusion.28), channel_id=1, source_target_pairs={{0,1},{1,0},{2,3},{3,2},{4,5},{5,4},{6,7},{7,6},{8,9},{9,8},{10,11... | collective-permute-start | bytes 1382408 | tf_op jit(solution)/shard_map/ppermute | solution.py:106
  614.2 17.2 %collective-permute-start.41 = (bf16[336,960]{1,0:T(8,128)(2,1)S(1)}, bf16[336,960]{1,0:T(8,128)(2,1)S(1)}, u32[]{:S(2)}, u32[]{:S(2)}) collective-permute-start(bf16[336,960]{1,0:T(8,128)(2,1)S(1)} %pad_maximum_fusion.13), channel_id=1, source_target_pairs={{0,1},{1,0},{2,3},{3,2},{4,5},{5,4},{6,7},{7,6},{8,9},{9,8},{10,11... | collective-permute-start | bytes 1935368 | tf_op jit(solution)/shard_map/ppermute | solution.py:106
  659.9 17.7 %collective-permute-start.47 = (bf16[336,960]{1,0:T(8,128)(2,1)}, bf16[336,960]{1,0:T(8,128)(2,1)}, u32[]{:S(2)}, u32[]{:S(2)}) collective-permute-start(bf16[336,960]{1,0:T(8,128)(2,1)} %pad_maximum_fusion.12), channel_id=1, source_target_pairs={{0,16},{16,0},{1,17},{17,1},{2,18},{18,2},{3,19},{19,3},{4,20},{20... | collective-permute-start | bytes 1935368 | tf_op jit(solution)/shard_map/ppermute | solution.py:106
  (100 other events, 1169.8 us)

commit v5 on v4

--- a/solution.py
+++ b/solution.py
@@ -246,7 +246,8 @@
 
 
 def splits_rows(rows):
-    return lax.axis_size("x") == 2 and rows % 32 == 0
+    along_x, along_y, along_z = bit_groups()
+    return (len(along_x), len(along_y), len(along_z)) == (1, 1, 2) and rows % 64 == 0
 
 
 def spread(values, order):
@@ -270,24 +271,47 @@
     return [(0, first), (first, rows)]
 
 
-def step_ctx(held, come, left, where):
-    dim = 1 + left.index(where[1])
-    rest = [bit for bit in left if bit != where[1]]
-    pick = lambda values, side: lax.index_in_dim(values, side, dim, False)
-    sent = add_low(pick(held, 1), pick(come, 1))
-    return add_low(pick(held, 0), pick(come, 0)), sent, rest
+def slot_bits():
+    along_x, along_y, along_z = bit_groups()
+    return list(reversed(along_z)) + along_y
+
+
+def total_low(*terms):
+    total = terms[0].astype(jnp.float32)
+    for term in terms[1:]:
+        total = total + term.astype(jnp.float32)
+    return total.astype(jnp.bfloat16)
 
 
 def reduce_start(keep, away):
-    arrived = swap(away, ("core", 0))
-    states = []
-    for (low, high), order in zip(row_cuts(keep.shape[2]), ctx_orders()):
-        shape = (keep.shape[0],) + (2,) * len(order) + (high - low, keep.shape[3])
-        held = keep[:, :, low:high].reshape(shape)
-        come = arrived[:, :, low:high].reshape(shape)
-        left = list(reversed(range(len(order))))
-        states.append(step_ctx(held, come, left, order[0]))
-    return states
+    come = swap(away, ("core", 0))
+    quarter = keep.shape[2] // 2
+    near, far = slice(0, quarter), slice(quarter, 2 * quarter)
+    sends = [
+        add_low(keep[:, 4:, far], come[:, 4:, far]),
+        add_low(keep[:, :4, far], come[:, :4, far]),
+    ]
+    return sends, (keep[:, :, near], come[:, :, near])
+
+
+def reduce_y(held, x_upper, ride=None):
+    upper = [part[:, 4:] for part in held] + [x_upper]
+    return swap_with(total_low(*upper), ride, slot_bits()[2])
+
+
+def reduce_near(rest, ride=None):
+    return swap_with(total_low(*[part[:, 2:] for part in rest]), ride, slot_bits()[1])
+
+
+def reduce_far(rest, ride=None):
+    return swap_with(total_low(*[part[:, 1] for part in rest]), ride, slot_bits()[0])
+
+
+def reduce_end(rest, z_far):
+    total = z_far.astype(jnp.float32)
+    for part in rest:
+        total = total + part[:, 0].astype(jnp.float32)
+    return total
 
 
 def ride_parts(ride):
@@ -301,6 +325,8 @@
 
 
 def swap_with(sent, ride, where):
+    if ride is None:
+        return swap(sent, where), None
     parts = ride_parts(ride)
     come, other = off_ride(swap(with_ride(sent, parts), where), sent.shape)
     return come, (parts[0] + parts[1]) + other
@@ -309,20 +335,6 @@
 def off_ride(come, shape):
     parts = come[-16:].astype(jnp.float32)
     return come[:-16].reshape(shape), parts[0:2] + parts[2:4]
-
-
-def reduce_finish(states, ride=None):
-    sums = []
-    for member, ((held, sent, left), order) in enumerate(zip(states, ctx_orders())):
-        for position, where in enumerate(order):
-            if ride is not None and member == 0:
-                come, ride = swap_with(sent, ride, where)
-            else:
-                come = swap(sent, where)
-            if position + 1 < len(order):
-                held, sent, left = step_ctx(held, come, left, order[position + 1])
-        sums.append(add_low(held, come))
-    return jnp.concatenate(sums, axis=1), ride
 
 
 def gather_halves(weights):
@@ -337,7 +349,8 @@
     come = swap(jnp.where(core == 0, both[:, half:], both[:, :half]), ("core", 0))
     first = jnp.where(core == 0, keep, come)
     second = jnp.where(core == 0, come, keep)
-    return first[0], jnp.stack([second[0], first[1], second[1]])
+    feed = jnp.stack([second[0], first[1], second[1]])
+    return first[0], jnp.where(x_index == 0, feed[:, : half // 2], feed[:, half // 2 :])
 
 
 def place_rows(own, far):
@@ -511,13 +524,12 @@
             d_value = matmul_t(probs.astype(jnp.bfloat16), d_out).astype(jnp.bfloat16)
             if aligned:
                 length = key_refs[0].shape[1] // 2
-                near = pair_refs[0].shape[0]
+                places_out = [(ref, slot) for ref in pair_refs for slot in range(ref.shape[0])]
                 for piece in range(KEY_TILE // length):
-                    slot = tile * (KEY_TILE // length) + piece
-                    ref = pair_refs[slot // near]
+                    ref, slot = places_out[tile * (KEY_TILE // length) + piece]
                     rows = slice(piece * length, (piece + 1) * length)
-                    ref[slot % near, 0, side, :, :HD] = d_key[rows]
-                    ref[slot % near, 0, side, :, HD:] = d_value[rows]
+                    ref[slot, 0, side, :, :HD] = d_key[rows]
+                    ref[slot, 0, side, :, HD:] = d_value[rows]
             else:
                 rows = slice(tile * KEY_TILE, (tile + 1) * KEY_TILE)
                 pair_refs[0][side, 0, rows, :HD] = d_key
@@ -538,7 +550,8 @@
     store_packed(d_queries_ref, (turned_back * SCALE_QK).astype(jnp.bfloat16), aligned)
 
 
-def head_specs(count, aligned, cols, keys, local_rows, seq):
+def head_specs(leads, aligned, cols, keys, local_rows, seq):
+    count = len(leads)
     if aligned:
         packed = pl.BlockSpec((GROUP * HD, local_rows), lambda head: (head, seq))
     else:
@@ -548,15 +561,22 @@
         pl.BlockSpec((2, keys, 1), lambda head: (0, 0, 0)),
         pl.BlockSpec((1, cols), lambda head: (0, 0)),
     ]
-    specs += [pl.BlockSpec((HD, 2 * keys // count), lambda head: (head, seq))] * count
-    specs += [pl.BlockSpec((HD, 2 * keys // count), lambda head: (KV + head, seq))] * count
+    for first in (0, KV):
+        specs += [
+            pl.BlockSpec(
+                (None, HD, 2 * keys // count),
+                lambda head, lead=lead, first=first: (lead, first + head, seq),
+            )
+            for lead in leads
+        ]
     return packed, specs
 
 
 def attend(queries, pairs, key_pos, query_pos, local_rows, seq):
     aligned = queries.ndim == 2
     cols, keys, count = query_pos.shape[1], key_pos.shape[1], len(pairs)
-    _, specs = head_specs(count, aligned, cols, keys, local_rows, seq)
+    leads, arrays = [lead for _, lead in pairs], [array for array, _ in pairs]
+    _, specs = head_specs(leads, aligned, cols, keys, local_rows, seq)
     work = HEADS * keys * cols // GROUP * 3 // 2
     if aligned:
         out_spec = pl.BlockSpec((GROUP * HD, local_rows), lambda head: (head, 0))
@@ -575,26 +595,28 @@
             flops=work * HD, bytes_accessed=1024 * 1024, transcendentals=0
         ),
         compiler_params=pltpu.CompilerParams(vmem_limit_bytes=VMEM_BYTES),
-    )(queries, key_pos, query_pos, *pairs, *pairs)
+    )(queries, key_pos, query_pos, *arrays, *arrays)
 
 
 def attend_back(
-    queries, pairs, key_pos, query_pos, mixed, log_total, d_mixed, tables, local_rows, seq, near
+    queries, pairs, key_pos, query_pos, mixed, log_total, d_mixed, tables, local_rows, seq, sets
 ):
     aligned = queries.ndim == 2
     cols, keys, count = query_pos.shape[1], key_pos.shape[1], len(pairs)
-    packed, specs = head_specs(count, aligned, cols, keys, local_rows, seq)
+    leads, arrays = [lead for _, lead in pairs], [array for array, _ in pairs]
+    packed, specs = head_specs(leads, aligned, cols, keys, local_rows, seq)
     work = HEADS * keys * cols // GROUP * 3 // 2
     if aligned:
         own = pl.BlockSpec((GROUP * HD, local_rows), lambda head: (head, 0))
         own_shape = jax.ShapeDtypeStruct((HEADS * HD, local_rows), jnp.bfloat16)
         length = keys // count
         pair_specs = [
-            pl.BlockSpec((near, 1, 2, length, 2 * HD), lambda head: (0, head, 0, 0, 0))
-        ] * (count // near)
-        pair_shapes = [jax.ShapeDtypeStruct((near, KV, 2, length, 2 * HD), jnp.bfloat16)] * (
-            count // near
-        )
+            pl.BlockSpec((slots, 1, 2, length, 2 * HD), lambda head: (0, head, 0, 0, 0))
+            for slots in sets
+        ]
+        pair_shapes = [
+            jax.ShapeDtypeStruct((slots, KV, 2, length, 2 * HD), jnp.bfloat16) for slots in sets
+        ]
     else:
         own = pl.BlockSpec((1, 1, HD, cols), lambda head: (0, head, 0, 0))
         own_shape = jax.ShapeDtypeStruct((1, KV, HD, cols), jnp.bfloat16)
@@ -618,17 +640,21 @@
             flops=work * HD, bytes_accessed=1024 * 1024, transcendentals=0
         ),
         compiler_params=pltpu.CompilerParams(vmem_limit_bytes=VMEM_BYTES),
-    )(queries, key_pos, query_pos, *pairs, *pairs, mixed, log_total, d_mixed, *tables)
-
-
-def put_rows(values, keep_ref, away_ref, member, core):
-    half = values.shape[0] // 2
-    for mine, low, far in ((0, 0, half), (1, half, 0)):
-
-        @pl.when(core == mine)
-        def _(low=low, far=far):
-            keep_ref[member, 0] = values[low : low + half]
-            away_ref[member, 0] = values[far : far + half]
+    )(queries, key_pos, query_pos, *arrays, *arrays, mixed, log_total, d_mixed, *tables)
+
+
+def put_rows(values, keep_ref, away_ref, member, core, x_index):
+    quarter = values.shape[0] // 4
+    for mine in range(4):
+
+        @pl.when(2 * core + x_index == mine)
+        def _(mine=mine):
+            for ref, side in ((keep_ref, mine // 2), (away_ref, 1 - mine // 2)):
+                for place, along_x in enumerate((mine % 2, 1 - mine % 2)):
+                    start = (2 * side + along_x) * quarter
+                    ref[member, 0, place * quarter : (place + 1) * quarter] = values[
+                        start : start + quarter
+                    ]
 
 
 def feed_body(
@@ -640,7 +666,7 @@
         refs[count : count + 2],
         refs[count + 2 :],
     )
-    core = me_ref[0]
+    core, x_index = me_ref[0], me_ref[1]
     step = pl.program_id(0)
 
     @pl.when(step == 0)
@@ -650,11 +676,14 @@
 
     def rows_of(member):
         if split:
-            own = jnp.concatenate([weight_refs[0][0, member], weight_refs[1][0, member]], axis=0)
-            far = jnp.concatenate([weight_refs[2][0, member], weight_refs[3][0, member]], axis=0)
-            return jnp.concatenate(
-                [jnp.where(core == 0, own, far), jnp.where(core == 0, far, own)], axis=0
-            )
+            parts_here = [ref[0, member] for ref in weight_refs]
+            rows_out = []
+            for side in range(2):
+                for along_x in range(2):
+                    near = jnp.where(x_index == along_x, parts_here[0], parts_here[1])
+                    far = jnp.where(x_index == along_x, parts_here[2], parts_here[3])
+                    rows_out.append(jnp.where(core == side, near, far))
+            return jnp.concatenate(rows_out, axis=0)
         wanted = feed_core(member, step, parts)
         return jnp.where(wanted == core, weight_refs[2 * member][0], weight_refs[2 * member + 1][0])
 
@@ -673,7 +702,7 @@
     for member, (left, right) in enumerate(((d_gate, a_two), (d_up, a_two), (hidden, dy_low))):
         grad = matmul_n(left, right).astype(jnp.bfloat16)
         if split:
-            put_rows(grad, grad_refs[0], grad_refs[1], member, core)
+            put_rows(grad, grad_refs[0], grad_refs[1], member, core, x_index)
         else:
             grad_refs[member][0] = grad
 
@@ -702,14 +731,9 @@
         return pl.BlockSpec((1, rows, width), index)
 
     if split:
-        tables = [rel_offsets(list(reversed(order))) for order in ctx_orders()]
         weight_specs = [
-            pl.BlockSpec(
-                (1, 3, part.shape[2], width),
-                lambda step, me_ref, table=table: (find(step, table), 0, 0, 0),
-            )
-            for part, table in zip(mine, tables)
-        ] * 2
+            pl.BlockSpec((1, 3, rows // 4, width), lambda step, me_ref: (step, 0, 0, 0))
+        ] * 4
         weight_args = [*mine, *far]
         half = pl.BlockSpec((3, 1, rows // 2, width), lambda step, me_ref: (0, step, 0, 0))
         grad_specs = [half, half]
@@ -719,7 +743,7 @@
         weight_args = [mine, far] * 3
         grad_specs = [pl.BlockSpec((1, rows, width), lambda step, me_ref: (step, 0, 0))] * 3
         grad_shapes = [jax.ShapeDtypeStruct((blocks, rows, width), jnp.bfloat16)] * 3
-    me = jnp.stack([lax.axis_index("core"), lax.axis_index("ctx")]).astype(jnp.int32)
+    me = jnp.stack([lax.axis_index("core"), lax.axis_index("x")]).astype(jnp.int32)
     return pl.pallas_call(
         lambda *refs: feed_body(parts, split, *refs),
         grid_spec=pltpu.PrefetchScalarGridSpec(
@@ -748,21 +772,22 @@
         right = jnp.where(first, one_ref[...], resid_ref[...])
         grad = matmul_n(left, right).astype(jnp.bfloat16)
         if split:
-            put_rows(grad, grad_refs[0], grad_refs[1], 0, me_ref[0])
+            put_rows(grad, grad_refs[0], grad_refs[1], 0, me_ref[0], me_ref[2])
         else:
             grad_refs[0][0] = grad
 
     whole = pl.BlockSpec((tokens, width), lambda step, me_ref: (0, 0))
     if split:
+        table = rel_offsets(slot_bits())
         half = pl.BlockSpec(
-            (1, 1, rows // 2, width), lambda step, me_ref: (0, step ^ me_ref[1], 0, 0)
+            (1, 1, rows // 2, width), lambda step, me_ref: (0, find(step ^ me_ref[1], table), 0, 0)
         )
         grad_specs = [half, half]
         grad_shapes = [jax.ShapeDtypeStruct((1, blocks, rows // 2, width), jnp.bfloat16)] * 2
     else:
         grad_specs = [pl.BlockSpec((1, rows, width), lambda step, me_ref: (step, 0, 0))]
         grad_shapes = [jax.ShapeDtypeStruct((blocks, rows, width), jnp.bfloat16)]
-    me = jnp.stack([lax.axis_index("core"), lax.axis_index("ctx")]).astype(jnp.int32)
+    me = jnp.stack([lax.axis_index(name) for name in ("core", "ctx", "x")]).astype(jnp.int32)
     return pl.pallas_call(
         body,
         grid_spec=pltpu.PrefetchScalarGridSpec(
@@ -804,10 +829,9 @@
     q_cols = HEADS * HD
     kv_cols = KV * HD
     cut_o = q_cols + 2 * kv_cols
-    along_y, along_z = bit_groups()[1:]
-    y_count, z_count = 1 << len(along_y), 1 << len(along_z)
-    slot_offsets = [z * y_count + y for y in range(y_count) for z in range(z_count)]
-    aligned = half_rows % 128 == 0
+    split = splits_rows(weight_rows)
+    slots = slot_bits()
+    aligned = split and half_rows % 128 == 0
     local_index = jnp.arange(local_rows, dtype=jnp.int32)
     pos_here = places(ctx_index * local_rows + local_index, local_rows, ctx_count)
     cosine, sine_part = angle_tables(pos_here, 1.0)
@@ -838,7 +862,7 @@
             row.reshape(rows, 2, 1, half_rows), (rows, 2, GROUP, half_rows)
         ).reshape(rows, 2 * GROUP * half_rows)
 
-    owners = ctx_index ^ jnp.asarray(slot_offsets, jnp.int32)
+    owners = ctx_index ^ jnp.asarray(rel_offsets(slots), jnp.int32)
     inner = jnp.arange(half_rows, dtype=jnp.int32)
     key_pos = jnp.stack(
         [
@@ -849,17 +873,15 @@
     query_pos = by_columns(pos_here[None, :])
     packed_tables = (by_columns(cosine), by_columns(sine_part))
 
-    split = splits_rows(weight_rows)
     if split:
-        first_half, feed_half = gather_halves(weights)
+        first_half, feed_quarter = gather_halves(weights)
         cuts = row_cuts(weight_rows // 2)
         backward = [list(reversed(order)) for order in ctx_orders()]
         first_own = [spread(first_half[low:high], order) for (low, high), order in zip(cuts, backward)]
         first_far = [swap(part, ("core", 0)) for part in first_own]
-        feed_half, first_own = lax.optimization_barrier((feed_half, first_own))
-        mine = [feed_half[None, :, low:high] for low, high in cuts]
-        mine = [double(part, order[0]) for part, order in zip(mine, backward)]
         first_rows = place_rows(first_own, first_far)
+        feed_quarter, first_rows = lax.optimization_barrier((feed_quarter, first_rows))
+        feed_own = double(feed_quarter[None], slots[0])
     else:
         mine = lax.all_gather(weights, ("x", "ctx"), axis=0, tiled=True)
         mine = mine.reshape(x_count * ctx_count, weight_rows, model_width)
@@ -882,28 +904,51 @@
         axis=0,
     )
     if split:
-        joined, mine = lax.optimization_barrier((joined, mine))
-        for position in range(1, len(backward[0])):
-            mine = [double(part, order[position]) for part, order in zip(mine, backward)]
-    near = [joined] + [swap_by(joined, "ctx", z * y_count) for z in range(1, z_count)]
-    pairs = list(near)
-    for y in range(1, y_count):
-        pairs += [swap_by(part, "ctx", y) for part in near]
-    if not aligned:
+        joined, feed_own = lax.optimization_barrier((joined, feed_own))
+    if aligned:
+        far_z, y_own = swap(joined, slots[0]), swap(joined, slots[2])
+    if split:
+        feed_near, feed_y = swap(feed_own, slots[1]), swap(feed_own, slots[2])
+        feed_x = swap(feed_own, ("x", 0))
+    if aligned:
+        far_z, y_own, feed_near, feed_y, feed_x = lax.optimization_barrier(
+            (far_z, y_own, feed_near, feed_y, feed_x)
+        )
+        near_z = swap(jnp.stack([joined, far_z]), slots[1])
+        y_far = swap(far_z, slots[2])
+    if split:
+        feed_near_y = swap(feed_near, slots[2])
+        x_parts = [feed_x, swap(feed_near, ("x", 0)), swap(feed_y, ("x", 0))]
+    if aligned:
+        near_z, y_far, feed_near_y, x_parts = lax.optimization_barrier(
+            (near_z, y_far, feed_near_y, x_parts)
+        )
+        y_near = swap(near_z, slots[2])
+        pairs = [(joined[None], 0), (far_z[None], 0), (near_z, 0), (near_z, 1)]
+        pairs += [(y_own[None], 0), (y_far[None], 0), (y_near, 0), (y_near, 1)]
+    else:
+        pairs = spread(joined, slots).reshape(ctx_count, 2 * kv_cols, seqs, 2, half_rows)
         pairs = [
-            jnp.stack(pairs)
-            .reshape(ctx_count, 2 * kv_cols, seqs, 2, half_rows)
-            .transpose(1, 2, 3, 0, 4)
-            .reshape(2 * kv_cols, seqs * 2 * ctx_count * half_rows)
+            (
+                pairs.transpose(1, 2, 3, 0, 4).reshape(
+                    1, 2 * kv_cols, seqs * 2 * ctx_count * half_rows
+                ),
+                0,
+            )
         ]
+    if split:
+        x_parts.append(swap(feed_near_y, ("x", 0)))
+        feed_own = jnp.concatenate([feed_own, feed_near, feed_y, feed_near_y], axis=0)
+        feed_far = swap(feed_own, ("core", 0))
     q_rot = rotate(matmul_t(qkv_rows[:q_cols], a_one), turn).astype(jnp.bfloat16)
     queries = pack((q_rot * SCALE_QK).astype(jnp.bfloat16))
     attended = []
     for seq in range(seqs):
         attended.append(attend(queries, pairs, key_pos, query_pos, local_rows, seq))
         if split and seq == 0:
-            attended, mine = lax.optimization_barrier((attended, mine))
-            far = [swap(part, ("core", 0)) for part in mine]
+            attended, x_parts, feed_far = lax.optimization_barrier((attended, x_parts, feed_far))
+            feed_x = jnp.concatenate(x_parts, axis=0)
+            mine, far = [feed_own, feed_x], [feed_far, swap(feed_x, ("core", 0))]
     attn_low = jnp.concatenate([unpack(mixed) for mixed, _ in attended], axis=1)
     resid = tokens_in + matmul_c(attn_low, o_rows)
     a_two = (normalize(resid) * gains[1]).astype(jnp.bfloat16)
@@ -914,37 +959,40 @@
     d_resid_low = d_resid.astype(jnp.bfloat16)
     d_attn = pack(matmul_t(o_rows, d_resid_low).astype(jnp.bfloat16))
     if split:
-        feed_states = reduce_start(*feed_grads)
-        feed_states = [list(state) for state in feed_states]
-        d_attn, sends = lax.optimization_barrier((d_attn, [state[1] for state in feed_states]))
-        for state, sent in zip(feed_states, sends):
-            state[1] = sent
-        feed_sums, _ = reduce_finish(feed_states)
+        sends, feed_held = reduce_start(*feed_grads)
+        d_attn, sends = lax.optimization_barrier((d_attn, sends))
+        feed_upper, feed_lower = swap(sends[0], ("x", 0)), swap(sends[1], ("x", 0))
     d_q, d_pair = [], []
     for seq in range(seqs):
         mixed, log_total = attended[seq]
         d_queries, *d_slots = attend_back(
             queries, pairs, key_pos, query_pos, mixed, log_total, d_attn, packed_tables,
-            local_rows, seq, z_count,
+            local_rows, seq, (2, 2, 4),
         )
+        if split and seq == seqs - 1:
+            d_slots, feed_upper, feed_lower = lax.optimization_barrier(
+                (d_slots, feed_upper, feed_lower)
+            )
+            feed_y, _ = reduce_y(feed_held, feed_upper)
         d_q.append(unpack(d_queries))
-        if not aligned:
-            d_slots = (
+        if aligned:
+            lower, near_part, upper = d_slots
+            y_come = swap(upper, slots[2])
+            near_come = swap(add_low(near_part, y_come[2:]), slots[1])
+            if seq == seqs - 1:
+                near_come, feed_y = lax.optimization_barrier((near_come, feed_y))
+            far_come = swap(total_low(lower[1], y_come[1], near_come[1]), slots[0])
+            total = far_come.astype(jnp.float32)
+            for part in (lower, y_come, near_come):
+                total = total + part[0].astype(jnp.float32)
+        else:
+            total = collect(
                 d_slots[0]
                 .reshape(2, KV, ctx_count, half_rows, 2 * HD)
-                .transpose(2, 1, 0, 3, 4)
-                .reshape(y_count, z_count, KV, 2, half_rows, 2 * HD)
+                .transpose(2, 1, 0, 3, 4),
+                list(reversed(slots)),
             )
-            d_slots = [d_slots[y] for y in range(y_count)]
-        line = d_slots[0].astype(jnp.float32)
-        for y in range(1, y_count):
-            line = line + swap_by(d_slots[y], "ctx", y).astype(jnp.float32)
-        total = line[0]
-        for z in range(1, z_count):
-            total = total + swap_by(line[z].astype(jnp.bfloat16), "ctx", z * y_count).astype(jnp.float32)
         d_pair.append(total)
-    if split:
-        d_pair, feed_sums = lax.optimization_barrier((d_pair, feed_sums))
     d_own = jnp.stack(d_pair).transpose(1, 4, 0, 2, 3).reshape(KV, 2 * HD, tokens)
     d_qkv = jnp.concatenate(
         [
@@ -955,17 +1003,37 @@
         axis=0,
     )
     first_terms = first_grads(d_qkv, attn_low, a_one, d_resid_low, weight_rows)
+    if split:
+        feed_rest = [part[:, :4] for part in feed_held] + [feed_lower, feed_y]
+        feed_near, _ = reduce_near(feed_rest)
+        first_terms, feed_near = lax.optimization_barrier((first_terms, feed_near))
+        feed_rest = [part[:, :2] for part in feed_rest] + [feed_near]
+        feed_far, _ = reduce_far(feed_rest)
     d_one = matmul_c(d_qkv, qkv_rows)
     d_norm_one, d_gain_one = norm_back(tokens_in, d_one, gains[0])
     d_tokens = d_resid + d_norm_one
     gain_grad = jnp.stack([d_gain_one, d_gain_two], axis=0)
     if split:
-        first_sums, gain_grad = reduce_finish(reduce_start(*first_terms), gain_grad)
+        sends, first_held = reduce_start(*first_terms)
+        first_upper = swap(sends[0], ("x", 0))
+        first_lower, gain_grad = swap_with(sends[1], gain_grad, ("x", 0))
+        first_upper, feed_far = lax.optimization_barrier((first_upper, feed_far))
+        feed_sums = reduce_end(feed_rest, feed_far)
+        first_y, gain_grad = reduce_y(first_held, first_upper, gain_grad)
+        rest = [part[:, :4] for part in first_held] + [first_lower, first_y]
+        first_near, gain_grad = reduce_near(rest, gain_grad)
+        rest = [part[:, :2] for part in rest] + [first_near]
+        first_far, gain_grad = reduce_far(rest, gain_grad)
+        first_sums = reduce_end(rest, first_far)
         sums = [first_sums[0], feed_sums[0], feed_sums[1], feed_sums[2]]
         own_x = jnp.stack([jnp.where(x_index == 0, sums[c], sums[2 + c]) for c in range(2)])
         other_x = jnp.stack([jnp.where(x_index == 0, sums[2 + c], sums[c]) for c in range(2)])
-        come, gain_grad = swap_with(other_x, gain_grad, ("x", 0))
-        halves = own_x.astype(jnp.float32) + come.astype(jnp.float32)
+        far_x = swap(other_x.astype(jnp.bfloat16), ("x", 0)).astype(jnp.float32)
+        halves = jnp.where(
+            x_index == 0,
+            jnp.concatenate([own_x, far_x], axis=1),
+            jnp.concatenate([far_x, own_x], axis=1),
+        )
         own_half = jnp.where(core == 0, halves[0], halves[1])
         other_half = jnp.where(core == 0, halves[1], halves[0]).astype(jnp.bfloat16)
         come, gain_grad = swap_with(other_half, gain_grad, ("core", 0))

time: 703 us -> 638 us (0.908)
  waiting for transfers between devices: 385 us -> 337 us
  local copies, waits for them, and re-layouts: 60.4 us -> 43.4 us
  other arithmetic: 63.9 us -> 50.3 us
  matrix products: 9.33 us -> 18.7 us
  starting transfers between devices: 44.9 us -> 53 us
    ppermute x49 -> x45, waiting for transfers between devices: 385 us -> 337 us  [swap_by(): return lax.ppermute(values, axis, [(i, i ^ offset) for i in range(size)])]
    slice x15 -> x2, local copies, waits for them, and re-layouts: 20 us -> 0.07 us  [gather_halves(): feed = jnp.stack([second[0], first[1], second[1]])]
    concatenate x12 -> x7, other arithmetic: 15 us -> 1.75 us  [double(): return jnp.concatenate([values, swap(values, where)], axis=0)]
    convert_element_type x0 -> x9, other arithmetic: none -> 12.2 us  [the longest x8 12.2 us: total_low(): return total.astype(jnp.bfloat16)]
    ppermute x49 -> x45, starting transfers between devices: 44.9 us -> 53 us  [swap_by(): return lax.ppermute(values, axis, [(i, i ^ offset) for i in range(size)])]
    convert_element_type x19 -> x4, other arithmetic: 13.3 us -> 5.23 us  [add_low(): (left.astype(jnp.float32) + right.astype(jnp.float32)).astype(jnp.bfloat16)]
    pallas_call x0 -> x1, local copies, waits for them, and re-layouts: none -> 7.69 us  [feed_forward(): pl.pallas_call(lambda *refs: feed_body(parts, split, *refs), grid_spec=pl...]
    unnamed x171 -> x113, local copies, waits for them, and re-layouts: 27.1 us -> 24.8 us
  transfers between devices with their start and end apart: 49 -> 45, of which waited for: 28 -> 28; matrix products, arithmetic and copies ran while one was open for 11% -> 11% of each run, Pallas kernels for 7% -> 12%
where the time goes in v5:
time: 638 us; the launch traced here: 629 us
  waiting for transfers between devices  337 us (53%)
  Pallas kernels  124 us (19%)
  starting transfers between devices  53 us (8%)
  other arithmetic  50.3 us (8%)
  local copies, waits for them, and re-layouts  43.4 us (7%)
  matrix products  18.7 us (3%)
    ppermute x45, waiting for transfers between devices, swap_by(): return lax.ppermute(values, axis, [(i, i ^ offset) for i in range(size)])  337 us
    ppermute x45, starting transfers between devices, swap_by(): return lax.ppermute(values, axis, [(i, i ^ offset) for i in range(size)])  53 us
    pallas_call x2, Pallas kernels, attend_back(): pl.pallas_call(lambda *refs: attend_back_body(count, aligned, *refs), gri...  45.3 us
    pallas_call x1, Pallas kernels, feed_forward(): pl.pallas_call(lambda *refs: feed_body(parts, split, *refs), grid_spec=pl...  42.1 us
    unnamed x113, local copies, waits for them, and re-layouts  24.8 us
    pallas_call x2, Pallas kernels, attend(): pl.pallas_call(lambda *refs: attend_body(count, aligned, *refs), grid=(KV...  24.8 us
  transfers between devices with their start and end apart: 45, of which 28 were waited for; matrix products, arithmetic and copies ran while one was open for 11% of the time, Pallas kernels for 12%

profile of v5, /device:TPU:0, one launch (start us, length us, event | category | flops | bytes accessed | tf_op | source)
XLA Modules:
  0.0 628.6 jit_solution(9185444027829650450)
XLA Ops:
  3.6 14.9 %collective-permute-done = bf16[320,960]{1,0:T(8,128)(2,1)S(1)} collective-permute-done((bf16[320,960]{1,0:T(8,128)(2,1)}, bf16[320,960]{1,0:T(8,128)(2,1)S(1)}, u32[]{:S(2)}, u32[]{:S(2)}) %collective-permute-start) | collective-permute-done | bytes 614432 | tf_op jit(solution)/shard_map/ppermute | solution.py:106
  35.6 7.9 %collective-permute-start.3 = (bf16[2,80,960]{2,1,0:T(8,128)(2,1)S(1)}, bf16[2,80,960]{2,1,0:T(8,128)(2,1)S(1)}, u32[]{:S(2)}, u32[]{:S(2)}) collective-permute-start(bf16[2,80,960]{2,1,0:T(8,128)(2,1)S(1)} %pad_maximum_fusion.17), channel_id=1, source_target_pairs={{0,2},{1,3},{2,0},{3,1},{4,6},{5,7},{6,4},{7,5},{8,10},{9,11},{10,... | collective-permute-start | bytes 921608 | tf_op jit(solution)/shard_map/ppermute | solution.py:106
  43.7 6.9 %collective-permute-done.6 = bf16[2,80,960]{2,1,0:T(8,128)(2,1)S(1)} collective-permute-done((bf16[2,80,960]{2,1,0:T(8,128)(2,1)S(1)}, bf16[2,80,960]{2,1,0:T(8,128)(2,1)S(1)}, u32[]{:S(2)}, u32[]{:S(2)}) %collective-permute-start.6) | collective-permute-done | bytes 307232 | tf_op jit(solution)/shard_map/ppermute | solution.py:106
  50.8 6.8 %collective-permute-done.3 = bf16[2,80,960]{2,1,0:T(8,128)(2,1)S(1)} collective-permute-done((bf16[2,80,960]{2,1,0:T(8,128)(2,1)S(1)}, bf16[2,80,960]{2,1,0:T(8,128)(2,1)S(1)}, u32[]{:S(2)}, u32[]{:S(2)}) %collective-permute-start.3) | collective-permute-done | bytes 307232 | tf_op jit(solution)/shard_map/ppermute | solution.py:106
  58.3 12.9 %collective-permute-done.7 = bf16[4,80,960]{2,1,0:T(8,128)(2,1)S(1)} collective-permute-done((bf16[4,80,960]{2,1,0:T(8,128)(2,1)S(1)}, bf16[4,80,960]{2,1,0:T(8,128)(2,1)S(1)}, u32[]{:S(2)}, u32[]{:S(2)}) %collective-permute-start.7) | collective-permute-done | bytes 614432 | tf_op jit(solution)/shard_map/ppermute | solution.py:106
  88.9 19.9 %collective-permute-done.10 = bf16[1,3,80,960]{3,2,1,0:T(8,128)(2,1)} collective-permute-done((bf16[1,3,80,960]{3,2,1,0:T(8,128)(2,1)}, bf16[1,3,80,960]{3,2,1,0:T(8,128)(2,1)}, u32[]{:S(2)}, u32[]{:S(2)}) %collective-permute-start.10) | collective-permute-done | bytes 460832 | tf_op jit(solution)/shard_map/ppermute | solution.py:106
  116.5 28.5 %collective-permute-done.11 = bf16[640,512]{1,0:T(8,128)(2,1)S(1)} collective-permute-done((bf16[640,512]{1,0:T(8,128)(2,1)S(1)}, bf16[640,512]{1,0:T(8,128)(2,1)S(1)}, u32[]{:S(2)}, u32[]{:S(2)}) %collective-permute-start.11) | collective-permute-done | bytes 655392 | tf_op jit(solution)/shard_map/ppermute | solution.py:106
  157.3 29.7 %collective-permute-done.17 = bf16[640,512]{1,0:T(8,128)(2,1)S(1)} collective-permute-done((bf16[640,512]{1,0:T(8,128)(2,1)S(1)}, bf16[640,512]{1,0:T(8,128)(2,1)S(1)}, u32[]{:S(2)}, u32[]{:S(2)}) %collective-permute-start.17) | collective-permute-done | bytes 655392 | tf_op jit(solution)/shard_map/ppermute | solution.py:106
  187.1 7.2 %collective-permute-done.20 = bf16[2,3,80,960]{3,2,1,0:T(8,128)(2,1)S(1)} collective-permute-done((bf16[2,3,80,960]{3,2,1,0:T(8,128)(2,1)S(1)}, bf16[2,3,80,960]{3,2,1,0:T(8,128)(2,1)S(1)}, u32[]{:S(2)}, u32[]{:S(2)}) %collective-permute-start.20) | collective-permute-done | bytes 921632 | tf_op jit(solution)/shard_map/ppermute | solution.py:106
  205.2 21.9 %collective-permute-done.21.refs_9_.refs_10_.refs_17_.refs_18_ = bf16[2,640,512]{2,1,0:T(8,128)(2,1)} collective-permute-done((bf16[2,640,512]{2,1,0:T(8,128)(2,1)}, bf16[2,640,512]{2,1,0:T(8,128)(2,1)}, u32[]{:S(2)}, u32[]{:S(2)}) %collective-permute-start.21) | collective-permute-done | bytes 1310752 | tf_op jit(solution)/shard_map/ppermute | solution.py:106
  227.1 12.6 %shard_map.153 = (bf16[960,256]{1,0:T(8,128)(2,1)S(1)}, f32[1,5,1,768]{3,2,1,0:T(1,128)S(1)}) custom-call(bf16[960,512]{1,0:T(8,128)(2,1)S(1)} %bitcast.188, s32[2,1024,1]{2,1,0:T(8,128)S(1)} %pad_add_fusion.refs_1_, s32[1,768]{1,0:T(1,128)S(1)} %broadcast_in_dim.19.refs_2_, bf16[1,640,512]{2,1,0:T(8,128)(2,1)S(1)} %bitcast.155, ...), custom_call_target="tpu_custom_call" | custom-call | flops 377487360 | bytes 1048576 | tf_op jit(solution)/shard_map/pallas_call | solution.py:587
  244.6 12.2 %shard_map.154 = (bf16[960,256]{1,0:T(8,128)(2,1)S(1)}, f32[1,5,1,768]{3,2,1,0:T(1,128)S(1)}) custom-call(bf16[960,512]{1,0:T(8,128)(2,1)S(1)} %bitcast.189, s32[2,1024,1]{2,1,0:T(8,128)S(1)} %pad_add_fusion.refs_1_, s32[1,768]{1,0:T(1,128)S(1)} %broadcast_in_dim.19.refs_2_, bf16[1,640,512]{2,1,0:T(8,128)(2,1)S(1)} %bitcast.157, ...), custom_call_target="tpu_custom_call" | custom-call | flops 377487360 | bytes 1048576 | tf_op jit(solution)/shard_map/pallas_call | solution.py:587
  260.6 42.1 %shard_map.155 = (f32[512,960]{1,0:T(8,128)S(1)}, f32[512,960]{1,0:T(8,128)}, bf16[3,8,160,960]{3,2,1,0:T(8,128)(2,1)}, bf16[3,8,160,960]{3,2,1,0:T(8,128)(2,1)}) custom-call(s32[2]{0:T(128)S(1)} %pad_add_fusion.2.refs_0_, bf16[512,960]{1,0:T(8,128)(2,1)S(1)} %multiply_convert_fusion.refs_1_, bf16[512,960]{1,0:T(8,128)(2,1)S(1)} %convert_element_type.406.refs_2_, ...), custom_call_target="tpu_custom_call" | custom-call | flops 22649241600 | bytes 29491200 | tf_op jit(solution)/shard_map/pallas_call | solution.py:747
  302.8 7.7 %copy.94 = bf16[3,8,160,960]{3,2,0,1:T(8,128)(2,1)} copy(bf16[3,8,160,960]{3,2,1,0:T(8,128)(2,1)} %get-tuple-element.95) | data formatting | bytes 14745600 | tf_op jit(solution)/shard_map/pallas_call | solution.py:747
  317.2 4.5 fusion.11.refs_21_
  323.2 4.6 add_convert_fusion.1
  331.8 22.6 %shard_map.156 = (bf16[960,256]{1,0:T(8,128)(2,1)S(1)}, bf16[2,5,2,128,128]{4,3,2,1,0:T(8,128)(2,1)S(1)}, bf16[2,5,2,128,128]{4,3,2,1,0:T(8,128)(2,1)S(1)}, bf16[4,5,2,128,128]{4,3,2,1,0:T(8,128)(2,1)}) custom-call(bf16[960,512]{1,0:T(8,128)(2,1)S(1)} %bitcast.190, s32[2,1024,1]{2,1,0:T(8,128)} %copy-done, s32[1,768]{1,0:T(1,128)S(1)} %broadcast_in_dim.19.refs_2_, ...), custom_call_target="tpu_custom_call" | custom-call | flops 377487360 | bytes 1048576 | tf_op jit(solution)/shard_map/pallas_call | solution.py:626
  356.7 22.7 %shard_map.157 = (bf16[960,256]{1,0:T(8,128)(2,1)S(1)}, bf16[2,5,2,128,128]{4,3,2,1,0:T(8,128)(2,1)S(1)}, bf16[2,5,2,128,128]{4,3,2,1,0:T(8,128)(2,1)S(1)}, bf16[4,5,2,128,128]{4,3,2,1,0:T(8,128)(2,1)}) custom-call(bf16[960,512]{1,0:T(8,128)(2,1)S(1)} %bitcast.191, s32[2,1024,1]{2,1,0:T(8,128)} %copy-done, s32[1,768]{1,0:T(1,128)S(1)} %broadcast_in_dim.19.refs_2_, ...), custom_call_target="tpu_custom_call" | custom-call | flops 377487360 | bytes 1048576 | tf_op jit(solution)/shard_map/pallas_call | solution.py:626
  379.5 35.9 %collective-permute-done.30 = bf16[3,4,80,960]{3,2,0,1:T(8,128)(2,1)} collective-permute-done((bf16[3,4,80,960]{3,2,0,1:T(8,128)(2,1)}, bf16[3,4,80,960]{3,2,0,1:T(8,128)(2,1)}, u32[]{:S(2)}, u32[]{:S(2)}) %collective-permute-start.30) | collective-permute-done | bytes 1843232 | tf_op jit(solution)/shard_map/ppermute | solution.py:106
  422.3 25.0 %collective-permute-done.31 = bf16[4,5,2,128,128]{4,3,2,1,0:T(8,128)(2,1)S(1)} collective-permute-done((bf16[4,5,2,128,128]{4,3,2,1,0:T(8,128)(2,1)}, bf16[4,5,2,128,128]{4,3,2,1,0:T(8,128)(2,1)S(1)}, u32[]{:S(2)}, u32[]{:S(2)}) %collective-permute-start.31) | collective-permute-done | bytes 1310752 | tf_op jit(solution)/shard_map/ppermute | solution.py:106
  450.7 15.6 %collective-permute-done.28 = bf16[5,2,128,128]{3,2,1,0:T(8,128)(2,1)S(1)} collective-permute-done((bf16[5,2,128,128]{3,2,1,0:T(8,128)(2,1)S(1)}, bf16[5,2,128,128]{3,2,1,0:T(8,128)(2,1)S(1)}, u32[]{:S(2)}, u32[]{:S(2)}) %collective-permute-start.28) | collective-permute-done | bytes 327712 | tf_op jit(solution)/shard_map/ppermute | solution.py:106
  466.5 21.5 %collective-permute-done.33 = bf16[3,4,80,960]{3,2,0,1:T(8,128)(2,1)S(1)} collective-permute-done((bf16[3,4,80,960]{3,2,0,1:T(8,128)(2,1)S(1)}, bf16[3,4,80,960]{3,2,0,1:T(8,128)(2,1)S(1)}, u32[]{:S(2)}, u32[]{:S(2)}) %collective-permute-start.33) | collective-permute-done | bytes 1843232 | tf_op jit(solution)/shard_map/ppermute | solution.py:106
  494.6 9.7 %collective-permute-done.34 = bf16[5,2,128,128]{3,2,1,0:T(8,128)(2,1)S(1)} collective-permute-done((bf16[5,2,128,128]{3,2,1,0:T(8,128)(2,1)S(1)}, bf16[5,2,128,128]{3,2,1,0:T(8,128)(2,1)S(1)}, u32[]{:S(2)}, u32[]{:S(2)}) %collective-permute-start.34) | collective-permute-done | bytes 327712 | tf_op jit(solution)/shard_map/ppermute | solution.py:106
  510.4 7.3 %shard_map.158 = (bf16[1,8,160,960]{3,2,1,0:T(8,128)(2,1)}, bf16[1,8,160,960]{3,2,1,0:T(8,128)(2,1)}) custom-call(s32[3]{0:T(128)S(1)} %pad_add_fusion.3.me_ref, bf16[1600,512]{1,0:T(8,128)(2,1)S(1)} %pad_maximum_fusion.qkv_ref, bf16[960,512]{1,0:T(8,128)(2,1)S(1)} %copy-done.13, bf16[512,960]{1,0:T(8,128)(2,1)S(1)} %copy-done.9, bf16[512,960]{1,0:T(8,128)(2,1)S(1)} %copy-done.6), custom_call_target="tpu_custom_call" | custom-call | flops 2516582400 | bytes 4915200 | tf_op jit(solution)/shard_map/pallas_call | solution.py:791
  517.7 4.8 collective-permute-done.35
  529.5 5.5 multiply_reduce_fusion.1
  535.0 13.7 %collective-permute-done.39 = bf16[3,80,960]{2,1,0:T(8,128)(2,1)S(1)} collective-permute-done((bf16[3,80,960]{2,1,0:T(8,128)(2,1)S(1)}, bf16[3,80,960]{2,1,0:T(8,128)(2,1)S(1)}, u32[]{:S(2)}, u32[]{:S(2)}) %collective-permute-start.39) | collective-permute-done | bytes 460832 | tf_op jit(solution)/shard_map/ppermute | solution.py:106
  551.1 15.9 %collective-permute-done.37 = bf16[336,960]{1,0:T(8,128)(2,1)S(1)} collective-permute-done((bf16[336,960]{1,0:T(8,128)(2,1)S(1)}, bf16[336,960]{1,0:T(8,128)(2,1)S(1)}, u32[]{:S(2)}, u32[]{:S(2)}) %collective-permute-start.37) | collective-permute-done | bytes 645152 | tf_op jit(solution)/shard_map/ppermute | solution.py:106
  568.8 15.0 %collective-permute-done.40 = bf16[336,960]{1,0:T(8,128)(2,1)S(1)} collective-permute-done((bf16[336,960]{1,0:T(8,128)(2,1)S(1)}, bf16[336,960]{1,0:T(8,128)(2,1)S(1)}, u32[]{:S(2)}, u32[]{:S(2)}) %collective-permute-start.40) | collective-permute-done | bytes 645152 | tf_op jit(solution)/shard_map/ppermute | solution.py:106
  587.7 6.1 collective-permute-done.41
  600.0 6.1 collective-permute-done.42
  610.2 5.6 collective-permute-done.43
  (304 shorter events, 152.8 us)
Async XLA Ops:
  0.6 17.9 %collective-permute-start = (bf16[320,960]{1,0:T(8,128)(2,1)}, bf16[320,960]{1,0:T(8,128)(2,1)S(1)}, u32[]{:S(2)}, u32[]{:S(2)}) collective-permute-start(bf16[320,960]{1,0:T(8,128)(2,1)} %param.11), channel_id=1, source_target_pairs={{0,16},{16,0},{1,17},{17,1},{2,18},{18,2},{3,19},{19,3},{4,20},{20... | collective-permute-start | bytes 1843208 | tf_op jit(solution)/shard_map/ppermute | solution.py:106
  33.4 17.3 %collective-permute-start.6 = (bf16[2,80,960]{2,1,0:T(8,128)(2,1)S(1)}, bf16[2,80,960]{2,1,0:T(8,128)(2,1)S(1)}, u32[]{:S(2)}, u32[]{:S(2)}) collective-permute-start(bf16[2,80,960]{2,1,0:T(8,128)(2,1)S(1)} %pad_maximum_fusion.18), channel_id=1, source_target_pairs={{0,4},{1,5},{2,6},{3,7},{4,0},{5,1},{6,2},{7,3},{8,12},{9,13},{10,... | collective-permute-start | bytes 921608 | tf_op jit(solution)/shard_map/ppermute | solution.py:106
  35.6 22.0 %collective-permute-start.3 = (bf16[2,80,960]{2,1,0:T(8,128)(2,1)S(1)}, bf16[2,80,960]{2,1,0:T(8,128)(2,1)S(1)}, u32[]{:S(2)}, u32[]{:S(2)}) collective-permute-start(bf16[2,80,960]{2,1,0:T(8,128)(2,1)S(1)} %pad_maximum_fusion.17), channel_id=1, source_target_pairs={{0,2},{1,3},{2,0},{3,1},{4,6},{5,7},{6,4},{7,5},{8,10},{9,11},{10,... | collective-permute-start | bytes 921608 | tf_op jit(solution)/shard_map/ppermute | solution.py:106
  50.7 20.5 %collective-permute-start.7 = (bf16[4,80,960]{2,1,0:T(8,128)(2,1)S(1)}, bf16[4,80,960]{2,1,0:T(8,128)(2,1)S(1)}, u32[]{:S(2)}, u32[]{:S(2)}) collective-permute-start(bf16[4,80,960]{2,1,0:T(8,128)(2,1)S(1)} %pad_maximum_fusion.11), channel_id=1, source_target_pairs={{0,2},{1,3},{2,0},{3,1},{4,6},{5,7},{6,4},{7,5},{8,10},{9,11},{10,... | collective-permute-start | bytes 1843208 | tf_op jit(solution)/shard_map/ppermute | solution.py:106
  83.7 25.1 %collective-permute-start.10 = (bf16[1,3,80,960]{3,2,1,0:T(8,128)(2,1)}, bf16[1,3,80,960]{3,2,1,0:T(8,128)(2,1)}, u32[]{:S(2)}, u32[]{:S(2)}) collective-permute-start(bf16[1,3,80,960]{3,2,1,0:T(8,128)(2,1)} %bitcast.16), channel_id=1, source_target_pairs={{0,4},{1,5},{2,6},{3,7},{4,0},{5,1},{6,2},{7,3},{8,12},{9,13},{10,... | collective-permute-start | bytes 1382408 | tf_op jit(solution)/shard_map/ppermute | solution.py:106
  110.1 37.2 %collective-permute-start.13 = (bf16[2,3,80,960]{3,2,1,0:T(8,128)(2,1)S(1)}, bf16[2,3,80,960]{3,2,1,0:T(8,128)(2,1)S(1)}, u32[]{:S(2)}, u32[]{:S(2)}) collective-permute-start(bf16[2,3,80,960]{3,2,1,0:T(8,128)(2,1)S(1)} %pad_maximum_fusion.6), channel_id=1, source_target_pairs={{0,2},{1,3},{2,0},{3,1},{4,6},{5,7},{6,4},{7,5},{8,10},{9,11},{10,... | collective-permute-start | bytes 2764808 | tf_op jit(solution)/shard_map/ppermute | solution.py:106
  110.1 37.2 %collective-permute-start.14 = (bf16[2,3,80,960]{3,2,1,0:T(8,128)(2,1)S(1)}, bf16[2,3,80,960]{3,2,1,0:T(8,128)(2,1)S(1)}, u32[]{:S(2)}, u32[]{:S(2)}) collective-permute-start(bf16[2,3,80,960]{3,2,1,0:T(8,128)(2,1)S(1)} %pad_maximum_fusion.6), channel_id=1, source_target_pairs={{0,1},{1,0},{2,3},{3,2},{4,5},{5,4},{6,7},{7,6},{8,9},{9,8},{10,11... | collective-permute-start | bytes 2764808 | tf_op jit(solution)/shard_map/ppermute | solution.py:106
  110.7 36.6 %collective-permute-start.15 = (bf16[2,3,80,960]{3,2,1,0:T(8,128)(2,1)S(1)}, bf16[2,3,80,960]{3,2,1,0:T(8,128)(2,1)S(1)}, u32[]{:S(2)}, u32[]{:S(2)}) collective-permute-start(bf16[2,3,80,960]{3,2,1,0:T(8,128)(2,1)S(1)} %pad_maximum_fusion.6), channel_id=1, source_target_pairs={{0,16},{16,0},{1,17},{17,1},{2,18},{18,2},{3,19},{19,3},{4,20},{20... | collective-permute-start | bytes 2764808 | tf_op jit(solution)/shard_map/ppermute | solution.py:106
  112.2 32.8 %collective-permute-start.11 = (bf16[640,512]{1,0:T(8,128)(2,1)S(1)}, bf16[640,512]{1,0:T(8,128)(2,1)S(1)}, u32[]{:S(2)}, u32[]{:S(2)}) collective-permute-start(bf16[640,512]{1,0:T(8,128)(2,1)S(1)} %pad_maximum_fusion.13), channel_id=1, source_target_pairs={{0,4},{1,5},{2,6},{3,7},{4,0},{5,1},{6,2},{7,3},{8,12},{9,13},{10,... | collective-permute-start | bytes 1966088 | tf_op jit(solution)/shard_map/ppermute | solution.py:106
  115.0 32.3 %collective-permute-start.12 = (bf16[640,512]{1,0:T(8,128)(2,1)S(1)}, bf16[640,512]{1,0:T(8,128)(2,1)S(1)}, u32[]{:S(2)}, u32[]{:S(2)}) collective-permute-start(bf16[640,512]{1,0:T(8,128)(2,1)S(1)} %pad_maximum_fusion.13), channel_id=1, source_target_pairs={{0,1},{1,0},{2,3},{3,2},{4,5},{5,4},{6,7},{7,6},{8,9},{9,8},{10,11... | collective-permute-start | bytes 1966088 | tf_op jit(solution)/shard_map/ppermute | solution.py:106
  148.4 45.9 %collective-permute-start.16 = (bf16[2,640,512]{2,1,0:T(8,128)(2,1)S(1)}, bf16[2,640,512]{2,1,0:T(8,128)(2,1)}, u32[]{:S(2)}, u32[]{:S(2)}) collective-permute-start(bf16[2,640,512]{2,1,0:T(8,128)(2,1)S(1)} %pad_maximum_fusion.3), channel_id=1, source_target_pairs={{0,2},{1,3},{2,0},{3,1},{4,6},{5,7},{6,4},{7,5},{8,10},{9,11},{10,... | collective-permute-start | bytes 3932168 | tf_op jit(solution)/shard_map/ppermute | solution.py:106
  150.1 36.9 %collective-permute-start.18 = (bf16[2,3,80,960]{3,2,1,0:T(8,128)(2,1)S(1)}, bf16[2,3,80,960]{3,2,1,0:T(8,128)(2,1)S(1)}, u32[]{:S(2)}, u32[]{:S(2)}) collective-permute-start(bf16[2,3,80,960]{3,2,1,0:T(8,128)(2,1)S(1)} %collective-permute-done.13), channel_id=1, source_target_pairs={{0,1},{1,0},{2,3},{3,2},{4,5},{5,4},{6,7},{7,6},{8,9},{9,8},{10,11... | collective-permute-start | bytes 2764808 | tf_op jit(solution)/shard_map/ppermute | solution.py:106
  150.6 36.4 %collective-permute-start.19 = (bf16[2,3,80,960]{3,2,1,0:T(8,128)(2,1)S(1)}, bf16[2,3,80,960]{3,2,1,0:T(8,128)(2,1)S(1)}, u32[]{:S(2)}, u32[]{:S(2)}) collective-permute-start(bf16[2,3,80,960]{3,2,1,0:T(8,128)(2,1)S(1)} %collective-permute-done.13), channel_id=1, source_target_pairs={{0,16},{16,0},{1,17},{17,1},{2,18},{18,2},{3,19},{19,3},{4,20},{20... | collective-permute-start | bytes 2764808 | tf_op jit(solution)/shard_map/ppermute | solution.py:106
  152.1 42.2 %collective-permute-start.20 = (bf16[2,3,80,960]{3,2,1,0:T(8,128)(2,1)S(1)}, bf16[2,3,80,960]{3,2,1,0:T(8,128)(2,1)S(1)}, u32[]{:S(2)}, u32[]{:S(2)}) collective-permute-start(bf16[2,3,80,960]{3,2,1,0:T(8,128)(2,1)S(1)} %collective-permute-done.14), channel_id=1, source_target_pairs={{0,16},{16,0},{1,17},{17,1},{2,18},{18,2},{3,19},{19,3},{4,20},{20... | collective-permute-start | bytes 2764808 | tf_op jit(solution)/shard_map/ppermute | solution.py:106
  152.7 34.4 %collective-permute-start.17 = (bf16[640,512]{1,0:T(8,128)(2,1)S(1)}, bf16[640,512]{1,0:T(8,128)(2,1)S(1)}, u32[]{:S(2)}, u32[]{:S(2)}) collective-permute-start(bf16[640,512]{1,0:T(8,128)(2,1)S(1)} %collective-permute-done.11), channel_id=1, source_target_pairs={{0,1},{1,0},{2,3},{3,2},{4,5},{5,4},{6,7},{7,6},{8,9},{9,8},{10,11... | collective-permute-start | bytes 1966088 | tf_op jit(solution)/shard_map/ppermute | solution.py:106
  195.6 44.1 %collective-permute-start.23 = (bf16[8,3,80,960]{3,2,1,0:T(8,128)(2,1)}, bf16[8,3,80,960]{3,2,1,0:T(8,128)(2,1)}, u32[]{:S(2)}, u32[]{:S(2)}) collective-permute-start(bf16[8,3,80,960]{3,2,1,0:T(8,128)(2,1)} %constant_dynamic-update-slice_fusion.refs_3_), channel_id=1, source_target_pairs={{0,8},{8,0},{1,9},{9,1},{2,10},{10,2},{3,11},{11,3},{4,12},{12,4},... | collective-permute-start | bytes 11059208 | tf_op jit(solution)/shard_map/ppermute | solution.py:106
  195.6 31.5 %collective-permute-start.21 = (bf16[2,640,512]{2,1,0:T(8,128)(2,1)}, bf16[2,640,512]{2,1,0:T(8,128)(2,1)}, u32[]{:S(2)}, u32[]{:S(2)}) collective-permute-start(bf16[2,640,512]{2,1,0:T(8,128)(2,1)} %collective-permute-done.16.refs_5_.refs_6_.refs_13_.refs_14_), channel_id=1, source_target_pairs={{0,1},{1,0},{2,3},{3,2},{4,5},{5,4},{6,7},{7,6},{8,9},{9,8},{10,11... | collective-permute-start | bytes 3932168 | tf_op jit(solution)/shard_map/ppermute | solution.py:106
  198.7 41.0 %collective-permute-start.22 = (bf16[2,3,80,960]{3,2,1,0:T(8,128)(2,1)}, bf16[2,3,80,960]{3,2,1,0:T(8,128)(2,1)S(1)}, u32[]{:S(2)}, u32[]{:S(2)}) collective-permute-start(bf16[2,3,80,960]{3,2,1,0:T(8,128)(2,1)} %copy-done.41), channel_id=1, source_target_pairs={{0,16},{16,0},{1,17},{17,1},{2,18},{18,2},{3,19},{19,3},{4,20},{20... | collective-permute-start | bytes 2764808 | tf_op jit(solution)/shard_map/ppermute | solution.py:106
  244.4 16.2 %collective-permute-start.24 = (bf16[8,3,80,960]{3,2,1,0:T(8,128)(2,1)}, bf16[8,3,80,960]{3,2,1,0:T(8,128)(2,1)}, u32[]{:S(2)}, u32[]{:S(2)}) collective-permute-start(bf16[8,3,80,960]{3,2,1,0:T(8,128)(2,1)} %constant_dynamic-update-slice_fusion.6.refs_4_), channel_id=1, source_target_pairs={{0,8},{8,0},{1,9},{9,1},{2,10},{10,2},{3,11},{11,3},{4,12},{12,4},... | collective-permute-start | bytes 11059208 | tf_op jit(solution)/shard_map/ppermute | solution.py:106
  327.9 51.6 %collective-permute-start.29 = (bf16[3,4,80,960]{3,2,0,1:T(8,128)(2,1)}, bf16[3,4,80,960]{3,2,0,1:T(8,128)(2,1)}, u32[]{:S(2)}, u32[]{:S(2)}) collective-permute-start(bf16[3,4,80,960]{3,2,0,1:T(8,128)(2,1)} %get-tuple-element.106), channel_id=1, source_target_pairs={{0,16},{16,0},{1,17},{17,1},{2,18},{18,2},{3,19},{19,3},{4,20},{20... | collective-permute-start | bytes 5529608 | tf_op jit(solution)/shard_map/ppermute | solution.py:106
  329.4 86.0 %collective-permute-start.30 = (bf16[3,4,80,960]{3,2,0,1:T(8,128)(2,1)}, bf16[3,4,80,960]{3,2,0,1:T(8,128)(2,1)}, u32[]{:S(2)}, u32[]{:S(2)}) collective-permute-start(bf16[3,4,80,960]{3,2,0,1:T(8,128)(2,1)} %get-tuple-element.107), channel_id=1, source_target_pairs={{0,16},{16,0},{1,17},{17,1},{2,18},{18,2},{3,19},{19,3},{4,20},{20... | collective-permute-start | bytes 5529608 | tf_op jit(solution)/shard_map/ppermute | solution.py:106
  355.2 66.4 %collective-permute-start.26 = (bf16[4,5,2,128,128]{4,3,2,1,0:T(8,128)(2,1)}, bf16[4,5,2,128,128]{4,3,2,1,0:T(8,128)(2,1)S(1)}, u32[]{:S(2)}, u32[]{:S(2)}) collective-permute-start(bf16[4,5,2,128,128]{4,3,2,1,0:T(8,128)(2,1)} %get-tuple-element.101), channel_id=1, source_target_pairs={{0,1},{1,0},{2,3},{3,2},{4,5},{5,4},{6,7},{7,6},{8,9},{9,8},{10,11... | collective-permute-start | bytes 3932168 | tf_op jit(solution)/shard_map/ppermute | solution.py:106
  415.4 31.9 %collective-permute-start.31 = (bf16[4,5,2,128,128]{4,3,2,1,0:T(8,128)(2,1)}, bf16[4,5,2,128,128]{4,3,2,1,0:T(8,128)(2,1)S(1)}, u32[]{:S(2)}, u32[]{:S(2)}) collective-permute-start(bf16[4,5,2,128,128]{4,3,2,1,0:T(8,128)(2,1)} %get-tuple-element.109), channel_id=1, source_target_pairs={{0,1},{1,0},{2,3},{3,2},{4,5},{5,4},{6,7},{7,6},{8,9},{9,8},{10,11... | collective-permute-start | bytes 3932168 | tf_op jit(solution)/shard_map/ppermute | solution.py:106
  421.1 66.9 %collective-permute-start.33 = (bf16[3,4,80,960]{3,2,0,1:T(8,128)(2,1)S(1)}, bf16[3,4,80,960]{3,2,0,1:T(8,128)(2,1)S(1)}, u32[]{:S(2)}, u32[]{:S(2)}) collective-permute-start(bf16[3,4,80,960]{3,2,0,1:T(8,128)(2,1)S(1)} %add_convert_fusion), channel_id=1, source_target_pairs={{0,1},{1,0},{2,3},{3,2},{4,5},{5,4},{6,7},{7,6},{8,9},{9,8},{10,11... | collective-permute-start | bytes 5529608 | tf_op jit(solution)/shard_map/ppermute | solution.py:106
  421.8 26.1 %collective-permute-start.27 = (bf16[2,5,2,128,128]{4,3,2,1,0:T(8,128)(2,1)S(1)}, bf16[2,5,2,128,128]{4,3,2,1,0:T(8,128)(2,1)S(1)}, u32[]{:S(2)}, u32[]{:S(2)}) collective-permute-start(bf16[2,5,2,128,128]{4,3,2,1,0:T(8,128)(2,1)S(1)} %add_convert_fusion.9), channel_id=1, source_target_pairs={{0,2},{1,3},{2,0},{3,1},{4,6},{5,7},{6,4},{7,5},{8,10},{9,11},{10,... | collective-permute-start | bytes 1966088 | tf_op jit(solution)/shard_map/ppermute | solution.py:106
  447.5 40.5 %collective-permute-start.32 = (bf16[2,5,2,128,128]{4,3,2,1,0:T(8,128)(2,1)S(1)}, bf16[2,5,2,128,128]{4,3,2,1,0:T(8,128)(2,1)S(1)}, u32[]{:S(2)}, u32[]{:S(2)}) collective-permute-start(bf16[2,5,2,128,128]{4,3,2,1,0:T(8,128)(2,1)S(1)} %add_convert_fusion.8), channel_id=1, source_target_pairs={{0,2},{1,3},{2,0},{3,1},{4,6},{5,7},{6,4},{7,5},{8,10},{9,11},{10,... | collective-permute-start | bytes 1966088 | tf_op jit(solution)/shard_map/ppermute | solution.py:106
  448.1 18.2 %collective-permute-start.28 = (bf16[5,2,128,128]{3,2,1,0:T(8,128)(2,1)S(1)}, bf16[5,2,128,128]{3,2,1,0:T(8,128)(2,1)S(1)}, u32[]{:S(2)}, u32[]{:S(2)}) collective-permute-start(bf16[5,2,128,128]{3,2,1,0:T(8,128)(2,1)S(1)} %fusion.23), channel_id=1, source_target_pairs={{0,4},{1,5},{2,6},{3,7},{4,0},{5,1},{6,2},{7,3},{8,12},{9,13},{10,... | collective-permute-start | bytes 983048 | tf_op jit(solution)/shard_map/ppermute | solution.py:106
  493.2 29.3 %collective-permute-start.35 = (bf16[3,2,80,960]{3,2,0,1:T(8,128)(2,1)}, bf16[3,2,80,960]{3,2,0,1:T(8,128)(2,1)}, u32[]{:S(2)}, u32[]{:S(2)}) collective-permute-start(bf16[3,2,80,960]{3,2,0,1:T(8,128)(2,1)} %add_convert_fusion.3), channel_id=1, source_target_pairs={{0,2},{1,3},{2,0},{3,1},{4,6},{5,7},{6,4},{7,5},{8,10},{9,11},{10,... | collective-permute-start | bytes 2764808 | tf_op jit(solution)/shard_map/ppermute | solution.py:106
  524.7 24.0 %collective-permute-start.39 = (bf16[3,80,960]{2,1,0:T(8,128)(2,1)S(1)}, bf16[3,80,960]{2,1,0:T(8,128)(2,1)S(1)}, u32[]{:S(2)}, u32[]{:S(2)}) collective-permute-start(bf16[3,80,960]{2,1,0:T(8,128)(2,1)S(1)} %fusion.22), channel_id=1, source_target_pairs={{0,4},{1,5},{2,6},{3,7},{4,0},{5,1},{6,2},{7,3},{8,12},{9,13},{10,... | collective-permute-start | bytes 1382408 | tf_op jit(solution)/shard_map/ppermute | solution.py:106
  527.9 20.8 %collective-permute-start.38 = (bf16[1,4,80,960]{3,2,1,0:T(8,128)(2,1)S(1)}, bf16[1,4,80,960]{3,2,1,0:T(8,128)(2,1)S(1)}, u32[]{:S(2)}, u32[]{:S(2)}) collective-permute-start(bf16[1,4,80,960]{3,2,1,0:T(8,128)(2,1)S(1)} %add_convert_fusion.5), channel_id=1, source_target_pairs={{0,16},{16,0},{1,17},{17,1},{2,18},{18,2},{3,19},{19,3},{4,20},{20... | collective-permute-start | bytes 1843208 | tf_op jit(solution)/shard_map/ppermute | solution.py:106
  549.6 17.5 %collective-permute-start.37 = (bf16[336,960]{1,0:T(8,128)(2,1)S(1)}, bf16[336,960]{1,0:T(8,128)(2,1)S(1)}, u32[]{:S(2)}, u32[]{:S(2)}) collective-permute-start(bf16[336,960]{1,0:T(8,128)(2,1)S(1)} %pad_maximum_fusion.8), channel_id=1, source_target_pairs={{0,16},{16,0},{1,17},{17,1},{2,18},{18,2},{3,19},{19,3},{4,20},{20... | collective-permute-start | bytes 1935368 | tf_op jit(solution)/shard_map/ppermute | solution.py:106
  567.2 16.6 %collective-permute-start.40 = (bf16[336,960]{1,0:T(8,128)(2,1)S(1)}, bf16[336,960]{1,0:T(8,128)(2,1)S(1)}, u32[]{:S(2)}, u32[]{:S(2)}) collective-permute-start(bf16[336,960]{1,0:T(8,128)(2,1)S(1)} %pad_maximum_fusion.7), channel_id=1, source_target_pairs={{0,1},{1,0},{2,3},{3,2},{4,5},{5,4},{6,7},{7,6},{8,9},{9,8},{10,11... | collective-permute-start | bytes 1935368 | tf_op jit(solution)/shard_map/ppermute | solution.py:106
  (63 other events, 752.2 us)

commit v6 on v5

--- a/solution.py
+++ b/solution.py
@@ -288,30 +288,55 @@
     quarter = keep.shape[2] // 2
     near, far = slice(0, quarter), slice(quarter, 2 * quarter)
     sends = [
-        add_low(keep[:, 4:, far], come[:, 4:, far]),
-        add_low(keep[:, :4, far], come[:, :4, far]),
+        add_low(keep[4:, :, far], come[4:, :, far]),
+        add_low(keep[:4, :, far], come[:4, :, far]),
     ]
     return sends, (keep[:, :, near], come[:, :, near])
 
 
-def reduce_y(held, x_upper, ride=None):
-    upper = [part[:, 4:] for part in held] + [x_upper]
-    return swap_with(total_low(*upper), ride, slot_bits()[2])
-
-
-def reduce_near(rest, ride=None):
-    return swap_with(total_low(*[part[:, 2:] for part in rest]), ride, slot_bits()[1])
-
-
-def reduce_far(rest, ride=None):
-    return swap_with(total_low(*[part[:, 1] for part in rest]), ride, slot_bits()[0])
+def reduce_y(held, x_upper):
+    return swap(total_low(*[part[4:] for part in held], x_upper), slot_bits()[2])
+
+
+def reduce_near(rest):
+    return swap(total_low(*[part[2:] for part in rest]), slot_bits()[1])
+
+
+def reduce_far(rest):
+    return swap(total_low(*[part[1] for part in rest]), slot_bits()[0])
 
 
 def reduce_end(rest, z_far):
     total = z_far.astype(jnp.float32)
     for part in rest:
-        total = total + part[:, 0].astype(jnp.float32)
+        total = total + part[0].astype(jnp.float32)
     return total
+
+
+def reduce_halves(keep, away, ride):
+    far_z, near_z, along_y = slot_bits()
+    come = swap(away, ("core", 0))
+    sums = []
+    for (low, high), order in zip(
+        row_cuts(keep.shape[1]), ([along_y, near_z, far_z], [near_z, far_z, along_y])
+    ):
+        shape = (2, 2, 2, high - low, keep.shape[2])
+        terms = [keep[:, low:high].reshape(shape), come[:, low:high].reshape(shape)]
+        left = [along_y, near_z, far_z]
+        for where in order:
+            dim = left.index(where)
+            left.remove(where)
+            sent = total_low(*[lax.index_in_dim(term, 1, dim, False) for term in terms])
+            if low == 0:
+                arrived, ride = swap_with(sent, ride, where)
+            else:
+                arrived = swap(sent, where)
+            terms = [lax.index_in_dim(term, 0, dim, False) for term in terms] + [arrived]
+        total = terms[0].astype(jnp.float32)
+        for term in terms[1:]:
+            total = total + term.astype(jnp.float32)
+        sums.append(total)
+    return jnp.concatenate(sums, axis=0), ride
 
 
 def ride_parts(ride):
@@ -325,8 +350,6 @@
 
 
 def swap_with(sent, ride, where):
-    if ride is None:
-        return swap(sent, where), None
     parts = ride_parts(ride)
     come, other = off_ride(swap(with_ride(sent, parts), where), sent.shape)
     return come, (parts[0] + parts[1]) + other
@@ -550,6 +573,248 @@
     store_packed(d_queries_ref, (turned_back * SCALE_QK).astype(jnp.bfloat16), aligned)
 
 
+def own_mask(rows, cols):
+    return lax.broadcasted_iota(jnp.int32, (rows, cols), 0) <= (
+        lax.broadcasted_iota(jnp.int32, (rows, cols), 1) % rows
+    )
+
+
+def slot_keys(ref, length):
+    both = turned(ref[...])
+    return both[:length], both[length:]
+
+
+def attend_slots_body(count, flags_ref, queries_ref, *refs):
+    key_refs, value_refs = refs[:count], refs[count : 2 * count]
+    out_ref, total_ref, both_queries, work, largest, totals, mixed = refs[2 * count :]
+    length = key_refs[0].shape[1] // 2
+    cols = GROUP * length
+    packed = load_packed(queries_ref, True)
+    for side in range(2):
+        both_queries[side] = packed[:, side * cols : (side + 1) * cols]
+    visible = own_mask(length, cols)
+    low_keys, high_keys = zip(*[slot_keys(ref, length) for ref in key_refs])
+    row = 0
+
+    def keep_scores(scores, row):
+        work[row : row + scores.shape[0]] = scores
+        return jnp.max(scores, axis=0, keepdims=True)
+
+    for side, keys in ((0, low_keys[0]), (1, high_keys[0])):
+        scores = jnp.where(visible, matmul_n(keys, both_queries[side]), HIDDEN)
+        largest[side] = keep_scores(scores, row)
+        row += length
+    for slot in range(0, count, 2):
+        keys = jnp.concatenate([low_keys[slot], low_keys[slot + 1]], axis=0)
+        top = keep_scores(matmul_n(keys, both_queries[1]), row)
+        largest[1] = jnp.maximum(largest[1], top)
+        row += 2 * length
+    for slot in range(1, count):
+        side = flags_ref[slot]
+        keys = jnp.where(side == 0, low_keys[slot], high_keys[slot])
+        top = keep_scores(matmul_n(keys, both_queries[side]), row)
+        largest[side] = jnp.maximum(largest[side], top)
+        row += length
+    row = 0
+    for side in range(2):
+        values = value_refs[0][:, side * length : (side + 1) * length]
+        expos = jnp.exp(work[row : row + length] - largest[side])
+        totals[side] = jnp.sum(expos, axis=0, keepdims=True)
+        mixed[side] = matmul_n(values, expos.astype(jnp.bfloat16))
+        row += length
+    for slot in range(0, count, 2):
+        values = jnp.concatenate(
+            [value_refs[slot][:, :length], value_refs[slot + 1][:, :length]], axis=1
+        )
+        expos = jnp.exp(work[row : row + 2 * length] - largest[1])
+        totals[1] += jnp.sum(expos, axis=0, keepdims=True)
+        mixed[1] += matmul_n(values, expos.astype(jnp.bfloat16))
+        row += 2 * length
+    for slot in range(1, count):
+        side = flags_ref[slot]
+        values = jnp.where(side == 0, value_refs[slot][:, :length], value_refs[slot][:, length:])
+        expos = jnp.exp(work[row : row + length] - largest[side])
+        totals[side] += jnp.sum(expos, axis=0, keepdims=True)
+        mixed[side] += matmul_n(values, expos.astype(jnp.bfloat16))
+        row += length
+    result = [(mixed[side] / totals[side]).astype(jnp.bfloat16) for side in range(2)]
+    store_packed(out_ref, jnp.concatenate(result, axis=1), True)
+    logs = [largest[side] + jnp.log(totals[side]) for side in range(2)]
+    total_ref[0, 0] = jnp.concatenate(logs, axis=1)
+
+
+def attend_slots_back_body(count, flags_ref, queries_ref, *refs):
+    key_refs, value_refs = refs[:count], refs[count : 2 * count]
+    out_ref, total_ref, d_out_ref, cosine_ref, sine_ref = refs[2 * count : 2 * count + 5]
+    d_queries_ref = refs[2 * count + 5]
+    pair_refs = refs[2 * count + 6 : -5]
+    both_queries, both_d_out, log_totals, deltas, sums = refs[-5:]
+    length = key_refs[0].shape[1] // 2
+    cols = GROUP * length
+    queries, d_out = load_packed(queries_ref, True), load_packed(d_out_ref, True)
+    delta = jnp.sum(
+        d_out.astype(jnp.float32) * load_packed(out_ref, True).astype(jnp.float32),
+        axis=0,
+        keepdims=True,
+    )
+    for side in range(2):
+        part = slice(side * cols, (side + 1) * cols)
+        both_queries[side] = queries[:, part]
+        both_d_out[side] = d_out[:, part]
+        log_totals[side] = total_ref[0, 0, :, part]
+        deltas[side] = delta[:, part]
+    sums[...] = jnp.zeros_like(sums)
+    visible = own_mask(length, cols)
+    low_keys, high_keys = zip(*[slot_keys(ref, length) for ref in key_refs])
+    low_values, high_values = zip(*[slot_keys(ref, length) for ref in value_refs])
+    places_out = [(ref, slot) for ref in pair_refs for slot in range(ref.shape[0])]
+
+    def block(keys, keys_flat, values, side, mask=None):
+        probs = jnp.exp(matmul_n(keys, both_queries[side]) - log_totals[side])
+        if mask is not None:
+            probs = jnp.where(mask, probs, 0.0)
+        d_probs = matmul_n(values, both_d_out[side])
+        d_scores = (probs * (d_probs - deltas[side])).astype(jnp.bfloat16)
+        sums[side] += matmul_n(keys_flat, d_scores)
+        return jnp.concatenate(
+            [
+                matmul_t(d_scores, both_queries[side]),
+                matmul_t(probs.astype(jnp.bfloat16), both_d_out[side]),
+            ],
+            axis=1,
+        )
+
+    low_terms = []
+    for slot in range(0, count, 2):
+        keys, values = [
+            jnp.concatenate([part[slot], part[slot + 1]], axis=0) for part in (low_keys, low_values)
+        ]
+        flat = jnp.concatenate([key_refs[slot][:, :length], key_refs[slot + 1][:, :length]], axis=1)
+        terms = block(keys, flat, values, 1)
+        low_terms += [terms[:length], terms[length:]]
+    ref, slot = places_out[0]
+    own = [
+        block(keys, key_refs[0][:, side * length : (side + 1) * length], values, side, visible)
+        for side, (keys, values) in enumerate(
+            ((low_keys[0], low_values[0]), (high_keys[0], high_values[0]))
+        )
+    ]
+    ref[slot, 0, 0] = (low_terms[0] + own[0]).astype(jnp.bfloat16)
+    ref[slot, 0, 1] = own[1].astype(jnp.bfloat16)
+    for member in range(1, count):
+        side = flags_ref[member]
+        low = side == 0
+        keys = jnp.where(low, low_keys[member], high_keys[member])
+        flat = jnp.where(low, key_refs[member][:, :length], key_refs[member][:, length:])
+        values = jnp.where(low, low_values[member], high_values[member])
+        terms = block(keys, flat, values, side)
+        ref, slot = places_out[member]
+        ref[slot, 0, 0] = (low_terms[member] + jnp.where(low, terms, 0.0)).astype(jnp.bfloat16)
+        ref[slot, 0, 1] = jnp.where(low, 0.0, terms).astype(jnp.bfloat16)
+    d_queries = jnp.concatenate([sums[0], sums[1]], axis=1)
+    store_packed(d_queries_ref, turn_queries_back(d_queries, cosine_ref, sine_ref), True)
+
+
+def turn_queries_back(d_queries, cosine_ref, sine_ref):
+    cosine, sine_part = cosine_ref[...], sine_ref[...]
+    first_half, second_half = d_queries[: HD // 2], d_queries[HD // 2 :]
+    turned_back = jnp.concatenate(
+        [
+            first_half * cosine + second_half * sine_part,
+            second_half * cosine - first_half * sine_part,
+        ],
+        axis=0,
+    )
+    return (turned_back * SCALE_QK).astype(jnp.bfloat16)
+
+
+def slot_specs(leads, local_rows, seq):
+    specs = [
+        pl.BlockSpec(memory_space=pltpu.SMEM),
+        pl.BlockSpec((GROUP * HD, local_rows), lambda head: (head, seq)),
+    ]
+    for first in (0, KV):
+        specs += [
+            pl.BlockSpec(
+                (None, HD, local_rows),
+                lambda head, lead=lead, first=first: (lead, first + head, seq),
+            )
+            for lead in leads
+        ]
+    return specs
+
+
+def attend_slots(queries, pairs, flags, local_rows, seq):
+    count, cols = len(pairs), GROUP * local_rows // 2
+    leads, arrays = [lead for _, lead in pairs], [array for array, _ in pairs]
+    work = HEADS * local_rows * local_rows * count // 2
+    return pl.pallas_call(
+        lambda *refs: attend_slots_body(count, *refs),
+        grid=(KV,),
+        in_specs=slot_specs(leads, local_rows, seq),
+        out_specs=[
+            pl.BlockSpec((GROUP * HD, local_rows), lambda head: (head, 0)),
+            pl.BlockSpec((1, 1, 1, 2 * cols), lambda head: (0, head, 0, 0)),
+        ],
+        out_shape=[
+            jax.ShapeDtypeStruct((HEADS * HD, local_rows), jnp.bfloat16),
+            jax.ShapeDtypeStruct((1, KV, 1, 2 * cols), jnp.float32),
+        ],
+        scratch_shapes=[
+            pltpu.VMEM((2, HD, cols), jnp.bfloat16),
+            pltpu.VMEM(((2 * count + 1) * local_rows // 2, cols), jnp.float32),
+            pltpu.VMEM((2, 1, cols), jnp.float32),
+            pltpu.VMEM((2, 1, cols), jnp.float32),
+            pltpu.VMEM((2, HD, cols), jnp.float32),
+        ],
+        cost_estimate=pl.CostEstimate(
+            flops=work * HD, bytes_accessed=1024 * 1024, transcendentals=0
+        ),
+        compiler_params=pltpu.CompilerParams(vmem_limit_bytes=VMEM_BYTES),
+    )(flags, queries, *arrays, *arrays)
+
+
+def attend_slots_back(
+    queries, pairs, flags, mixed, log_total, d_mixed, tables, local_rows, seq, sets
+):
+    count, cols = len(pairs), GROUP * local_rows // 2
+    leads, arrays = [lead for _, lead in pairs], [array for array, _ in pairs]
+    work = HEADS * local_rows * local_rows * count // 2
+    own = pl.BlockSpec((GROUP * HD, local_rows), lambda head: (head, 0))
+    table_spec = pl.BlockSpec((HD // 2, 2 * cols), lambda head: (0, 0))
+    length = local_rows // 2
+    return pl.pallas_call(
+        lambda *refs: attend_slots_back_body(count, *refs),
+        grid=(KV,),
+        in_specs=slot_specs(leads, local_rows, seq)
+        + [
+            own,
+            pl.BlockSpec((1, 1, 1, 2 * cols), lambda head: (0, head, 0, 0)),
+            pl.BlockSpec((GROUP * HD, local_rows), lambda head: (head, seq)),
+            table_spec,
+            table_spec,
+        ],
+        out_specs=[own]
+        + [
+            pl.BlockSpec((slots, 1, 2, length, 2 * HD), lambda head: (0, head, 0, 0, 0))
+            for slots in sets
+        ],
+        out_shape=[jax.ShapeDtypeStruct((HEADS * HD, local_rows), jnp.bfloat16)]
+        + [jax.ShapeDtypeStruct((slots, KV, 2, length, 2 * HD), jnp.bfloat16) for slots in sets],
+        scratch_shapes=[
+            pltpu.VMEM((2, HD, cols), jnp.bfloat16),
+            pltpu.VMEM((2, HD, cols), jnp.bfloat16),
+            pltpu.VMEM((2, 1, cols), jnp.float32),
+            pltpu.VMEM((2, 1, cols), jnp.float32),
+            pltpu.VMEM((2, HD, cols), jnp.float32),
+        ],
+        cost_estimate=pl.CostEstimate(
+            flops=work * HD, bytes_accessed=1024 * 1024, transcendentals=0
+        ),
+        compiler_params=pltpu.CompilerParams(vmem_limit_bytes=VMEM_BYTES),
+    )(flags, queries, *arrays, *arrays, mixed, log_total, d_mixed, *tables)
+
+
 def head_specs(leads, aligned, cols, keys, local_rows, seq):
     count = len(leads)
     if aligned:
@@ -652,7 +917,7 @@
             for ref, side in ((keep_ref, mine // 2), (away_ref, 1 - mine // 2)):
                 for place, along_x in enumerate((mine % 2, 1 - mine % 2)):
                     start = (2 * side + along_x) * quarter
-                    ref[member, 0, place * quarter : (place + 1) * quarter] = values[
+                    ref[0, member, place * quarter : (place + 1) * quarter] = values[
                         start : start + quarter
                     ]
 
@@ -735,9 +1000,9 @@
             pl.BlockSpec((1, 3, rows // 4, width), lambda step, me_ref: (step, 0, 0, 0))
         ] * 4
         weight_args = [*mine, *far]
-        half = pl.BlockSpec((3, 1, rows // 2, width), lambda step, me_ref: (0, step, 0, 0))
+        half = pl.BlockSpec((1, 3, rows // 2, width), lambda step, me_ref: (step, 0, 0, 0))
         grad_specs = [half, half]
-        grad_shapes = [jax.ShapeDtypeStruct((3, blocks, rows // 2, width), jnp.bfloat16)] * 2
+        grad_shapes = [jax.ShapeDtypeStruct((blocks, 3, rows // 2, width), jnp.bfloat16)] * 2
     else:
         weight_specs = [weight_spec(member, own) for member in range(3) for own in (True, False)]
         weight_args = [mine, far] * 3
@@ -772,7 +1037,7 @@
         right = jnp.where(first, one_ref[...], resid_ref[...])
         grad = matmul_n(left, right).astype(jnp.bfloat16)
         if split:
-            put_rows(grad, grad_refs[0], grad_refs[1], 0, me_ref[0], me_ref[2])
+            put_rows(grad, grad_refs[0], grad_refs[1], 0, me_ref[0], 0)
         else:
             grad_refs[0][0] = grad
 
@@ -780,14 +1045,14 @@
     if split:
         table = rel_offsets(slot_bits())
         half = pl.BlockSpec(
-            (1, 1, rows // 2, width), lambda step, me_ref: (0, find(step ^ me_ref[1], table), 0, 0)
+            (1, 1, rows // 2, width), lambda step, me_ref: (find(step ^ me_ref[1], table), 0, 0, 0)
         )
         grad_specs = [half, half]
-        grad_shapes = [jax.ShapeDtypeStruct((1, blocks, rows // 2, width), jnp.bfloat16)] * 2
+        grad_shapes = [jax.ShapeDtypeStruct((blocks, 1, rows // 2, width), jnp.bfloat16)] * 2
     else:
         grad_specs = [pl.BlockSpec((1, rows, width), lambda step, me_ref: (step, 0, 0))]
         grad_shapes = [jax.ShapeDtypeStruct((blocks, rows, width), jnp.bfloat16)]
-    me = jnp.stack([lax.axis_index(name) for name in ("core", "ctx", "x")]).astype(jnp.int32)
+    me = jnp.stack([lax.axis_index(name) for name in ("core", "ctx")]).astype(jnp.int32)
     return pl.pallas_call(
         body,
         grid_spec=pltpu.PrefetchScalarGridSpec(
@@ -863,6 +1128,7 @@
         ).reshape(rows, 2 * GROUP * half_rows)
 
     owners = ctx_index ^ jnp.asarray(rel_offsets(slots), jnp.int32)
+    flags = (owners > ctx_index).astype(jnp.int32)
     inner = jnp.arange(half_rows, dtype=jnp.int32)
     key_pos = jnp.stack(
         [
@@ -878,10 +1144,11 @@
         cuts = row_cuts(weight_rows // 2)
         backward = [list(reversed(order)) for order in ctx_orders()]
         first_own = [spread(first_half[low:high], order) for (low, high), order in zip(cuts, backward)]
+        feed_quarter, first_own = lax.optimization_barrier((feed_quarter, first_own))
+        feed_far_z = swap(feed_quarter[None], slots[0])
         first_far = [swap(part, ("core", 0)) for part in first_own]
         first_rows = place_rows(first_own, first_far)
-        feed_quarter, first_rows = lax.optimization_barrier((feed_quarter, first_rows))
-        feed_own = double(feed_quarter[None], slots[0])
+        first_rows, feed_far_z = lax.optimization_barrier((first_rows, feed_far_z))
     else:
         mine = lax.all_gather(weights, ("x", "ctx"), axis=0, tiled=True)
         mine = mine.reshape(x_count * ctx_count, weight_rows, model_width)
@@ -904,24 +1171,25 @@
         axis=0,
     )
     if split:
-        joined, feed_own = lax.optimization_barrier((joined, feed_own))
+        joined, feed_far_z = lax.optimization_barrier((joined, feed_far_z))
+        feed_own = jnp.concatenate([feed_quarter[None], feed_far_z], axis=0)
     if aligned:
         far_z, y_own = swap(joined, slots[0]), swap(joined, slots[2])
     if split:
         feed_near, feed_y = swap(feed_own, slots[1]), swap(feed_own, slots[2])
         feed_x = swap(feed_own, ("x", 0))
     if aligned:
-        far_z, y_own, feed_near, feed_y, feed_x = lax.optimization_barrier(
-            (far_z, y_own, feed_near, feed_y, feed_x)
+        far_z, y_own, feed_near, feed_y = lax.optimization_barrier(
+            (far_z, y_own, feed_near, feed_y)
         )
         near_z = swap(jnp.stack([joined, far_z]), slots[1])
         y_far = swap(far_z, slots[2])
     if split:
         feed_near_y = swap(feed_near, slots[2])
-        x_parts = [feed_x, swap(feed_near, ("x", 0)), swap(feed_y, ("x", 0))]
+        x_parts = [swap(feed_near, ("x", 0)), swap(feed_y, ("x", 0))]
     if aligned:
-        near_z, y_far, feed_near_y, x_parts = lax.optimization_barrier(
-            (near_z, y_far, feed_near_y, x_parts)
+        near_z, y_far, feed_near_y, feed_x = lax.optimization_barrier(
+            (near_z, y_far, feed_near_y, feed_x)
         )
         y_near = swap(near_z, slots[2])
         pairs = [(joined[None], 0), (far_z[None], 0), (near_z, 0), (near_z, 1)]
@@ -937,14 +1205,17 @@
             )
         ]
     if split:
-        x_parts.append(swap(feed_near_y, ("x", 0)))
+        x_parts = [feed_x] + x_parts + [swap(feed_near_y, ("x", 0))]
         feed_own = jnp.concatenate([feed_own, feed_near, feed_y, feed_near_y], axis=0)
         feed_far = swap(feed_own, ("core", 0))
     q_rot = rotate(matmul_t(qkv_rows[:q_cols], a_one), turn).astype(jnp.bfloat16)
     queries = pack((q_rot * SCALE_QK).astype(jnp.bfloat16))
     attended = []
     for seq in range(seqs):
-        attended.append(attend(queries, pairs, key_pos, query_pos, local_rows, seq))
+        if aligned:
+            attended.append(attend_slots(queries, pairs, flags, local_rows, seq))
+        else:
+            attended.append(attend(queries, pairs, key_pos, query_pos, local_rows, seq))
         if split and seq == 0:
             attended, x_parts, feed_far = lax.optimization_barrier((attended, x_parts, feed_far))
             feed_x = jnp.concatenate(x_parts, axis=0)
@@ -965,15 +1236,18 @@
     d_q, d_pair = [], []
     for seq in range(seqs):
         mixed, log_total = attended[seq]
-        d_queries, *d_slots = attend_back(
-            queries, pairs, key_pos, query_pos, mixed, log_total, d_attn, packed_tables,
-            local_rows, seq, (2, 2, 4),
-        )
+        if aligned:
+            d_queries, *d_slots = attend_slots_back(
+                queries, pairs, flags, mixed, log_total, d_attn, packed_tables, local_rows, seq, (2, 2, 4)
+            )
+        else:
+            d_queries, *d_slots = attend_back(
+                queries, pairs, key_pos, query_pos, mixed, log_total, d_attn, packed_tables,
+                local_rows, seq, (1,),
+            )
         if split and seq == seqs - 1:
-            d_slots, feed_upper, feed_lower = lax.optimization_barrier(
-                (d_slots, feed_upper, feed_lower)
-            )
-            feed_y, _ = reduce_y(feed_held, feed_upper)
+            d_slots, feed_upper = lax.optimization_barrier((d_slots, feed_upper))
+            feed_y = reduce_y(feed_held, feed_upper)
         d_q.append(unpack(d_queries))
         if aligned:
             lower, near_part, upper = d_slots
@@ -1004,36 +1278,36 @@
     )
     first_terms = first_grads(d_qkv, attn_low, a_one, d_resid_low, weight_rows)
     if split:
-        feed_rest = [part[:, :4] for part in feed_held] + [feed_lower, feed_y]
-        feed_near, _ = reduce_near(feed_rest)
+        feed_rest = [part[:4] for part in feed_held] + [feed_lower, feed_y]
+        feed_near = reduce_near(feed_rest)
         first_terms, feed_near = lax.optimization_barrier((first_terms, feed_near))
-        feed_rest = [part[:, :2] for part in feed_rest] + [feed_near]
-        feed_far, _ = reduce_far(feed_rest)
+        feed_rest = [part[:2] for part in feed_rest] + [feed_near]
+        feed_sums = reduce_end(feed_rest, reduce_far(feed_rest))
+        sent = jnp.where(
+            x_index == 0,
+            feed_sums[1:],
+            jnp.broadcast_to(feed_sums[:1], (2,) + feed_sums.shape[1:]),
+        )
+        feed_come = swap(sent.astype(jnp.bfloat16), ("x", 0)).astype(jnp.float32)
     d_one = matmul_c(d_qkv, qkv_rows)
     d_norm_one, d_gain_one = norm_back(tokens_in, d_one, gains[0])
     d_tokens = d_resid + d_norm_one
     gain_grad = jnp.stack([d_gain_one, d_gain_two], axis=0)
     if split:
-        sends, first_held = reduce_start(*first_terms)
-        first_upper = swap(sends[0], ("x", 0))
-        first_lower, gain_grad = swap_with(sends[1], gain_grad, ("x", 0))
-        first_upper, feed_far = lax.optimization_barrier((first_upper, feed_far))
-        feed_sums = reduce_end(feed_rest, feed_far)
-        first_y, gain_grad = reduce_y(first_held, first_upper, gain_grad)
-        rest = [part[:, :4] for part in first_held] + [first_lower, first_y]
-        first_near, gain_grad = reduce_near(rest, gain_grad)
-        rest = [part[:, :2] for part in rest] + [first_near]
-        first_far, gain_grad = reduce_far(rest, gain_grad)
-        first_sums = reduce_end(rest, first_far)
-        sums = [first_sums[0], feed_sums[0], feed_sums[1], feed_sums[2]]
-        own_x = jnp.stack([jnp.where(x_index == 0, sums[c], sums[2 + c]) for c in range(2)])
-        other_x = jnp.stack([jnp.where(x_index == 0, sums[2 + c], sums[c]) for c in range(2)])
-        far_x = swap(other_x.astype(jnp.bfloat16), ("x", 0)).astype(jnp.float32)
-        halves = jnp.where(
-            x_index == 0,
-            jnp.concatenate([own_x, far_x], axis=1),
-            jnp.concatenate([far_x, own_x], axis=1),
-        )
+        keep, away = [part[:, 0] for part in first_terms]
+        first_half, gain_grad = reduce_halves(keep, away, gain_grad)
+        first_half, feed_come = lax.optimization_barrier((first_half, feed_come))
+        low_first = first_half.astype(jnp.bfloat16)
+        first_come, gain_grad = swap_with(low_first, gain_grad, ("x", 0))
+        first_half = first_half + first_come.astype(jnp.float32)
+        halves = [
+            jnp.where(x_index == 0, first_half, jnp.concatenate([feed_come[0], feed_sums[1]])),
+            jnp.where(
+                x_index == 0,
+                jnp.concatenate([feed_sums[0], feed_come[0]]),
+                jnp.concatenate([feed_come[1], feed_sums[2]]),
+            ),
+        ]
         own_half = jnp.where(core == 0, halves[0], halves[1])
         other_half = jnp.where(core == 0, halves[1], halves[0]).astype(jnp.bfloat16)
         come, gain_grad = swap_with(other_half, gain_grad, ("core", 0))

time: 638 us -> 617 us (0.967)
  waiting for transfers between devices: 337 us -> 315 us
  other arithmetic: 50.3 us -> 57 us
    ppermute x45 -> x47, waiting for transfers between devices: 337 us -> 315 us  [swap_by(): return lax.ppermute(values, axis, [(i, i ^ offset) for i in range(size)])]
    pallas_call x1 -> x0, local copies, waits for them, and re-layouts: 7.69 us -> none  [feed_forward(): pl.pallas_call(lambda *refs: feed_body(parts, split, *refs), grid_spec=pl...]
    convert_element_type x8 -> x11, other arithmetic: 12.2 us -> 15.3 us  [total_low(): return total.astype(jnp.bfloat16)]
    unnamed x113 -> x150, local copies, waits for them, and re-layouts: 24.8 us -> 25.6 us
    ppermute x45 -> x47, starting transfers between devices: 53 us -> 53 us  [swap_by(): return lax.ppermute(values, axis, [(i, i ^ offset) for i in range(size)])]
  transfers between devices with their start and end apart: 45 -> 47, of which waited for: 28 -> 28; matrix products, arithmetic and copies ran while one was open for 11% -> 13% of each run, Pallas kernels for 12% -> 13%
where the time goes in v6:
time: 617 us; the launch traced here: 607 us
  waiting for transfers between devices  315 us (51%)
  Pallas kernels  122 us (20%)
  other arithmetic  57 us (9%)
  starting transfers between devices  53 us (9%)
  local copies, waits for them, and re-layouts  40.8 us (7%)
  matrix products  17.2 us (3%)
    ppermute x47, waiting for transfers between devices, swap_by(): return lax.ppermute(values, axis, [(i, i ^ offset) for i in range(size)])  315 us
    ppermute x47, starting transfers between devices, swap_by(): return lax.ppermute(values, axis, [(i, i ^ offset) for i in range(size)])  53 us
    pallas_call x2, Pallas kernels, attend_slots_back(): pl.pallas_call(lambda *refs: attend_slots_back_body(count, *refs), grid=(...  46.8 us
    pallas_call x1, Pallas kernels, feed_forward(): pl.pallas_call(lambda *refs: feed_body(parts, split, *refs), grid_spec=pl...  41.9 us
    unnamed x150, local copies, waits for them, and re-layouts  25.6 us
    pallas_call x2, Pallas kernels, attend_slots(): pl.pallas_call(lambda *refs: attend_slots_body(count, *refs), grid=(KV,),...  18.4 us
    convert_element_type x11, other arithmetic, total_low(): return total.astype(jnp.bfloat16)  15.3 us
  transfers between devices with their start and end apart: 47, of which 28 were waited for; matrix products, arithmetic and copies ran while one was open for 13% of the time, Pallas kernels for 13%

profile of v6, /device:TPU:0, one launch (start us, length us, event | category | flops | bytes accessed | tf_op | source)
XLA Modules:
  0.0 606.8 jit_solution(13471352889033558066)
XLA Ops:
  3.6 14.9 %collective-permute-done = bf16[320,960]{1,0:T(8,128)(2,1)S(1)} collective-permute-done((bf16[320,960]{1,0:T(8,128)(2,1)}, bf16[320,960]{1,0:T(8,128)(2,1)S(1)}, u32[]{:S(2)}, u32[]{:S(2)}) %collective-permute-start) | collective-permute-done | bytes 614432 | tf_op jit(solution)/shard_map/ppermute | solution.py:106
  34.9 7.9 %collective-permute-start.3 = (bf16[2,80,960]{2,1,0:T(8,128)(2,1)S(1)}, bf16[2,80,960]{2,1,0:T(8,128)(2,1)S(1)}, u32[]{:S(2)}, u32[]{:S(2)}) collective-permute-start(bf16[2,80,960]{2,1,0:T(8,128)(2,1)S(1)} %pad_maximum_fusion.18), channel_id=1, source_target_pairs={{0,2},{1,3},{2,0},{3,1},{4,6},{5,7},{6,4},{7,5},{8,10},{9,11},{10,... | collective-permute-start | bytes 921608 | tf_op jit(solution)/shard_map/ppermute | solution.py:106
  44.6 5.6 collective-permute-done.6
  50.3 6.8 %collective-permute-done.3 = bf16[2,80,960]{2,1,0:T(8,128)(2,1)S(1)} collective-permute-done((bf16[2,80,960]{2,1,0:T(8,128)(2,1)S(1)}, bf16[2,80,960]{2,1,0:T(8,128)(2,1)S(1)}, u32[]{:S(2)}, u32[]{:S(2)}) %collective-permute-start.3) | collective-permute-done | bytes 307232 | tf_op jit(solution)/shard_map/ppermute | solution.py:106
  58.1 12.4 %collective-permute-done.7 = bf16[4,80,960]{2,1,0:T(8,128)(2,1)S(1)} collective-permute-done((bf16[4,80,960]{2,1,0:T(8,128)(2,1)S(1)}, bf16[4,80,960]{2,1,0:T(8,128)(2,1)S(1)}, u32[]{:S(2)}, u32[]{:S(2)}) %collective-permute-start.7) | collective-permute-done | bytes 614432 | tf_op jit(solution)/shard_map/ppermute | solution.py:106
  77.9 7.2 %shard_map.152 = bf16[8,320,960]{2,1,0:T(8,128)(2,1)} custom-call(s32[2]{0:T(128)S(1)} %pad_add_fusion.me_ref, bf16[8,80,960]{2,1,0:T(8,128)(2,1)S(1)} %pad_maximum_fusion.1.refs_0_, bf16[8,80,960]{2,1,0:T(8,128)(2,1)S(1)} %pad_maximum_fusion.2.refs_1_, bf16[8,80,960]{2,1,0:T(8,128)(2,1)} %collective-permute-done.8.refs_2_, ...), custom_call_target="tpu_custom_call" | custom-call | bytes 9830400 | tf_op jit(solution)/shard_map/pallas_call | solution.py:403
  85.1 13.6 %collective-permute-done.10 = bf16[1,3,80,960]{3,2,1,0:T(8,128)(2,1)S(1)} collective-permute-done((bf16[1,3,80,960]{3,2,1,0:T(8,128)(2,1)S(1)}, bf16[1,3,80,960]{3,2,1,0:T(8,128)(2,1)S(1)}, u32[]{:S(2)}, u32[]{:S(2)}) %collective-permute-start.10) | collective-permute-done | bytes 460832 | tf_op jit(solution)/shard_map/ppermute | solution.py:106
  111.7 29.8 %collective-permute-done.11 = bf16[640,512]{1,0:T(8,128)(2,1)S(1)} collective-permute-done((bf16[640,512]{1,0:T(8,128)(2,1)S(1)}, bf16[640,512]{1,0:T(8,128)(2,1)S(1)}, u32[]{:S(2)}, u32[]{:S(2)}) %collective-permute-start.11) | collective-permute-done | bytes 655392 | tf_op jit(solution)/shard_map/ppermute | solution.py:106
  153.3 15.5 %collective-permute-done.18 = bf16[2,3,80,960]{3,2,1,0:T(8,128)(2,1)S(1)} collective-permute-done((bf16[2,3,80,960]{3,2,1,0:T(8,128)(2,1)S(1)}, bf16[2,3,80,960]{3,2,1,0:T(8,128)(2,1)S(1)}, u32[]{:S(2)}, u32[]{:S(2)}) %collective-permute-start.18) | collective-permute-done | bytes 921632 | tf_op jit(solution)/shard_map/ppermute | solution.py:106
  168.8 15.3 %collective-permute-done.16 = bf16[640,512]{1,0:T(8,128)(2,1)S(1)} collective-permute-done((bf16[640,512]{1,0:T(8,128)(2,1)S(1)}, bf16[640,512]{1,0:T(8,128)(2,1)S(1)}, u32[]{:S(2)}, u32[]{:S(2)}) %collective-permute-start.16) | collective-permute-done | bytes 655392 | tf_op jit(solution)/shard_map/ppermute | solution.py:106
  195.0 21.6 %collective-permute-done.19.refs_8_.refs_9_.refs_16_.refs_17_ = bf16[2,640,512]{2,1,0:T(8,128)(2,1)} collective-permute-done((bf16[2,640,512]{2,1,0:T(8,128)(2,1)S(1)}, bf16[2,640,512]{2,1,0:T(8,128)(2,1)}, u32[]{:S(2)}, u32[]{:S(2)}) %collective-permute-start.19) | collective-permute-done | bytes 1310752 | tf_op jit(solution)/shard_map/ppermute | solution.py:106
  216.6 9.0 %shard_map.153 = (bf16[960,256]{1,0:T(8,128)(2,1)S(1)}, f32[1,5,1,768]{3,2,1,0:T(1,128)S(1)}) custom-call(s32[8]{0:T(128)S(1)} %compare_convert_fusion.refs_0_, bf16[960,512]{1,0:T(8,128)(2,1)S(1)} %bitcast.190, bf16[1,640,512]{2,1,0:T(8,128)(2,1)S(1)} %bitcast.157, bf16[1,640,512]{2,1,0:T(8,128)(2,1)S(1)} %bitcast.166, ...), custom_call_target="tpu_custom_call" | custom-call | flops 251658240 | bytes 1048576 | tf_op jit(solution)/shard_map/pallas_call | solution.py:751
  225.7 9.0 %collective-permute-done.21 = bf16[2,3,80,960]{3,2,1,0:T(8,128)(2,1)S(1)} collective-permute-done((bf16[2,3,80,960]{3,2,1,0:T(8,128)(2,1)}, bf16[2,3,80,960]{3,2,1,0:T(8,128)(2,1)S(1)}, u32[]{:S(2)}, u32[]{:S(2)}) %collective-permute-start.21) | collective-permute-done | bytes 921632 | tf_op jit(solution)/shard_map/ppermute | solution.py:106
  234.7 20.1 %collective-permute-done.22 = bf16[2,3,80,960]{3,2,1,0:T(8,128)(2,1)S(1)} collective-permute-done((bf16[2,3,80,960]{3,2,1,0:T(8,128)(2,1)}, bf16[2,3,80,960]{3,2,1,0:T(8,128)(2,1)S(1)}, u32[]{:S(2)}, u32[]{:S(2)}) %collective-permute-start.22) | collective-permute-done | bytes 921632 | tf_op jit(solution)/shard_map/ppermute | solution.py:106
  259.4 9.3 %shard_map.154 = (bf16[960,256]{1,0:T(8,128)(2,1)S(1)}, f32[1,5,1,768]{3,2,1,0:T(1,128)S(1)}) custom-call(s32[8]{0:T(128)S(1)} %compare_convert_fusion.refs_0_, bf16[960,512]{1,0:T(8,128)(2,1)S(1)} %bitcast.191, bf16[1,640,512]{2,1,0:T(8,128)(2,1)S(1)} %bitcast.159, bf16[1,640,512]{2,1,0:T(8,128)(2,1)S(1)} %bitcast.168, ...), custom_call_target="tpu_custom_call" | custom-call | flops 251658240 | bytes 1048576 | tf_op jit(solution)/shard_map/pallas_call | solution.py:751
  272.4 41.9 %shard_map.155 = (f32[512,960]{1,0:T(8,128)S(1)}, f32[512,960]{1,0:T(8,128)}, bf16[8,3,160,960]{3,2,1,0:T(8,128)(2,1)}, bf16[8,3,160,960]{3,2,1,0:T(8,128)(2,1)}) custom-call(s32[2]{0:T(128)S(1)} %pad_add_fusion.1.refs_0_, bf16[512,960]{1,0:T(8,128)(2,1)S(1)} %multiply_convert_fusion.refs_1_, bf16[512,960]{1,0:T(8,128)(2,1)S(1)} %convert_element_type.431.refs_2_, ...), custom_call_target="tpu_custom_call" | custom-call | flops 22649241600 | bytes 29491200 | tf_op jit(solution)/shard_map/pallas_call | solution.py:1012
  320.0 4.8 fusion.11.refs_20_
  327.2 6.2 %add_convert_fusion.1 = (bf16[4,3,80,960]{3,2,1,0:T(8,128)(2,1)}, bf16[4,3,80,960]{3,2,1,0:T(8,128)(2,1)}) fusion(bf16[8,3,160,960]{3,2,1,0:T(8,128)(2,1)} %collective-permute-done.25, bf16[8,3,160,960]{3,2,1,0:T(8,128)(2,1)S(1)} %bitcast.206), kind=kLoop, calls=%fused_computation.1 | loop fusion | flops 7372800 | bytes 11059200 | tf_op jit(solution)/shard_map/convert_element_type | solution.py:114
  339.0 23.3 %shard_map.156 = (bf16[960,256]{1,0:T(8,128)(2,1)S(1)}, bf16[2,5,2,128,128]{4,3,2,1,0:T(8,128)(2,1)S(1)}, bf16[2,5,2,128,128]{4,3,2,1,0:T(8,128)(2,1)S(1)}, bf16[4,5,2,128,128]{4,3,2,1,0:T(8,128)(2,1)}) custom-call(s32[8]{0:T(128)S(1)} %compare_convert_fusion.refs_0_, bf16[960,512]{1,0:T(8,128)(2,1)S(1)} %bitcast.192, bf16[1,640,512]{2,1,0:T(8,128)(2,1)S(1)} %bitcast.161, ...), custom_call_target="tpu_custom_call" | custom-call | flops 251658240 | bytes 1048576 | tf_op jit(solution)/shard_map/pallas_call | solution.py:786
  364.7 23.5 %shard_map.157 = (bf16[960,256]{1,0:T(8,128)(2,1)S(1)}, bf16[2,5,2,128,128]{4,3,2,1,0:T(8,128)(2,1)S(1)}, bf16[2,5,2,128,128]{4,3,2,1,0:T(8,128)(2,1)S(1)}, bf16[4,5,2,128,128]{4,3,2,1,0:T(8,128)(2,1)}) custom-call(s32[8]{0:T(128)S(1)} %compare_convert_fusion.refs_0_, bf16[960,512]{1,0:T(8,128)(2,1)S(1)} %bitcast.193, bf16[1,640,512]{2,1,0:T(8,128)(2,1)S(1)} %bitcast.163, ...), custom_call_target="tpu_custom_call" | custom-call | flops 251658240 | bytes 1048576 | tf_op jit(solution)/shard_map/pallas_call | solution.py:786
  388.8 4.3 add_convert_fusion
  397.7 25.4 %collective-permute-done.30 = bf16[4,5,2,128,128]{4,3,2,1,0:T(8,128)(2,1)S(1)} collective-permute-done((bf16[4,5,2,128,128]{4,3,2,1,0:T(8,128)(2,1)}, bf16[4,5,2,128,128]{4,3,2,1,0:T(8,128)(2,1)S(1)}, u32[]{:S(2)}, u32[]{:S(2)}) %collective-permute-start.30) | collective-permute-done | bytes 1310752 | tf_op jit(solution)/shard_map/ppermute | solution.py:106
  427.4 15.9 %collective-permute-done.28 = bf16[5,2,128,128]{3,2,1,0:T(8,128)(2,1)S(1)} collective-permute-done((bf16[5,2,128,128]{3,2,1,0:T(8,128)(2,1)S(1)}, bf16[5,2,128,128]{3,2,1,0:T(8,128)(2,1)S(1)}, u32[]{:S(2)}, u32[]{:S(2)}) %collective-permute-start.28) | collective-permute-done | bytes 327712 | tf_op jit(solution)/shard_map/ppermute | solution.py:106
  444.4 20.0 %collective-permute-done.32 = bf16[4,3,80,960]{3,2,1,0:T(8,128)(2,1)S(1)} collective-permute-done((bf16[4,3,80,960]{3,2,1,0:T(8,128)(2,1)S(1)}, bf16[4,3,80,960]{3,2,1,0:T(8,128)(2,1)S(1)}, u32[]{:S(2)}, u32[]{:S(2)}) %collective-permute-start.32) | collective-permute-done | bytes 1843232 | tf_op jit(solution)/shard_map/ppermute | solution.py:106
  471.4 9.8 %collective-permute-done.33 = bf16[5,2,128,128]{3,2,1,0:T(8,128)(2,1)S(1)} collective-permute-done((bf16[5,2,128,128]{3,2,1,0:T(8,128)(2,1)S(1)}, bf16[5,2,128,128]{3,2,1,0:T(8,128)(2,1)S(1)}, u32[]{:S(2)}, u32[]{:S(2)}) %collective-permute-start.33) | collective-permute-done | bytes 327712 | tf_op jit(solution)/shard_map/ppermute | solution.py:106
  487.3 7.2 %shard_map.158 = (bf16[8,1,160,960]{3,2,1,0:T(8,128)(2,1)}, bf16[8,1,160,960]{3,2,1,0:T(8,128)(2,1)}) custom-call(s32[2]{0:T(128)S(1)} %pad_add_fusion.me_ref, bf16[1600,512]{1,0:T(8,128)(2,1)S(1)} %pad_maximum_fusion.qkv_ref, bf16[960,512]{1,0:T(8,128)(2,1)S(1)} %copy-done.19, bf16[512,960]{1,0:T(8,128)(2,1)S(1)} %copy-done.13, bf16[512,960]{1,0:T(8,128)(2,1)S(1)} %copy-done.11), custom_call_target="tpu_custom_call" | custom-call | flops 2516582400 | bytes 4915200 | tf_op jit(solution)/shard_map/pallas_call | solution.py:1056
  494.6 5.3 collective-permute-done.35
  505.9 20.2 %collective-permute-done.43 = bf16[3,80,960]{2,1,0:T(8,128)(2,1)S(1)} collective-permute-done((bf16[3,80,960]{2,1,0:T(8,128)(2,1)S(1)}, bf16[3,80,960]{2,1,0:T(8,128)(2,1)S(1)}, u32[]{:S(2)}, u32[]{:S(2)}) %collective-permute-start.43) | collective-permute-done | bytes 460832 | tf_op jit(solution)/shard_map/ppermute | solution.py:106
  534.0 14.3 %collective-permute-done.40 = bf16[2,2,80,960]{3,2,1,0:T(8,128)(2,1)S(1)} collective-permute-done((bf16[2,2,80,960]{3,2,1,0:T(8,128)(2,1)S(1)}, bf16[2,2,80,960]{3,2,1,0:T(8,128)(2,1)S(1)}, u32[]{:S(2)}, u32[]{:S(2)}) %collective-permute-start.40) | collective-permute-done | bytes 614432 | tf_op jit(solution)/shard_map/ppermute | solution.py:106
  556.9 9.2 %collective-permute-done.41 = bf16[2,80,960]{2,1,0:T(8,128)(2,1)} collective-permute-done((bf16[2,80,960]{2,1,0:T(8,128)(2,1)}, bf16[2,80,960]{2,1,0:T(8,128)(2,1)}, u32[]{:S(2)}, u32[]{:S(2)}) %collective-permute-start.41) | collective-permute-done | bytes 307232 | tf_op jit(solution)/shard_map/ppermute | solution.py:106
  574.3 7.7 %collective-permute-done.39 = bf16[96,960]{1,0:T(8,128)(2,1)S(1)} collective-permute-done((bf16[96,960]{1,0:T(8,128)(2,1)S(1)}, bf16[96,960]{1,0:T(8,128)(2,1)S(1)}, u32[]{:S(2)}, u32[]{:S(2)}) %collective-permute-start.39) | collective-permute-done | bytes 184352 | tf_op jit(solution)/shard_map/ppermute | solution.py:106
  584.2 9.7 %collective-permute-done.45 = bf16[176,960]{1,0:T(8,128)(2,1)S(1)} collective-permute-done((bf16[176,960]{1,0:T(8,128)(2,1)S(1)}, bf16[176,960]{1,0:T(8,128)(2,1)S(1)}, u32[]{:S(2)}, u32[]{:S(2)}) %collective-permute-start.45) | collective-permute-done | bytes 337952 | tf_op jit(solution)/shard_map/ppermute | solution.py:106
  (345 shorter events, 157.6 us)
Async XLA Ops:
  0.6 17.9 %collective-permute-start = (bf16[320,960]{1,0:T(8,128)(2,1)}, bf16[320,960]{1,0:T(8,128)(2,1)S(1)}, u32[]{:S(2)}, u32[]{:S(2)}) collective-permute-start(bf16[320,960]{1,0:T(8,128)(2,1)} %param.11), channel_id=1, source_target_pairs={{0,16},{16,0},{1,17},{17,1},{2,18},{18,2},{3,19},{19,3},{4,20},{20... | collective-permute-start | bytes 1843208 | tf_op jit(solution)/shard_map/ppermute | solution.py:106
  32.9 17.3 %collective-permute-start.6 = (bf16[2,80,960]{2,1,0:T(8,128)(2,1)S(1)}, bf16[2,80,960]{2,1,0:T(8,128)(2,1)S(1)}, u32[]{:S(2)}, u32[]{:S(2)}) collective-permute-start(bf16[2,80,960]{2,1,0:T(8,128)(2,1)S(1)} %pad_maximum_fusion.19), channel_id=1, source_target_pairs={{0,4},{1,5},{2,6},{3,7},{4,0},{5,1},{6,2},{7,3},{8,12},{9,13},{10,... | collective-permute-start | bytes 921608 | tf_op jit(solution)/shard_map/ppermute | solution.py:106
  34.9 22.3 %collective-permute-start.3 = (bf16[2,80,960]{2,1,0:T(8,128)(2,1)S(1)}, bf16[2,80,960]{2,1,0:T(8,128)(2,1)S(1)}, u32[]{:S(2)}, u32[]{:S(2)}) collective-permute-start(bf16[2,80,960]{2,1,0:T(8,128)(2,1)S(1)} %pad_maximum_fusion.18), channel_id=1, source_target_pairs={{0,2},{1,3},{2,0},{3,1},{4,6},{5,7},{6,4},{7,5},{8,10},{9,11},{10,... | collective-permute-start | bytes 921608 | tf_op jit(solution)/shard_map/ppermute | solution.py:106
  50.3 20.2 %collective-permute-start.7 = (bf16[4,80,960]{2,1,0:T(8,128)(2,1)S(1)}, bf16[4,80,960]{2,1,0:T(8,128)(2,1)S(1)}, u32[]{:S(2)}, u32[]{:S(2)}) collective-permute-start(bf16[4,80,960]{2,1,0:T(8,128)(2,1)S(1)} %pad_maximum_fusion.10), channel_id=1, source_target_pairs={{0,2},{1,3},{2,0},{3,1},{4,6},{5,7},{6,4},{7,5},{8,10},{9,11},{10,... | collective-permute-start | bytes 1843208 | tf_op jit(solution)/shard_map/ppermute | solution.py:106
  74.0 24.7 %collective-permute-start.10 = (bf16[1,3,80,960]{3,2,1,0:T(8,128)(2,1)S(1)}, bf16[1,3,80,960]{3,2,1,0:T(8,128)(2,1)S(1)}, u32[]{:S(2)}, u32[]{:S(2)}) collective-permute-start(bf16[1,3,80,960]{3,2,1,0:T(8,128)(2,1)S(1)} %bitcast.218), channel_id=1, source_target_pairs={{0,4},{1,5},{2,6},{3,7},{4,0},{5,1},{6,2},{7,3},{8,12},{9,13},{10,... | collective-permute-start | bytes 1382408 | tf_op jit(solution)/shard_map/ppermute | solution.py:106
  106.5 37.2 %collective-permute-start.13 = (bf16[2,3,80,960]{3,2,1,0:T(8,128)(2,1)S(1)}, bf16[2,3,80,960]{3,2,1,0:T(8,128)(2,1)S(1)}, u32[]{:S(2)}, u32[]{:S(2)}) collective-permute-start(bf16[2,3,80,960]{3,2,1,0:T(8,128)(2,1)S(1)} %pad_maximum_fusion.6), channel_id=1, source_target_pairs={{0,2},{1,3},{2,0},{3,1},{4,6},{5,7},{6,4},{7,5},{8,10},{9,11},{10,... | collective-permute-start | bytes 2764808 | tf_op jit(solution)/shard_map/ppermute | solution.py:106
  106.6 37.2 %collective-permute-start.14 = (bf16[2,3,80,960]{3,2,1,0:T(8,128)(2,1)S(1)}, bf16[2,3,80,960]{3,2,1,0:T(8,128)(2,1)S(1)}, u32[]{:S(2)}, u32[]{:S(2)}) collective-permute-start(bf16[2,3,80,960]{3,2,1,0:T(8,128)(2,1)S(1)} %pad_maximum_fusion.6), channel_id=1, source_target_pairs={{0,1},{1,0},{2,3},{3,2},{4,5},{5,4},{6,7},{7,6},{8,9},{9,8},{10,11... | collective-permute-start | bytes 2764808 | tf_op jit(solution)/shard_map/ppermute | solution.py:106
  107.2 34.4 %collective-permute-start.11 = (bf16[640,512]{1,0:T(8,128)(2,1)S(1)}, bf16[640,512]{1,0:T(8,128)(2,1)S(1)}, u32[]{:S(2)}, u32[]{:S(2)}) collective-permute-start(bf16[640,512]{1,0:T(8,128)(2,1)S(1)} %pad_maximum_fusion.12), channel_id=1, source_target_pairs={{0,4},{1,5},{2,6},{3,7},{4,0},{5,1},{6,2},{7,3},{8,12},{9,13},{10,... | collective-permute-start | bytes 1966088 | tf_op jit(solution)/shard_map/ppermute | solution.py:106
  110.2 33.6 %collective-permute-start.12 = (bf16[640,512]{1,0:T(8,128)(2,1)S(1)}, bf16[640,512]{1,0:T(8,128)(2,1)S(1)}, u32[]{:S(2)}, u32[]{:S(2)}) collective-permute-start(bf16[640,512]{1,0:T(8,128)(2,1)S(1)} %pad_maximum_fusion.12), channel_id=1, source_target_pairs={{0,1},{1,0},{2,3},{3,2},{4,5},{5,4},{6,7},{7,6},{8,9},{9,8},{10,11... | collective-permute-start | bytes 1966088 | tf_op jit(solution)/shard_map/ppermute | solution.py:106
  143.9 40.1 %collective-permute-start.15 = (bf16[2,640,512]{2,1,0:T(8,128)(2,1)S(1)}, bf16[2,640,512]{2,1,0:T(8,128)(2,1)S(1)}, u32[]{:S(2)}, u32[]{:S(2)}) collective-permute-start(bf16[2,640,512]{2,1,0:T(8,128)(2,1)S(1)} %pad_maximum_fusion.3), channel_id=1, source_target_pairs={{0,2},{1,3},{2,0},{3,1},{4,6},{5,7},{6,4},{7,5},{8,10},{9,11},{10,... | collective-permute-start | bytes 3932168 | tf_op jit(solution)/shard_map/ppermute | solution.py:106
  145.9 22.9 %collective-permute-start.18 = (bf16[2,3,80,960]{3,2,1,0:T(8,128)(2,1)S(1)}, bf16[2,3,80,960]{3,2,1,0:T(8,128)(2,1)S(1)}, u32[]{:S(2)}, u32[]{:S(2)}) collective-permute-start(bf16[2,3,80,960]{3,2,1,0:T(8,128)(2,1)S(1)} %pad_maximum_fusion.6), channel_id=1, source_target_pairs={{0,16},{16,0},{1,17},{17,1},{2,18},{18,2},{3,19},{19,3},{4,20},{20... | collective-permute-start | bytes 2764808 | tf_op jit(solution)/shard_map/ppermute | solution.py:106
  147.4 36.6 %collective-permute-start.17 = (bf16[2,3,80,960]{3,2,1,0:T(8,128)(2,1)S(1)}, bf16[2,3,80,960]{3,2,1,0:T(8,128)(2,1)S(1)}, u32[]{:S(2)}, u32[]{:S(2)}) collective-permute-start(bf16[2,3,80,960]{3,2,1,0:T(8,128)(2,1)S(1)} %collective-permute-done.13), channel_id=1, source_target_pairs={{0,1},{1,0},{2,3},{3,2},{4,5},{5,4},{6,7},{7,6},{8,9},{9,8},{10,11... | collective-permute-start | bytes 2764808 | tf_op jit(solution)/shard_map/ppermute | solution.py:106
  147.9 36.1 %collective-permute-start.16 = (bf16[640,512]{1,0:T(8,128)(2,1)S(1)}, bf16[640,512]{1,0:T(8,128)(2,1)S(1)}, u32[]{:S(2)}, u32[]{:S(2)}) collective-permute-start(bf16[640,512]{1,0:T(8,128)(2,1)S(1)} %collective-permute-done.11), channel_id=1, source_target_pairs={{0,1},{1,0},{2,3},{3,2},{4,5},{5,4},{6,7},{7,6},{8,9},{9,8},{10,11... | collective-permute-start | bytes 1966088 | tf_op jit(solution)/shard_map/ppermute | solution.py:106
  185.3 69.5 %collective-permute-start.23 = (bf16[8,3,80,960]{3,2,1,0:T(8,128)(2,1)}, bf16[8,3,80,960]{3,2,1,0:T(8,128)(2,1)}, u32[]{:S(2)}, u32[]{:S(2)}) collective-permute-start(bf16[8,3,80,960]{3,2,1,0:T(8,128)(2,1)} %constant_dynamic-update-slice_fusion.refs_3_), channel_id=1, source_target_pairs={{0,8},{8,0},{1,9},{9,1},{2,10},{10,2},{3,11},{11,3},{4,12},{12,4},... | collective-permute-start | bytes 11059208 | tf_op jit(solution)/shard_map/ppermute | solution.py:106
  185.5 31.1 %collective-permute-start.19 = (bf16[2,640,512]{2,1,0:T(8,128)(2,1)S(1)}, bf16[2,640,512]{2,1,0:T(8,128)(2,1)}, u32[]{:S(2)}, u32[]{:S(2)}) collective-permute-start(bf16[2,640,512]{2,1,0:T(8,128)(2,1)S(1)} %collective-permute-done.15.refs_4_.refs_5_.refs_12_.refs_13_), channel_id=1, source_target_pairs={{0,1},{1,0},{2,3},{3,2},{4,5},{5,4},{6,7},{7,6},{8,9},{9,8},{10,11... | collective-permute-start | bytes 3932168 | tf_op jit(solution)/shard_map/ppermute | solution.py:106
  188.8 36.9 %collective-permute-start.20 = (bf16[2,3,80,960]{3,2,1,0:T(8,128)(2,1)}, bf16[2,3,80,960]{3,2,1,0:T(8,128)(2,1)S(1)}, u32[]{:S(2)}, u32[]{:S(2)}) collective-permute-start(bf16[2,3,80,960]{3,2,1,0:T(8,128)(2,1)} %copy-done.50), channel_id=1, source_target_pairs={{0,16},{16,0},{1,17},{17,1},{2,18},{18,2},{3,19},{19,3},{4,20},{20... | collective-permute-start | bytes 2764808 | tf_op jit(solution)/shard_map/ppermute | solution.py:106
  189.3 45.4 %collective-permute-start.21 = (bf16[2,3,80,960]{3,2,1,0:T(8,128)(2,1)}, bf16[2,3,80,960]{3,2,1,0:T(8,128)(2,1)S(1)}, u32[]{:S(2)}, u32[]{:S(2)}) collective-permute-start(bf16[2,3,80,960]{3,2,1,0:T(8,128)(2,1)} %copy-done.51), channel_id=1, source_target_pairs={{0,16},{16,0},{1,17},{17,1},{2,18},{18,2},{3,19},{19,3},{4,20},{20... | collective-permute-start | bytes 2764808 | tf_op jit(solution)/shard_map/ppermute | solution.py:106
  190.8 64.0 %collective-permute-start.22 = (bf16[2,3,80,960]{3,2,1,0:T(8,128)(2,1)}, bf16[2,3,80,960]{3,2,1,0:T(8,128)(2,1)S(1)}, u32[]{:S(2)}, u32[]{:S(2)}) collective-permute-start(bf16[2,3,80,960]{3,2,1,0:T(8,128)(2,1)} %copy-done.54), channel_id=1, source_target_pairs={{0,16},{16,0},{1,17},{17,1},{2,18},{18,2},{3,19},{19,3},{4,20},{20... | collective-permute-start | bytes 2764808 | tf_op jit(solution)/shard_map/ppermute | solution.py:106
  333.4 54.7 %collective-permute-start.29 = (bf16[4,3,80,960]{3,2,1,0:T(8,128)(2,1)}, bf16[4,3,80,960]{3,2,1,0:T(8,128)(2,1)}, u32[]{:S(2)}, u32[]{:S(2)}) collective-permute-start(bf16[4,3,80,960]{3,2,1,0:T(8,128)(2,1)} %get-tuple-element.105), channel_id=1, source_target_pairs={{0,16},{16,0},{1,17},{17,1},{2,18},{18,2},{3,19},{19,3},{4,20},{20... | collective-permute-start | bytes 5529608 | tf_op jit(solution)/shard_map/ppermute | solution.py:106
  363.2 32.8 %collective-permute-start.26 = (bf16[4,5,2,128,128]{4,3,2,1,0:T(8,128)(2,1)}, bf16[4,5,2,128,128]{4,3,2,1,0:T(8,128)(2,1)}, u32[]{:S(2)}, u32[]{:S(2)}) collective-permute-start(bf16[4,5,2,128,128]{4,3,2,1,0:T(8,128)(2,1)} %get-tuple-element.100), channel_id=1, source_target_pairs={{0,1},{1,0},{2,3},{3,2},{4,5},{5,4},{6,7},{7,6},{8,9},{9,8},{10,11... | collective-permute-start | bytes 3932168 | tf_op jit(solution)/shard_map/ppermute | solution.py:106
  388.2 34.9 %collective-permute-start.30 = (bf16[4,5,2,128,128]{4,3,2,1,0:T(8,128)(2,1)}, bf16[4,5,2,128,128]{4,3,2,1,0:T(8,128)(2,1)S(1)}, u32[]{:S(2)}, u32[]{:S(2)}) collective-permute-start(bf16[4,5,2,128,128]{4,3,2,1,0:T(8,128)(2,1)} %get-tuple-element.107), channel_id=1, source_target_pairs={{0,1},{1,0},{2,3},{3,2},{4,5},{5,4},{6,7},{7,6},{8,9},{9,8},{10,11... | collective-permute-start | bytes 3932168 | tf_op jit(solution)/shard_map/ppermute | solution.py:106
  393.1 71.3 %collective-permute-start.32 = (bf16[4,3,80,960]{3,2,1,0:T(8,128)(2,1)S(1)}, bf16[4,3,80,960]{3,2,1,0:T(8,128)(2,1)S(1)}, u32[]{:S(2)}, u32[]{:S(2)}) collective-permute-start(bf16[4,3,80,960]{3,2,1,0:T(8,128)(2,1)S(1)} %add_convert_fusion), channel_id=1, source_target_pairs={{0,1},{1,0},{2,3},{3,2},{4,5},{5,4},{6,7},{7,6},{8,9},{9,8},{10,11... | collective-permute-start | bytes 5529608 | tf_op jit(solution)/shard_map/ppermute | solution.py:106
  394.5 71.6 %collective-permute-start.34 = (bf16[4,3,80,960]{3,2,1,0:T(8,128)(2,1)S(1)}, bf16[4,3,80,960]{3,2,1,0:T(8,128)(2,1)S(1)}, u32[]{:S(2)}, u32[]{:S(2)}) collective-permute-start(bf16[4,3,80,960]{3,2,1,0:T(8,128)(2,1)S(1)} %copy-done.37), channel_id=1, source_target_pairs={{0,16},{16,0},{1,17},{17,1},{2,18},{18,2},{3,19},{19,3},{4,20},{20... | collective-permute-start | bytes 5529608 | tf_op jit(solution)/shard_map/ppermute | solution.py:106
  397.3 26.4 %collective-permute-start.27 = (bf16[2,5,2,128,128]{4,3,2,1,0:T(8,128)(2,1)S(1)}, bf16[2,5,2,128,128]{4,3,2,1,0:T(8,128)(2,1)S(1)}, u32[]{:S(2)}, u32[]{:S(2)}) collective-permute-start(bf16[2,5,2,128,128]{4,3,2,1,0:T(8,128)(2,1)S(1)} %add_convert_fusion.8), channel_id=1, source_target_pairs={{0,2},{1,3},{2,0},{3,1},{4,6},{5,7},{6,4},{7,5},{8,10},{9,11},{10,... | collective-permute-start | bytes 1966088 | tf_op jit(solution)/shard_map/ppermute | solution.py:106
  423.3 41.1 %collective-permute-start.31 = (bf16[2,5,2,128,128]{4,3,2,1,0:T(8,128)(2,1)S(1)}, bf16[2,5,2,128,128]{4,3,2,1,0:T(8,128)(2,1)S(1)}, u32[]{:S(2)}, u32[]{:S(2)}) collective-permute-start(bf16[2,5,2,128,128]{4,3,2,1,0:T(8,128)(2,1)S(1)} %add_convert_fusion.7), channel_id=1, source_target_pairs={{0,2},{1,3},{2,0},{3,1},{4,6},{5,7},{6,4},{7,5},{8,10},{9,11},{10,... | collective-permute-start | bytes 1966088 | tf_op jit(solution)/shard_map/ppermute | solution.py:106
  424.8 18.5 %collective-permute-start.28 = (bf16[5,2,128,128]{3,2,1,0:T(8,128)(2,1)S(1)}, bf16[5,2,128,128]{3,2,1,0:T(8,128)(2,1)S(1)}, u32[]{:S(2)}, u32[]{:S(2)}) collective-permute-start(bf16[5,2,128,128]{3,2,1,0:T(8,128)(2,1)S(1)} %fusion.26), channel_id=1, source_target_pairs={{0,4},{1,5},{2,6},{3,7},{4,0},{5,1},{6,2},{7,3},{8,12},{9,13},{10,... | collective-permute-start | bytes 983048 | tf_op jit(solution)/shard_map/ppermute | solution.py:106
  470.1 29.9 %collective-permute-start.35 = (bf16[2,3,80,960]{3,2,1,0:T(8,128)(2,1)}, bf16[2,3,80,960]{3,2,1,0:T(8,128)(2,1)}, u32[]{:S(2)}, u32[]{:S(2)}) collective-permute-start(bf16[2,3,80,960]{3,2,1,0:T(8,128)(2,1)} %add_convert_fusion.3), channel_id=1, source_target_pairs={{0,2},{1,3},{2,0},{3,1},{4,6},{5,7},{6,4},{7,5},{8,10},{9,11},{10,... | collective-permute-start | bytes 2764808 | tf_op jit(solution)/shard_map/ppermute | solution.py:106
  499.9 31.6 %collective-permute-start.36 = (bf16[8,160,960]{2,1,0:T(8,128)(2,1)}, bf16[8,160,960]{2,1,0:T(8,128)(2,1)S(1)}, u32[]{:S(2)}, u32[]{:S(2)}) collective-permute-start(bf16[8,160,960]{2,1,0:T(8,128)(2,1)} %bitcast.248), channel_id=1, source_target_pairs={{0,8},{8,0},{1,9},{9,1},{2,10},{10,2},{3,11},{11,3},{4,12},{12,4},... | collective-permute-start | bytes 7372808 | tf_op jit(solution)/shard_map/ppermute | solution.py:106
  502.0 24.1 %collective-permute-start.43 = (bf16[3,80,960]{2,1,0:T(8,128)(2,1)S(1)}, bf16[3,80,960]{2,1,0:T(8,128)(2,1)S(1)}, u32[]{:S(2)}, u32[]{:S(2)}) collective-permute-start(bf16[3,80,960]{2,1,0:T(8,128)(2,1)S(1)} %fusion.25), channel_id=1, source_target_pairs={{0,4},{1,5},{2,6},{3,7},{4,0},{5,1},{6,2},{7,3},{8,12},{9,13},{10,... | collective-permute-start | bytes 1382408 | tf_op jit(solution)/shard_map/ppermute | solution.py:106
  530.0 25.9 %collective-permute-start.44 = (bf16[2,80,960]{2,1,0:T(8,128)(2,1)}, bf16[2,80,960]{2,1,0:T(8,128)(2,1)}, u32[]{:S(2)}, u32[]{:S(2)}) collective-permute-start(bf16[2,80,960]{2,1,0:T(8,128)(2,1)} %fusion.21), channel_id=1, source_target_pairs={{0,16},{16,0},{1,17},{17,1},{2,18},{18,2},{3,19},{19,3},{4,20},{20... | collective-permute-start | bytes 921608 | tf_op jit(solution)/shard_map/ppermute | solution.py:106
  532.3 18.0 %collective-permute-start.37 = (bf16[336,960]{1,0:T(8,128)(2,1)S(1)}, bf16[336,960]{1,0:T(8,128)(2,1)S(1)}, u32[]{:S(2)}, u32[]{:S(2)}) collective-permute-start(bf16[336,960]{1,0:T(8,128)(2,1)S(1)} %pad_maximum_fusion.7), channel_id=1, source_target_pairs={{0,1},{1,0},{2,3},{3,2},{4,5},{5,4},{6,7},{7,6},{8,9},{9,8},{10,11... | collective-permute-start | bytes 1935368 | tf_op jit(solution)/shard_map/ppermute | solution.py:106
  551.3 17.5 %collective-permute-start.38 = (bf16[176,960]{1,0:T(8,128)(2,1)}, bf16[176,960]{1,0:T(8,128)(2,1)}, u32[]{:S(2)}, u32[]{:S(2)}) collective-permute-start(bf16[176,960]{1,0:T(8,128)(2,1)} %pad_maximum_fusion.17), channel_id=1, source_target_pairs={{0,2},{1,3},{2,0},{3,1},{4,6},{5,7},{6,4},{7,5},{8,10},{9,11},{10,... | collective-permute-start | bytes 1013768 | tf_op jit(solution)/shard_map/ppermute | solution.py:106
  (83 other events, 957.5 us)

commit v7 on v6

--- a/solution.py
+++ b/solution.py
@@ -313,9 +313,9 @@
     return total
 
 
-def reduce_halves(keep, away, ride):
+def reduce_halves(keep, away, ride, beside):
     far_z, near_z, along_y = slot_bits()
-    come = swap(away, ("core", 0))
+    come = beside(0, swap(away, ("core", 0)))
     sums = []
     for (low, high), order in zip(
         row_cuts(keep.shape[1]), ([along_y, near_z, far_z], [near_z, far_z, along_y])
@@ -323,12 +323,13 @@
         shape = (2, 2, 2, high - low, keep.shape[2])
         terms = [keep[:, low:high].reshape(shape), come[:, low:high].reshape(shape)]
         left = [along_y, near_z, far_z]
-        for where in order:
+        for position, where in enumerate(order):
             dim = left.index(where)
             left.remove(where)
             sent = total_low(*[lax.index_in_dim(term, 1, dim, False) for term in terms])
             if low == 0:
                 arrived, ride = swap_with(sent, ride, where)
+                arrived = beside(position + 1, arrived)
             else:
                 arrived = swap(sent, where)
             terms = [lax.index_in_dim(term, 0, dim, False) for term in terms] + [arrived]
@@ -647,8 +648,8 @@
     key_refs, value_refs = refs[:count], refs[count : 2 * count]
     out_ref, total_ref, d_out_ref, cosine_ref, sine_ref = refs[2 * count : 2 * count + 5]
     d_queries_ref = refs[2 * count + 5]
-    pair_refs = refs[2 * count + 6 : -5]
-    both_queries, both_d_out, log_totals, deltas, sums = refs[-5:]
+    pair_refs = refs[2 * count + 6 : -7]
+    both_queries, both_d_out, turned_queries, turned_d_out, log_totals, deltas, sums = refs[-7:]
     length = key_refs[0].shape[1] // 2
     cols = GROUP * length
     queries, d_out = load_packed(queries_ref, True), load_packed(d_out_ref, True)
@@ -661,6 +662,8 @@
         part = slice(side * cols, (side + 1) * cols)
         both_queries[side] = queries[:, part]
         both_d_out[side] = d_out[:, part]
+        turned_queries[side] = turned(queries[:, part])
+        turned_d_out[side] = turned(d_out[:, part])
         log_totals[side] = total_ref[0, 0, :, part]
         deltas[side] = delta[:, part]
     sums[...] = jnp.zeros_like(sums)
@@ -678,8 +681,8 @@
         sums[side] += matmul_n(keys_flat, d_scores)
         return jnp.concatenate(
             [
-                matmul_t(d_scores, both_queries[side]),
-                matmul_t(probs.astype(jnp.bfloat16), both_d_out[side]),
+                matmul_n(d_scores, turned_queries[side]),
+                matmul_n(probs.astype(jnp.bfloat16), turned_d_out[side]),
             ],
             axis=1,
         )
@@ -804,6 +807,8 @@
         scratch_shapes=[
             pltpu.VMEM((2, HD, cols), jnp.bfloat16),
             pltpu.VMEM((2, HD, cols), jnp.bfloat16),
+            pltpu.VMEM((2, cols, HD), jnp.bfloat16),
+            pltpu.VMEM((2, cols, HD), jnp.bfloat16),
             pltpu.VMEM((2, 1, cols), jnp.float32),
             pltpu.VMEM((2, 1, cols), jnp.float32),
             pltpu.VMEM((2, HD, cols), jnp.float32),
@@ -908,16 +913,16 @@
     )(queries, key_pos, query_pos, *arrays, *arrays, mixed, log_total, d_mixed, *tables)
 
 
-def put_rows(values, keep_ref, away_ref, member, core, x_index):
+def put_rows(values, keep_ref, away_ref, place, core, x_index):
     quarter = values.shape[0] // 4
     for mine in range(4):
 
         @pl.when(2 * core + x_index == mine)
         def _(mine=mine):
             for ref, side in ((keep_ref, mine // 2), (away_ref, 1 - mine // 2)):
-                for place, along_x in enumerate((mine % 2, 1 - mine % 2)):
+                for position, along_x in enumerate((mine % 2, 1 - mine % 2)):
                     start = (2 * side + along_x) * quarter
-                    ref[0, member, place * quarter : (place + 1) * quarter] = values[
+                    ref[place[0], place[1], position * quarter : (position + 1) * quarter] = values[
                         start : start + quarter
                     ]
 
@@ -941,13 +946,14 @@
 
     def rows_of(member):
         if split:
-            parts_here = [ref[0, member] for ref in weight_refs]
             rows_out = []
-            for side in range(2):
-                for along_x in range(2):
-                    near = jnp.where(x_index == along_x, parts_here[0], parts_here[1])
-                    far = jnp.where(x_index == along_x, parts_here[2], parts_here[3])
-                    rows_out.append(jnp.where(core == side, near, far))
+            for slot in range(weight_refs[0].shape[0]):
+                parts_here = [ref[slot, member] for ref in weight_refs]
+                for side in range(2):
+                    for along_x in range(2):
+                        near = jnp.where(x_index == along_x, parts_here[0], parts_here[1])
+                        far = jnp.where(x_index == along_x, parts_here[2], parts_here[3])
+                        rows_out.append(jnp.where(core == side, near, far))
             return jnp.concatenate(rows_out, axis=0)
         wanted = feed_core(member, step, parts)
         return jnp.where(wanted == core, weight_refs[2 * member][0], weight_refs[2 * member + 1][0])
@@ -967,7 +973,12 @@
     for member, (left, right) in enumerate(((d_gate, a_two), (d_up, a_two), (hidden, dy_low))):
         grad = matmul_n(left, right).astype(jnp.bfloat16)
         if split:
-            put_rows(grad, grad_refs[0], grad_refs[1], member, core, x_index)
+            slots = grad_refs[0].shape[0]
+            rows = grad.shape[0] // slots
+            for slot in range(slots):
+                put_rows(
+                    grad[slot * rows : (slot + 1) * rows], *grad_refs, (slot, member), core, x_index
+                )
         else:
             grad_refs[member][0] = grad
 
@@ -997,10 +1008,10 @@
 
     if split:
         weight_specs = [
-            pl.BlockSpec((1, 3, rows // 4, width), lambda step, me_ref: (step, 0, 0, 0))
+            pl.BlockSpec((2, 3, rows // 4, width), lambda step, me_ref: (step, 0, 0, 0))
         ] * 4
         weight_args = [*mine, *far]
-        half = pl.BlockSpec((1, 3, rows // 2, width), lambda step, me_ref: (step, 0, 0, 0))
+        half = pl.BlockSpec((2, 3, rows // 2, width), lambda step, me_ref: (step, 0, 0, 0))
         grad_specs = [half, half]
         grad_shapes = [jax.ShapeDtypeStruct((blocks, 3, rows // 2, width), jnp.bfloat16)] * 2
     else:
@@ -1013,7 +1024,7 @@
         lambda *refs: feed_body(parts, split, *refs),
         grid_spec=pltpu.PrefetchScalarGridSpec(
             num_scalar_prefetch=1,
-            grid=(blocks,),
+            grid=(blocks // 2 if split else blocks,),
             in_specs=[whole, whole] + weight_specs,
             out_specs=[whole, whole] + grad_specs,
         ),
@@ -1037,7 +1048,7 @@
         right = jnp.where(first, one_ref[...], resid_ref[...])
         grad = matmul_n(left, right).astype(jnp.bfloat16)
         if split:
-            put_rows(grad, grad_refs[0], grad_refs[1], 0, me_ref[0], 0)
+            put_rows(grad, *grad_refs, (0, 0), me_ref[0], 0)
         else:
             grad_refs[0][0] = grad
 
@@ -1148,7 +1159,6 @@
         feed_far_z = swap(feed_quarter[None], slots[0])
         first_far = [swap(part, ("core", 0)) for part in first_own]
         first_rows = place_rows(first_own, first_far)
-        first_rows, feed_far_z = lax.optimization_barrier((first_rows, feed_far_z))
     else:
         mine = lax.all_gather(weights, ("x", "ctx"), axis=0, tiled=True)
         mine = mine.reshape(x_count * ctx_count, weight_rows, model_width)
@@ -1166,21 +1176,23 @@
     dy_low = cot_in.astype(jnp.bfloat16)
     a_one = (normalize(tokens_in) * gains[0]).astype(jnp.bfloat16)
     pair_rows = matmul_t(qkv_rows[q_cols:], a_one)
+    if split:
+        pair_rows, feed_far_z = lax.optimization_barrier((pair_rows, feed_far_z))
     joined = jnp.concatenate(
         [rotate(pair_rows[:kv_cols], turn).astype(jnp.bfloat16), pair_rows[kv_cols:].astype(jnp.bfloat16)],
         axis=0,
     )
     if split:
-        joined, feed_far_z = lax.optimization_barrier((joined, feed_far_z))
         feed_own = jnp.concatenate([feed_quarter[None], feed_far_z], axis=0)
+        joined, feed_own = lax.optimization_barrier((joined, feed_own))
     if aligned:
         far_z, y_own = swap(joined, slots[0]), swap(joined, slots[2])
     if split:
         feed_near, feed_y = swap(feed_own, slots[1]), swap(feed_own, slots[2])
         feed_x = swap(feed_own, ("x", 0))
     if aligned:
-        far_z, y_own, feed_near, feed_y = lax.optimization_barrier(
-            (far_z, y_own, feed_near, feed_y)
+        far_z, y_own, feed_near, feed_y, feed_x = lax.optimization_barrier(
+            (far_z, y_own, feed_near, feed_y, feed_x)
         )
         near_z = swap(jnp.stack([joined, far_z]), slots[1])
         y_far = swap(far_z, slots[2])
@@ -1188,8 +1200,8 @@
         feed_near_y = swap(feed_near, slots[2])
         x_parts = [swap(feed_near, ("x", 0)), swap(feed_y, ("x", 0))]
     if aligned:
-        near_z, y_far, feed_near_y, feed_x = lax.optimization_barrier(
-            (near_z, y_far, feed_near_y, feed_x)
+        near_z, y_far, feed_near_y, x_parts = lax.optimization_barrier(
+            (near_z, y_far, feed_near_y, x_parts)
         )
         y_near = swap(near_z, slots[2])
         pairs = [(joined[None], 0), (far_z[None], 0), (near_z, 0), (near_z, 1)]
@@ -1254,8 +1266,10 @@
             y_come = swap(upper, slots[2])
             near_come = swap(add_low(near_part, y_come[2:]), slots[1])
             if seq == seqs - 1:
-                near_come, feed_y = lax.optimization_barrier((near_come, feed_y))
+                near_come, feed_lower = lax.optimization_barrier((near_come, feed_lower))
             far_come = swap(total_low(lower[1], y_come[1], near_come[1]), slots[0])
+            if seq == seqs - 1:
+                far_come, feed_y = lax.optimization_barrier((far_come, feed_y))
             total = far_come.astype(jnp.float32)
             for part in (lower, y_come, near_come):
                 total = total + part[0].astype(jnp.float32)
@@ -1282,21 +1296,29 @@
         feed_near = reduce_near(feed_rest)
         first_terms, feed_near = lax.optimization_barrier((first_terms, feed_near))
         feed_rest = [part[:2] for part in feed_rest] + [feed_near]
-        feed_sums = reduce_end(feed_rest, reduce_far(feed_rest))
-        sent = jnp.where(
-            x_index == 0,
-            feed_sums[1:],
-            jnp.broadcast_to(feed_sums[:1], (2,) + feed_sums.shape[1:]),
-        )
-        feed_come = swap(sent.astype(jnp.bfloat16), ("x", 0)).astype(jnp.float32)
+        feed_far = reduce_far(feed_rest)
+        feed_later = {}
+
+        def beside(step, value):
+            if step == 2:
+                value, far_come = lax.optimization_barrier((value, feed_far))
+                sums = reduce_end(feed_rest, far_come)
+                sent = jnp.where(
+                    x_index == 0, sums[1:], jnp.broadcast_to(sums[:1], (2,) + sums.shape[1:])
+                )
+                feed_later["sums"] = sums
+                feed_later["come"] = swap(sent.astype(jnp.bfloat16), ("x", 0))
+            return value
+
     d_one = matmul_c(d_qkv, qkv_rows)
     d_norm_one, d_gain_one = norm_back(tokens_in, d_one, gains[0])
     d_tokens = d_resid + d_norm_one
     gain_grad = jnp.stack([d_gain_one, d_gain_two], axis=0)
     if split:
         keep, away = [part[:, 0] for part in first_terms]
-        first_half, gain_grad = reduce_halves(keep, away, gain_grad)
-        first_half, feed_come = lax.optimization_barrier((first_half, feed_come))
+        first_half, gain_grad = reduce_halves(keep, away, gain_grad, beside)
+        first_half, feed_come = lax.optimization_barrier((first_half, feed_later["come"]))
+        feed_sums, feed_come = feed_later["sums"], feed_come.astype(jnp.float32)
         low_first = first_half.astype(jnp.bfloat16)
         first_come, gain_grad = swap_with(low_first, gain_grad, ("x", 0))
         first_half = first_half + first_come.astype(jnp.float32)

time: 617 us -> 585 us (0.948)
  waiting for transfers between devices: 315 us -> 285 us
  local copies, waits for them, and re-layouts: 40.8 us -> 48.4 us
  matrix products: 17.2 us -> 10.2 us
    ppermute x47, waiting for transfers between devices: 315 us -> 285 us  [swap_by(): return lax.ppermute(values, axis, [(i, i ^ offset) for i in range(size)])]
    unnamed x150 -> x147, local copies, waits for them, and re-layouts: 25.6 us -> 27.4 us
  transfers between devices with their start and end apart: 47 -> 47, of which waited for: 28 -> 27; matrix products, arithmetic and copies ran while one was open for 13% -> 12% of each run, Pallas kernels for 13% -> 14%
where the time goes in v7:
time: 585 us; the launch traced here: 575 us
  waiting for transfers between devices  285 us (49%)
  Pallas kernels  117 us (20%)
  other arithmetic  58.5 us (10%)
  starting transfers between devices  53.4 us (9%)
  local copies, waits for them, and re-layouts  48.4 us (8%)
  matrix products  10.2 us (2%)
    ppermute x47, waiting for transfers between devices, swap_by(): return lax.ppermute(values, axis, [(i, i ^ offset) for i in range(size)])  285 us
    ppermute x47, starting transfers between devices, swap_by(): return lax.ppermute(values, axis, [(i, i ^ offset) for i in range(size)])  53.4 us
    pallas_call x2, Pallas kernels, attend_slots_back(): pl.pallas_call(lambda *refs: attend_slots_back_body(count, *refs), grid=(...  46.6 us
    pallas_call x1, Pallas kernels, feed_forward(): pl.pallas_call(lambda *refs: feed_body(parts, split, *refs), grid_spec=pl...  37.9 us
    unnamed x147, local copies, waits for them, and re-layouts  27.4 us
    pallas_call x2, Pallas kernels, attend_slots(): pl.pallas_call(lambda *refs: attend_slots_body(count, *refs), grid=(KV,),...  18.5 us
    convert_element_type x11, other arithmetic, total_low(): return total.astype(jnp.bfloat16)  16.1 us
  transfers between devices with their start and end apart: 47, of which 27 were waited for; matrix products, arithmetic and copies ran while one was open for 12% of the time, Pallas kernels for 14%

profile of v7, /device:TPU:0, one launch (start us, length us, event | category | flops | bytes accessed | tf_op | source)
XLA Modules:
  0.0 575.4 jit_solution(2323661504658462559)
XLA Ops:
  3.6 14.9 %collective-permute-done = bf16[320,960]{1,0:T(8,128)(2,1)S(1)} collective-permute-done((bf16[320,960]{1,0:T(8,128)(2,1)}, bf16[320,960]{1,0:T(8,128)(2,1)S(1)}, u32[]{:S(2)}, u32[]{:S(2)}) %collective-permute-start) | collective-permute-done | bytes 614432 | tf_op jit(solution)/shard_map/ppermute | solution.py:106
  35.7 7.9 %collective-permute-start.3 = (bf16[2,80,960]{2,1,0:T(8,128)(2,1)S(1)}, bf16[2,80,960]{2,1,0:T(8,128)(2,1)S(1)}, u32[]{:S(2)}, u32[]{:S(2)}) collective-permute-start(bf16[2,80,960]{2,1,0:T(8,128)(2,1)S(1)} %pad_maximum_fusion.18), channel_id=1, source_target_pairs={{0,2},{1,3},{2,0},{3,1},{4,6},{5,7},{6,4},{7,5},{8,10},{9,11},{10,... | collective-permute-start | bytes 921608 | tf_op jit(solution)/shard_map/ppermute | solution.py:106
  43.8 7.0 %collective-permute-done.6 = bf16[2,80,960]{2,1,0:T(8,128)(2,1)S(1)} collective-permute-done((bf16[2,80,960]{2,1,0:T(8,128)(2,1)S(1)}, bf16[2,80,960]{2,1,0:T(8,128)(2,1)S(1)}, u32[]{:S(2)}, u32[]{:S(2)}) %collective-permute-start.6) | collective-permute-done | bytes 307232 | tf_op jit(solution)/shard_map/ppermute | solution.py:106
  50.9 6.8 %collective-permute-done.3 = bf16[2,80,960]{2,1,0:T(8,128)(2,1)S(1)} collective-permute-done((bf16[2,80,960]{2,1,0:T(8,128)(2,1)S(1)}, bf16[2,80,960]{2,1,0:T(8,128)(2,1)S(1)}, u32[]{:S(2)}, u32[]{:S(2)}) %collective-permute-start.3) | collective-permute-done | bytes 307232 | tf_op jit(solution)/shard_map/ppermute | solution.py:106
  58.7 12.7 %collective-permute-done.7 = bf16[4,80,960]{2,1,0:T(8,128)(2,1)S(1)} collective-permute-done((bf16[4,80,960]{2,1,0:T(8,128)(2,1)S(1)}, bf16[4,80,960]{2,1,0:T(8,128)(2,1)S(1)}, u32[]{:S(2)}, u32[]{:S(2)}) %collective-permute-start.7) | collective-permute-done | bytes 614432 | tf_op jit(solution)/shard_map/ppermute | solution.py:106
  80.8 7.2 %shard_map.152 = bf16[8,320,960]{2,1,0:T(8,128)(2,1)} custom-call(s32[2]{0:T(128)S(1)} %pad_add_fusion.me_ref, bf16[8,80,960]{2,1,0:T(8,128)(2,1)S(1)} %pad_maximum_fusion.1.refs_0_, bf16[8,80,960]{2,1,0:T(8,128)(2,1)S(1)} %pad_maximum_fusion.2.refs_1_, bf16[8,80,960]{2,1,0:T(8,128)(2,1)} %collective-permute-done.8.refs_2_, ...), custom_call_target="tpu_custom_call" | custom-call | bytes 9830400 | tf_op jit(solution)/shard_map/pallas_call | solution.py:404
  90.5 11.6 %collective-permute-done.10 = bf16[1,3,80,960]{3,2,1,0:T(8,128)(2,1)} collective-permute-done((bf16[1,3,80,960]{3,2,1,0:T(8,128)(2,1)S(1)}, bf16[1,3,80,960]{3,2,1,0:T(8,128)(2,1)}, u32[]{:S(2)}, u32[]{:S(2)}) %collective-permute-start.10) | collective-permute-done | bytes 460832 | tf_op jit(solution)/shard_map/ppermute | solution.py:106
  114.9 31.9 %collective-permute-done.12 = bf16[640,512]{1,0:T(8,128)(2,1)S(1)} collective-permute-done((bf16[640,512]{1,0:T(8,128)(2,1)S(1)}, bf16[640,512]{1,0:T(8,128)(2,1)S(1)}, u32[]{:S(2)}, u32[]{:S(2)}) %collective-permute-start.12) | collective-permute-done | bytes 655392 | tf_op jit(solution)/shard_map/ppermute | solution.py:106
  156.3 30.4 %collective-permute-done.17 = bf16[640,512]{1,0:T(8,128)(2,1)S(1)} collective-permute-done((bf16[640,512]{1,0:T(8,128)(2,1)S(1)}, bf16[640,512]{1,0:T(8,128)(2,1)S(1)}, u32[]{:S(2)}, u32[]{:S(2)}) %collective-permute-start.17) | collective-permute-done | bytes 655392 | tf_op jit(solution)/shard_map/ppermute | solution.py:106
  186.8 5.5 collective-permute-done.19
  201.1 25.5 %collective-permute-done.21.refs_8_.refs_9_.refs_16_.refs_17_ = bf16[2,640,512]{2,1,0:T(8,128)(2,1)S(1)} collective-permute-done((bf16[2,640,512]{2,1,0:T(8,128)(2,1)S(1)}, bf16[2,640,512]{2,1,0:T(8,128)(2,1)S(1)}, u32[]{:S(2)}, u32[]{:S(2)}) %collective-permute-start.21) | collective-permute-done | bytes 1310752 | tf_op jit(solution)/shard_map/ppermute | solution.py:106
  227.6 9.0 %shard_map.153 = (bf16[960,256]{1,0:T(8,128)(2,1)S(1)}, f32[1,5,1,768]{3,2,1,0:T(1,128)S(1)}) custom-call(s32[8]{0:T(128)S(1)} %compare_convert_fusion.refs_0_, bf16[960,512]{1,0:T(8,128)(2,1)S(1)} %bitcast.200, bf16[1,640,512]{2,1,0:T(8,128)(2,1)S(1)} %bitcast.167, bf16[1,640,512]{2,1,0:T(8,128)(2,1)S(1)} %bitcast.176, ...), custom_call_target="tpu_custom_call" | custom-call | flops 251658240 | bytes 1048576 | tf_op jit(solution)/shard_map/pallas_call | solution.py:754
  243.1 9.5 %shard_map.154 = (bf16[960,256]{1,0:T(8,128)(2,1)S(1)}, f32[1,5,1,768]{3,2,1,0:T(1,128)S(1)}) custom-call(s32[8]{0:T(128)S(1)} %compare_convert_fusion.refs_0_, bf16[960,512]{1,0:T(8,128)(2,1)S(1)} %bitcast.201, bf16[1,640,512]{2,1,0:T(8,128)(2,1)S(1)} %bitcast.169, bf16[1,640,512]{2,1,0:T(8,128)(2,1)S(1)} %bitcast.178, ...), custom_call_target="tpu_custom_call" | custom-call | flops 251658240 | bytes 1048576 | tf_op jit(solution)/shard_map/pallas_call | solution.py:754
  256.4 37.9 %shard_map.155 = (f32[512,960]{1,0:T(8,128)S(1)}, f32[512,960]{1,0:T(8,128)}, bf16[8,3,160,960]{3,2,1,0:T(8,128)(2,1)}, bf16[8,3,160,960]{3,2,1,0:T(8,128)(2,1)}) custom-call(s32[2]{0:T(128)S(1)} %pad_add_fusion.1.refs_0_, bf16[512,960]{1,0:T(8,128)(2,1)S(1)} %multiply_convert_fusion.refs_1_, bf16[512,960]{1,0:T(8,128)(2,1)S(1)} %convert_element_type.437.refs_2_, ...), custom_call_target="tpu_custom_call" | custom-call | flops 22649241600 | bytes 29491200 | tf_op jit(solution)/shard_map/pallas_call | solution.py:1023
  302.3 4.9 collective-permute-done.25
  307.2 6.2 %add_convert_fusion.1 = (bf16[4,3,80,960]{3,2,1,0:T(8,128)(2,1)}, bf16[4,3,80,960]{3,2,1,0:T(8,128)(2,1)}) fusion(bf16[8,3,160,960]{3,2,1,0:T(8,128)(2,1)} %collective-permute-done.25, bf16[8,3,160,960]{3,2,1,0:T(8,128)(2,1)S(1)} %bitcast.221), kind=kLoop, calls=%fused_computation.1 | loop fusion | flops 7372800 | bytes 11059200 | tf_op jit(solution)/shard_map/convert_element_type | solution.py:114
  319.0 23.2 %shard_map.156 = (bf16[960,256]{1,0:T(8,128)(2,1)S(1)}, bf16[2,5,2,128,128]{4,3,2,1,0:T(8,128)(2,1)S(1)}, bf16[2,5,2,128,128]{4,3,2,1,0:T(8,128)(2,1)S(1)}, bf16[4,5,2,128,128]{4,3,2,1,0:T(8,128)(2,1)}) custom-call(s32[8]{0:T(128)S(1)} %compare_convert_fusion.refs_0_, bf16[960,512]{1,0:T(8,128)(2,1)S(1)} %bitcast.202, bf16[1,640,512]{2,1,0:T(8,128)(2,1)S(1)} %bitcast.171, ...), custom_call_target="tpu_custom_call" | custom-call | flops 251658240 | bytes 1048576 | tf_op jit(solution)/shard_map/pallas_call | solution.py:789
  344.5 23.4 %shard_map.157 = (bf16[960,256]{1,0:T(8,128)(2,1)S(1)}, bf16[2,5,2,128,128]{4,3,2,1,0:T(8,128)(2,1)S(1)}, bf16[2,5,2,128,128]{4,3,2,1,0:T(8,128)(2,1)S(1)}, bf16[4,5,2,128,128]{4,3,2,1,0:T(8,128)(2,1)}) custom-call(s32[8]{0:T(128)S(1)} %compare_convert_fusion.refs_0_, bf16[960,512]{1,0:T(8,128)(2,1)S(1)} %bitcast.203, bf16[1,640,512]{2,1,0:T(8,128)(2,1)S(1)} %bitcast.173, ...), custom_call_target="tpu_custom_call" | custom-call | flops 251658240 | bytes 1048576 | tf_op jit(solution)/shard_map/pallas_call | solution.py:789
  370.1 5.4 add_convert_fusion
  377.6 25.3 %collective-permute-done.30 = bf16[4,5,2,128,128]{4,3,2,1,0:T(8,128)(2,1)S(1)} collective-permute-done((bf16[4,5,2,128,128]{4,3,2,1,0:T(8,128)(2,1)}, bf16[4,5,2,128,128]{4,3,2,1,0:T(8,128)(2,1)S(1)}, u32[]{:S(2)}, u32[]{:S(2)}) %collective-permute-start.30) | collective-permute-done | bytes 1310752 | tf_op jit(solution)/shard_map/ppermute | solution.py:106
  406.1 6.8 %collective-permute-done.32 = bf16[4,3,80,960]{3,2,1,0:T(8,128)(2,1)S(1)} collective-permute-done((bf16[4,3,80,960]{3,2,1,0:T(8,128)(2,1)S(1)}, bf16[4,3,80,960]{3,2,1,0:T(8,128)(2,1)S(1)}, u32[]{:S(2)}, u32[]{:S(2)}) %collective-permute-start.32) | collective-permute-done | bytes 1843232 | tf_op jit(solution)/shard_map/ppermute | solution.py:106
  412.8 12.4 %collective-permute-done.31 = bf16[2,5,2,128,128]{4,3,2,1,0:T(8,128)(2,1)S(1)} collective-permute-done((bf16[2,5,2,128,128]{4,3,2,1,0:T(8,128)(2,1)S(1)}, bf16[2,5,2,128,128]{4,3,2,1,0:T(8,128)(2,1)S(1)}, u32[]{:S(2)}, u32[]{:S(2)}) %collective-permute-start.31) | collective-permute-done | bytes 655392 | tf_op jit(solution)/shard_map/ppermute | solution.py:106
  428.5 15.8 %collective-permute-done.34 = bf16[4,3,80,960]{3,2,1,0:T(8,128)(2,1)} collective-permute-done((bf16[4,3,80,960]{3,2,1,0:T(8,128)(2,1)}, bf16[4,3,80,960]{3,2,1,0:T(8,128)(2,1)}, u32[]{:S(2)}, u32[]{:S(2)}) %collective-permute-start.34) | collective-permute-done | bytes 1843232 | tf_op jit(solution)/shard_map/ppermute | solution.py:106
  446.3 4.0 add_convert_fusion.3
  455.8 7.1 %shard_map.158 = (bf16[8,1,160,960]{3,2,1,0:T(8,128)(2,1)}, bf16[8,1,160,960]{3,2,1,0:T(8,128)(2,1)}) custom-call(s32[2]{0:T(128)S(1)} %pad_add_fusion.me_ref, bf16[1600,512]{1,0:T(8,128)(2,1)S(1)} %pad_maximum_fusion.qkv_ref, bf16[960,512]{1,0:T(8,128)(2,1)S(1)} %copy-done.23, bf16[512,960]{1,0:T(8,128)(2,1)S(1)} %copy-done.13, bf16[512,960]{1,0:T(8,128)(2,1)S(1)} %copy-done.10), custom_call_target="tpu_custom_call" | custom-call | flops 2516582400 | bytes 4915200 | tf_op jit(solution)/shard_map/pallas_call | solution.py:1067
  463.0 10.5 %collective-permute-done.35 = bf16[2,3,80,960]{3,2,1,0:T(8,128)(2,1)} collective-permute-done((bf16[2,3,80,960]{3,2,1,0:T(8,128)(2,1)}, bf16[2,3,80,960]{3,2,1,0:T(8,128)(2,1)}, u32[]{:S(2)}, u32[]{:S(2)}) %collective-permute-start.35) | collective-permute-done | bytes 921632 | tf_op jit(solution)/shard_map/ppermute | solution.py:106
  478.8 4.5 multiply_reduce_fusion.1
  489.7 12.6 %collective-permute-done.41 = bf16[2,2,80,960]{3,2,1,0:T(8,128)(2,1)S(1)} collective-permute-done((bf16[2,2,80,960]{3,2,1,0:T(8,128)(2,1)S(1)}, bf16[2,2,80,960]{3,2,1,0:T(8,128)(2,1)S(1)}, u32[]{:S(2)}, u32[]{:S(2)}) %collective-permute-start.41) | collective-permute-done | bytes 614432 | tf_op jit(solution)/shard_map/ppermute | solution.py:106
  510.1 10.4 %collective-permute-done.42 = bf16[2,80,960]{2,1,0:T(8,128)(2,1)S(1)} collective-permute-done((bf16[2,80,960]{2,1,0:T(8,128)(2,1)S(1)}, bf16[2,80,960]{2,1,0:T(8,128)(2,1)S(1)}, u32[]{:S(2)}, u32[]{:S(2)}) %collective-permute-start.42) | collective-permute-done | bytes 307232 | tf_op jit(solution)/shard_map/ppermute | solution.py:106
  522.4 18.3 %collective-permute-done.39 = bf16[3,80,960]{2,1,0:T(8,128)(2,1)S(1)} collective-permute-done((bf16[3,80,960]{2,1,0:T(8,128)(2,1)S(1)}, bf16[3,80,960]{2,1,0:T(8,128)(2,1)S(1)}, u32[]{:S(2)}, u32[]{:S(2)}) %collective-permute-start.39) | collective-permute-done | bytes 460832 | tf_op jit(solution)/shard_map/ppermute | solution.py:106
  545.7 5.8 %collective-permute-done.40 = bf16[96,960]{1,0:T(8,128)(2,1)S(1)} collective-permute-done((bf16[96,960]{1,0:T(8,128)(2,1)S(1)}, bf16[96,960]{1,0:T(8,128)(2,1)S(1)}, u32[]{:S(2)}, u32[]{:S(2)}) %collective-permute-start.40) | collective-permute-done | bytes 184352 | tf_op jit(solution)/shard_map/ppermute | solution.py:106
  555.5 7.9 %collective-permute-done.45 = bf16[176,960]{1,0:T(8,128)(2,1)S(1)} collective-permute-done((bf16[176,960]{1,0:T(8,128)(2,1)S(1)}, bf16[176,960]{1,0:T(8,128)(2,1)S(1)}, u32[]{:S(2)}, u32[]{:S(2)}) %collective-permute-start.45) | collective-permute-done | bytes 337952 | tf_op jit(solution)/shard_map/ppermute | solution.py:106
  (349 shorter events, 150.6 us)
Async XLA Ops:
  0.6 17.9 %collective-permute-start = (bf16[320,960]{1,0:T(8,128)(2,1)}, bf16[320,960]{1,0:T(8,128)(2,1)S(1)}, u32[]{:S(2)}, u32[]{:S(2)}) collective-permute-start(bf16[320,960]{1,0:T(8,128)(2,1)} %param.11), channel_id=1, source_target_pairs={{0,16},{16,0},{1,17},{17,1},{2,18},{18,2},{3,19},{19,3},{4,20},{20... | collective-permute-start | bytes 1843208 | tf_op jit(solution)/shard_map/ppermute | solution.py:106
  35.7 22.0 %collective-permute-start.3 = (bf16[2,80,960]{2,1,0:T(8,128)(2,1)S(1)}, bf16[2,80,960]{2,1,0:T(8,128)(2,1)S(1)}, u32[]{:S(2)}, u32[]{:S(2)}) collective-permute-start(bf16[2,80,960]{2,1,0:T(8,128)(2,1)S(1)} %pad_maximum_fusion.18), channel_id=1, source_target_pairs={{0,2},{1,3},{2,0},{3,1},{4,6},{5,7},{6,4},{7,5},{8,10},{9,11},{10,... | collective-permute-start | bytes 921608 | tf_op jit(solution)/shard_map/ppermute | solution.py:106
  50.8 20.5 %collective-permute-start.7 = (bf16[4,80,960]{2,1,0:T(8,128)(2,1)S(1)}, bf16[4,80,960]{2,1,0:T(8,128)(2,1)S(1)}, u32[]{:S(2)}, u32[]{:S(2)}) collective-permute-start(bf16[4,80,960]{2,1,0:T(8,128)(2,1)S(1)} %pad_maximum_fusion.10), channel_id=1, source_target_pairs={{0,2},{1,3},{2,0},{3,1},{4,6},{5,7},{6,4},{7,5},{8,10},{9,11},{10,... | collective-permute-start | bytes 1843208 | tf_op jit(solution)/shard_map/ppermute | solution.py:106
  77.3 24.7 %collective-permute-start.10 = (bf16[1,3,80,960]{3,2,1,0:T(8,128)(2,1)S(1)}, bf16[1,3,80,960]{3,2,1,0:T(8,128)(2,1)}, u32[]{:S(2)}, u32[]{:S(2)}) collective-permute-start(bf16[1,3,80,960]{3,2,1,0:T(8,128)(2,1)S(1)} %bitcast.237), channel_id=1, source_target_pairs={{0,4},{1,5},{2,6},{3,7},{4,0},{5,1},{6,2},{7,3},{8,12},{9,13},{10,... | collective-permute-start | bytes 1382408 | tf_op jit(solution)/shard_map/ppermute | solution.py:106
  108.5 38.3 %collective-permute-start.15 = (bf16[2,3,80,960]{3,2,1,0:T(8,128)(2,1)S(1)}, bf16[2,3,80,960]{3,2,1,0:T(8,128)(2,1)S(1)}, u32[]{:S(2)}, u32[]{:S(2)}) collective-permute-start(bf16[2,3,80,960]{3,2,1,0:T(8,128)(2,1)S(1)} %copy-done.31), channel_id=1, source_target_pairs={{0,16},{16,0},{1,17},{17,1},{2,18},{18,2},{3,19},{19,3},{4,20},{20... | collective-permute-start | bytes 2764808 | tf_op jit(solution)/shard_map/ppermute | solution.py:106
  110.0 36.8 %collective-permute-start.14 = (bf16[2,3,80,960]{3,2,1,0:T(8,128)(2,1)S(1)}, bf16[2,3,80,960]{3,2,1,0:T(8,128)(2,1)S(1)}, u32[]{:S(2)}, u32[]{:S(2)}) collective-permute-start(bf16[2,3,80,960]{3,2,1,0:T(8,128)(2,1)S(1)} %copy-done.31), channel_id=1, source_target_pairs={{0,1},{1,0},{2,3},{3,2},{4,5},{5,4},{6,7},{7,6},{8,9},{9,8},{10,11... | collective-permute-start | bytes 2764808 | tf_op jit(solution)/shard_map/ppermute | solution.py:106
  110.5 36.5 %collective-permute-start.13 = (bf16[2,3,80,960]{3,2,1,0:T(8,128)(2,1)S(1)}, bf16[2,3,80,960]{3,2,1,0:T(8,128)(2,1)S(1)}, u32[]{:S(2)}, u32[]{:S(2)}) collective-permute-start(bf16[2,3,80,960]{3,2,1,0:T(8,128)(2,1)S(1)} %copy-done.31), channel_id=1, source_target_pairs={{0,2},{1,3},{2,0},{3,1},{4,6},{5,7},{6,4},{7,5},{8,10},{9,11},{10,... | collective-permute-start | bytes 2764808 | tf_op jit(solution)/shard_map/ppermute | solution.py:106
  110.5 36.3 %collective-permute-start.12 = (bf16[640,512]{1,0:T(8,128)(2,1)S(1)}, bf16[640,512]{1,0:T(8,128)(2,1)S(1)}, u32[]{:S(2)}, u32[]{:S(2)}) collective-permute-start(bf16[640,512]{1,0:T(8,128)(2,1)S(1)} %pad_maximum_fusion.12), channel_id=1, source_target_pairs={{0,1},{1,0},{2,3},{3,2},{4,5},{5,4},{6,7},{7,6},{8,9},{9,8},{10,11... | collective-permute-start | bytes 1966088 | tf_op jit(solution)/shard_map/ppermute | solution.py:106
  112.0 34.8 %collective-permute-start.11 = (bf16[640,512]{1,0:T(8,128)(2,1)S(1)}, bf16[640,512]{1,0:T(8,128)(2,1)S(1)}, u32[]{:S(2)}, u32[]{:S(2)}) collective-permute-start(bf16[640,512]{1,0:T(8,128)(2,1)S(1)} %pad_maximum_fusion.12), channel_id=1, source_target_pairs={{0,4},{1,5},{2,6},{3,7},{4,0},{5,1},{6,2},{7,3},{8,12},{9,13},{10,... | collective-permute-start | bytes 1966088 | tf_op jit(solution)/shard_map/ppermute | solution.py:106
  147.2 45.2 %collective-permute-start.16 = (bf16[2,640,512]{2,1,0:T(8,128)(2,1)S(1)}, bf16[2,640,512]{2,1,0:T(8,128)(2,1)S(1)}, u32[]{:S(2)}, u32[]{:S(2)}) collective-permute-start(bf16[2,640,512]{2,1,0:T(8,128)(2,1)S(1)} %pad_maximum_fusion.3), channel_id=1, source_target_pairs={{0,2},{1,3},{2,0},{3,1},{4,6},{5,7},{6,4},{7,5},{8,10},{9,11},{10,... | collective-permute-start | bytes 3932168 | tf_op jit(solution)/shard_map/ppermute | solution.py:106
  149.0 37.8 %collective-permute-start.20 = (bf16[2,3,80,960]{3,2,1,0:T(8,128)(2,1)S(1)}, bf16[2,3,80,960]{3,2,1,0:T(8,128)(2,1)S(1)}, u32[]{:S(2)}, u32[]{:S(2)}) collective-permute-start(bf16[2,3,80,960]{3,2,1,0:T(8,128)(2,1)S(1)} %collective-permute-done.14), channel_id=1, source_target_pairs={{0,16},{16,0},{1,17},{17,1},{2,18},{18,2},{3,19},{19,3},{4,20},{20... | collective-permute-start | bytes 2764808 | tf_op jit(solution)/shard_map/ppermute | solution.py:106
  149.5 42.8 %collective-permute-start.19 = (bf16[2,3,80,960]{3,2,1,0:T(8,128)(2,1)S(1)}, bf16[2,3,80,960]{3,2,1,0:T(8,128)(2,1)S(1)}, u32[]{:S(2)}, u32[]{:S(2)}) collective-permute-start(bf16[2,3,80,960]{3,2,1,0:T(8,128)(2,1)S(1)} %collective-permute-done.13), channel_id=1, source_target_pairs={{0,16},{16,0},{1,17},{17,1},{2,18},{18,2},{3,19},{19,3},{4,20},{20... | collective-permute-start | bytes 2764808 | tf_op jit(solution)/shard_map/ppermute | solution.py:106
  151.0 41.3 %collective-permute-start.18 = (bf16[2,3,80,960]{3,2,1,0:T(8,128)(2,1)S(1)}, bf16[2,3,80,960]{3,2,1,0:T(8,128)(2,1)}, u32[]{:S(2)}, u32[]{:S(2)}) collective-permute-start(bf16[2,3,80,960]{3,2,1,0:T(8,128)(2,1)S(1)} %collective-permute-done.13), channel_id=1, source_target_pairs={{0,1},{1,0},{2,3},{3,2},{4,5},{5,4},{6,7},{7,6},{8,9},{9,8},{10,11... | collective-permute-start | bytes 2764808 | tf_op jit(solution)/shard_map/ppermute | solution.py:106
  152.5 34.2 %collective-permute-start.17 = (bf16[640,512]{1,0:T(8,128)(2,1)S(1)}, bf16[640,512]{1,0:T(8,128)(2,1)S(1)}, u32[]{:S(2)}, u32[]{:S(2)}) collective-permute-start(bf16[640,512]{1,0:T(8,128)(2,1)S(1)} %collective-permute-done.11), channel_id=1, source_target_pairs={{0,1},{1,0},{2,3},{3,2},{4,5},{5,4},{6,7},{7,6},{8,9},{9,8},{10,11... | collective-permute-start | bytes 1966088 | tf_op jit(solution)/shard_map/ppermute | solution.py:106
  195.4 41.3 %collective-permute-start.23 = (bf16[8,3,80,960]{3,2,1,0:T(8,128)(2,1)}, bf16[8,3,80,960]{3,2,1,0:T(8,128)(2,1)}, u32[]{:S(2)}, u32[]{:S(2)}) collective-permute-start(bf16[8,3,80,960]{3,2,1,0:T(8,128)(2,1)} %constant_dynamic-update-slice_fusion.refs_3_), channel_id=1, source_target_pairs={{0,8},{8,0},{1,9},{9,1},{2,10},{10,2},{3,11},{11,3},{4,12},{12,4},... | collective-permute-start | bytes 11059208 | tf_op jit(solution)/shard_map/ppermute | solution.py:106
  195.4 31.2 %collective-permute-start.21 = (bf16[2,640,512]{2,1,0:T(8,128)(2,1)S(1)}, bf16[2,640,512]{2,1,0:T(8,128)(2,1)S(1)}, u32[]{:S(2)}, u32[]{:S(2)}) collective-permute-start(bf16[2,640,512]{2,1,0:T(8,128)(2,1)S(1)} %collective-permute-done.16.refs_4_.refs_5_.refs_12_.refs_13_), channel_id=1, source_target_pairs={{0,1},{1,0},{2,3},{3,2},{4,5},{5,4},{6,7},{7,6},{8,9},{9,8},{10,11... | collective-permute-start | bytes 3932168 | tf_op jit(solution)/shard_map/ppermute | solution.py:106
  196.9 39.7 %collective-permute-start.22 = (bf16[2,3,80,960]{3,2,1,0:T(8,128)(2,1)}, bf16[2,3,80,960]{3,2,1,0:T(8,128)(2,1)}, u32[]{:S(2)}, u32[]{:S(2)}) collective-permute-start(bf16[2,3,80,960]{3,2,1,0:T(8,128)(2,1)} %collective-permute-done.18), channel_id=1, source_target_pairs={{0,16},{16,0},{1,17},{17,1},{2,18},{18,2},{3,19},{19,3},{4,20},{20... | collective-permute-start | bytes 2764808 | tf_op jit(solution)/shard_map/ppermute | solution.py:106
  313.4 54.6 %collective-permute-start.29 = (bf16[4,3,80,960]{3,2,1,0:T(8,128)(2,1)}, bf16[4,3,80,960]{3,2,1,0:T(8,128)(2,1)}, u32[]{:S(2)}, u32[]{:S(2)}) collective-permute-start(bf16[4,3,80,960]{3,2,1,0:T(8,128)(2,1)} %get-tuple-element.113), channel_id=1, source_target_pairs={{0,16},{16,0},{1,17},{17,1},{2,18},{18,2},{3,19},{19,3},{4,20},{20... | collective-permute-start | bytes 5529608 | tf_op jit(solution)/shard_map/ppermute | solution.py:106
  343.0 34.0 %collective-permute-start.26 = (bf16[4,5,2,128,128]{4,3,2,1,0:T(8,128)(2,1)}, bf16[4,5,2,128,128]{4,3,2,1,0:T(8,128)(2,1)S(1)}, u32[]{:S(2)}, u32[]{:S(2)}) collective-permute-start(bf16[4,5,2,128,128]{4,3,2,1,0:T(8,128)(2,1)} %get-tuple-element.108), channel_id=1, source_target_pairs={{0,1},{1,0},{2,3},{3,2},{4,5},{5,4},{6,7},{7,6},{8,9},{9,8},{10,11... | collective-permute-start | bytes 3932168 | tf_op jit(solution)/shard_map/ppermute | solution.py:106
  368.0 34.9 %collective-permute-start.30 = (bf16[4,5,2,128,128]{4,3,2,1,0:T(8,128)(2,1)}, bf16[4,5,2,128,128]{4,3,2,1,0:T(8,128)(2,1)S(1)}, u32[]{:S(2)}, u32[]{:S(2)}) collective-permute-start(bf16[4,5,2,128,128]{4,3,2,1,0:T(8,128)(2,1)} %get-tuple-element.115), channel_id=1, source_target_pairs={{0,1},{1,0},{2,3},{3,2},{4,5},{5,4},{6,7},{7,6},{8,9},{9,8},{10,11... | collective-permute-start | bytes 3932168 | tf_op jit(solution)/shard_map/ppermute | solution.py:106
  368.6 44.2 %collective-permute-start.32 = (bf16[4,3,80,960]{3,2,1,0:T(8,128)(2,1)S(1)}, bf16[4,3,80,960]{3,2,1,0:T(8,128)(2,1)S(1)}, u32[]{:S(2)}, u32[]{:S(2)}) collective-permute-start(bf16[4,3,80,960]{3,2,1,0:T(8,128)(2,1)S(1)} %copy-done.39), channel_id=1, source_target_pairs={{0,16},{16,0},{1,17},{17,1},{2,18},{18,2},{3,19},{19,3},{4,20},{20... | collective-permute-start | bytes 5529608 | tf_op jit(solution)/shard_map/ppermute | solution.py:106
  375.5 68.8 %collective-permute-start.34 = (bf16[4,3,80,960]{3,2,1,0:T(8,128)(2,1)}, bf16[4,3,80,960]{3,2,1,0:T(8,128)(2,1)}, u32[]{:S(2)}, u32[]{:S(2)}) collective-permute-start(bf16[4,3,80,960]{3,2,1,0:T(8,128)(2,1)} %add_convert_fusion), channel_id=1, source_target_pairs={{0,1},{1,0},{2,3},{3,2},{4,5},{5,4},{6,7},{7,6},{8,9},{9,8},{10,11... | collective-permute-start | bytes 5529608 | tf_op jit(solution)/shard_map/ppermute | solution.py:106
  377.2 26.4 %collective-permute-start.27 = (bf16[2,5,2,128,128]{4,3,2,1,0:T(8,128)(2,1)S(1)}, bf16[2,5,2,128,128]{4,3,2,1,0:T(8,128)(2,1)S(1)}, u32[]{:S(2)}, u32[]{:S(2)}) collective-permute-start(bf16[2,5,2,128,128]{4,3,2,1,0:T(8,128)(2,1)S(1)} %add_convert_fusion.8), channel_id=1, source_target_pairs={{0,2},{1,3},{2,0},{3,1},{4,6},{5,7},{6,4},{7,5},{8,10},{9,11},{10,... | collective-permute-start | bytes 1966088 | tf_op jit(solution)/shard_map/ppermute | solution.py:106
  403.1 22.1 %collective-permute-start.31 = (bf16[2,5,2,128,128]{4,3,2,1,0:T(8,128)(2,1)S(1)}, bf16[2,5,2,128,128]{4,3,2,1,0:T(8,128)(2,1)S(1)}, u32[]{:S(2)}, u32[]{:S(2)}) collective-permute-start(bf16[2,5,2,128,128]{4,3,2,1,0:T(8,128)(2,1)S(1)} %add_convert_fusion.7), channel_id=1, source_target_pairs={{0,2},{1,3},{2,0},{3,1},{4,6},{5,7},{6,4},{7,5},{8,10},{9,11},{10,... | collective-permute-start | bytes 1966088 | tf_op jit(solution)/shard_map/ppermute | solution.py:106
  404.5 22.6 %collective-permute-start.28 = (bf16[5,2,128,128]{3,2,1,0:T(8,128)(2,1)}, bf16[5,2,128,128]{3,2,1,0:T(8,128)(2,1)}, u32[]{:S(2)}, u32[]{:S(2)}) collective-permute-start(bf16[5,2,128,128]{3,2,1,0:T(8,128)(2,1)} %fusion.12), channel_id=1, source_target_pairs={{0,4},{1,5},{2,6},{3,7},{4,0},{5,1},{6,2},{7,3},{8,12},{9,13},{10,... | collective-permute-start | bytes 983048 | tf_op jit(solution)/shard_map/ppermute | solution.py:106
  426.2 18.1 %collective-permute-start.33 = (bf16[5,2,128,128]{3,2,1,0:T(8,128)(2,1)}, bf16[5,2,128,128]{3,2,1,0:T(8,128)(2,1)}, u32[]{:S(2)}, u32[]{:S(2)}) collective-permute-start(bf16[5,2,128,128]{3,2,1,0:T(8,128)(2,1)} %fusion.13), channel_id=1, source_target_pairs={{0,4},{1,5},{2,6},{3,7},{4,0},{5,1},{6,2},{7,3},{8,12},{9,13},{10,... | collective-permute-start | bytes 983048 | tf_op jit(solution)/shard_map/ppermute | solution.py:106
  450.3 23.2 %collective-permute-start.35 = (bf16[2,3,80,960]{3,2,1,0:T(8,128)(2,1)}, bf16[2,3,80,960]{3,2,1,0:T(8,128)(2,1)}, u32[]{:S(2)}, u32[]{:S(2)}) collective-permute-start(bf16[2,3,80,960]{3,2,1,0:T(8,128)(2,1)} %add_convert_fusion.3), channel_id=1, source_target_pairs={{0,2},{1,3},{2,0},{3,1},{4,6},{5,7},{6,4},{7,5},{8,10},{9,11},{10,... | collective-permute-start | bytes 2764808 | tf_op jit(solution)/shard_map/ppermute | solution.py:106
  487.0 17.6 %collective-permute-start.37 = (bf16[336,960]{1,0:T(8,128)(2,1)S(1)}, bf16[336,960]{1,0:T(8,128)(2,1)S(1)}, u32[]{:S(2)}, u32[]{:S(2)}) collective-permute-start(bf16[336,960]{1,0:T(8,128)(2,1)S(1)} %pad_maximum_fusion.7), channel_id=1, source_target_pairs={{0,1},{1,0},{2,3},{3,2},{4,5},{5,4},{6,7},{7,6},{8,9},{9,8},{10,11... | collective-permute-start | bytes 1935368 | tf_op jit(solution)/shard_map/ppermute | solution.py:106
  502.5 17.9 %collective-permute-start.42 = (bf16[2,80,960]{2,1,0:T(8,128)(2,1)S(1)}, bf16[2,80,960]{2,1,0:T(8,128)(2,1)S(1)}, u32[]{:S(2)}, u32[]{:S(2)}) collective-permute-start(bf16[2,80,960]{2,1,0:T(8,128)(2,1)S(1)} %fusion.14), channel_id=1, source_target_pairs={{0,4},{1,5},{2,6},{3,7},{4,0},{5,1},{6,2},{7,3},{8,12},{9,13},{10,... | collective-permute-start | bytes 921608 | tf_op jit(solution)/shard_map/ppermute | solution.py:106
  504.8 17.5 %collective-permute-start.38 = (bf16[176,960]{1,0:T(8,128)(2,1)S(1)}, bf16[176,960]{1,0:T(8,128)(2,1)S(1)}, u32[]{:S(2)}, u32[]{:S(2)}) collective-permute-start(bf16[176,960]{1,0:T(8,128)(2,1)S(1)} %pad_maximum_fusion.17), channel_id=1, source_target_pairs={{0,2},{1,3},{2,0},{3,1},{4,6},{5,7},{6,4},{7,5},{8,10},{9,11},{10,... | collective-permute-start | bytes 1013768 | tf_op jit(solution)/shard_map/ppermute | solution.py:106
  508.5 32.3 %collective-permute-start.39 = (bf16[3,80,960]{2,1,0:T(8,128)(2,1)S(1)}, bf16[3,80,960]{2,1,0:T(8,128)(2,1)S(1)}, u32[]{:S(2)}, u32[]{:S(2)}) collective-permute-start(bf16[3,80,960]{2,1,0:T(8,128)(2,1)S(1)} %fusion.11), channel_id=1, source_target_pairs={{0,4},{1,5},{2,6},{3,7},{4,0},{5,1},{6,2},{7,3},{8,12},{9,13},{10,... | collective-permute-start | bytes 1382408 | tf_op jit(solution)/shard_map/ppermute | solution.py:106
  520.5 25.1 %collective-permute-start.43 = (bf16[80,960]{1,0:T(8,128)(2,1)S(1)}, bf16[80,960]{1,0:T(8,128)(2,1)S(1)}, u32[]{:S(2)}, u32[]{:S(2)}) collective-permute-start(bf16[80,960]{1,0:T(8,128)(2,1)S(1)} %fusion.15), channel_id=1, source_target_pairs={{0,1},{1,0},{2,3},{3,2},{4,5},{5,4},{6,7},{7,6},{8,9},{9,8},{10,11... | collective-permute-start | bytes 460808 | tf_op jit(solution)/shard_map/ppermute | solution.py:106
  (82 other events, 1149.2 us)

commit v8 on v7

--- a/solution.py
+++ b/solution.py
@@ -281,25 +281,6 @@
     for term in terms[1:]:
         total = total + term.astype(jnp.float32)
     return total.astype(jnp.bfloat16)
-
-
-def reduce_start(keep, away):
-    come = swap(away, ("core", 0))
-    quarter = keep.shape[2] // 2
-    near, far = slice(0, quarter), slice(quarter, 2 * quarter)
-    sends = [
-        add_low(keep[4:, :, far], come[4:, :, far]),
-        add_low(keep[:4, :, far], come[:4, :, far]),
-    ]
-    return sends, (keep[:, :, near], come[:, :, near])
-
-
-def reduce_y(held, x_upper):
-    return swap(total_low(*[part[4:] for part in held], x_upper), slot_bits()[2])
-
-
-def reduce_near(rest):
-    return swap(total_low(*[part[2:] for part in rest]), slot_bits()[1])
 
 
 def reduce_far(rest):
@@ -740,7 +721,7 @@
         specs += [
             pl.BlockSpec(
                 (None, HD, local_rows),
-                lambda head, lead=lead, first=first: (lead, first + head, seq),
+                lambda head, lead=lead, first=first: (lead, first + head, 0),
             )
             for lead in leads
         ]
@@ -928,9 +909,10 @@
 
 
 def feed_body(
-    parts, split, me_ref, a_two_ref, dy_ref, *refs
+    parts, split, chained, me_ref, a_two_ref, dy_ref, *refs
 ):
     count = 4 if split else 6
+    before, refs = (refs[:2], refs[2:]) if chained else (None, refs)
     weight_refs, (out_ref, d_two_ref), grad_refs = (
         refs[:count],
         refs[count : count + 2],
@@ -941,8 +923,8 @@
 
     @pl.when(step == 0)
     def _():
-        out_ref[...] = jnp.zeros_like(out_ref)
-        d_two_ref[...] = jnp.zeros_like(d_two_ref)
+        for place, ref in enumerate((out_ref, d_two_ref)):
+            ref[...] = before[place][...] if chained else jnp.zeros_like(ref)
 
     def rows_of(member):
         if split:
@@ -988,12 +970,12 @@
     return (member + 1) % 2 if single else step // ctx_count
 
 
-def feed_forward(a_two, dy_low, mine, far, rows):
+def feed_forward(a_two, dy_low, mine, far, rows, before=()):
     tokens, width = a_two.shape
     ctx_count = lax.axis_size("ctx")
     blocks = FF // rows
     single = blocks == ctx_count
-    split = splits_rows(rows)
+    split = mine[0].ndim == 4 if isinstance(mine, list) else False
     parts = (ctx_count, single)
     whole = pl.BlockSpec((tokens, width), lambda step, me_ref: (0, 0))
 
@@ -1013,6 +995,7 @@
         weight_args = [*mine, *far]
         half = pl.BlockSpec((2, 3, rows // 2, width), lambda step, me_ref: (step, 0, 0, 0))
         grad_specs = [half, half]
+        blocks = mine[0].shape[0]
         grad_shapes = [jax.ShapeDtypeStruct((blocks, 3, rows // 2, width), jnp.bfloat16)] * 2
     else:
         weight_specs = [weight_spec(member, own) for member in range(3) for own in (True, False)]
@@ -1021,24 +1004,24 @@
         grad_shapes = [jax.ShapeDtypeStruct((blocks, rows, width), jnp.bfloat16)] * 3
     me = jnp.stack([lax.axis_index("core"), lax.axis_index("x")]).astype(jnp.int32)
     return pl.pallas_call(
-        lambda *refs: feed_body(parts, split, *refs),
+        lambda *refs: feed_body(parts, split, bool(before), *refs),
         grid_spec=pltpu.PrefetchScalarGridSpec(
             num_scalar_prefetch=1,
             grid=(blocks // 2 if split else blocks,),
-            in_specs=[whole, whole] + weight_specs,
+            in_specs=[whole] * (2 + len(before)) + weight_specs,
             out_specs=[whole, whole] + grad_specs,
         ),
         out_shape=[jax.ShapeDtypeStruct((tokens, width), jnp.float32)] * 2 + grad_shapes,
         cost_estimate=pl.CostEstimate(
-            flops=18 * tokens * width * FF, bytes_accessed=12 * FF * width, transcendentals=FF * tokens
+            flops=18 * tokens * width * blocks * rows, bytes_accessed=12 * blocks * rows * width,
+            transcendentals=0,
         ),
         compiler_params=pltpu.CompilerParams(vmem_limit_bytes=VMEM_BYTES),
-    )(me, a_two, dy_low, *weight_args)
-
-
-def first_grads(d_qkv, attn_low, a_one, d_resid_low, rows):
+    )(me, a_two, dy_low, *before, *weight_args)
+
+
+def first_grads(d_qkv, attn_low, a_one, d_resid_low, rows, split):
     tokens, width = a_one.shape
-    split = splits_rows(rows)
     early = d_qkv.shape[0] // rows
     blocks = early + attn_low.shape[0] // rows
 
@@ -1105,9 +1088,9 @@
     q_cols = HEADS * HD
     kv_cols = KV * HD
     cut_o = q_cols + 2 * kv_cols
-    split = splits_rows(weight_rows)
     slots = slot_bits()
-    aligned = split and half_rows % 128 == 0
+    aligned = splits_rows(weight_rows) and half_rows % 128 == 0 and seqs == 2
+    split = aligned
     local_index = jnp.arange(local_rows, dtype=jnp.int32)
     pos_here = places(ctx_index * local_rows + local_index, local_rows, ctx_count)
     cosine, sine_part = angle_tables(pos_here, 1.0)
@@ -1186,26 +1169,42 @@
         feed_own = jnp.concatenate([feed_quarter[None], feed_far_z], axis=0)
         joined, feed_own = lax.optimization_barrier((joined, feed_own))
     if aligned:
-        far_z, y_own = swap(joined, slots[0]), swap(joined, slots[2])
-    if split:
+        mine_0, mine_1 = [
+            joined[:, seq * local_rows : (seq + 1) * local_rows] for seq in range(2)
+        ]
+        far_0, own_y_0 = swap(mine_0, slots[0]), swap(mine_0, slots[2])
         feed_near, feed_y = swap(feed_own, slots[1]), swap(feed_own, slots[2])
         feed_x = swap(feed_own, ("x", 0))
-    if aligned:
-        far_z, y_own, feed_near, feed_y, feed_x = lax.optimization_barrier(
-            (far_z, y_own, feed_near, feed_y, feed_x)
+        far_0, own_y_0, feed_near, feed_y, feed_x, mine_1 = lax.optimization_barrier(
+            (far_0, own_y_0, feed_near, feed_y, feed_x, mine_1)
         )
-        near_z = swap(jnp.stack([joined, far_z]), slots[1])
-        y_far = swap(far_z, slots[2])
-    if split:
-        feed_near_y = swap(feed_near, slots[2])
-        x_parts = [swap(feed_near, ("x", 0)), swap(feed_y, ("x", 0))]
-    if aligned:
-        near_z, y_far, feed_near_y, x_parts = lax.optimization_barrier(
-            (near_z, y_far, feed_near_y, x_parts)
+        near_0, far_y_0 = swap(jnp.stack([mine_0, far_0]), slots[1]), swap(far_0, slots[2])
+        far_1, own_y_1 = swap(mine_1, slots[0]), swap(mine_1, slots[2])
+        near_x = swap(feed_near, ("x", 0))
+        near_0, far_y_0, far_1, own_y_1, near_x, feed_y = lax.optimization_barrier(
+            (near_0, far_y_0, far_1, own_y_1, near_x, feed_y)
         )
-        y_near = swap(near_z, slots[2])
-        pairs = [(joined[None], 0), (far_z[None], 0), (near_z, 0), (near_z, 1)]
-        pairs += [(y_own[None], 0), (y_far[None], 0), (y_near, 0), (y_near, 1)]
+        near_y_0 = swap(near_0, slots[2])
+        near_1, far_y_1 = swap(jnp.stack([mine_1, far_1]), slots[1]), swap(far_1, slots[2])
+        y_x = swap(feed_y, ("x", 0))
+        near_y_0, near_1, far_y_1, y_x, feed_near = lax.optimization_barrier(
+            (near_y_0, near_1, far_y_1, y_x, feed_near)
+        )
+        near_y_1 = swap(near_1, slots[2])
+        pairs = [
+            [(own[None], 0), (far_z[None], 0), (near, 0), (near, 1)]
+            + [(own_y[None], 0), (far_y[None], 0), (near_y, 0), (near_y, 1)]
+            for own, far_z, near, own_y, far_y, near_y in (
+                (mine_0, far_0, near_0, own_y_0, far_y_0, near_y_0),
+                (mine_1, far_1, near_1, own_y_1, far_y_1, near_y_1),
+            )
+        ]
+        feed_lower = [
+            jnp.concatenate([feed_own, feed_near], axis=0),
+            jnp.concatenate([feed_x, near_x], axis=0),
+        ]
+        feed_lower_far = [swap(part, ("core", 0)) for part in feed_lower]
+        feed_y_far = [swap(part, ("core", 0)) for part in (feed_y, y_x)]
     else:
         pairs = spread(joined, slots).reshape(ctx_count, 2 * kv_cols, seqs, 2, half_rows)
         pairs = [
@@ -1216,60 +1215,98 @@
                 0,
             )
         ]
-    if split:
-        x_parts = [feed_x] + x_parts + [swap(feed_near_y, ("x", 0))]
-        feed_own = jnp.concatenate([feed_own, feed_near, feed_y, feed_near_y], axis=0)
-        feed_far = swap(feed_own, ("core", 0))
     q_rot = rotate(matmul_t(qkv_rows[:q_cols], a_one), turn).astype(jnp.bfloat16)
     queries = pack((q_rot * SCALE_QK).astype(jnp.bfloat16))
     attended = []
     for seq in range(seqs):
         if aligned:
-            attended.append(attend_slots(queries, pairs, flags, local_rows, seq))
+            attended.append(attend_slots(queries, pairs[seq], flags, local_rows, seq))
+            if seq == 0:
+                attended, feed_near = lax.optimization_barrier((attended, feed_near))
+                feed_near_y = swap(feed_near, slots[2])
         else:
             attended.append(attend(queries, pairs, key_pos, query_pos, local_rows, seq))
-        if split and seq == 0:
-            attended, x_parts, feed_far = lax.optimization_barrier((attended, x_parts, feed_far))
-            feed_x = jnp.concatenate(x_parts, axis=0)
-            mine, far = [feed_own, feed_x], [feed_far, swap(feed_x, ("core", 0))]
     attn_low = jnp.concatenate([unpack(mixed) for mixed, _ in attended], axis=1)
     resid = tokens_in + matmul_c(attn_low, o_rows)
     a_two = (normalize(resid) * gains[1]).astype(jnp.bfloat16)
-    fed, d_two, *feed_grads = feed_forward(a_two, dy_low, mine, far, weight_rows)
+    if aligned:
+        a_two, feed_near_y = lax.optimization_barrier((a_two, feed_near_y))
+        near_y_x = swap(feed_near_y, ("x", 0))
+        near_y_far = swap(feed_near_y, ("core", 0))
+        *sums_fed, keep_lower, away_lower = feed_forward(
+            a_two, dy_low, feed_lower, feed_lower_far, weight_rows
+        )
+        sums_fed, near_y_x = lax.optimization_barrier((sums_fed, near_y_x))
+        near_y_x_far = swap(near_y_x, ("core", 0))
+        come_lower = swap(away_lower, ("core", 0))
+        *sums_fed, keep_upper, away_upper = feed_forward(
+            a_two, dy_low, [feed_y, y_x], feed_y_far, weight_rows, sums_fed
+        )
+        come_upper = swap(away_upper, ("core", 0))
+        fed, d_two, keep_last, away_last = feed_forward(
+            a_two, dy_low, [feed_near_y, near_y_x], [near_y_far, near_y_x_far], weight_rows, sums_fed
+        )
+        come_last = swap(away_last, ("core", 0))
+    else:
+        fed, d_two, *feed_grads = feed_forward(a_two, dy_low, mine, far, weight_rows)
     result = resid + fed
     d_norm_two, d_gain_two = norm_back(resid, d_two, gains[1])
     d_resid = cot_in + d_norm_two
     d_resid_low = d_resid.astype(jnp.bfloat16)
     d_attn = pack(matmul_t(o_rows, d_resid_low).astype(jnp.bfloat16))
-    if split:
-        sends, feed_held = reduce_start(*feed_grads)
-        d_attn, sends = lax.optimization_barrier((d_attn, sends))
-        feed_upper, feed_lower = swap(sends[0], ("x", 0)), swap(sends[1], ("x", 0))
+    if aligned:
+        quarter = weight_rows // 4
+        held_upper, held_last, held_lower = [
+            [(part[:, :, :quarter], part[:, :, quarter:]) for part in parts]
+            for parts in (
+                (keep_upper, come_upper), (keep_last, come_last), (keep_lower, come_lower)
+            )
+        ]
+        send_upper, send_last, send_lower = [
+            total_low(*[far_part for _, far_part in parts])
+            for parts in (held_upper, held_last, held_lower)
+        ]
+        x_upper = swap(send_upper, ("x", 0))
+        y_send = total_low(*[part for part, _ in held_upper], x_upper)
+        d_attn, y_send, send_last, send_lower = lax.optimization_barrier(
+            (d_attn, y_send, send_last, send_lower)
+        )
+        feed_y_come = swap(y_send, slots[2])
+        x_last = swap(send_last, ("x", 0))
+        x_lower = swap(send_lower, ("x", 0))
     d_q, d_pair = [], []
     for seq in range(seqs):
         mixed, log_total = attended[seq]
         if aligned:
             d_queries, *d_slots = attend_slots_back(
-                queries, pairs, flags, mixed, log_total, d_attn, packed_tables, local_rows, seq, (2, 2, 4)
+                queries, pairs[seq], flags, mixed, log_total, d_attn, packed_tables, local_rows, seq, (2, 2, 4)
             )
         else:
             d_queries, *d_slots = attend_back(
                 queries, pairs, key_pos, query_pos, mixed, log_total, d_attn, packed_tables,
                 local_rows, seq, (1,),
             )
-        if split and seq == seqs - 1:
-            d_slots, feed_upper = lax.optimization_barrier((d_slots, feed_upper))
-            feed_y = reduce_y(feed_held, feed_upper)
+        if aligned and seq == 0:
+            d_slots, x_last, feed_y_come = lax.optimization_barrier((d_slots, x_last, feed_y_come))
+            last_y_come = swap(total_low(*[part for part, _ in held_last], x_last), slots[2])
         d_q.append(unpack(d_queries))
         if aligned:
             lower, near_part, upper = d_slots
             y_come = swap(upper, slots[2])
             near_come = swap(add_low(near_part, y_come[2:]), slots[1])
             if seq == seqs - 1:
-                near_come, feed_lower = lax.optimization_barrier((near_come, feed_lower))
+                near_come, x_lower, last_y_come = lax.optimization_barrier(
+                    (near_come, x_lower, last_y_come)
+                )
+                rest = [part for part, _ in held_lower] + [x_lower]
+                feed_near_come = swap(
+                    total_low(*[part[2:] for part in rest], last_y_come), slots[1]
+                )
             far_come = swap(total_low(lower[1], y_come[1], near_come[1]), slots[0])
             if seq == seqs - 1:
-                far_come, feed_y = lax.optimization_barrier((far_come, feed_y))
+                far_come, feed_near_come = lax.optimization_barrier((far_come, feed_near_come))
+                feed_rest = [part[:2] for part in rest] + [feed_y_come, feed_near_come]
+                feed_far = reduce_far(feed_rest)
             total = far_come.astype(jnp.float32)
             for part in (lower, y_come, near_come):
                 total = total + part[0].astype(jnp.float32)
@@ -1290,17 +1327,13 @@
         ],
         axis=0,
     )
-    first_terms = first_grads(d_qkv, attn_low, a_one, d_resid_low, weight_rows)
+    first_terms = first_grads(d_qkv, attn_low, a_one, d_resid_low, weight_rows, split)
     if split:
-        feed_rest = [part[:4] for part in feed_held] + [feed_lower, feed_y]
-        feed_near = reduce_near(feed_rest)
-        first_terms, feed_near = lax.optimization_barrier((first_terms, feed_near))
-        feed_rest = [part[:2] for part in feed_rest] + [feed_near]
-        feed_far = reduce_far(feed_rest)
+        first_terms, feed_far = lax.optimization_barrier((first_terms, feed_far))
         feed_later = {}
 
         def beside(step, value):
-            if step == 2:
+            if step == 0:
                 value, far_come = lax.optimization_barrier((value, feed_far))
                 sums = reduce_end(feed_rest, far_come)
                 sent = jnp.where(

time: 585 us -> 631 us (1.079)
  waiting for transfers between devices: 285 us -> 318 us
  local copies, waits for them, and re-layouts: 48.4 us -> 35.8 us
  Pallas kernels: 117 us -> 128 us
  starting transfers between devices: 53.4 us -> 60.8 us
    ppermute x47 -> x60, waiting for transfers between devices: 285 us -> 318 us  [swap_by(): return lax.ppermute(values, axis, [(i, i ^ offset) for i in range(size)])]
    pallas_call x1 -> x3, Pallas kernels: 37.9 us -> 51 us  [feed_forward(): pl.pallas_call(lambda *refs: feed_body(parts, split, bool(before), *refs)...]
    unnamed x147 -> x175, local copies, waits for them, and re-layouts: 27.4 us -> 18.4 us
    convert_element_type x11 -> x15, other arithmetic: 16.1 us -> 24.5 us  [total_low(): return total.astype(jnp.bfloat16)]
    ppermute x47 -> x60, starting transfers between devices: 53.4 us -> 60.8 us  [swap_by(): return lax.ppermute(values, axis, [(i, i ^ offset) for i in range(size)])]
  transfers between devices with their start and end apart: 47 -> 60, of which waited for: 27 -> 29; matrix products, arithmetic and copies ran while one was open for 12% -> 13% of each run, Pallas kernels for 14% -> 17%
where the time goes in v8:
time: 631 us; the launch traced here: 620 us
  waiting for transfers between devices  318 us (50%)
  Pallas kernels  128 us (20%)
  other arithmetic  62.6 us (10%)
  starting transfers between devices  60.8 us (10%)
  local copies, waits for them, and re-layouts  35.8 us (6%)
  matrix products  12.2 us (2%)
    ppermute x60, waiting for transfers between devices, swap_by(): return lax.ppermute(values, axis, [(i, i ^ offset) for i in range(size)])  318 us
    ppermute x60, starting transfers between devices, swap_by(): return lax.ppermute(values, axis, [(i, i ^ offset) for i in range(size)])  60.8 us
    pallas_call x3, Pallas kernels, feed_forward(): pl.pallas_call(lambda *refs: feed_body(parts, split, bool(before), *refs)...  51 us
    pallas_call x2, Pallas kernels, attend_slots_back(): pl.pallas_call(lambda *refs: attend_slots_back_body(count, *refs), grid=(...  46 us
    convert_element_type x15, other arithmetic, total_low(): return total.astype(jnp.bfloat16)  24.5 us
    unnamed x175, local copies, waits for them, and re-layouts  18.4 us
    pallas_call x2, Pallas kernels, attend_slots(): pl.pallas_call(lambda *refs: attend_slots_body(count, *refs), grid=(KV,),...  17.2 us
  transfers between devices with their start and end apart: 60, of which 29 were waited for; matrix products, arithmetic and copies ran while one was open for 13% of the time, Pallas kernels for 17%

profile of v8, /device:TPU:0, one launch (start us, length us, event | category | flops | bytes accessed | tf_op | source)
XLA Modules:
  0.0 620.3 jit_solution(6474186796729691540)
XLA Ops:
  3.6 14.9 %collective-permute-done = bf16[320,960]{1,0:T(8,128)(2,1)S(1)} collective-permute-done((bf16[320,960]{1,0:T(8,128)(2,1)}, bf16[320,960]{1,0:T(8,128)(2,1)S(1)}, u32[]{:S(2)}, u32[]{:S(2)}) %collective-permute-start) | collective-permute-done | bytes 614432 | tf_op jit(solution)/shard_map/ppermute | solution.py:106
  35.7 7.9 %collective-permute-start.3 = (bf16[2,80,960]{2,1,0:T(8,128)(2,1)S(1)}, bf16[2,80,960]{2,1,0:T(8,128)(2,1)S(1)}, u32[]{:S(2)}, u32[]{:S(2)}) collective-permute-start(bf16[2,80,960]{2,1,0:T(8,128)(2,1)S(1)} %pad_maximum_fusion.19), channel_id=1, source_target_pairs={{0,2},{1,3},{2,0},{3,1},{4,6},{5,7},{6,4},{7,5},{8,10},{9,11},{10,... | collective-permute-start | bytes 921608 | tf_op jit(solution)/shard_map/ppermute | solution.py:106
  43.8 7.0 %collective-permute-done.6 = bf16[2,80,960]{2,1,0:T(8,128)(2,1)S(1)} collective-permute-done((bf16[2,80,960]{2,1,0:T(8,128)(2,1)S(1)}, bf16[2,80,960]{2,1,0:T(8,128)(2,1)S(1)}, u32[]{:S(2)}, u32[]{:S(2)}) %collective-permute-start.6) | collective-permute-done | bytes 307232 | tf_op jit(solution)/shard_map/ppermute | solution.py:106
  50.9 6.8 %collective-permute-done.3 = bf16[2,80,960]{2,1,0:T(8,128)(2,1)S(1)} collective-permute-done((bf16[2,80,960]{2,1,0:T(8,128)(2,1)S(1)}, bf16[2,80,960]{2,1,0:T(8,128)(2,1)S(1)}, u32[]{:S(2)}, u32[]{:S(2)}) %collective-permute-start.3) | collective-permute-done | bytes 307232 | tf_op jit(solution)/shard_map/ppermute | solution.py:106
  58.7 12.7 %collective-permute-done.7 = bf16[4,80,960]{2,1,0:T(8,128)(2,1)S(1)} collective-permute-done((bf16[4,80,960]{2,1,0:T(8,128)(2,1)S(1)}, bf16[4,80,960]{2,1,0:T(8,128)(2,1)S(1)}, u32[]{:S(2)}, u32[]{:S(2)}) %collective-permute-start.7) | collective-permute-done | bytes 614432 | tf_op jit(solution)/shard_map/ppermute | solution.py:106
  80.1 7.2 %shard_map.152 = bf16[8,320,960]{2,1,0:T(8,128)(2,1)} custom-call(s32[2]{0:T(128)S(1)} %pad_add_fusion.me_ref, bf16[8,80,960]{2,1,0:T(8,128)(2,1)S(1)} %pad_maximum_fusion.1.refs_0_, bf16[8,80,960]{2,1,0:T(8,128)(2,1)S(1)} %pad_maximum_fusion.2.refs_1_, bf16[8,80,960]{2,1,0:T(8,128)(2,1)} %collective-permute-done.8.refs_2_, ...), custom_call_target="tpu_custom_call" | custom-call | bytes 9830400 | tf_op jit(solution)/shard_map/pallas_call | solution.py:385
  89.8 12.2 %collective-permute-done.10 = bf16[1,3,80,960]{3,2,1,0:T(8,128)(2,1)} collective-permute-done((bf16[1,3,80,960]{3,2,1,0:T(8,128)(2,1)S(1)}, bf16[1,3,80,960]{3,2,1,0:T(8,128)(2,1)}, u32[]{:S(2)}, u32[]{:S(2)}) %collective-permute-start.10) | collective-permute-done | bytes 460832 | tf_op jit(solution)/shard_map/ppermute | solution.py:106
  114.1 22.8 %collective-permute-done.11 = bf16[640,256]{1,0:T(8,128)(2,1)S(1)} collective-permute-done((bf16[640,256]{1,0:T(8,128)(2,1)S(1)}, bf16[640,256]{1,0:T(8,128)(2,1)S(1)}, u32[]{:S(2)}, u32[]{:S(2)}) %collective-permute-start.11) | collective-permute-done | bytes 327712 | tf_op jit(solution)/shard_map/ppermute | solution.py:106
  145.4 6.9 %collective-permute-done.17 = bf16[640,256]{1,0:T(8,128)(2,1)S(1)} collective-permute-done((bf16[640,256]{1,0:T(8,128)(2,1)S(1)}, bf16[640,256]{1,0:T(8,128)(2,1)S(1)}, u32[]{:S(2)}, u32[]{:S(2)}) %collective-permute-start.17) | collective-permute-done | bytes 327712 | tf_op jit(solution)/shard_map/ppermute | solution.py:106
  152.3 4.3 collective-permute-done.19
  156.6 4.8 collective-permute-done.18
  172.2 15.5 %collective-permute-done.23 = bf16[640,256]{1,0:T(8,128)(2,1)S(1)} collective-permute-done((bf16[640,256]{1,0:T(8,128)(2,1)S(1)}, bf16[640,256]{1,0:T(8,128)(2,1)S(1)}, u32[]{:S(2)}, u32[]{:S(2)}) %collective-permute-start.23) | collective-permute-done | bytes 327712 | tf_op jit(solution)/shard_map/ppermute | solution.py:106
  193.2 8.5 %shard_map.153 = (bf16[960,256]{1,0:T(8,128)(2,1)S(1)}, f32[1,5,1,768]{3,2,1,0:T(1,128)S(1)}) custom-call(s32[8]{0:T(128)S(1)} %compare_convert_fusion.refs_0_, bf16[960,512]{1,0:T(8,128)(2,1)S(1)} %bitcast.168, bf16[1,640,256]{2,1,0:T(8,128)(2,1)S(1)} %get-tuple-element.230.refs_2_.refs_10_, bf16[1,640,256]{2,1,0:T(8,128)(2,1)S(1)} %bitcast.178, ...), custom_call_target="tpu_custom_call" | custom-call | flops 251658240 | bytes 1048576 | tf_op jit(solution)/shard_map/pallas_call | solution.py:735
  203.0 8.7 %shard_map.154 = (bf16[960,256]{1,0:T(8,128)(2,1)S(1)}, f32[1,5,1,768]{3,2,1,0:T(1,128)S(1)}) custom-call(s32[8]{0:T(128)S(1)} %compare_convert_fusion.refs_0_, bf16[960,512]{1,0:T(8,128)(2,1)S(1)} %bitcast.169, bf16[1,640,256]{2,1,0:T(8,128)(2,1)S(1)} %bitcast.173, bf16[1,640,256]{2,1,0:T(8,128)(2,1)S(1)} %bitcast.183, ...), custom_call_target="tpu_custom_call" | custom-call | flops 251658240 | bytes 1048576 | tf_op jit(solution)/shard_map/pallas_call | solution.py:735
  215.5 11.4 %collective-permute-done.26.refs_5_ = bf16[2,3,80,960]{3,2,1,0:T(8,128)(2,1)} collective-permute-done((bf16[2,3,80,960]{3,2,1,0:T(8,128)(2,1)}, bf16[2,3,80,960]{3,2,1,0:T(8,128)(2,1)}, u32[]{:S(2)}, u32[]{:S(2)}) %collective-permute-start.26) | collective-permute-done | bytes 921632 | tf_op jit(solution)/shard_map/ppermute | solution.py:106
  227.5 22.1 %shard_map.155 = (f32[512,960]{1,0:T(8,128)}, f32[512,960]{1,0:T(8,128)}, bf16[4,3,160,960]{3,2,1,0:T(8,128)(2,1)}, bf16[4,3,160,960]{3,2,1,0:T(8,128)(2,1)}) custom-call(s32[2]{0:T(128)S(1)} %pad_add_fusion.1.refs_0_, bf16[512,960]{1,0:T(8,128)(2,1)S(1)} %multiply_convert_fusion.refs_1_, bf16[512,960]{1,0:T(8,128)(2,1)S(1)} %convert_element_type.452.refs_2_, ...), custom_call_target="tpu_custom_call" | custom-call | flops 11324620800 | bytes 14745600 | tf_op jit(solution)/shard_map/pallas_call | solution.py:1006
  251.3 14.5 %shard_map.156 = (f32[512,960]{1,0:T(8,128)}, f32[512,960]{1,0:T(8,128)}, bf16[2,3,160,960]{3,2,1,0:T(8,128)(2,1)}, bf16[2,3,160,960]{3,2,1,0:T(8,128)(2,1)}) custom-call(s32[2]{0:T(128)S(1)} %pad_add_fusion.1.refs_0_, bf16[512,960]{1,0:T(8,128)(2,1)S(1)} %multiply_convert_fusion.refs_1_, bf16[512,960]{1,0:T(8,128)(2,1)S(1)} %convert_element_type.452.refs_2_, ...), custom_call_target="tpu_custom_call" | custom-call | flops 5662310400 | bytes 7372800 | tf_op jit(solution)/shard_map/pallas_call | solution.py:1006
  267.6 14.4 %shard_map.157 = (f32[512,960]{1,0:T(8,128)}, f32[512,960]{1,0:T(8,128)}, bf16[2,3,160,960]{3,2,1,0:T(8,128)(2,1)}, bf16[2,3,160,960]{3,2,1,0:T(8,128)(2,1)}) custom-call(s32[2]{0:T(128)S(1)} %pad_add_fusion.1.refs_0_, bf16[512,960]{1,0:T(8,128)(2,1)S(1)} %multiply_convert_fusion.refs_1_, bf16[512,960]{1,0:T(8,128)(2,1)S(1)} %convert_element_type.452.refs_2_, ...), custom_call_target="tpu_custom_call" | custom-call | flops 5662310400 | bytes 7372800 | tf_op jit(solution)/shard_map/pallas_call | solution.py:1006
  291.8 4.5 fusion.47
  301.2 13.8 %collective-permute-done.35 = bf16[2,3,80,960]{3,2,1,0:T(8,128)(2,1)S(1)} collective-permute-done((bf16[2,3,80,960]{3,2,1,0:T(8,128)(2,1)S(1)}, bf16[2,3,80,960]{3,2,1,0:T(8,128)(2,1)S(1)}, u32[]{:S(2)}, u32[]{:S(2)}) %collective-permute-start.35) | collective-permute-done | bytes 921632 | tf_op jit(solution)/shard_map/ppermute | solution.py:106
  321.7 23.0 %shard_map.159 = (bf16[960,256]{1,0:T(8,128)(2,1)S(1)}, bf16[2,5,2,128,128]{4,3,2,1,0:T(8,128)(2,1)S(1)}, bf16[2,5,2,128,128]{4,3,2,1,0:T(8,128)(2,1)S(1)}, bf16[4,5,2,128,128]{4,3,2,1,0:T(8,128)(2,1)}) custom-call(s32[8]{0:T(128)S(1)} %compare_convert_fusion.refs_0_, bf16[960,512]{1,0:T(8,128)(2,1)S(1)} %bitcast.170, bf16[1,640,256]{2,1,0:T(8,128)(2,1)S(1)} %bitcast.175, ...), custom_call_target="tpu_custom_call" | custom-call | flops 251658240 | bytes 1048576 | tf_op jit(solution)/shard_map/pallas_call | solution.py:770
  348.8 22.9 %shard_map.158 = (bf16[960,256]{1,0:T(8,128)(2,1)S(1)}, bf16[2,5,2,128,128]{4,3,2,1,0:T(8,128)(2,1)S(1)}, bf16[2,5,2,128,128]{4,3,2,1,0:T(8,128)(2,1)S(1)}, bf16[4,5,2,128,128]{4,3,2,1,0:T(8,128)(2,1)}) custom-call(s32[8]{0:T(128)S(1)} %compare_convert_fusion.refs_0_, bf16[960,512]{1,0:T(8,128)(2,1)S(1)} %bitcast.171, ...), custom_call_target="tpu_custom_call" | custom-call | flops 251658240 | bytes 1048576 | tf_op jit(solution)/shard_map/pallas_call | solution.py:770
  371.8 24.2 %collective-permute-done.39 = bf16[2,3,80,960]{3,2,1,0:T(8,128)(2,1)S(1)} collective-permute-done((bf16[2,3,80,960]{3,2,1,0:T(8,128)(2,1)}, bf16[2,3,80,960]{3,2,1,0:T(8,128)(2,1)S(1)}, u32[]{:S(2)}, u32[]{:S(2)}) %collective-permute-start.39) | collective-permute-done | bytes 921632 | tf_op jit(solution)/shard_map/ppermute | solution.py:106
  400.9 45.3 %collective-permute-done.46 = bf16[2,3,80,960]{3,2,1,0:T(8,128)(2,1)S(1)} collective-permute-done((bf16[2,3,80,960]{3,2,1,0:T(8,128)(2,1)S(1)}, bf16[2,3,80,960]{3,2,1,0:T(8,128)(2,1)S(1)}, u32[]{:S(2)}, u32[]{:S(2)}) %collective-permute-start.46) | collective-permute-done | bytes 921632 | tf_op jit(solution)/shard_map/ppermute | solution.py:106
  455.3 34.9 %collective-permute-done.47 = bf16[5,2,128,128]{3,2,1,0:T(8,128)(2,1)} collective-permute-done((bf16[5,2,128,128]{3,2,1,0:T(8,128)(2,1)S(1)}, bf16[5,2,128,128]{3,2,1,0:T(8,128)(2,1)}, u32[]{:S(2)}, u32[]{:S(2)}) %collective-permute-start.47) | collective-permute-done | bytes 327712 | tf_op jit(solution)/shard_map/ppermute | solution.py:106
  500.7 18.6 %collective-permute-done.42 = bf16[5,2,128,128]{3,2,1,0:T(8,128)(2,1)S(1)} collective-permute-done((bf16[5,2,128,128]{3,2,1,0:T(8,128)(2,1)S(1)}, bf16[5,2,128,128]{3,2,1,0:T(8,128)(2,1)S(1)}, u32[]{:S(2)}, u32[]{:S(2)}) %collective-permute-start.42) | collective-permute-done | bytes 327712 | tf_op jit(solution)/shard_map/ppermute | solution.py:106
  527.0 7.1 %shard_map.160 = (bf16[8,1,160,960]{3,2,1,0:T(8,128)(2,1)}, bf16[8,1,160,960]{3,2,1,0:T(8,128)(2,1)}) custom-call(s32[2]{0:T(128)S(1)} %pad_add_fusion.me_ref, bf16[1600,512]{1,0:T(8,128)(2,1)S(1)} %pad_maximum_fusion.qkv_ref, bf16[960,512]{1,0:T(8,128)(2,1)S(1)} %copy-done.30, bf16[512,960]{1,0:T(8,128)(2,1)S(1)} %copy-done.22, bf16[512,960]{1,0:T(8,128)(2,1)S(1)} %copy-done.19), custom_call_target="tpu_custom_call" | custom-call | flops 2516582400 | bytes 4915200 | tf_op jit(solution)/shard_map/pallas_call | solution.py:1050
  539.7 4.6 multiply_reduce_fusion.1
  551.8 14.4 %collective-permute-done.54 = bf16[2,2,80,960]{3,2,1,0:T(8,128)(2,1)S(1)} collective-permute-done((bf16[2,2,80,960]{3,2,1,0:T(8,128)(2,1)S(1)}, bf16[2,2,80,960]{3,2,1,0:T(8,128)(2,1)S(1)}, u32[]{:S(2)}, u32[]{:S(2)}) %collective-permute-start.54) | collective-permute-done | bytes 614432 | tf_op jit(solution)/shard_map/ppermute | solution.py:106
  569.9 13.4 %collective-permute-done.55 = bf16[2,80,960]{2,1,0:T(8,128)(2,1)S(1)} collective-permute-done((bf16[2,80,960]{2,1,0:T(8,128)(2,1)S(1)}, bf16[2,80,960]{2,1,0:T(8,128)(2,1)S(1)}, u32[]{:S(2)}, u32[]{:S(2)}) %collective-permute-start.55) | collective-permute-done | bytes 307232 | tf_op jit(solution)/shard_map/ppermute | solution.py:106
  589.7 7.6 %collective-permute-done.53 = bf16[96,960]{1,0:T(8,128)(2,1)S(1)} collective-permute-done((bf16[96,960]{1,0:T(8,128)(2,1)S(1)}, bf16[96,960]{1,0:T(8,128)(2,1)S(1)}, u32[]{:S(2)}, u32[]{:S(2)}) %collective-permute-start.53) | collective-permute-done | bytes 184352 | tf_op jit(solution)/shard_map/ppermute | solution.py:106
  599.2 9.7 %collective-permute-done.58 = bf16[176,960]{1,0:T(8,128)(2,1)S(1)} collective-permute-done((bf16[176,960]{1,0:T(8,128)(2,1)S(1)}, bf16[176,960]{1,0:T(8,128)(2,1)S(1)}, u32[]{:S(2)}, u32[]{:S(2)}) %collective-permute-start.58) | collective-permute-done | bytes 337952 | tf_op jit(solution)/shard_map/ppermute | solution.py:106
  (406 shorter events, 170.9 us)
Async XLA Ops:
  77.3 24.7 %collective-permute-start.10 = (bf16[1,3,80,960]{3,2,1,0:T(8,128)(2,1)S(1)}, bf16[1,3,80,960]{3,2,1,0:T(8,128)(2,1)}, u32[]{:S(2)}, u32[]{:S(2)}) collective-permute-start(bf16[1,3,80,960]{3,2,1,0:T(8,128)(2,1)S(1)} %bitcast.232), channel_id=1, source_target_pairs={{0,4},{1,5},{2,6},{3,7},{4,0},{5,1},{6,2},{7,3},{8,12},{9,13},{10,... | collective-permute-start | bytes 1382408 | tf_op jit(solution)/shard_map/ppermute | solution.py:106
  107.6 31.3 %collective-permute-start.15 = (bf16[2,3,80,960]{3,2,1,0:T(8,128)(2,1)S(1)}, bf16[2,3,80,960]{3,2,1,0:T(8,128)(2,1)S(1)}, u32[]{:S(2)}, u32[]{:S(2)}) collective-permute-start(bf16[2,3,80,960]{3,2,1,0:T(8,128)(2,1)S(1)} %copy-done.43), channel_id=1, source_target_pairs={{0,16},{16,0},{1,17},{17,1},{2,18},{18,2},{3,19},{19,3},{4,20},{20... | collective-permute-start | bytes 2764808 | tf_op jit(solution)/shard_map/ppermute | solution.py:106
  109.1 29.8 %collective-permute-start.14 = (bf16[2,3,80,960]{3,2,1,0:T(8,128)(2,1)S(1)}, bf16[2,3,80,960]{3,2,1,0:T(8,128)(2,1)S(1)}, u32[]{:S(2)}, u32[]{:S(2)}) collective-permute-start(bf16[2,3,80,960]{3,2,1,0:T(8,128)(2,1)S(1)} %copy-done.43), channel_id=1, source_target_pairs={{0,1},{1,0},{2,3},{3,2},{4,5},{5,4},{6,7},{7,6},{8,9},{9,8},{10,11... | collective-permute-start | bytes 2764808 | tf_op jit(solution)/shard_map/ppermute | solution.py:106
  109.6 29.6 %collective-permute-start.13 = (bf16[2,3,80,960]{3,2,1,0:T(8,128)(2,1)S(1)}, bf16[2,3,80,960]{3,2,1,0:T(8,128)(2,1)}, u32[]{:S(2)}, u32[]{:S(2)}) collective-permute-start(bf16[2,3,80,960]{3,2,1,0:T(8,128)(2,1)S(1)} %copy-done.43), channel_id=1, source_target_pairs={{0,2},{1,3},{2,0},{3,1},{4,6},{5,7},{6,4},{7,5},{8,10},{9,11},{10,... | collective-permute-start | bytes 2764808 | tf_op jit(solution)/shard_map/ppermute | solution.py:106
  109.7 27.2 %collective-permute-start.11 = (bf16[640,256]{1,0:T(8,128)(2,1)S(1)}, bf16[640,256]{1,0:T(8,128)(2,1)S(1)}, u32[]{:S(2)}, u32[]{:S(2)}) collective-permute-start(bf16[640,256]{1,0:T(8,128)(2,1)S(1)} %get-tuple-element.231), channel_id=1, source_target_pairs={{0,4},{1,5},{2,6},{3,7},{4,0},{5,1},{6,2},{7,3},{8,12},{9,13},{10,... | collective-permute-start | bytes 983048 | tf_op jit(solution)/shard_map/ppermute | solution.py:106
  112.6 26.3 %collective-permute-start.12 = (bf16[640,256]{1,0:T(8,128)(2,1)S(1)}, bf16[640,256]{1,0:T(8,128)(2,1)S(1)}, u32[]{:S(2)}, u32[]{:S(2)}) collective-permute-start(bf16[640,256]{1,0:T(8,128)(2,1)S(1)} %get-tuple-element.231), channel_id=1, source_target_pairs={{0,1},{1,0},{2,3},{3,2},{4,5},{5,4},{6,7},{7,6},{8,9},{9,8},{10,11... | collective-permute-start | bytes 983048 | tf_op jit(solution)/shard_map/ppermute | solution.py:106
  139.2 22.9 %collective-permute-start.20 = (bf16[2,3,80,960]{3,2,1,0:T(8,128)(2,1)}, bf16[2,3,80,960]{3,2,1,0:T(8,128)(2,1)S(1)}, u32[]{:S(2)}, u32[]{:S(2)}) collective-permute-start(bf16[2,3,80,960]{3,2,1,0:T(8,128)(2,1)} %collective-permute-done.13), channel_id=1, source_target_pairs={{0,16},{16,0},{1,17},{17,1},{2,18},{18,2},{3,19},{19,3},{4,20},{20... | collective-permute-start | bytes 2764808 | tf_op jit(solution)/shard_map/ppermute | solution.py:106
  162.1 25.6 %collective-permute-start.24 = (bf16[2,3,80,960]{3,2,1,0:T(8,128)(2,1)S(1)}, bf16[2,3,80,960]{3,2,1,0:T(8,128)(2,1)S(1)}, u32[]{:S(2)}, u32[]{:S(2)}) collective-permute-start(bf16[2,3,80,960]{3,2,1,0:T(8,128)(2,1)S(1)} %collective-permute-done.14.refs_5_), channel_id=1, source_target_pairs={{0,16},{16,0},{1,17},{17,1},{2,18},{18,2},{3,19},{19,3},{4,20},{20... | collective-permute-start | bytes 2764808 | tf_op jit(solution)/shard_map/ppermute | solution.py:106
  164.0 23.8 %collective-permute-start.22 = (bf16[2,640,256]{2,1,0:T(8,128)(2,1)S(1)}, bf16[2,640,256]{2,1,0:T(8,128)(2,1)S(1)}, u32[]{:S(2)}, u32[]{:S(2)}) collective-permute-start(bf16[2,640,256]{2,1,0:T(8,128)(2,1)S(1)} %pad_maximum_fusion.13), channel_id=1, source_target_pairs={{0,2},{1,3},{2,0},{3,1},{4,6},{5,7},{6,4},{7,5},{8,10},{9,11},{10,... | collective-permute-start | bytes 1966088 | tf_op jit(solution)/shard_map/ppermute | solution.py:106
  172.1 54.8 %collective-permute-start.28 = (bf16[4,3,80,960]{3,2,1,0:T(8,128)(2,1)S(1)}, bf16[4,3,80,960]{3,2,1,0:T(8,128)(2,1)}, u32[]{:S(2)}, u32[]{:S(2)}) collective-permute-start(bf16[4,3,80,960]{3,2,1,0:T(8,128)(2,1)S(1)} %constant_dynamic-update-slice_fusion.4.refs_4_), channel_id=1, source_target_pairs={{0,8},{8,0},{1,9},{9,1},{2,10},{10,2},{3,11},{11,3},{4,12},{12,4},... | collective-permute-start | bytes 5529608 | tf_op jit(solution)/shard_map/ppermute | solution.py:106
  190.6 36.9 %collective-permute-start.27 = (bf16[4,3,80,960]{3,2,1,0:T(8,128)(2,1)S(1)}, bf16[4,3,80,960]{3,2,1,0:T(8,128)(2,1)}, u32[]{:S(2)}, u32[]{:S(2)}) collective-permute-start(bf16[4,3,80,960]{3,2,1,0:T(8,128)(2,1)S(1)} %constant_dynamic-update-slice_fusion.2.refs_3_), channel_id=1, source_target_pairs={{0,8},{8,0},{1,9},{9,1},{2,10},{10,2},{3,11},{11,3},{4,12},{12,4},... | collective-permute-start | bytes 5529608 | tf_op jit(solution)/shard_map/ppermute | solution.py:106
  192.6 58.7 %collective-permute-start.30 = (bf16[2,3,80,960]{3,2,1,0:T(8,128)(2,1)S(1)}, bf16[2,3,80,960]{3,2,1,0:T(8,128)(2,1)}, u32[]{:S(2)}, u32[]{:S(2)}) collective-permute-start(bf16[2,3,80,960]{3,2,1,0:T(8,128)(2,1)S(1)} %collective-permute-done.14.refs_5_), channel_id=1, source_target_pairs={{0,8},{8,0},{1,9},{9,1},{2,10},{10,2},{3,11},{11,3},{4,12},{12,4},... | collective-permute-start | bytes 2764808 | tf_op jit(solution)/shard_map/ppermute | solution.py:106
  193.1 58.2 %collective-permute-start.31 = (bf16[2,3,80,960]{3,2,1,0:T(8,128)(2,1)S(1)}, bf16[2,3,80,960]{3,2,1,0:T(8,128)(2,1)}, u32[]{:S(2)}, u32[]{:S(2)}) collective-permute-start(bf16[2,3,80,960]{3,2,1,0:T(8,128)(2,1)S(1)} %collective-permute-done.24.refs_6_), channel_id=1, source_target_pairs={{0,8},{8,0},{1,9},{9,1},{2,10},{10,2},{3,11},{11,3},{4,12},{12,4},... | collective-permute-start | bytes 2764808 | tf_op jit(solution)/shard_map/ppermute | solution.py:106
  202.5 24.4 %collective-permute-start.26 = (bf16[2,3,80,960]{3,2,1,0:T(8,128)(2,1)}, bf16[2,3,80,960]{3,2,1,0:T(8,128)(2,1)}, u32[]{:S(2)}, u32[]{:S(2)}) collective-permute-start(bf16[2,3,80,960]{3,2,1,0:T(8,128)(2,1)} %collective-permute-done.13), channel_id=1, source_target_pairs={{0,1},{1,0},{2,3},{3,2},{4,5},{5,4},{6,7},{7,6},{8,9},{9,8},{10,11... | collective-permute-start | bytes 2764808 | tf_op jit(solution)/shard_map/ppermute | solution.py:106
  226.9 39.5 %collective-permute-start.32 = (bf16[2,3,80,960]{3,2,1,0:T(8,128)(2,1)}, bf16[2,3,80,960]{3,2,1,0:T(8,128)(2,1)S(1)}, u32[]{:S(2)}, u32[]{:S(2)}) collective-permute-start(bf16[2,3,80,960]{3,2,1,0:T(8,128)(2,1)} %collective-permute-done.26.refs_5_), channel_id=1, source_target_pairs={{0,8},{8,0},{1,9},{9,1},{2,10},{10,2},{3,11},{11,3},{4,12},{12,4},... | collective-permute-start | bytes 2764808 | tf_op jit(solution)/shard_map/ppermute | solution.py:106
  226.9 24.4 %collective-permute-start.29 = (bf16[2,3,80,960]{3,2,1,0:T(8,128)(2,1)}, bf16[2,3,80,960]{3,2,1,0:T(8,128)(2,1)S(1)}, u32[]{:S(2)}, u32[]{:S(2)}) collective-permute-start(bf16[2,3,80,960]{3,2,1,0:T(8,128)(2,1)} %collective-permute-done.26.refs_5_), channel_id=1, source_target_pairs={{0,16},{16,0},{1,17},{17,1},{2,18},{18,2},{3,19},{19,3},{4,20},{20... | collective-permute-start | bytes 2764808 | tf_op jit(solution)/shard_map/ppermute | solution.py:106
  265.8 23.3 %collective-permute-start.34 = (bf16[2,3,160,960]{3,2,1,0:T(8,128)(2,1)}, bf16[2,3,160,960]{3,2,1,0:T(8,128)(2,1)}, u32[]{:S(2)}, u32[]{:S(2)}) collective-permute-start(bf16[2,3,160,960]{3,2,1,0:T(8,128)(2,1)} %get-tuple-element.133), channel_id=1, source_target_pairs={{0,8},{8,0},{1,9},{9,1},{2,10},{10,2},{3,11},{11,3},{4,12},{12,4},... | collective-permute-start | bytes 5529608 | tf_op jit(solution)/shard_map/ppermute | solution.py:106
  266.3 51.4 %collective-permute-start.37 = (bf16[4,3,160,960]{3,2,1,0:T(8,128)(2,1)}, bf16[4,3,160,960]{3,2,1,0:T(8,128)(2,1)}, u32[]{:S(2)}, u32[]{:S(2)}) collective-permute-start(bf16[4,3,160,960]{3,2,1,0:T(8,128)(2,1)} %get-tuple-element.137), channel_id=1, source_target_pairs={{0,8},{8,0},{1,9},{9,1},{2,10},{10,2},{3,11},{11,3},{4,12},{12,4},... | collective-permute-start | bytes 11059208 | tf_op jit(solution)/shard_map/ppermute | solution.py:106
  291.2 23.8 %collective-permute-start.35 = (bf16[2,3,80,960]{3,2,1,0:T(8,128)(2,1)S(1)}, bf16[2,3,80,960]{3,2,1,0:T(8,128)(2,1)S(1)}, u32[]{:S(2)}, u32[]{:S(2)}) collective-permute-start(bf16[2,3,80,960]{3,2,1,0:T(8,128)(2,1)S(1)} %add_convert_fusion.5), channel_id=1, source_target_pairs={{0,16},{16,0},{1,17},{17,1},{2,18},{18,2},{3,19},{19,3},{4,20},{20... | collective-permute-start | bytes 2764808 | tf_op jit(solution)/shard_map/ppermute | solution.py:106
  344.8 55.7 %collective-permute-start.43 = (bf16[4,5,2,128,128]{4,3,2,1,0:T(8,128)(2,1)}, bf16[4,5,2,128,128]{4,3,2,1,0:T(8,128)(2,1)S(1)}, u32[]{:S(2)}, u32[]{:S(2)}) collective-permute-start(bf16[4,5,2,128,128]{4,3,2,1,0:T(8,128)(2,1)} %get-tuple-element.151), channel_id=1, source_target_pairs={{0,1},{1,0},{2,3},{3,2},{4,5},{5,4},{6,7},{7,6},{8,9},{9,8},{10,11... | collective-permute-start | bytes 3932168 | tf_op jit(solution)/shard_map/ppermute | solution.py:106
  345.3 26.5 %collective-permute-start.38 = (bf16[2,3,80,960]{3,2,1,0:T(8,128)(2,1)}, bf16[2,3,80,960]{3,2,1,0:T(8,128)(2,1)}, u32[]{:S(2)}, u32[]{:S(2)}) collective-permute-start(bf16[2,3,80,960]{3,2,1,0:T(8,128)(2,1)} %add_convert_fusion.3), channel_id=1, source_target_pairs={{0,16},{16,0},{1,17},{17,1},{2,18},{18,2},{3,19},{19,3},{4,20},{20... | collective-permute-start | bytes 2764808 | tf_op jit(solution)/shard_map/ppermute | solution.py:106
  345.8 50.2 %collective-permute-start.39 = (bf16[2,3,80,960]{3,2,1,0:T(8,128)(2,1)}, bf16[2,3,80,960]{3,2,1,0:T(8,128)(2,1)S(1)}, u32[]{:S(2)}, u32[]{:S(2)}) collective-permute-start(bf16[2,3,80,960]{3,2,1,0:T(8,128)(2,1)} %add_convert_fusion.4), channel_id=1, source_target_pairs={{0,1},{1,0},{2,3},{3,2},{4,5},{5,4},{6,7},{7,6},{8,9},{9,8},{10,11... | collective-permute-start | bytes 2764808 | tf_op jit(solution)/shard_map/ppermute | solution.py:106
  347.3 98.9 %collective-permute-start.45 = (bf16[4,3,80,960]{3,2,1,0:T(8,128)(2,1)}, bf16[4,3,80,960]{3,2,1,0:T(8,128)(2,1)S(1)}, u32[]{:S(2)}, u32[]{:S(2)}) collective-permute-start(bf16[4,3,80,960]{3,2,1,0:T(8,128)(2,1)} %add_convert_fusion), channel_id=1, source_target_pairs={{0,16},{16,0},{1,17},{17,1},{2,18},{18,2},{3,19},{19,3},{4,20},{20... | collective-permute-start | bytes 5529608 | tf_op jit(solution)/shard_map/ppermute | solution.py:106
  396.0 54.2 %collective-permute-start.40 = (bf16[4,5,2,128,128]{4,3,2,1,0:T(8,128)(2,1)}, bf16[4,5,2,128,128]{4,3,2,1,0:T(8,128)(2,1)S(1)}, u32[]{:S(2)}, u32[]{:S(2)}) collective-permute-start(bf16[4,5,2,128,128]{4,3,2,1,0:T(8,128)(2,1)} %get-tuple-element.148), channel_id=1, source_target_pairs={{0,1},{1,0},{2,3},{3,2},{4,5},{5,4},{6,7},{7,6},{8,9},{9,8},{10,11... | collective-permute-start | bytes 3932168 | tf_op jit(solution)/shard_map/ppermute | solution.py:106
  398.9 47.3 %collective-permute-start.46 = (bf16[2,3,80,960]{3,2,1,0:T(8,128)(2,1)S(1)}, bf16[2,3,80,960]{3,2,1,0:T(8,128)(2,1)S(1)}, u32[]{:S(2)}, u32[]{:S(2)}) collective-permute-start(bf16[2,3,80,960]{3,2,1,0:T(8,128)(2,1)S(1)} %add_convert_fusion.2), channel_id=1, source_target_pairs={{0,1},{1,0},{2,3},{3,2},{4,5},{5,4},{6,7},{7,6},{8,9},{9,8},{10,11... | collective-permute-start | bytes 2764808 | tf_op jit(solution)/shard_map/ppermute | solution.py:106
  400.7 45.6 %collective-permute-start.44 = (bf16[2,5,2,128,128]{4,3,2,1,0:T(8,128)(2,1)S(1)}, bf16[2,5,2,128,128]{4,3,2,1,0:T(8,128)(2,1)S(1)}, u32[]{:S(2)}, u32[]{:S(2)}) collective-permute-start(bf16[2,5,2,128,128]{4,3,2,1,0:T(8,128)(2,1)S(1)} %add_convert_fusion.9), channel_id=1, source_target_pairs={{0,2},{1,3},{2,0},{3,1},{4,6},{5,7},{6,4},{7,5},{8,10},{9,11},{10,... | collective-permute-start | bytes 1966088 | tf_op jit(solution)/shard_map/ppermute | solution.py:106
  450.0 40.1 %collective-permute-start.48 = (bf16[2,3,80,960]{3,2,1,0:T(8,128)(2,1)}, bf16[2,3,80,960]{3,2,1,0:T(8,128)(2,1)}, u32[]{:S(2)}, u32[]{:S(2)}) collective-permute-start(bf16[2,3,80,960]{3,2,1,0:T(8,128)(2,1)} %add_convert_fusion.1), channel_id=1, source_target_pairs={{0,2},{1,3},{2,0},{3,1},{4,6},{5,7},{6,4},{7,5},{8,10},{9,11},{10,... | collective-permute-start | bytes 2764808 | tf_op jit(solution)/shard_map/ppermute | solution.py:106
  451.4 41.1 %collective-permute-start.41 = (bf16[2,5,2,128,128]{4,3,2,1,0:T(8,128)(2,1)}, bf16[2,5,2,128,128]{4,3,2,1,0:T(8,128)(2,1)}, u32[]{:S(2)}, u32[]{:S(2)}) collective-permute-start(bf16[2,5,2,128,128]{4,3,2,1,0:T(8,128)(2,1)} %add_convert_fusion.10), channel_id=1, source_target_pairs={{0,2},{1,3},{2,0},{3,1},{4,6},{5,7},{6,4},{7,5},{8,10},{9,11},{10,... | collective-permute-start | bytes 1966088 | tf_op jit(solution)/shard_map/ppermute | solution.py:106
  453.4 36.8 %collective-permute-start.47 = (bf16[5,2,128,128]{3,2,1,0:T(8,128)(2,1)S(1)}, bf16[5,2,128,128]{3,2,1,0:T(8,128)(2,1)}, u32[]{:S(2)}, u32[]{:S(2)}) collective-permute-start(bf16[5,2,128,128]{3,2,1,0:T(8,128)(2,1)S(1)} %fusion.13), channel_id=1, source_target_pairs={{0,4},{1,5},{2,6},{3,7},{4,0},{5,1},{6,2},{7,3},{8,12},{9,13},{10,... | collective-permute-start | bytes 983048 | tf_op jit(solution)/shard_map/ppermute | solution.py:106
  493.6 25.7 %collective-permute-start.42 = (bf16[5,2,128,128]{3,2,1,0:T(8,128)(2,1)S(1)}, bf16[5,2,128,128]{3,2,1,0:T(8,128)(2,1)S(1)}, u32[]{:S(2)}, u32[]{:S(2)}) collective-permute-start(bf16[5,2,128,128]{3,2,1,0:T(8,128)(2,1)S(1)} %fusion.12), channel_id=1, source_target_pairs={{0,4},{1,5},{2,6},{3,7},{4,0},{5,1},{6,2},{7,3},{8,12},{9,13},{10,... | collective-permute-start | bytes 983048 | tf_op jit(solution)/shard_map/ppermute | solution.py:106
  497.7 36.4 %collective-permute-start.49 = (bf16[3,80,960]{2,1,0:T(8,128)(2,1)}, bf16[3,80,960]{2,1,0:T(8,128)(2,1)}, u32[]{:S(2)}, u32[]{:S(2)}) collective-permute-start(bf16[3,80,960]{2,1,0:T(8,128)(2,1)} %fusion.11), channel_id=1, source_target_pairs={{0,4},{1,5},{2,6},{3,7},{4,0},{5,1},{6,2},{7,3},{8,12},{9,13},{10,... | collective-permute-start | bytes 1382408 | tf_op jit(solution)/shard_map/ppermute | solution.py:106
  569.4 29.1 %collective-permute-start.57 = (bf16[2,80,960]{2,1,0:T(8,128)(2,1)S(1)}, bf16[2,80,960]{2,1,0:T(8,128)(2,1)S(1)}, u32[]{:S(2)}, u32[]{:S(2)}) collective-permute-start(bf16[2,80,960]{2,1,0:T(8,128)(2,1)S(1)} %fusion.7), channel_id=1, source_target_pairs={{0,16},{16,0},{1,17},{17,1},{2,18},{18,2},{3,19},{19,3},{4,20},{20... | collective-permute-start | bytes 921608 | tf_op jit(solution)/shard_map/ppermute | solution.py:106
  (111 other events, 1709.2 us)

commit v9 on v8

--- a/solution.py
+++ b/solution.py
@@ -1204,7 +1204,6 @@
             jnp.concatenate([feed_x, near_x], axis=0),
         ]
         feed_lower_far = [swap(part, ("core", 0)) for part in feed_lower]
-        feed_y_far = [swap(part, ("core", 0)) for part in (feed_y, y_x)]
     else:
         pairs = spread(joined, slots).reshape(ctx_count, 2 * kv_cols, seqs, 2, half_rows)
         pairs = [
@@ -1232,21 +1231,23 @@
     if aligned:
         a_two, feed_near_y = lax.optimization_barrier((a_two, feed_near_y))
         near_y_x = swap(feed_near_y, ("x", 0))
-        near_y_far = swap(feed_near_y, ("core", 0))
+        upper_own = jnp.concatenate([feed_y, feed_near_y], axis=0)
+        upper_far = swap(upper_own, ("core", 0))
         *sums_fed, keep_lower, away_lower = feed_forward(
             a_two, dy_low, feed_lower, feed_lower_far, weight_rows
         )
-        sums_fed, near_y_x = lax.optimization_barrier((sums_fed, near_y_x))
-        near_y_x_far = swap(near_y_x, ("core", 0))
+        sums_fed, near_y_x, upper_far = lax.optimization_barrier((sums_fed, near_y_x, upper_far))
+        upper_x = jnp.concatenate([y_x, near_y_x], axis=0)
         come_lower = swap(away_lower, ("core", 0))
-        *sums_fed, keep_upper, away_upper = feed_forward(
-            a_two, dy_low, [feed_y, y_x], feed_y_far, weight_rows, sums_fed
+        fed, d_two, keep_upper, away_upper = feed_forward(
+            a_two,
+            dy_low,
+            [upper_own, upper_x],
+            [upper_far, swap(upper_x, ("core", 0))],
+            weight_rows,
+            sums_fed,
         )
         come_upper = swap(away_upper, ("core", 0))
-        fed, d_two, keep_last, away_last = feed_forward(
-            a_two, dy_low, [feed_near_y, near_y_x], [near_y_far, near_y_x_far], weight_rows, sums_fed
-        )
-        come_last = swap(away_last, ("core", 0))
     else:
         fed, d_two, *feed_grads = feed_forward(a_two, dy_low, mine, far, weight_rows)
     result = resid + fed
@@ -1256,24 +1257,16 @@
     d_attn = pack(matmul_t(o_rows, d_resid_low).astype(jnp.bfloat16))
     if aligned:
         quarter = weight_rows // 4
-        held_upper, held_last, held_lower = [
+        held_upper, held_lower = [
             [(part[:, :, :quarter], part[:, :, quarter:]) for part in parts]
-            for parts in (
-                (keep_upper, come_upper), (keep_last, come_last), (keep_lower, come_lower)
-            )
+            for parts in ((keep_upper, come_upper), (keep_lower, come_lower))
         ]
-        send_upper, send_last, send_lower = [
-            total_low(*[far_part for _, far_part in parts])
-            for parts in (held_upper, held_last, held_lower)
+        send_upper, send_lower = [
+            total_low(*[far_part for _, far_part in parts]) for parts in (held_upper, held_lower)
         ]
+        x_lower = swap(send_lower, ("x", 0))
+        d_attn, send_upper = lax.optimization_barrier((d_attn, send_upper))
         x_upper = swap(send_upper, ("x", 0))
-        y_send = total_low(*[part for part, _ in held_upper], x_upper)
-        d_attn, y_send, send_last, send_lower = lax.optimization_barrier(
-            (d_attn, y_send, send_last, send_lower)
-        )
-        feed_y_come = swap(y_send, slots[2])
-        x_last = swap(send_last, ("x", 0))
-        x_lower = swap(send_lower, ("x", 0))
     d_q, d_pair = [], []
     for seq in range(seqs):
         mixed, log_total = attended[seq]
@@ -1287,26 +1280,20 @@
                 local_rows, seq, (1,),
             )
         if aligned and seq == 0:
-            d_slots, x_last, feed_y_come = lax.optimization_barrier((d_slots, x_last, feed_y_come))
-            last_y_come = swap(total_low(*[part for part, _ in held_last], x_last), slots[2])
+            d_slots, d_attn, x_lower = lax.optimization_barrier((d_slots, d_attn, x_lower))
+        if aligned and seq == 1:
+            d_slots, x_upper = lax.optimization_barrier((d_slots, x_upper))
+            feed_y_come = swap(total_low(*[part for part, _ in held_upper], x_upper), slots[2])
         d_q.append(unpack(d_queries))
         if aligned:
             lower, near_part, upper = d_slots
             y_come = swap(upper, slots[2])
             near_come = swap(add_low(near_part, y_come[2:]), slots[1])
-            if seq == seqs - 1:
-                near_come, x_lower, last_y_come = lax.optimization_barrier(
-                    (near_come, x_lower, last_y_come)
-                )
-                rest = [part for part, _ in held_lower] + [x_lower]
-                feed_near_come = swap(
-                    total_low(*[part[2:] for part in rest], last_y_come), slots[1]
-                )
             far_come = swap(total_low(lower[1], y_come[1], near_come[1]), slots[0])
-            if seq == seqs - 1:
-                far_come, feed_near_come = lax.optimization_barrier((far_come, feed_near_come))
-                feed_rest = [part[:2] for part in rest] + [feed_y_come, feed_near_come]
-                feed_far = reduce_far(feed_rest)
+            if seq == 1:
+                far_come, feed_y_come = lax.optimization_barrier((far_come, feed_y_come))
+                rest = [part for part, _ in held_lower] + [x_lower, feed_y_come]
+                feed_near_come = swap(total_low(*[part[2:] for part in rest]), slots[1])
             total = far_come.astype(jnp.float32)
             for part in (lower, y_come, near_come):
                 total = total + part[0].astype(jnp.float32)
@@ -1329,11 +1316,13 @@
     )
     first_terms = first_grads(d_qkv, attn_low, a_one, d_resid_low, weight_rows, split)
     if split:
-        first_terms, feed_far = lax.optimization_barrier((first_terms, feed_far))
+        first_terms, feed_near_come = lax.optimization_barrier((first_terms, feed_near_come))
+        feed_rest = [part[:2] for part in rest] + [feed_near_come]
+        feed_far = reduce_far(feed_rest)
         feed_later = {}
 
         def beside(step, value):
-            if step == 0:
+            if step == 2:
                 value, far_come = lax.optimization_barrier((value, feed_far))
                 sums = reduce_end(feed_rest, far_come)
                 sent = jnp.where(

time: 631 us -> 596 us (0.945)
  waiting for transfers between devices: 318 us -> 288 us
  local copies, waits for them, and re-layouts: 35.8 us -> 42.7 us
    ppermute x60 -> x55, waiting for transfers between devices: 318 us -> 288 us  [swap_by(): return lax.ppermute(values, axis, [(i, i ^ offset) for i in range(size)])]
    unnamed x175 -> x173, local copies, waits for them, and re-layouts: 18.4 us -> 24.8 us
    pallas_call x3 -> x2, Pallas kernels: 51 us -> 45 us  [feed_forward(): pl.pallas_call(lambda *refs: feed_body(parts, split, bool(before), *refs)...]
    convert_element_type x15 -> x13, other arithmetic: 24.5 us -> 21.5 us  [total_low(): return total.astype(jnp.bfloat16)]
    ppermute x60 -> x55, starting transfers between devices: 60.8 us -> 58.2 us  [swap_by(): return lax.ppermute(values, axis, [(i, i ^ offset) for i in range(size)])]
  transfers between devices with their start and end apart: 60 -> 55, of which waited for: 29 -> 33; matrix products, arithmetic and copies ran while one was open for 13% -> 14% of each run, Pallas kernels for 17% -> 21%
where the time goes in v9:
time: 596 us; the launch traced here: 586 us
  waiting for transfers between devices  288 us (48%)
  Pallas kernels  122 us (20%)
  other arithmetic  59.6 us (10%)
  starting transfers between devices  58.2 us (10%)
  local copies, waits for them, and re-layouts  42.7 us (7%)
  matrix products  12.2 us (2%)
    ppermute x55, waiting for transfers between devices, swap_by(): return lax.ppermute(values, axis, [(i, i ^ offset) for i in range(size)])  288 us
    ppermute x55, starting transfers between devices, swap_by(): return lax.ppermute(values, axis, [(i, i ^ offset) for i in range(size)])  58.2 us
    pallas_call x2, Pallas kernels, attend_slots_back(): pl.pallas_call(lambda *refs: attend_slots_back_body(count, *refs), grid=(...  45.8 us
    pallas_call x2, Pallas kernels, feed_forward(): pl.pallas_call(lambda *refs: feed_body(parts, split, bool(before), *refs)...  45 us
    unnamed x173, local copies, waits for them, and re-layouts  24.8 us
    convert_element_type x13, other arithmetic, total_low(): return total.astype(jnp.bfloat16)  21.5 us
    pallas_call x2, Pallas kernels, attend_slots(): pl.pallas_call(lambda *refs: attend_slots_body(count, *refs), grid=(KV,),...  17.1 us
  transfers between devices with their start and end apart: 55, of which 33 were waited for; matrix products, arithmetic and copies ran while one was open for 14% of the time, Pallas kernels for 21%

profile of v9, /device:TPU:0, one launch (start us, length us, event | category | flops | bytes accessed | tf_op | source)
XLA Modules:
  0.0 585.9 jit_solution(3291895700679217723)
XLA Ops:
  3.6 14.9 %collective-permute-done = bf16[320,960]{1,0:T(8,128)(2,1)S(1)} collective-permute-done((bf16[320,960]{1,0:T(8,128)(2,1)}, bf16[320,960]{1,0:T(8,128)(2,1)S(1)}, u32[]{:S(2)}, u32[]{:S(2)}) %collective-permute-start) | collective-permute-done | bytes 614432 | tf_op jit(solution)/shard_map/ppermute | solution.py:106
  35.7 7.9 %collective-permute-start.3 = (bf16[2,80,960]{2,1,0:T(8,128)(2,1)S(1)}, bf16[2,80,960]{2,1,0:T(8,128)(2,1)S(1)}, u32[]{:S(2)}, u32[]{:S(2)}) collective-permute-start(bf16[2,80,960]{2,1,0:T(8,128)(2,1)S(1)} %pad_maximum_fusion.19), channel_id=1, source_target_pairs={{0,2},{1,3},{2,0},{3,1},{4,6},{5,7},{6,4},{7,5},{8,10},{9,11},{10,... | collective-permute-start | bytes 921608 | tf_op jit(solution)/shard_map/ppermute | solution.py:106
  43.8 6.9 %collective-permute-done.6 = bf16[2,80,960]{2,1,0:T(8,128)(2,1)S(1)} collective-permute-done((bf16[2,80,960]{2,1,0:T(8,128)(2,1)S(1)}, bf16[2,80,960]{2,1,0:T(8,128)(2,1)S(1)}, u32[]{:S(2)}, u32[]{:S(2)}) %collective-permute-start.6) | collective-permute-done | bytes 307232 | tf_op jit(solution)/shard_map/ppermute | solution.py:106
  50.9 6.8 %collective-permute-done.3 = bf16[2,80,960]{2,1,0:T(8,128)(2,1)S(1)} collective-permute-done((bf16[2,80,960]{2,1,0:T(8,128)(2,1)S(1)}, bf16[2,80,960]{2,1,0:T(8,128)(2,1)S(1)}, u32[]{:S(2)}, u32[]{:S(2)}) %collective-permute-start.3) | collective-permute-done | bytes 307232 | tf_op jit(solution)/shard_map/ppermute | solution.py:106
  58.6 12.7 %collective-permute-done.7 = bf16[4,80,960]{2,1,0:T(8,128)(2,1)S(1)} collective-permute-done((bf16[4,80,960]{2,1,0:T(8,128)(2,1)S(1)}, bf16[4,80,960]{2,1,0:T(8,128)(2,1)S(1)}, u32[]{:S(2)}, u32[]{:S(2)}) %collective-permute-start.7) | collective-permute-done | bytes 614432 | tf_op jit(solution)/shard_map/ppermute | solution.py:106
  80.1 7.2 %shard_map.152 = bf16[8,320,960]{2,1,0:T(8,128)(2,1)} custom-call(s32[2]{0:T(128)S(1)} %pad_add_fusion.me_ref, bf16[8,80,960]{2,1,0:T(8,128)(2,1)S(1)} %pad_maximum_fusion.1.refs_0_, bf16[8,80,960]{2,1,0:T(8,128)(2,1)S(1)} %pad_maximum_fusion.2.refs_1_, bf16[8,80,960]{2,1,0:T(8,128)(2,1)} %collective-permute-done.8.refs_2_, ...), custom_call_target="tpu_custom_call" | custom-call | bytes 9830400 | tf_op jit(solution)/shard_map/pallas_call | solution.py:385
  89.8 12.3 %collective-permute-done.10 = bf16[1,3,80,960]{3,2,1,0:T(8,128)(2,1)} collective-permute-done((bf16[1,3,80,960]{3,2,1,0:T(8,128)(2,1)S(1)}, bf16[1,3,80,960]{3,2,1,0:T(8,128)(2,1)}, u32[]{:S(2)}, u32[]{:S(2)}) %collective-permute-start.10) | collective-permute-done | bytes 460832 | tf_op jit(solution)/shard_map/ppermute | solution.py:106
  114.1 22.9 %collective-permute-done.11 = bf16[640,256]{1,0:T(8,128)(2,1)S(1)} collective-permute-done((bf16[640,256]{1,0:T(8,128)(2,1)S(1)}, bf16[640,256]{1,0:T(8,128)(2,1)S(1)}, u32[]{:S(2)}, u32[]{:S(2)}) %collective-permute-start.11) | collective-permute-done | bytes 327712 | tf_op jit(solution)/shard_map/ppermute | solution.py:106
  156.7 4.7 collective-permute-done.18
  169.8 17.5 %collective-permute-done.23 = bf16[640,256]{1,0:T(8,128)(2,1)S(1)} collective-permute-done((bf16[640,256]{1,0:T(8,128)(2,1)S(1)}, bf16[640,256]{1,0:T(8,128)(2,1)S(1)}, u32[]{:S(2)}, u32[]{:S(2)}) %collective-permute-start.23) | collective-permute-done | bytes 327712 | tf_op jit(solution)/shard_map/ppermute | solution.py:106
  190.0 8.4 %shard_map.153 = (bf16[960,256]{1,0:T(8,128)(2,1)S(1)}, f32[1,5,1,768]{3,2,1,0:T(1,128)S(1)}) custom-call(s32[8]{0:T(128)S(1)} %compare_convert_fusion.refs_0_, bf16[960,512]{1,0:T(8,128)(2,1)S(1)} %bitcast.173, bf16[1,640,256]{2,1,0:T(8,128)(2,1)S(1)} %get-tuple-element.222.refs_2_.refs_10_, bf16[1,640,256]{2,1,0:T(8,128)(2,1)S(1)} %bitcast.183, ...), custom_call_target="tpu_custom_call" | custom-call | flops 251658240 | bytes 1048576 | tf_op jit(solution)/shard_map/pallas_call | solution.py:735
  200.7 8.7 %shard_map.154 = (bf16[960,256]{1,0:T(8,128)(2,1)S(1)}, f32[1,5,1,768]{3,2,1,0:T(1,128)S(1)}) custom-call(s32[8]{0:T(128)S(1)} %compare_convert_fusion.refs_0_, bf16[960,512]{1,0:T(8,128)(2,1)S(1)} %bitcast.174, bf16[1,640,256]{2,1,0:T(8,128)(2,1)S(1)} %bitcast.178, bf16[1,640,256]{2,1,0:T(8,128)(2,1)S(1)} %bitcast.188, ...), custom_call_target="tpu_custom_call" | custom-call | flops 251658240 | bytes 1048576 | tf_op jit(solution)/shard_map/pallas_call | solution.py:735
  213.1 9.2 %collective-permute-done.26 = bf16[2,3,80,960]{3,2,1,0:T(8,128)(2,1)} collective-permute-done((bf16[2,3,80,960]{3,2,1,0:T(8,128)(2,1)S(1)}, bf16[2,3,80,960]{3,2,1,0:T(8,128)(2,1)}, u32[]{:S(2)}, u32[]{:S(2)}) %collective-permute-start.26) | collective-permute-done | bytes 921632 | tf_op jit(solution)/shard_map/ppermute | solution.py:106
  225.6 21.6 %shard_map.155 = (f32[512,960]{1,0:T(8,128)}, f32[512,960]{1,0:T(8,128)}, bf16[4,3,160,960]{3,2,1,0:T(8,128)(2,1)}, bf16[4,3,160,960]{3,2,1,0:T(8,128)(2,1)}) custom-call(s32[2]{0:T(128)S(1)} %pad_add_fusion.1.refs_0_, bf16[512,960]{1,0:T(8,128)(2,1)S(1)} %multiply_convert_fusion.refs_1_, bf16[512,960]{1,0:T(8,128)(2,1)S(1)} %convert_element_type.437.refs_2_, ...), custom_call_target="tpu_custom_call" | custom-call | flops 11324620800 | bytes 14745600 | tf_op jit(solution)/shard_map/pallas_call | solution.py:1006
  249.3 5.4 collective-permute-done.31.refs_8_
  255.9 23.4 %shard_map.156 = (f32[512,960]{1,0:T(8,128)}, f32[512,960]{1,0:T(8,128)}, bf16[4,3,160,960]{3,2,1,0:T(8,128)(2,1)}, bf16[4,3,160,960]{3,2,1,0:T(8,128)(2,1)}) custom-call(s32[2]{0:T(128)S(1)} %pad_add_fusion.1.refs_0_, bf16[512,960]{1,0:T(8,128)(2,1)S(1)} %multiply_convert_fusion.refs_1_, bf16[512,960]{1,0:T(8,128)(2,1)S(1)} %convert_element_type.437.refs_2_, ...), custom_call_target="tpu_custom_call" | custom-call | flops 11324620800 | bytes 14745600 | tf_op jit(solution)/shard_map/pallas_call | solution.py:1006
  282.6 4.4 fusion.45
  307.1 22.8 %shard_map.157 = (bf16[960,256]{1,0:T(8,128)(2,1)S(1)}, bf16[2,5,2,128,128]{4,3,2,1,0:T(8,128)(2,1)S(1)}, bf16[2,5,2,128,128]{4,3,2,1,0:T(8,128)(2,1)S(1)}, bf16[4,5,2,128,128]{4,3,2,1,0:T(8,128)(2,1)}) custom-call(s32[8]{0:T(128)S(1)} %compare_convert_fusion.refs_0_, bf16[960,512]{1,0:T(8,128)(2,1)S(1)} %bitcast.175, ...), custom_call_target="tpu_custom_call" | custom-call | flops 251658240 | bytes 1048576 | tf_op jit(solution)/shard_map/pallas_call | solution.py:770
  330.7 8.9 %collective-permute-done.34 = bf16[4,3,80,960]{3,2,1,0:T(8,128)(2,1)} collective-permute-done((bf16[4,3,80,960]{3,2,1,0:T(8,128)(2,1)}, bf16[4,3,80,960]{3,2,1,0:T(8,128)(2,1)}, u32[]{:S(2)}, u32[]{:S(2)}) %collective-permute-start.34) | collective-permute-done | bytes 1843232 | tf_op jit(solution)/shard_map/ppermute | solution.py:106
  340.7 23.0 %shard_map.158 = (bf16[960,256]{1,0:T(8,128)(2,1)S(1)}, bf16[2,5,2,128,128]{4,3,2,1,0:T(8,128)(2,1)S(1)}, bf16[2,5,2,128,128]{4,3,2,1,0:T(8,128)(2,1)S(1)}, bf16[4,5,2,128,128]{4,3,2,1,0:T(8,128)(2,1)}) custom-call(s32[8]{0:T(128)S(1)} %compare_convert_fusion.refs_0_, bf16[960,512]{1,0:T(8,128)(2,1)S(1)} %bitcast.176, bf16[1,640,256]{2,1,0:T(8,128)(2,1)S(1)} %bitcast.180, ...), custom_call_target="tpu_custom_call" | custom-call | flops 251658240 | bytes 1048576 | tf_op jit(solution)/shard_map/pallas_call | solution.py:770
  363.7 17.6 %collective-permute-done.38 = bf16[4,3,80,960]{3,2,1,0:T(8,128)(2,1)} collective-permute-done((bf16[4,3,80,960]{3,2,1,0:T(8,128)(2,1)}, bf16[4,3,80,960]{3,2,1,0:T(8,128)(2,1)}, u32[]{:S(2)}, u32[]{:S(2)}) %collective-permute-start.38) | collective-permute-done | bytes 1843232 | tf_op jit(solution)/shard_map/ppermute | solution.py:106
  389.2 24.0 %collective-permute-done.39 = bf16[4,5,2,128,128]{4,3,2,1,0:T(8,128)(2,1)S(1)} collective-permute-done((bf16[4,5,2,128,128]{4,3,2,1,0:T(8,128)(2,1)}, bf16[4,5,2,128,128]{4,3,2,1,0:T(8,128)(2,1)S(1)}, u32[]{:S(2)}, u32[]{:S(2)}) %collective-permute-start.39) | collective-permute-done | bytes 1310752 | tf_op jit(solution)/shard_map/ppermute | solution.py:106
  418.3 16.2 %collective-permute-done.40 = bf16[2,5,2,128,128]{4,3,2,1,0:T(8,128)(2,1)S(1)} collective-permute-done((bf16[2,5,2,128,128]{4,3,2,1,0:T(8,128)(2,1)S(1)}, bf16[2,5,2,128,128]{4,3,2,1,0:T(8,128)(2,1)S(1)}, u32[]{:S(2)}, u32[]{:S(2)}) %collective-permute-start.40) | collective-permute-done | bytes 655392 | tf_op jit(solution)/shard_map/ppermute | solution.py:106
  436.4 17.7 %collective-permute-done.42 = bf16[4,3,80,960]{3,2,1,0:T(8,128)(2,1)} collective-permute-done((bf16[4,3,80,960]{3,2,1,0:T(8,128)(2,1)}, bf16[4,3,80,960]{3,2,1,0:T(8,128)(2,1)}, u32[]{:S(2)}, u32[]{:S(2)}) %collective-permute-start.42) | collective-permute-done | bytes 1843232 | tf_op jit(solution)/shard_map/ppermute | solution.py:106
  465.5 7.1 %shard_map.159 = (bf16[8,1,160,960]{3,2,1,0:T(8,128)(2,1)}, bf16[8,1,160,960]{3,2,1,0:T(8,128)(2,1)}) custom-call(s32[2]{0:T(128)S(1)} %pad_add_fusion.me_ref, bf16[1600,512]{1,0:T(8,128)(2,1)S(1)} %pad_maximum_fusion.qkv_ref, bf16[960,512]{1,0:T(8,128)(2,1)S(1)} %copy-done.30, bf16[512,960]{1,0:T(8,128)(2,1)S(1)} %copy-done.22, bf16[512,960]{1,0:T(8,128)(2,1)S(1)} %copy-done.19), custom_call_target="tpu_custom_call" | custom-call | flops 2516582400 | bytes 4915200 | tf_op jit(solution)/shard_map/pallas_call | solution.py:1050
  472.6 10.1 %collective-permute-done.43 = bf16[2,3,80,960]{3,2,1,0:T(8,128)(2,1)} collective-permute-done((bf16[2,3,80,960]{3,2,1,0:T(8,128)(2,1)}, bf16[2,3,80,960]{3,2,1,0:T(8,128)(2,1)}, u32[]{:S(2)}, u32[]{:S(2)}) %collective-permute-start.43) | collective-permute-done | bytes 921632 | tf_op jit(solution)/shard_map/ppermute | solution.py:106
  488.3 4.6 multiply_reduce_fusion.1
  498.7 13.2 %collective-permute-done.49 = bf16[2,2,80,960]{3,2,1,0:T(8,128)(2,1)S(1)} collective-permute-done((bf16[2,2,80,960]{3,2,1,0:T(8,128)(2,1)S(1)}, bf16[2,2,80,960]{3,2,1,0:T(8,128)(2,1)S(1)}, u32[]{:S(2)}, u32[]{:S(2)}) %collective-permute-start.49) | collective-permute-done | bytes 614432 | tf_op jit(solution)/shard_map/ppermute | solution.py:106
  519.8 10.2 %collective-permute-done.50 = bf16[2,80,960]{2,1,0:T(8,128)(2,1)S(1)} collective-permute-done((bf16[2,80,960]{2,1,0:T(8,128)(2,1)S(1)}, bf16[2,80,960]{2,1,0:T(8,128)(2,1)S(1)}, u32[]{:S(2)}, u32[]{:S(2)}) %collective-permute-start.50) | collective-permute-done | bytes 307232 | tf_op jit(solution)/shard_map/ppermute | solution.py:106
  532.0 18.3 %collective-permute-done.47 = bf16[3,80,960]{2,1,0:T(8,128)(2,1)S(1)} collective-permute-done((bf16[3,80,960]{2,1,0:T(8,128)(2,1)S(1)}, bf16[3,80,960]{2,1,0:T(8,128)(2,1)S(1)}, u32[]{:S(2)}, u32[]{:S(2)}) %collective-permute-start.47) | collective-permute-done | bytes 460832 | tf_op jit(solution)/shard_map/ppermute | solution.py:106
  554.4 8.6 %collective-permute-done.48 = bf16[96,960]{1,0:T(8,128)(2,1)S(1)} collective-permute-done((bf16[96,960]{1,0:T(8,128)(2,1)S(1)}, bf16[96,960]{1,0:T(8,128)(2,1)S(1)}, u32[]{:S(2)}, u32[]{:S(2)}) %collective-permute-start.48) | collective-permute-done | bytes 184352 | tf_op jit(solution)/shard_map/ppermute | solution.py:106
  565.0 9.7 %collective-permute-done.53 = bf16[176,960]{1,0:T(8,128)(2,1)S(1)} collective-permute-done((bf16[176,960]{1,0:T(8,128)(2,1)S(1)}, bf16[176,960]{1,0:T(8,128)(2,1)S(1)}, u32[]{:S(2)}, u32[]{:S(2)}) %collective-permute-start.53) | collective-permute-done | bytes 337952 | tf_op jit(solution)/shard_map/ppermute | solution.py:106
  (395 shorter events, 176.3 us)
Async XLA Ops:
  35.7 22.0 %collective-permute-start.3 = (bf16[2,80,960]{2,1,0:T(8,128)(2,1)S(1)}, bf16[2,80,960]{2,1,0:T(8,128)(2,1)S(1)}, u32[]{:S(2)}, u32[]{:S(2)}) collective-permute-start(bf16[2,80,960]{2,1,0:T(8,128)(2,1)S(1)} %pad_maximum_fusion.19), channel_id=1, source_target_pairs={{0,2},{1,3},{2,0},{3,1},{4,6},{5,7},{6,4},{7,5},{8,10},{9,11},{10,... | collective-permute-start | bytes 921608 | tf_op jit(solution)/shard_map/ppermute | solution.py:106
  50.8 20.5 %collective-permute-start.7 = (bf16[4,80,960]{2,1,0:T(8,128)(2,1)S(1)}, bf16[4,80,960]{2,1,0:T(8,128)(2,1)S(1)}, u32[]{:S(2)}, u32[]{:S(2)}) collective-permute-start(bf16[4,80,960]{2,1,0:T(8,128)(2,1)S(1)} %pad_maximum_fusion.9), channel_id=1, source_target_pairs={{0,2},{1,3},{2,0},{3,1},{4,6},{5,7},{6,4},{7,5},{8,10},{9,11},{10,... | collective-permute-start | bytes 1843208 | tf_op jit(solution)/shard_map/ppermute | solution.py:106
  77.4 24.7 %collective-permute-start.10 = (bf16[1,3,80,960]{3,2,1,0:T(8,128)(2,1)S(1)}, bf16[1,3,80,960]{3,2,1,0:T(8,128)(2,1)}, u32[]{:S(2)}, u32[]{:S(2)}) collective-permute-start(bf16[1,3,80,960]{3,2,1,0:T(8,128)(2,1)S(1)} %bitcast.237), channel_id=1, source_target_pairs={{0,4},{1,5},{2,6},{3,7},{4,0},{5,1},{6,2},{7,3},{8,12},{9,13},{10,... | collective-permute-start | bytes 1382408 | tf_op jit(solution)/shard_map/ppermute | solution.py:106
  107.7 31.3 %collective-permute-start.15 = (bf16[2,3,80,960]{3,2,1,0:T(8,128)(2,1)S(1)}, bf16[2,3,80,960]{3,2,1,0:T(8,128)(2,1)S(1)}, u32[]{:S(2)}, u32[]{:S(2)}) collective-permute-start(bf16[2,3,80,960]{3,2,1,0:T(8,128)(2,1)S(1)} %copy-done.41), channel_id=1, source_target_pairs={{0,16},{16,0},{1,17},{17,1},{2,18},{18,2},{3,19},{19,3},{4,20},{20... | collective-permute-start | bytes 2764808 | tf_op jit(solution)/shard_map/ppermute | solution.py:106
  109.1 29.8 %collective-permute-start.14 = (bf16[2,3,80,960]{3,2,1,0:T(8,128)(2,1)S(1)}, bf16[2,3,80,960]{3,2,1,0:T(8,128)(2,1)S(1)}, u32[]{:S(2)}, u32[]{:S(2)}) collective-permute-start(bf16[2,3,80,960]{3,2,1,0:T(8,128)(2,1)S(1)} %copy-done.41), channel_id=1, source_target_pairs={{0,1},{1,0},{2,3},{3,2},{4,5},{5,4},{6,7},{7,6},{8,9},{9,8},{10,11... | collective-permute-start | bytes 2764808 | tf_op jit(solution)/shard_map/ppermute | solution.py:106
  109.6 29.5 %collective-permute-start.13 = (bf16[2,3,80,960]{3,2,1,0:T(8,128)(2,1)S(1)}, bf16[2,3,80,960]{3,2,1,0:T(8,128)(2,1)S(1)}, u32[]{:S(2)}, u32[]{:S(2)}) collective-permute-start(bf16[2,3,80,960]{3,2,1,0:T(8,128)(2,1)S(1)} %copy-done.41), channel_id=1, source_target_pairs={{0,2},{1,3},{2,0},{3,1},{4,6},{5,7},{6,4},{7,5},{8,10},{9,11},{10,... | collective-permute-start | bytes 2764808 | tf_op jit(solution)/shard_map/ppermute | solution.py:106
  109.7 27.3 %collective-permute-start.11 = (bf16[640,256]{1,0:T(8,128)(2,1)S(1)}, bf16[640,256]{1,0:T(8,128)(2,1)S(1)}, u32[]{:S(2)}, u32[]{:S(2)}) collective-permute-start(bf16[640,256]{1,0:T(8,128)(2,1)S(1)} %get-tuple-element.223), channel_id=1, source_target_pairs={{0,4},{1,5},{2,6},{3,7},{4,0},{5,1},{6,2},{7,3},{8,12},{9,13},{10,... | collective-permute-start | bytes 983048 | tf_op jit(solution)/shard_map/ppermute | solution.py:106
  112.6 26.3 %collective-permute-start.12 = (bf16[640,256]{1,0:T(8,128)(2,1)S(1)}, bf16[640,256]{1,0:T(8,128)(2,1)S(1)}, u32[]{:S(2)}, u32[]{:S(2)}) collective-permute-start(bf16[640,256]{1,0:T(8,128)(2,1)S(1)} %get-tuple-element.223), channel_id=1, source_target_pairs={{0,1},{1,0},{2,3},{3,2},{4,5},{5,4},{6,7},{7,6},{8,9},{9,8},{10,11... | collective-permute-start | bytes 983048 | tf_op jit(solution)/shard_map/ppermute | solution.py:106
  139.2 23.0 %collective-permute-start.20 = (bf16[2,3,80,960]{3,2,1,0:T(8,128)(2,1)S(1)}, bf16[2,3,80,960]{3,2,1,0:T(8,128)(2,1)S(1)}, u32[]{:S(2)}, u32[]{:S(2)}) collective-permute-start(bf16[2,3,80,960]{3,2,1,0:T(8,128)(2,1)S(1)} %collective-permute-done.13), channel_id=1, source_target_pairs={{0,16},{16,0},{1,17},{17,1},{2,18},{18,2},{3,19},{19,3},{4,20},{20... | collective-permute-start | bytes 2764808 | tf_op jit(solution)/shard_map/ppermute | solution.py:106
  139.8 22.4 %collective-permute-start.16 = (bf16[2,640,256]{2,1,0:T(8,128)(2,1)S(1)}, bf16[2,640,256]{2,1,0:T(8,128)(2,1)S(1)}, u32[]{:S(2)}, u32[]{:S(2)}) collective-permute-start(bf16[2,640,256]{2,1,0:T(8,128)(2,1)S(1)} %pad_maximum_fusion.12), channel_id=1, source_target_pairs={{0,2},{1,3},{2,0},{3,1},{4,6},{5,7},{6,4},{7,5},{8,10},{9,11},{10,... | collective-permute-start | bytes 1966088 | tf_op jit(solution)/shard_map/ppermute | solution.py:106
  162.1 25.2 %collective-permute-start.24 = (bf16[2,3,80,960]{3,2,1,0:T(8,128)(2,1)S(1)}, bf16[2,3,80,960]{3,2,1,0:T(8,128)(2,1)S(1)}, u32[]{:S(2)}, u32[]{:S(2)}) collective-permute-start(bf16[2,3,80,960]{3,2,1,0:T(8,128)(2,1)S(1)} %collective-permute-done.14), channel_id=1, source_target_pairs={{0,16},{16,0},{1,17},{17,1},{2,18},{18,2},{3,19},{19,3},{4,20},{20... | collective-permute-start | bytes 2764808 | tf_op jit(solution)/shard_map/ppermute | solution.py:106
  163.7 23.7 %collective-permute-start.22 = (bf16[2,640,256]{2,1,0:T(8,128)(2,1)S(1)}, bf16[2,640,256]{2,1,0:T(8,128)(2,1)S(1)}, u32[]{:S(2)}, u32[]{:S(2)}) collective-permute-start(bf16[2,640,256]{2,1,0:T(8,128)(2,1)S(1)} %pad_maximum_fusion.13), channel_id=1, source_target_pairs={{0,2},{1,3},{2,0},{3,1},{4,6},{5,7},{6,4},{7,5},{8,10},{9,11},{10,... | collective-permute-start | bytes 1966088 | tf_op jit(solution)/shard_map/ppermute | solution.py:106
  165.5 21.8 %collective-permute-start.21 = (bf16[2,640,256]{2,1,0:T(8,128)(2,1)S(1)}, bf16[2,640,256]{2,1,0:T(8,128)(2,1)S(1)}, u32[]{:S(2)}, u32[]{:S(2)}) collective-permute-start(bf16[2,640,256]{2,1,0:T(8,128)(2,1)S(1)} %collective-permute-done.16.refs_4_.refs_5_.refs_12_.refs_13_), channel_id=1, source_target_pairs={{0,1},{1,0},{2,3},{3,2},{4,5},{5,4},{6,7},{7,6},{8,9},{9,8},{10,11... | collective-permute-start | bytes 1966088 | tf_op jit(solution)/shard_map/ppermute | solution.py:106
  168.3 19.1 %collective-permute-start.23 = (bf16[640,256]{1,0:T(8,128)(2,1)S(1)}, bf16[640,256]{1,0:T(8,128)(2,1)S(1)}, u32[]{:S(2)}, u32[]{:S(2)}) collective-permute-start(bf16[640,256]{1,0:T(8,128)(2,1)S(1)} %collective-permute-done.18), channel_id=1, source_target_pairs={{0,1},{1,0},{2,3},{3,2},{4,5},{5,4},{6,7},{7,6},{8,9},{9,8},{10,11... | collective-permute-start | bytes 983048 | tf_op jit(solution)/shard_map/ppermute | solution.py:106
  189.2 36.4 %collective-permute-start.28 = (bf16[4,3,80,960]{3,2,1,0:T(8,128)(2,1)S(1)}, bf16[4,3,80,960]{3,2,1,0:T(8,128)(2,1)}, u32[]{:S(2)}, u32[]{:S(2)}) collective-permute-start(bf16[4,3,80,960]{3,2,1,0:T(8,128)(2,1)S(1)} %constant_dynamic-update-slice_fusion.4.refs_4_), channel_id=1, source_target_pairs={{0,8},{8,0},{1,9},{9,1},{2,10},{10,2},{3,11},{11,3},{4,12},{12,4},... | collective-permute-start | bytes 5529608 | tf_op jit(solution)/shard_map/ppermute | solution.py:106
  189.5 36.1 %collective-permute-start.27 = (bf16[4,3,80,960]{3,2,1,0:T(8,128)(2,1)S(1)}, bf16[4,3,80,960]{3,2,1,0:T(8,128)(2,1)}, u32[]{:S(2)}, u32[]{:S(2)}) collective-permute-start(bf16[4,3,80,960]{3,2,1,0:T(8,128)(2,1)S(1)} %constant_dynamic-update-slice_fusion.2.refs_3_), channel_id=1, source_target_pairs={{0,8},{8,0},{1,9},{9,1},{2,10},{10,2},{3,11},{11,3},{4,12},{12,4},... | collective-permute-start | bytes 5529608 | tf_op jit(solution)/shard_map/ppermute | solution.py:106
  198.5 23.9 %collective-permute-start.26 = (bf16[2,3,80,960]{3,2,1,0:T(8,128)(2,1)S(1)}, bf16[2,3,80,960]{3,2,1,0:T(8,128)(2,1)}, u32[]{:S(2)}, u32[]{:S(2)}) collective-permute-start(bf16[2,3,80,960]{3,2,1,0:T(8,128)(2,1)S(1)} %collective-permute-done.13), channel_id=1, source_target_pairs={{0,1},{1,0},{2,3},{3,2},{4,5},{5,4},{6,7},{7,6},{8,9},{9,8},{10,11... | collective-permute-start | bytes 2764808 | tf_op jit(solution)/shard_map/ppermute | solution.py:106
  223.7 24.9 %collective-permute-start.30 = (bf16[4,3,80,960]{3,2,1,0:T(8,128)(2,1)S(1)}, bf16[4,3,80,960]{3,2,1,0:T(8,128)(2,1)}, u32[]{:S(2)}, u32[]{:S(2)}) collective-permute-start(bf16[4,3,80,960]{3,2,1,0:T(8,128)(2,1)S(1)} %constant_dynamic-update-slice_fusion.6.refs_5_), channel_id=1, source_target_pairs={{0,8},{8,0},{1,9},{9,1},{2,10},{10,2},{3,11},{11,3},{4,12},{12,4},... | collective-permute-start | bytes 5529608 | tf_op jit(solution)/shard_map/ppermute | solution.py:106
  225.0 23.6 %collective-permute-start.29 = (bf16[2,3,80,960]{3,2,1,0:T(8,128)(2,1)}, bf16[2,3,80,960]{3,2,1,0:T(8,128)(2,1)S(1)}, u32[]{:S(2)}, u32[]{:S(2)}) collective-permute-start(bf16[2,3,80,960]{3,2,1,0:T(8,128)(2,1)} %collective-permute-done.26), channel_id=1, source_target_pairs={{0,16},{16,0},{1,17},{17,1},{2,18},{18,2},{3,19},{19,3},{4,20},{20... | collective-permute-start | bytes 2764808 | tf_op jit(solution)/shard_map/ppermute | solution.py:106
  248.8 40.4 %collective-permute-start.33 = (bf16[4,3,160,960]{3,2,1,0:T(8,128)(2,1)}, bf16[4,3,160,960]{3,2,1,0:T(8,128)(2,1)}, u32[]{:S(2)}, u32[]{:S(2)}) collective-permute-start(bf16[4,3,160,960]{3,2,1,0:T(8,128)(2,1)} %get-tuple-element.136), channel_id=1, source_target_pairs={{0,8},{8,0},{1,9},{9,1},{2,10},{10,2},{3,11},{11,3},{4,12},{12,4},... | collective-permute-start | bytes 11059208 | tf_op jit(solution)/shard_map/ppermute | solution.py:106
  293.7 45.9 %collective-permute-start.34 = (bf16[4,3,80,960]{3,2,1,0:T(8,128)(2,1)}, bf16[4,3,80,960]{3,2,1,0:T(8,128)(2,1)}, u32[]{:S(2)}, u32[]{:S(2)}) collective-permute-start(bf16[4,3,80,960]{3,2,1,0:T(8,128)(2,1)} %add_convert_fusion.1), channel_id=1, source_target_pairs={{0,16},{16,0},{1,17},{17,1},{2,18},{18,2},{3,19},{19,3},{4,20},{20... | collective-permute-start | bytes 5529608 | tf_op jit(solution)/shard_map/ppermute | solution.py:106
  296.8 84.5 %collective-permute-start.38 = (bf16[4,3,80,960]{3,2,1,0:T(8,128)(2,1)}, bf16[4,3,80,960]{3,2,1,0:T(8,128)(2,1)}, u32[]{:S(2)}, u32[]{:S(2)}) collective-permute-start(bf16[4,3,80,960]{3,2,1,0:T(8,128)(2,1)} %add_convert_fusion.2), channel_id=1, source_target_pairs={{0,16},{16,0},{1,17},{17,1},{2,18},{18,2},{3,19},{19,3},{4,20},{20... | collective-permute-start | bytes 5529608 | tf_op jit(solution)/shard_map/ppermute | solution.py:106
  339.6 47.9 %collective-permute-start.35 = (bf16[4,5,2,128,128]{4,3,2,1,0:T(8,128)(2,1)}, bf16[4,5,2,128,128]{4,3,2,1,0:T(8,128)(2,1)}, u32[]{:S(2)}, u32[]{:S(2)}) collective-permute-start(bf16[4,5,2,128,128]{4,3,2,1,0:T(8,128)(2,1)} %get-tuple-element.140), channel_id=1, source_target_pairs={{0,1},{1,0},{2,3},{3,2},{4,5},{5,4},{6,7},{7,6},{8,9},{9,8},{10,11... | collective-permute-start | bytes 3932168 | tf_op jit(solution)/shard_map/ppermute | solution.py:106
  381.3 31.9 %collective-permute-start.39 = (bf16[4,5,2,128,128]{4,3,2,1,0:T(8,128)(2,1)}, bf16[4,5,2,128,128]{4,3,2,1,0:T(8,128)(2,1)S(1)}, u32[]{:S(2)}, u32[]{:S(2)}) collective-permute-start(bf16[4,5,2,128,128]{4,3,2,1,0:T(8,128)(2,1)} %get-tuple-element.147), channel_id=1, source_target_pairs={{0,1},{1,0},{2,3},{3,2},{4,5},{5,4},{6,7},{7,6},{8,9},{9,8},{10,11... | collective-permute-start | bytes 3932168 | tf_op jit(solution)/shard_map/ppermute | solution.py:106
  386.5 67.6 %collective-permute-start.42 = (bf16[4,3,80,960]{3,2,1,0:T(8,128)(2,1)}, bf16[4,3,80,960]{3,2,1,0:T(8,128)(2,1)}, u32[]{:S(2)}, u32[]{:S(2)}) collective-permute-start(bf16[4,3,80,960]{3,2,1,0:T(8,128)(2,1)} %add_convert_fusion), channel_id=1, source_target_pairs={{0,1},{1,0},{2,3},{3,2},{4,5},{5,4},{6,7},{7,6},{8,9},{9,8},{10,11... | collective-permute-start | bytes 5529608 | tf_op jit(solution)/shard_map/ppermute | solution.py:106
  388.8 24.9 %collective-permute-start.36 = (bf16[2,5,2,128,128]{4,3,2,1,0:T(8,128)(2,1)S(1)}, bf16[2,5,2,128,128]{4,3,2,1,0:T(8,128)(2,1)S(1)}, u32[]{:S(2)}, u32[]{:S(2)}) collective-permute-start(bf16[2,5,2,128,128]{4,3,2,1,0:T(8,128)(2,1)S(1)} %add_convert_fusion.8), channel_id=1, source_target_pairs={{0,2},{1,3},{2,0},{3,1},{4,6},{5,7},{6,4},{7,5},{8,10},{9,11},{10,... | collective-permute-start | bytes 1966088 | tf_op jit(solution)/shard_map/ppermute | solution.py:106
  413.4 21.1 %collective-permute-start.40 = (bf16[2,5,2,128,128]{4,3,2,1,0:T(8,128)(2,1)S(1)}, bf16[2,5,2,128,128]{4,3,2,1,0:T(8,128)(2,1)S(1)}, u32[]{:S(2)}, u32[]{:S(2)}) collective-permute-start(bf16[2,5,2,128,128]{4,3,2,1,0:T(8,128)(2,1)S(1)} %add_convert_fusion.7), channel_id=1, source_target_pairs={{0,2},{1,3},{2,0},{3,1},{4,6},{5,7},{6,4},{7,5},{8,10},{9,11},{10,... | collective-permute-start | bytes 1966088 | tf_op jit(solution)/shard_map/ppermute | solution.py:106
  415.6 19.6 %collective-permute-start.37 = (bf16[5,2,128,128]{3,2,1,0:T(8,128)(2,1)}, bf16[5,2,128,128]{3,2,1,0:T(8,128)(2,1)}, u32[]{:S(2)}, u32[]{:S(2)}) collective-permute-start(bf16[5,2,128,128]{3,2,1,0:T(8,128)(2,1)} %fusion.12), channel_id=1, source_target_pairs={{0,4},{1,5},{2,6},{3,7},{4,0},{5,1},{6,2},{7,3},{8,12},{9,13},{10,... | collective-permute-start | bytes 983048 | tf_op jit(solution)/shard_map/ppermute | solution.py:106
  434.6 19.4 %collective-permute-start.41 = (bf16[5,2,128,128]{3,2,1,0:T(8,128)(2,1)S(1)}, bf16[5,2,128,128]{3,2,1,0:T(8,128)(2,1)}, u32[]{:S(2)}, u32[]{:S(2)}) collective-permute-start(bf16[5,2,128,128]{3,2,1,0:T(8,128)(2,1)S(1)} %fusion.13), channel_id=1, source_target_pairs={{0,4},{1,5},{2,6},{3,7},{4,0},{5,1},{6,2},{7,3},{8,12},{9,13},{10,... | collective-permute-start | bytes 983048 | tf_op jit(solution)/shard_map/ppermute | solution.py:106
  460.0 22.7 %collective-permute-start.43 = (bf16[2,3,80,960]{3,2,1,0:T(8,128)(2,1)}, bf16[2,3,80,960]{3,2,1,0:T(8,128)(2,1)}, u32[]{:S(2)}, u32[]{:S(2)}) collective-permute-start(bf16[2,3,80,960]{3,2,1,0:T(8,128)(2,1)} %add_convert_fusion.3), channel_id=1, source_target_pairs={{0,2},{1,3},{2,0},{3,1},{4,6},{5,7},{6,4},{7,5},{8,10},{9,11},{10,... | collective-permute-start | bytes 2764808 | tf_op jit(solution)/shard_map/ppermute | solution.py:106
  518.2 32.1 %collective-permute-start.47 = (bf16[3,80,960]{2,1,0:T(8,128)(2,1)S(1)}, bf16[3,80,960]{2,1,0:T(8,128)(2,1)S(1)}, u32[]{:S(2)}, u32[]{:S(2)}) collective-permute-start(bf16[3,80,960]{2,1,0:T(8,128)(2,1)S(1)} %fusion.11), channel_id=1, source_target_pairs={{0,4},{1,5},{2,6},{3,7},{4,0},{5,1},{6,2},{7,3},{8,12},{9,13},{10,... | collective-permute-start | bytes 1382408 | tf_op jit(solution)/shard_map/ppermute | solution.py:106
  530.1 24.2 %collective-permute-start.51 = (bf16[80,960]{1,0:T(8,128)(2,1)S(1)}, bf16[80,960]{1,0:T(8,128)(2,1)S(1)}, u32[]{:S(2)}, u32[]{:S(2)}) collective-permute-start(bf16[80,960]{1,0:T(8,128)(2,1)S(1)} %fusion.15), channel_id=1, source_target_pairs={{0,1},{1,0},{2,3},{3,2},{4,5},{5,4},{6,7},{7,6},{8,9},{9,8},{10,11... | collective-permute-start | bytes 460808 | tf_op jit(solution)/shard_map/ppermute | solution.py:106
  (104 other events, 1438.2 us)

commit v10 on v9

--- a/solution.py
+++ b/solution.py
@@ -281,10 +281,6 @@
     for term in terms[1:]:
         total = total + term.astype(jnp.float32)
     return total.astype(jnp.bfloat16)
-
-
-def reduce_far(rest):
-    return swap(total_low(*[part[1] for part in rest]), slot_bits()[0])
 
 
 def reduce_end(rest, z_far):
@@ -1264,9 +1260,9 @@
         send_upper, send_lower = [
             total_low(*[far_part for _, far_part in parts]) for parts in (held_upper, held_lower)
         ]
+        d_attn, send_upper, send_lower = lax.optimization_barrier((d_attn, send_upper, send_lower))
+        x_upper = swap(send_upper, ("x", 0))
         x_lower = swap(send_lower, ("x", 0))
-        d_attn, send_upper = lax.optimization_barrier((d_attn, send_upper))
-        x_upper = swap(send_upper, ("x", 0))
     d_q, d_pair = [], []
     for seq in range(seqs):
         mixed, log_total = attended[seq]
@@ -1279,8 +1275,6 @@
                 queries, pairs, key_pos, query_pos, mixed, log_total, d_attn, packed_tables,
                 local_rows, seq, (1,),
             )
-        if aligned and seq == 0:
-            d_slots, d_attn, x_lower = lax.optimization_barrier((d_slots, d_attn, x_lower))
         if aligned and seq == 1:
             d_slots, x_upper = lax.optimization_barrier((d_slots, x_upper))
             feed_y_come = swap(total_low(*[part for part, _ in held_upper], x_upper), slots[2])
@@ -1289,6 +1283,8 @@
             lower, near_part, upper = d_slots
             y_come = swap(upper, slots[2])
             near_come = swap(add_low(near_part, y_come[2:]), slots[1])
+            if seq == 1:
+                near_come, x_lower = lax.optimization_barrier((near_come, x_lower))
             far_come = swap(total_low(lower[1], y_come[1], near_come[1]), slots[0])
             if seq == 1:
                 far_come, feed_y_come = lax.optimization_barrier((far_come, feed_y_come))
@@ -1318,12 +1314,15 @@
     if split:
         first_terms, feed_near_come = lax.optimization_barrier((first_terms, feed_near_come))
         feed_rest = [part[:2] for part in rest] + [feed_near_come]
-        feed_far = reduce_far(feed_rest)
+        far_send = total_low(*[part[1] for part in feed_rest])
         feed_later = {}
 
         def beside(step, value):
-            if step == 2:
-                value, far_come = lax.optimization_barrier((value, feed_far))
+            if step == 0:
+                value, sent = lax.optimization_barrier((value, far_send))
+                feed_later["far"] = swap(sent, slots[0])
+            if step == 1:
+                value, far_come = lax.optimization_barrier((value, feed_later["far"]))
                 sums = reduce_end(feed_rest, far_come)
                 sent = jnp.where(
                     x_index == 0, sums[1:], jnp.broadcast_to(sums[:1], (2,) + sums.shape[1:])

time: 596 us -> 566 us (0.950)
  waiting for transfers between devices: 288 us -> 256 us
    ppermute x55, waiting for transfers between devices: 288 us -> 256 us  [swap_by(): return lax.ppermute(values, axis, [(i, i ^ offset) for i in range(size)])]
  transfers between devices with their start and end apart: 55 -> 55, of which waited for: 33 -> 32; matrix products, arithmetic and copies ran while one was open for 14% -> 14% of each run, Pallas kernels for 21% -> 22%
where the time goes in v10:
time: 566 us; the launch traced here: 556 us
  waiting for transfers between devices  256 us (45%)
  Pallas kernels  122 us (22%)
  starting transfers between devices  60.7 us (11%)
  other arithmetic  59.6 us (11%)
  local copies, waits for them, and re-layouts  42.8 us (8%)
  matrix products  12.2 us (2%)
    ppermute x55, waiting for transfers between devices, swap_by(): return lax.ppermute(values, axis, [(i, i ^ offset) for i in range(size)])  256 us
    ppermute x55, starting transfers between devices, swap_by(): return lax.ppermute(values, axis, [(i, i ^ offset) for i in range(size)])  60.7 us
    pallas_call x2, Pallas kernels, attend_slots_back(): pl.pallas_call(lambda *refs: attend_slots_back_body(count, *refs), grid=(...  45.8 us
    pallas_call x2, Pallas kernels, feed_forward(): pl.pallas_call(lambda *refs: feed_body(parts, split, bool(before), *refs)...  45 us
    unnamed x173, local copies, waits for them, and re-layouts  24.9 us
    convert_element_type x13, other arithmetic, total_low(): return total.astype(jnp.bfloat16)  21.5 us
    pallas_call x2, Pallas kernels, attend_slots(): pl.pallas_call(lambda *refs: attend_slots_body(count, *refs), grid=(KV,),...  17.1 us
  transfers between devices with their start and end apart: 55, of which 32 were waited for; matrix products, arithmetic and copies ran while one was open for 14% of the time, Pallas kernels for 22%

profile of v10, /device:TPU:0, one launch (start us, length us, event | category | flops | bytes accessed | tf_op | source)
XLA Modules:
  0.0 555.7 jit_solution(1610374219233316716)
XLA Ops:
  3.6 14.9 %collective-permute-done = bf16[320,960]{1,0:T(8,128)(2,1)S(1)} collective-permute-done((bf16[320,960]{1,0:T(8,128)(2,1)}, bf16[320,960]{1,0:T(8,128)(2,1)S(1)}, u32[]{:S(2)}, u32[]{:S(2)}) %collective-permute-start) | collective-permute-done | bytes 614432 | tf_op jit(solution)/shard_map/ppermute | solution.py:106
  35.7 7.9 %collective-permute-start.3 = (bf16[2,80,960]{2,1,0:T(8,128)(2,1)S(1)}, bf16[2,80,960]{2,1,0:T(8,128)(2,1)S(1)}, u32[]{:S(2)}, u32[]{:S(2)}) collective-permute-start(bf16[2,80,960]{2,1,0:T(8,128)(2,1)S(1)} %pad_maximum_fusion.19), channel_id=1, source_target_pairs={{0,2},{1,3},{2,0},{3,1},{4,6},{5,7},{6,4},{7,5},{8,10},{9,11},{10,... | collective-permute-start | bytes 921608 | tf_op jit(solution)/shard_map/ppermute | solution.py:106
  43.8 6.9 %collective-permute-done.6 = bf16[2,80,960]{2,1,0:T(8,128)(2,1)S(1)} collective-permute-done((bf16[2,80,960]{2,1,0:T(8,128)(2,1)S(1)}, bf16[2,80,960]{2,1,0:T(8,128)(2,1)S(1)}, u32[]{:S(2)}, u32[]{:S(2)}) %collective-permute-start.6) | collective-permute-done | bytes 307232 | tf_op jit(solution)/shard_map/ppermute | solution.py:106
  50.9 6.8 %collective-permute-done.3 = bf16[2,80,960]{2,1,0:T(8,128)(2,1)S(1)} collective-permute-done((bf16[2,80,960]{2,1,0:T(8,128)(2,1)S(1)}, bf16[2,80,960]{2,1,0:T(8,128)(2,1)S(1)}, u32[]{:S(2)}, u32[]{:S(2)}) %collective-permute-start.3) | collective-permute-done | bytes 307232 | tf_op jit(solution)/shard_map/ppermute | solution.py:106
  58.6 12.7 %collective-permute-done.7 = bf16[4,80,960]{2,1,0:T(8,128)(2,1)S(1)} collective-permute-done((bf16[4,80,960]{2,1,0:T(8,128)(2,1)S(1)}, bf16[4,80,960]{2,1,0:T(8,128)(2,1)S(1)}, u32[]{:S(2)}, u32[]{:S(2)}) %collective-permute-start.7) | collective-permute-done | bytes 614432 | tf_op jit(solution)/shard_map/ppermute | solution.py:106
  80.1 7.2 %shard_map.152 = bf16[8,320,960]{2,1,0:T(8,128)(2,1)} custom-call(s32[2]{0:T(128)S(1)} %pad_add_fusion.me_ref, bf16[8,80,960]{2,1,0:T(8,128)(2,1)S(1)} %pad_maximum_fusion.1.refs_0_, bf16[8,80,960]{2,1,0:T(8,128)(2,1)S(1)} %pad_maximum_fusion.2.refs_1_, bf16[8,80,960]{2,1,0:T(8,128)(2,1)} %collective-permute-done.8.refs_2_, ...), custom_call_target="tpu_custom_call" | custom-call | bytes 9830400 | tf_op jit(solution)/shard_map/pallas_call | solution.py:381
  89.8 12.2 %collective-permute-done.10 = bf16[1,3,80,960]{3,2,1,0:T(8,128)(2,1)} collective-permute-done((bf16[1,3,80,960]{3,2,1,0:T(8,128)(2,1)S(1)}, bf16[1,3,80,960]{3,2,1,0:T(8,128)(2,1)}, u32[]{:S(2)}, u32[]{:S(2)}) %collective-permute-start.10) | collective-permute-done | bytes 460832 | tf_op jit(solution)/shard_map/ppermute | solution.py:106
  114.1 22.8 %collective-permute-done.11 = bf16[640,256]{1,0:T(8,128)(2,1)S(1)} collective-permute-done((bf16[640,256]{1,0:T(8,128)(2,1)S(1)}, bf16[640,256]{1,0:T(8,128)(2,1)S(1)}, u32[]{:S(2)}, u32[]{:S(2)}) %collective-permute-start.11) | collective-permute-done | bytes 327712 | tf_op jit(solution)/shard_map/ppermute | solution.py:106
  152.4 4.3 collective-permute-done.19
  156.7 4.7 collective-permute-done.18
  169.8 17.5 %collective-permute-done.23 = bf16[640,256]{1,0:T(8,128)(2,1)S(1)} collective-permute-done((bf16[640,256]{1,0:T(8,128)(2,1)S(1)}, bf16[640,256]{1,0:T(8,128)(2,1)S(1)}, u32[]{:S(2)}, u32[]{:S(2)}) %collective-permute-start.23) | collective-permute-done | bytes 327712 | tf_op jit(solution)/shard_map/ppermute | solution.py:106
  190.0 8.4 %shard_map.153 = (bf16[960,256]{1,0:T(8,128)(2,1)S(1)}, f32[1,5,1,768]{3,2,1,0:T(1,128)S(1)}) custom-call(s32[8]{0:T(128)S(1)} %compare_convert_fusion.refs_0_, bf16[960,512]{1,0:T(8,128)(2,1)S(1)} %bitcast.168, bf16[1,640,256]{2,1,0:T(8,128)(2,1)S(1)} %get-tuple-element.222.refs_2_.refs_10_, bf16[1,640,256]{2,1,0:T(8,128)(2,1)S(1)} %bitcast.178, ...), custom_call_target="tpu_custom_call" | custom-call | flops 251658240 | bytes 1048576 | tf_op jit(solution)/shard_map/pallas_call | solution.py:731
  200.7 8.7 %shard_map.154 = (bf16[960,256]{1,0:T(8,128)(2,1)S(1)}, f32[1,5,1,768]{3,2,1,0:T(1,128)S(1)}) custom-call(s32[8]{0:T(128)S(1)} %compare_convert_fusion.refs_0_, bf16[960,512]{1,0:T(8,128)(2,1)S(1)} %bitcast.169, bf16[1,640,256]{2,1,0:T(8,128)(2,1)S(1)} %bitcast.173, bf16[1,640,256]{2,1,0:T(8,128)(2,1)S(1)} %bitcast.183, ...), custom_call_target="tpu_custom_call" | custom-call | flops 251658240 | bytes 1048576 | tf_op jit(solution)/shard_map/pallas_call | solution.py:731
  213.1 9.2 %collective-permute-done.26 = bf16[2,3,80,960]{3,2,1,0:T(8,128)(2,1)} collective-permute-done((bf16[2,3,80,960]{3,2,1,0:T(8,128)(2,1)S(1)}, bf16[2,3,80,960]{3,2,1,0:T(8,128)(2,1)}, u32[]{:S(2)}, u32[]{:S(2)}) %collective-permute-start.26) | collective-permute-done | bytes 921632 | tf_op jit(solution)/shard_map/ppermute | solution.py:106
  225.6 21.6 %shard_map.155 = (f32[512,960]{1,0:T(8,128)}, f32[512,960]{1,0:T(8,128)}, bf16[4,3,160,960]{3,2,1,0:T(8,128)(2,1)}, bf16[4,3,160,960]{3,2,1,0:T(8,128)(2,1)}) custom-call(s32[2]{0:T(128)S(1)} %pad_add_fusion.1.refs_0_, bf16[512,960]{1,0:T(8,128)(2,1)S(1)} %multiply_convert_fusion.refs_1_, bf16[512,960]{1,0:T(8,128)(2,1)S(1)} %convert_element_type.440.refs_2_, ...), custom_call_target="tpu_custom_call" | custom-call | flops 11324620800 | bytes 14745600 | tf_op jit(solution)/shard_map/pallas_call | solution.py:1002
  249.3 5.4 collective-permute-done.31.refs_8_
  255.9 23.4 %shard_map.156 = (f32[512,960]{1,0:T(8,128)}, f32[512,960]{1,0:T(8,128)}, bf16[4,3,160,960]{3,2,1,0:T(8,128)(2,1)}, bf16[4,3,160,960]{3,2,1,0:T(8,128)(2,1)}) custom-call(s32[2]{0:T(128)S(1)} %pad_add_fusion.1.refs_0_, bf16[512,960]{1,0:T(8,128)(2,1)S(1)} %multiply_convert_fusion.refs_1_, bf16[512,960]{1,0:T(8,128)(2,1)S(1)} %convert_element_type.440.refs_2_, ...), custom_call_target="tpu_custom_call" | custom-call | flops 11324620800 | bytes 14745600 | tf_op jit(solution)/shard_map/pallas_call | solution.py:1002
  282.6 4.4 fusion.47
  305.6 22.8 %shard_map.157 = (bf16[960,256]{1,0:T(8,128)(2,1)S(1)}, bf16[2,5,2,128,128]{4,3,2,1,0:T(8,128)(2,1)S(1)}, bf16[2,5,2,128,128]{4,3,2,1,0:T(8,128)(2,1)S(1)}, bf16[4,5,2,128,128]{4,3,2,1,0:T(8,128)(2,1)}) custom-call(s32[8]{0:T(128)S(1)} %compare_convert_fusion.refs_0_, bf16[960,512]{1,0:T(8,128)(2,1)S(1)} %bitcast.170, ...), custom_call_target="tpu_custom_call" | custom-call | flops 251658240 | bytes 1048576 | tf_op jit(solution)/shard_map/pallas_call | solution.py:766
  330.3 23.0 %shard_map.158 = (bf16[960,256]{1,0:T(8,128)(2,1)S(1)}, bf16[2,5,2,128,128]{4,3,2,1,0:T(8,128)(2,1)S(1)}, bf16[2,5,2,128,128]{4,3,2,1,0:T(8,128)(2,1)S(1)}, bf16[4,5,2,128,128]{4,3,2,1,0:T(8,128)(2,1)}) custom-call(s32[8]{0:T(128)S(1)} %compare_convert_fusion.refs_0_, bf16[960,512]{1,0:T(8,128)(2,1)S(1)} %bitcast.171, bf16[1,640,256]{2,1,0:T(8,128)(2,1)S(1)} %bitcast.175, ...), custom_call_target="tpu_custom_call" | custom-call | flops 251658240 | bytes 1048576 | tf_op jit(solution)/shard_map/pallas_call | solution.py:766
  355.8 4.2 add_convert_fusion
  362.8 26.3 %collective-permute-done.38 = bf16[4,5,2,128,128]{4,3,2,1,0:T(8,128)(2,1)S(1)} collective-permute-done((bf16[4,5,2,128,128]{4,3,2,1,0:T(8,128)(2,1)}, bf16[4,5,2,128,128]{4,3,2,1,0:T(8,128)(2,1)S(1)}, u32[]{:S(2)}, u32[]{:S(2)}) %collective-permute-start.38) | collective-permute-done | bytes 1310752 | tf_op jit(solution)/shard_map/ppermute | solution.py:106
  393.6 5.4 collective-permute-done.40
  399.0 12.7 %collective-permute-done.39 = bf16[2,5,2,128,128]{4,3,2,1,0:T(8,128)(2,1)S(1)} collective-permute-done((bf16[2,5,2,128,128]{4,3,2,1,0:T(8,128)(2,1)S(1)}, bf16[2,5,2,128,128]{4,3,2,1,0:T(8,128)(2,1)S(1)}, u32[]{:S(2)}, u32[]{:S(2)}) %collective-permute-start.39) | collective-permute-done | bytes 655392 | tf_op jit(solution)/shard_map/ppermute | solution.py:106
  414.4 16.2 %collective-permute-done.42 = bf16[4,3,80,960]{3,2,1,0:T(8,128)(2,1)} collective-permute-done((bf16[4,3,80,960]{3,2,1,0:T(8,128)(2,1)}, bf16[4,3,80,960]{3,2,1,0:T(8,128)(2,1)}, u32[]{:S(2)}, u32[]{:S(2)}) %collective-permute-start.42) | collective-permute-done | bytes 1843232 | tf_op jit(solution)/shard_map/ppermute | solution.py:106
  442.0 7.1 %shard_map.159 = (bf16[8,1,160,960]{3,2,1,0:T(8,128)(2,1)}, bf16[8,1,160,960]{3,2,1,0:T(8,128)(2,1)}) custom-call(s32[2]{0:T(128)S(1)} %pad_add_fusion.me_ref, bf16[1600,512]{1,0:T(8,128)(2,1)S(1)} %pad_maximum_fusion.qkv_ref, bf16[960,512]{1,0:T(8,128)(2,1)S(1)} %copy-done.30, bf16[512,960]{1,0:T(8,128)(2,1)S(1)} %copy-done.22, bf16[512,960]{1,0:T(8,128)(2,1)S(1)} %copy-done.19), custom_call_target="tpu_custom_call" | custom-call | flops 2516582400 | bytes 4915200 | tf_op jit(solution)/shard_map/pallas_call | solution.py:1046
  449.1 10.8 %collective-permute-done.43 = bf16[2,3,80,960]{3,2,1,0:T(8,128)(2,1)} collective-permute-done((bf16[2,3,80,960]{3,2,1,0:T(8,128)(2,1)}, bf16[2,3,80,960]{3,2,1,0:T(8,128)(2,1)}, u32[]{:S(2)}, u32[]{:S(2)}) %collective-permute-start.43) | collective-permute-done | bytes 921632 | tf_op jit(solution)/shard_map/ppermute | solution.py:106
  465.4 4.6 multiply_reduce_fusion.1
  480.2 22.7 %collective-permute-done.49 = bf16[2,2,80,960]{3,2,1,0:T(8,128)(2,1)S(1)} collective-permute-done((bf16[2,2,80,960]{3,2,1,0:T(8,128)(2,1)S(1)}, bf16[2,2,80,960]{3,2,1,0:T(8,128)(2,1)S(1)}, u32[]{:S(2)}, u32[]{:S(2)}) %collective-permute-start.49) | collective-permute-done | bytes 614432 | tf_op jit(solution)/shard_map/ppermute | solution.py:106
  510.3 9.9 %collective-permute-done.50 = bf16[2,80,960]{2,1,0:T(8,128)(2,1)S(1)} collective-permute-done((bf16[2,80,960]{2,1,0:T(8,128)(2,1)S(1)}, bf16[2,80,960]{2,1,0:T(8,128)(2,1)S(1)}, u32[]{:S(2)}, u32[]{:S(2)}) %collective-permute-start.50) | collective-permute-done | bytes 307232 | tf_op jit(solution)/shard_map/ppermute | solution.py:106
  526.5 6.3 %collective-permute-done.48 = bf16[96,960]{1,0:T(8,128)(2,1)S(1)} collective-permute-done((bf16[96,960]{1,0:T(8,128)(2,1)S(1)}, bf16[96,960]{1,0:T(8,128)(2,1)S(1)}, u32[]{:S(2)}, u32[]{:S(2)}) %collective-permute-start.48) | collective-permute-done | bytes 184352 | tf_op jit(solution)/shard_map/ppermute | solution.py:106
  535.9 8.6 %collective-permute-done.53 = bf16[176,960]{1,0:T(8,128)(2,1)S(1)} collective-permute-done((bf16[176,960]{1,0:T(8,128)(2,1)S(1)}, bf16[176,960]{1,0:T(8,128)(2,1)S(1)}, u32[]{:S(2)}, u32[]{:S(2)}) %collective-permute-start.53) | collective-permute-done | bytes 337952 | tf_op jit(solution)/shard_map/ppermute | solution.py:106
  (395 shorter events, 173.3 us)
Async XLA Ops:
  35.7 22.0 %collective-permute-start.3 = (bf16[2,80,960]{2,1,0:T(8,128)(2,1)S(1)}, bf16[2,80,960]{2,1,0:T(8,128)(2,1)S(1)}, u32[]{:S(2)}, u32[]{:S(2)}) collective-permute-start(bf16[2,80,960]{2,1,0:T(8,128)(2,1)S(1)} %pad_maximum_fusion.19), channel_id=1, source_target_pairs={{0,2},{1,3},{2,0},{3,1},{4,6},{5,7},{6,4},{7,5},{8,10},{9,11},{10,... | collective-permute-start | bytes 921608 | tf_op jit(solution)/shard_map/ppermute | solution.py:106
  50.8 20.5 %collective-permute-start.7 = (bf16[4,80,960]{2,1,0:T(8,128)(2,1)S(1)}, bf16[4,80,960]{2,1,0:T(8,128)(2,1)S(1)}, u32[]{:S(2)}, u32[]{:S(2)}) collective-permute-start(bf16[4,80,960]{2,1,0:T(8,128)(2,1)S(1)} %pad_maximum_fusion.9), channel_id=1, source_target_pairs={{0,2},{1,3},{2,0},{3,1},{4,6},{5,7},{6,4},{7,5},{8,10},{9,11},{10,... | collective-permute-start | bytes 1843208 | tf_op jit(solution)/shard_map/ppermute | solution.py:106
  77.3 24.7 %collective-permute-start.10 = (bf16[1,3,80,960]{3,2,1,0:T(8,128)(2,1)S(1)}, bf16[1,3,80,960]{3,2,1,0:T(8,128)(2,1)}, u32[]{:S(2)}, u32[]{:S(2)}) collective-permute-start(bf16[1,3,80,960]{3,2,1,0:T(8,128)(2,1)S(1)} %bitcast.235), channel_id=1, source_target_pairs={{0,4},{1,5},{2,6},{3,7},{4,0},{5,1},{6,2},{7,3},{8,12},{9,13},{10,... | collective-permute-start | bytes 1382408 | tf_op jit(solution)/shard_map/ppermute | solution.py:106
  107.6 31.3 %collective-permute-start.15 = (bf16[2,3,80,960]{3,2,1,0:T(8,128)(2,1)S(1)}, bf16[2,3,80,960]{3,2,1,0:T(8,128)(2,1)S(1)}, u32[]{:S(2)}, u32[]{:S(2)}) collective-permute-start(bf16[2,3,80,960]{3,2,1,0:T(8,128)(2,1)S(1)} %copy-done.41), channel_id=1, source_target_pairs={{0,16},{16,0},{1,17},{17,1},{2,18},{18,2},{3,19},{19,3},{4,20},{20... | collective-permute-start | bytes 2764808 | tf_op jit(solution)/shard_map/ppermute | solution.py:106
  109.1 29.8 %collective-permute-start.14 = (bf16[2,3,80,960]{3,2,1,0:T(8,128)(2,1)S(1)}, bf16[2,3,80,960]{3,2,1,0:T(8,128)(2,1)S(1)}, u32[]{:S(2)}, u32[]{:S(2)}) collective-permute-start(bf16[2,3,80,960]{3,2,1,0:T(8,128)(2,1)S(1)} %copy-done.41), channel_id=1, source_target_pairs={{0,1},{1,0},{2,3},{3,2},{4,5},{5,4},{6,7},{7,6},{8,9},{9,8},{10,11... | collective-permute-start | bytes 2764808 | tf_op jit(solution)/shard_map/ppermute | solution.py:106
  109.6 29.5 %collective-permute-start.13 = (bf16[2,3,80,960]{3,2,1,0:T(8,128)(2,1)S(1)}, bf16[2,3,80,960]{3,2,1,0:T(8,128)(2,1)S(1)}, u32[]{:S(2)}, u32[]{:S(2)}) collective-permute-start(bf16[2,3,80,960]{3,2,1,0:T(8,128)(2,1)S(1)} %copy-done.41), channel_id=1, source_target_pairs={{0,2},{1,3},{2,0},{3,1},{4,6},{5,7},{6,4},{7,5},{8,10},{9,11},{10,... | collective-permute-start | bytes 2764808 | tf_op jit(solution)/shard_map/ppermute | solution.py:106
  109.7 27.2 %collective-permute-start.11 = (bf16[640,256]{1,0:T(8,128)(2,1)S(1)}, bf16[640,256]{1,0:T(8,128)(2,1)S(1)}, u32[]{:S(2)}, u32[]{:S(2)}) collective-permute-start(bf16[640,256]{1,0:T(8,128)(2,1)S(1)} %get-tuple-element.223), channel_id=1, source_target_pairs={{0,4},{1,5},{2,6},{3,7},{4,0},{5,1},{6,2},{7,3},{8,12},{9,13},{10,... | collective-permute-start | bytes 983048 | tf_op jit(solution)/shard_map/ppermute | solution.py:106
  112.6 26.3 %collective-permute-start.12 = (bf16[640,256]{1,0:T(8,128)(2,1)S(1)}, bf16[640,256]{1,0:T(8,128)(2,1)S(1)}, u32[]{:S(2)}, u32[]{:S(2)}) collective-permute-start(bf16[640,256]{1,0:T(8,128)(2,1)S(1)} %get-tuple-element.223), channel_id=1, source_target_pairs={{0,1},{1,0},{2,3},{3,2},{4,5},{5,4},{6,7},{7,6},{8,9},{9,8},{10,11... | collective-permute-start | bytes 983048 | tf_op jit(solution)/shard_map/ppermute | solution.py:106
  139.1 23.0 %collective-permute-start.20 = (bf16[2,3,80,960]{3,2,1,0:T(8,128)(2,1)S(1)}, bf16[2,3,80,960]{3,2,1,0:T(8,128)(2,1)S(1)}, u32[]{:S(2)}, u32[]{:S(2)}) collective-permute-start(bf16[2,3,80,960]{3,2,1,0:T(8,128)(2,1)S(1)} %collective-permute-done.13), channel_id=1, source_target_pairs={{0,16},{16,0},{1,17},{17,1},{2,18},{18,2},{3,19},{19,3},{4,20},{20... | collective-permute-start | bytes 2764808 | tf_op jit(solution)/shard_map/ppermute | solution.py:106
  139.7 22.4 %collective-permute-start.16 = (bf16[2,640,256]{2,1,0:T(8,128)(2,1)S(1)}, bf16[2,640,256]{2,1,0:T(8,128)(2,1)S(1)}, u32[]{:S(2)}, u32[]{:S(2)}) collective-permute-start(bf16[2,640,256]{2,1,0:T(8,128)(2,1)S(1)} %pad_maximum_fusion.12), channel_id=1, source_target_pairs={{0,2},{1,3},{2,0},{3,1},{4,6},{5,7},{6,4},{7,5},{8,10},{9,11},{10,... | collective-permute-start | bytes 1966088 | tf_op jit(solution)/shard_map/ppermute | solution.py:106
  162.1 25.2 %collective-permute-start.24 = (bf16[2,3,80,960]{3,2,1,0:T(8,128)(2,1)S(1)}, bf16[2,3,80,960]{3,2,1,0:T(8,128)(2,1)S(1)}, u32[]{:S(2)}, u32[]{:S(2)}) collective-permute-start(bf16[2,3,80,960]{3,2,1,0:T(8,128)(2,1)S(1)} %collective-permute-done.14), channel_id=1, source_target_pairs={{0,16},{16,0},{1,17},{17,1},{2,18},{18,2},{3,19},{19,3},{4,20},{20... | collective-permute-start | bytes 2764808 | tf_op jit(solution)/shard_map/ppermute | solution.py:106
  163.7 23.7 %collective-permute-start.22 = (bf16[2,640,256]{2,1,0:T(8,128)(2,1)S(1)}, bf16[2,640,256]{2,1,0:T(8,128)(2,1)S(1)}, u32[]{:S(2)}, u32[]{:S(2)}) collective-permute-start(bf16[2,640,256]{2,1,0:T(8,128)(2,1)S(1)} %pad_maximum_fusion.13), channel_id=1, source_target_pairs={{0,2},{1,3},{2,0},{3,1},{4,6},{5,7},{6,4},{7,5},{8,10},{9,11},{10,... | collective-permute-start | bytes 1966088 | tf_op jit(solution)/shard_map/ppermute | solution.py:106
  165.5 21.8 %collective-permute-start.21 = (bf16[2,640,256]{2,1,0:T(8,128)(2,1)S(1)}, bf16[2,640,256]{2,1,0:T(8,128)(2,1)S(1)}, u32[]{:S(2)}, u32[]{:S(2)}) collective-permute-start(bf16[2,640,256]{2,1,0:T(8,128)(2,1)S(1)} %collective-permute-done.16.refs_4_.refs_5_.refs_12_.refs_13_), channel_id=1, source_target_pairs={{0,1},{1,0},{2,3},{3,2},{4,5},{5,4},{6,7},{7,6},{8,9},{9,8},{10,11... | collective-permute-start | bytes 1966088 | tf_op jit(solution)/shard_map/ppermute | solution.py:106
  189.2 36.4 %collective-permute-start.28 = (bf16[4,3,80,960]{3,2,1,0:T(8,128)(2,1)S(1)}, bf16[4,3,80,960]{3,2,1,0:T(8,128)(2,1)}, u32[]{:S(2)}, u32[]{:S(2)}) collective-permute-start(bf16[4,3,80,960]{3,2,1,0:T(8,128)(2,1)S(1)} %constant_dynamic-update-slice_fusion.4.refs_4_), channel_id=1, source_target_pairs={{0,8},{8,0},{1,9},{9,1},{2,10},{10,2},{3,11},{11,3},{4,12},{12,4},... | collective-permute-start | bytes 5529608 | tf_op jit(solution)/shard_map/ppermute | solution.py:106
  189.5 36.1 %collective-permute-start.27 = (bf16[4,3,80,960]{3,2,1,0:T(8,128)(2,1)S(1)}, bf16[4,3,80,960]{3,2,1,0:T(8,128)(2,1)}, u32[]{:S(2)}, u32[]{:S(2)}) collective-permute-start(bf16[4,3,80,960]{3,2,1,0:T(8,128)(2,1)S(1)} %constant_dynamic-update-slice_fusion.2.refs_3_), channel_id=1, source_target_pairs={{0,8},{8,0},{1,9},{9,1},{2,10},{10,2},{3,11},{11,3},{4,12},{12,4},... | collective-permute-start | bytes 5529608 | tf_op jit(solution)/shard_map/ppermute | solution.py:106
  198.5 23.9 %collective-permute-start.26 = (bf16[2,3,80,960]{3,2,1,0:T(8,128)(2,1)S(1)}, bf16[2,3,80,960]{3,2,1,0:T(8,128)(2,1)}, u32[]{:S(2)}, u32[]{:S(2)}) collective-permute-start(bf16[2,3,80,960]{3,2,1,0:T(8,128)(2,1)S(1)} %collective-permute-done.13), channel_id=1, source_target_pairs={{0,1},{1,0},{2,3},{3,2},{4,5},{5,4},{6,7},{7,6},{8,9},{9,8},{10,11... | collective-permute-start | bytes 2764808 | tf_op jit(solution)/shard_map/ppermute | solution.py:106
  223.7 24.9 %collective-permute-start.30 = (bf16[4,3,80,960]{3,2,1,0:T(8,128)(2,1)S(1)}, bf16[4,3,80,960]{3,2,1,0:T(8,128)(2,1)}, u32[]{:S(2)}, u32[]{:S(2)}) collective-permute-start(bf16[4,3,80,960]{3,2,1,0:T(8,128)(2,1)S(1)} %constant_dynamic-update-slice_fusion.6.refs_5_), channel_id=1, source_target_pairs={{0,8},{8,0},{1,9},{9,1},{2,10},{10,2},{3,11},{11,3},{4,12},{12,4},... | collective-permute-start | bytes 5529608 | tf_op jit(solution)/shard_map/ppermute | solution.py:106
  225.0 23.6 %collective-permute-start.29 = (bf16[2,3,80,960]{3,2,1,0:T(8,128)(2,1)}, bf16[2,3,80,960]{3,2,1,0:T(8,128)(2,1)S(1)}, u32[]{:S(2)}, u32[]{:S(2)}) collective-permute-start(bf16[2,3,80,960]{3,2,1,0:T(8,128)(2,1)} %collective-permute-done.26), channel_id=1, source_target_pairs={{0,16},{16,0},{1,17},{17,1},{2,18},{18,2},{3,19},{19,3},{4,20},{20... | collective-permute-start | bytes 2764808 | tf_op jit(solution)/shard_map/ppermute | solution.py:106
  248.8 40.4 %collective-permute-start.33 = (bf16[4,3,160,960]{3,2,1,0:T(8,128)(2,1)}, bf16[4,3,160,960]{3,2,1,0:T(8,128)(2,1)}, u32[]{:S(2)}, u32[]{:S(2)}) collective-permute-start(bf16[4,3,160,960]{3,2,1,0:T(8,128)(2,1)} %get-tuple-element.130), channel_id=1, source_target_pairs={{0,8},{8,0},{1,9},{9,1},{2,10},{10,2},{3,11},{11,3},{4,12},{12,4},... | collective-permute-start | bytes 11059208 | tf_op jit(solution)/shard_map/ppermute | solution.py:106
  296.3 57.0 %collective-permute-start.37 = (bf16[4,3,80,960]{3,2,1,0:T(8,128)(2,1)}, bf16[4,3,80,960]{3,2,1,0:T(8,128)(2,1)}, u32[]{:S(2)}, u32[]{:S(2)}) collective-permute-start(bf16[4,3,80,960]{3,2,1,0:T(8,128)(2,1)} %add_convert_fusion.2), channel_id=1, source_target_pairs={{0,16},{16,0},{1,17},{17,1},{2,18},{18,2},{3,19},{19,3},{4,20},{20... | collective-permute-start | bytes 5529608 | tf_op jit(solution)/shard_map/ppermute | solution.py:106
  329.2 31.9 %collective-permute-start.34 = (bf16[4,5,2,128,128]{4,3,2,1,0:T(8,128)(2,1)}, bf16[4,5,2,128,128]{4,3,2,1,0:T(8,128)(2,1)}, u32[]{:S(2)}, u32[]{:S(2)}) collective-permute-start(bf16[4,5,2,128,128]{4,3,2,1,0:T(8,128)(2,1)} %get-tuple-element.136), channel_id=1, source_target_pairs={{0,1},{1,0},{2,3},{3,2},{4,5},{5,4},{6,7},{7,6},{8,9},{9,8},{10,11... | collective-permute-start | bytes 3932168 | tf_op jit(solution)/shard_map/ppermute | solution.py:106
  353.3 35.8 %collective-permute-start.38 = (bf16[4,5,2,128,128]{4,3,2,1,0:T(8,128)(2,1)}, bf16[4,5,2,128,128]{4,3,2,1,0:T(8,128)(2,1)S(1)}, u32[]{:S(2)}, u32[]{:S(2)}) collective-permute-start(bf16[4,5,2,128,128]{4,3,2,1,0:T(8,128)(2,1)} %get-tuple-element.143), channel_id=1, source_target_pairs={{0,1},{1,0},{2,3},{3,2},{4,5},{5,4},{6,7},{7,6},{8,9},{9,8},{10,11... | collective-permute-start | bytes 3932168 | tf_op jit(solution)/shard_map/ppermute | solution.py:106
  354.3 44.6 %collective-permute-start.40 = (bf16[4,3,80,960]{3,2,1,0:T(8,128)(2,1)}, bf16[4,3,80,960]{3,2,1,0:T(8,128)(2,1)}, u32[]{:S(2)}, u32[]{:S(2)}) collective-permute-start(bf16[4,3,80,960]{3,2,1,0:T(8,128)(2,1)} %add_convert_fusion.1), channel_id=1, source_target_pairs={{0,16},{16,0},{1,17},{17,1},{2,18},{18,2},{3,19},{19,3},{4,20},{20... | collective-permute-start | bytes 5529608 | tf_op jit(solution)/shard_map/ppermute | solution.py:106
  360.1 70.5 %collective-permute-start.42 = (bf16[4,3,80,960]{3,2,1,0:T(8,128)(2,1)}, bf16[4,3,80,960]{3,2,1,0:T(8,128)(2,1)}, u32[]{:S(2)}, u32[]{:S(2)}) collective-permute-start(bf16[4,3,80,960]{3,2,1,0:T(8,128)(2,1)} %add_convert_fusion), channel_id=1, source_target_pairs={{0,1},{1,0},{2,3},{3,2},{4,5},{5,4},{6,7},{7,6},{8,9},{9,8},{10,11... | collective-permute-start | bytes 5529608 | tf_op jit(solution)/shard_map/ppermute | solution.py:106
  362.4 27.3 %collective-permute-start.35 = (bf16[2,5,2,128,128]{4,3,2,1,0:T(8,128)(2,1)S(1)}, bf16[2,5,2,128,128]{4,3,2,1,0:T(8,128)(2,1)S(1)}, u32[]{:S(2)}, u32[]{:S(2)}) collective-permute-start(bf16[2,5,2,128,128]{4,3,2,1,0:T(8,128)(2,1)S(1)} %add_convert_fusion.8), channel_id=1, source_target_pairs={{0,2},{1,3},{2,0},{3,1},{4,6},{5,7},{6,4},{7,5},{8,10},{9,11},{10,... | collective-permute-start | bytes 1966088 | tf_op jit(solution)/shard_map/ppermute | solution.py:106
  389.3 22.4 %collective-permute-start.39 = (bf16[2,5,2,128,128]{4,3,2,1,0:T(8,128)(2,1)S(1)}, bf16[2,5,2,128,128]{4,3,2,1,0:T(8,128)(2,1)S(1)}, u32[]{:S(2)}, u32[]{:S(2)}) collective-permute-start(bf16[2,5,2,128,128]{4,3,2,1,0:T(8,128)(2,1)S(1)} %add_convert_fusion.7), channel_id=1, source_target_pairs={{0,2},{1,3},{2,0},{3,1},{4,6},{5,7},{6,4},{7,5},{8,10},{9,11},{10,... | collective-permute-start | bytes 1966088 | tf_op jit(solution)/shard_map/ppermute | solution.py:106
  390.8 22.3 %collective-permute-start.36 = (bf16[5,2,128,128]{3,2,1,0:T(8,128)(2,1)S(1)}, bf16[5,2,128,128]{3,2,1,0:T(8,128)(2,1)}, u32[]{:S(2)}, u32[]{:S(2)}) collective-permute-start(bf16[5,2,128,128]{3,2,1,0:T(8,128)(2,1)S(1)} %fusion.12), channel_id=1, source_target_pairs={{0,4},{1,5},{2,6},{3,7},{4,0},{5,1},{6,2},{7,3},{8,12},{9,13},{10,... | collective-permute-start | bytes 983048 | tf_op jit(solution)/shard_map/ppermute | solution.py:106
  436.5 23.3 %collective-permute-start.43 = (bf16[2,3,80,960]{3,2,1,0:T(8,128)(2,1)}, bf16[2,3,80,960]{3,2,1,0:T(8,128)(2,1)}, u32[]{:S(2)}, u32[]{:S(2)}) collective-permute-start(bf16[2,3,80,960]{3,2,1,0:T(8,128)(2,1)} %add_convert_fusion.3), channel_id=1, source_target_pairs={{0,2},{1,3},{2,0},{3,1},{4,6},{5,7},{6,4},{7,5},{8,10},{9,11},{10,... | collective-permute-start | bytes 2764808 | tf_op jit(solution)/shard_map/ppermute | solution.py:106
  475.2 27.7 %collective-permute-start.49 = (bf16[2,2,80,960]{3,2,1,0:T(8,128)(2,1)S(1)}, bf16[2,2,80,960]{3,2,1,0:T(8,128)(2,1)S(1)}, u32[]{:S(2)}, u32[]{:S(2)}) collective-permute-start(bf16[2,2,80,960]{3,2,1,0:T(8,128)(2,1)S(1)} %fusion.5), channel_id=1, source_target_pairs={{0,2},{1,3},{2,0},{3,1},{4,6},{5,7},{6,4},{7,5},{8,10},{9,11},{10,... | collective-permute-start | bytes 1843208 | tf_op jit(solution)/shard_map/ppermute | solution.py:106
  475.6 27.9 %collective-permute-start.45 = (bf16[336,960]{1,0:T(8,128)(2,1)S(1)}, bf16[336,960]{1,0:T(8,128)(2,1)S(1)}, u32[]{:S(2)}, u32[]{:S(2)}) collective-permute-start(bf16[336,960]{1,0:T(8,128)(2,1)S(1)} %pad_maximum_fusion.6), channel_id=1, source_target_pairs={{0,1},{1,0},{2,3},{3,2},{4,5},{5,4},{6,7},{7,6},{8,9},{9,8},{10,11... | collective-permute-start | bytes 1935368 | tf_op jit(solution)/shard_map/ppermute | solution.py:106
  477.8 25.8 %collective-permute-start.46 = (bf16[3,80,960]{2,1,0:T(8,128)(2,1)S(1)}, bf16[3,80,960]{2,1,0:T(8,128)(2,1)S(1)}, u32[]{:S(2)}, u32[]{:S(2)}) collective-permute-start(bf16[3,80,960]{2,1,0:T(8,128)(2,1)S(1)} %fusion.11), channel_id=1, source_target_pairs={{0,4},{1,5},{2,6},{3,7},{4,0},{5,1},{6,2},{7,3},{8,12},{9,13},{10,... | collective-permute-start | bytes 1382408 | tf_op jit(solution)/shard_map/ppermute | solution.py:106
  508.7 25.3 %collective-permute-start.52 = (bf16[2,80,960]{2,1,0:T(8,128)(2,1)S(1)}, bf16[2,80,960]{2,1,0:T(8,128)(2,1)S(1)}, u32[]{:S(2)}, u32[]{:S(2)}) collective-permute-start(bf16[2,80,960]{2,1,0:T(8,128)(2,1)S(1)} %fusion.7), channel_id=1, source_target_pairs={{0,16},{16,0},{1,17},{17,1},{2,18},{18,2},{3,19},{19,3},{4,20},{20... | collective-permute-start | bytes 921608 | tf_op jit(solution)/shard_map/ppermute | solution.py:106
  (104 other events, 1337.9 us)

commit v11 on v10

--- a/solution.py
+++ b/solution.py
@@ -338,20 +338,26 @@
     return come[:-16].reshape(shape), parts[0:2] + parts[2:4]
 
 
-def gather_halves(weights):
-    rows = weights.shape[0]
+def gather_first(weights):
+    half = weights.shape[0] // 2
+    far = lax.ppermute(weights, ("x", "core"), [(0, 2)])
+    rows = jnp.where(lax.axis_index("x") == 0, weights, far)
+    come = swap(rows[half:], ("core", 0))
+    return jnp.where(lax.axis_index("core") == 0, rows[:half], come), far
+
+
+def gather_quarters(weights, first_far):
+    half = weights.shape[0] // 2
     x_index, core = lax.axis_index("x"), lax.axis_index("core")
-    half = rows // 2
-    far = swap(weights, ("x", 0))
-    low = jnp.where(x_index == 0, weights, far)
-    high = jnp.where(x_index == 0, far, weights)
-    both = jnp.stack([low, high])
+    far = lax.ppermute(weights, ("x", "core"), [(2, 0), (1, 3), (3, 1)])
+    far = jnp.where((x_index == 1) & (core == 0), first_far, far)
+    both = jnp.stack([jnp.where(x_index == 0, weights, far), jnp.where(x_index == 0, far, weights)])
     keep = jnp.where(core == 0, both[:, :half], both[:, half:])
     come = swap(jnp.where(core == 0, both[:, half:], both[:, :half]), ("core", 0))
     first = jnp.where(core == 0, keep, come)
     second = jnp.where(core == 0, come, keep)
     feed = jnp.stack([second[0], first[1], second[1]])
-    return first[0], jnp.where(x_index == 0, feed[:, : half // 2], feed[:, half // 2 :])
+    return jnp.where(x_index == 0, feed[:, : half // 2], feed[:, half // 2 :])
 
 
 def place_rows(own, far):
@@ -1091,7 +1097,6 @@
     pos_here = places(ctx_index * local_rows + local_index, local_rows, ctx_count)
     cosine, sine_part = angle_tables(pos_here, 1.0)
     turn = (jnp.tile(cosine, (1, seqs)), jnp.tile(sine_part, (1, seqs)))
-    turn_back = (turn[0], -turn[1])
 
     def pack(flat):
         if aligned:
@@ -1130,11 +1135,24 @@
     packed_tables = (by_columns(cosine), by_columns(sine_part))
 
     if split:
-        first_half, feed_quarter = gather_halves(weights)
+        first_half, first_far_x = gather_first(weights)
         cuts = row_cuts(weight_rows // 2)
         backward = [list(reversed(order)) for order in ctx_orders()]
-        first_own = [spread(first_half[low:high], order) for (low, high), order in zip(cuts, backward)]
-        feed_quarter, first_own = lax.optimization_barrier((feed_quarter, first_own))
+        first_own = [
+            double(first_half[None, low:high], order[0])
+            for (low, high), order in zip(cuts, backward)
+        ]
+        later_weights, first_far_x, first_own = lax.optimization_barrier(
+            (weights, first_far_x, first_own)
+        )
+        feed_quarter = gather_quarters(later_weights, first_far_x)
+        for position in (1, 2):
+            first_own = [
+                double(part, order[position]) for part, order in zip(first_own, backward)
+            ]
+        feed_quarter, first_own, packed_tables, flags, turn = lax.optimization_barrier(
+            (feed_quarter, first_own, packed_tables, flags, turn)
+        )
         feed_far_z = swap(feed_quarter[None], slots[0])
         first_far = [swap(part, ("core", 0)) for part in first_own]
         first_rows = place_rows(first_own, first_far)
@@ -1260,7 +1278,7 @@
         send_upper, send_lower = [
             total_low(*[far_part for _, far_part in parts]) for parts in (held_upper, held_lower)
         ]
-        d_attn, send_upper, send_lower = lax.optimization_barrier((d_attn, send_upper, send_lower))
+        d_attn, send_upper = lax.optimization_barrier((d_attn, send_upper))
         x_upper = swap(send_upper, ("x", 0))
         x_lower = swap(send_lower, ("x", 0))
     d_q, d_pair = [], []
@@ -1305,11 +1323,12 @@
     d_qkv = jnp.concatenate(
         [
             jnp.concatenate(d_q, axis=1),
-            rotate(d_own[:, :HD].reshape(kv_cols, tokens), turn_back).astype(jnp.bfloat16),
+            rotate(d_own[:, :HD].reshape(kv_cols, tokens), (turn[0], -turn[1])).astype(jnp.bfloat16),
             d_own[:, HD:].reshape(kv_cols, tokens).astype(jnp.bfloat16),
         ],
         axis=0,
     )
+    d_one = matmul_c(d_qkv, qkv_rows)
     first_terms = first_grads(d_qkv, attn_low, a_one, d_resid_low, weight_rows, split)
     if split:
         first_terms, feed_near_come = lax.optimization_barrier((first_terms, feed_near_come))
@@ -1331,7 +1350,6 @@
                 feed_later["come"] = swap(sent.astype(jnp.bfloat16), ("x", 0))
             return value
 
-    d_one = matmul_c(d_qkv, qkv_rows)
     d_norm_one, d_gain_one = norm_back(tokens_in, d_one, gains[0])
     d_tokens = d_resid + d_norm_one
     gain_grad = jnp.stack([d_gain_one, d_gain_two], axis=0)

time: 566 us -> 569 us (level)
  other arithmetic: 59.6 us -> 71.1 us
  waiting for transfers between devices: 256 us -> 247 us
  local copies, waits for them, and re-layouts: 42.8 us -> 51.4 us
    ppermute x55, waiting for transfers between devices: 256 us -> 239 us  [swap_by(): return lax.ppermute(values, axis, [(i, i ^ offset) for i in range(size)])]
    ppermute x55, starting transfers between devices: 60.7 us -> 51.1 us  [swap_by(): return lax.ppermute(values, axis, [(i, i ^ offset) for i in range(size)])]
    ppermute x0 -> x2, waiting for transfers between devices: none -> 8.36 us  [the longest x1 8.35 us: gather_first(): far = lax.ppermute(weights, ('x', 'core'), [(0, 2)])]
    ppermute x0 -> x2, starting transfers between devices: none -> 6.18 us  [the longest x1 4.89 us: gather_first(): far = lax.ppermute(weights, ('x', 'core'), [(0, 2)])]
    unnamed x173 -> x133, local copies, waits for them, and re-layouts: 24.9 us -> 28.6 us
  transfers between devices with their start and end apart: 55 -> 57, of which waited for: 32 -> 30; matrix products, arithmetic and copies ran while one was open for 14% -> 16% of each run, Pallas kernels for 22% -> 18%
where the time goes in v11:
time: 569 us; the launch traced here: 564 us
  waiting for transfers between devices  247 us (43%)
  Pallas kernels  123 us (22%)
  other arithmetic  71.1 us (12%)
  starting transfers between devices  57.3 us (10%)
  local copies, waits for them, and re-layouts  51.4 us (9%)
  matrix products  12.2 us (2%)
    ppermute x55, waiting for transfers between devices, swap_by(): return lax.ppermute(values, axis, [(i, i ^ offset) for i in range(size)])  239 us
    ppermute x55, starting transfers between devices, swap_by(): return lax.ppermute(values, axis, [(i, i ^ offset) for i in range(size)])  51.1 us
    pallas_call x2, Pallas kernels, attend_slots_back(): pl.pallas_call(lambda *refs: attend_slots_back_body(count, *refs), grid=(...  45.9 us
    pallas_call x2, Pallas kernels, feed_forward(): pl.pallas_call(lambda *refs: feed_body(parts, split, bool(before), *refs)...  45.5 us
    unnamed x133, local copies, waits for them, and re-layouts  28.6 us
    convert_element_type x13, other arithmetic, total_low(): return total.astype(jnp.bfloat16)  21.1 us
    pallas_call x2, Pallas kernels, attend_slots(): pl.pallas_call(lambda *refs: attend_slots_body(count, *refs), grid=(KV,),...  17.1 us
  transfers between devices with their start and end apart: 57, of which 30 were waited for; matrix products, arithmetic and copies ran while one was open for 16% of the time, Pallas kernels for 18%

profile of v11, /device:TPU:0, one launch (start us, length us, event | category | flops | bytes accessed | tf_op | source)
XLA Modules:
  0.0 563.7 jit_solution(15339023746477321747)
XLA Ops:
  0.6 4.9 collective-permute-start
  5.5 8.4 %collective-permute-done = bf16[320,960]{1,0:T(8,128)(2,1)S(1)} collective-permute-done((bf16[320,960]{1,0:T(8,128)(2,1)}, bf16[320,960]{1,0:T(8,128)(2,1)S(1)}, u32[]{:S(2)}, u32[]{:S(2)}) %collective-permute-start) | collective-permute-done | bytes 614432 | tf_op jit(solution)/shard_map/ppermute | solution.py:343
  23.2 5.6 collective-permute-done.2
  34.9 12.1 %collective-permute-done.6 = bf16[2,80,960]{2,1,0:T(8,128)(2,1)S(1)} collective-permute-done((bf16[2,80,960]{2,1,0:T(8,128)(2,1)S(1)}, bf16[2,80,960]{2,1,0:T(8,128)(2,1)S(1)}, u32[]{:S(2)}, u32[]{:S(2)}) %collective-permute-start.6) | collective-permute-done | bytes 307232 | tf_op jit(solution)/shard_map/ppermute | solution.py:106
  54.2 10.4 %collective-permute-done.7 = bf16[4,80,960]{2,1,0:T(8,128)(2,1)} collective-permute-done((bf16[4,80,960]{2,1,0:T(8,128)(2,1)}, bf16[4,80,960]{2,1,0:T(8,128)(2,1)}, u32[]{:S(2)}, u32[]{:S(2)}) %collective-permute-start.7) | collective-permute-done | bytes 614432 | tf_op jit(solution)/shard_map/ppermute | solution.py:106
  84.7 7.2 %shard_map.152 = bf16[8,320,960]{2,1,0:T(8,128)(2,1)} custom-call(s32[2]{0:T(128)S(1)} %pad_add_fusion.me_ref, bf16[8,80,960]{2,1,0:T(8,128)(2,1)S(1)} %pad_maximum_fusion.1.refs_0_, bf16[8,80,960]{2,1,0:T(8,128)(2,1)S(1)} %pad_maximum_fusion.2.refs_1_, bf16[8,80,960]{2,1,0:T(8,128)(2,1)} %collective-permute-done.10.refs_2_, ...), custom_call_target="tpu_custom_call" | custom-call | bytes 9830400 | tf_op jit(solution)/shard_map/pallas_call | solution.py:387
  94.5 10.0 %collective-permute-done.12 = bf16[1,3,80,960]{3,2,1,0:T(8,128)(2,1)} collective-permute-done((bf16[1,3,80,960]{3,2,1,0:T(8,128)(2,1)S(1)}, bf16[1,3,80,960]{3,2,1,0:T(8,128)(2,1)}, u32[]{:S(2)}, u32[]{:S(2)}) %collective-permute-start.12) | collective-permute-done | bytes 460832 | tf_op jit(solution)/shard_map/ppermute | solution.py:106
  124.4 23.7 %collective-permute-done.13 = bf16[640,256]{1,0:T(8,128)(2,1)S(1)} collective-permute-done((bf16[640,256]{1,0:T(8,128)(2,1)S(1)}, bf16[640,256]{1,0:T(8,128)(2,1)S(1)}, u32[]{:S(2)}, u32[]{:S(2)}) %collective-permute-start.13) | collective-permute-done | bytes 327712 | tf_op jit(solution)/shard_map/ppermute | solution.py:106
  163.9 4.3 collective-permute-done.21
  168.2 4.8 collective-permute-done.20
  180.3 17.1 %collective-permute-done.25 = bf16[640,256]{1,0:T(8,128)(2,1)S(1)} collective-permute-done((bf16[640,256]{1,0:T(8,128)(2,1)S(1)}, bf16[640,256]{1,0:T(8,128)(2,1)S(1)}, u32[]{:S(2)}, u32[]{:S(2)}) %collective-permute-start.25) | collective-permute-done | bytes 327712 | tf_op jit(solution)/shard_map/ppermute | solution.py:106
  202.8 8.4 %shard_map.153 = (bf16[960,256]{1,0:T(8,128)(2,1)S(1)}, f32[1,5,1,768]{3,2,1,0:T(1,128)S(1)}) custom-call(s32[8]{0:T(128)S(1)} %compare_convert_fusion.refs_0_, bf16[960,512]{1,0:T(8,128)(2,1)S(1)} %bitcast.172, bf16[1,640,256]{2,1,0:T(8,128)(2,1)S(1)} %get-tuple-element.238.refs_2_.refs_10_, bf16[1,640,256]{2,1,0:T(8,128)(2,1)S(1)} %bitcast.182, ...), custom_call_target="tpu_custom_call" | custom-call | flops 251658240 | bytes 1048576 | tf_op jit(solution)/shard_map/pallas_call | solution.py:737
  212.1 8.7 %shard_map.154 = (bf16[960,256]{1,0:T(8,128)(2,1)S(1)}, f32[1,5,1,768]{3,2,1,0:T(1,128)S(1)}) custom-call(s32[8]{0:T(128)S(1)} %compare_convert_fusion.refs_0_, bf16[960,512]{1,0:T(8,128)(2,1)S(1)} %bitcast.173, bf16[1,640,256]{2,1,0:T(8,128)(2,1)S(1)} %bitcast.177, bf16[1,640,256]{2,1,0:T(8,128)(2,1)S(1)} %bitcast.187, ...), custom_call_target="tpu_custom_call" | custom-call | flops 251658240 | bytes 1048576 | tf_op jit(solution)/shard_map/pallas_call | solution.py:737
  224.4 11.0 %collective-permute-done.28 = bf16[2,3,80,960]{3,2,1,0:T(8,128)(2,1)} collective-permute-done((bf16[2,3,80,960]{3,2,1,0:T(8,128)(2,1)}, bf16[2,3,80,960]{3,2,1,0:T(8,128)(2,1)}, u32[]{:S(2)}, u32[]{:S(2)}) %collective-permute-start.28) | collective-permute-done | bytes 921632 | tf_op jit(solution)/shard_map/ppermute | solution.py:106
  241.5 21.6 %shard_map.155 = (f32[512,960]{1,0:T(8,128)}, f32[512,960]{1,0:T(8,128)}, bf16[4,3,160,960]{3,2,1,0:T(8,128)(2,1)}, bf16[4,3,160,960]{3,2,1,0:T(8,128)(2,1)}) custom-call(s32[2]{0:T(128)S(1)} %pad_add_fusion.1.refs_0_, bf16[512,960]{1,0:T(8,128)(2,1)S(1)} %multiply_convert_fusion.refs_1_, bf16[512,960]{1,0:T(8,128)(2,1)S(1)} %convert_element_type.441.refs_2_, ...), custom_call_target="tpu_custom_call" | custom-call | flops 11324620800 | bytes 14745600 | tf_op jit(solution)/shard_map/pallas_call | solution.py:1008
  264.4 4.3 collective-permute-done.33.refs_8_
  270.3 23.9 %shard_map.156 = (f32[512,960]{1,0:T(8,128)}, f32[512,960]{1,0:T(8,128)}, bf16[4,3,160,960]{3,2,1,0:T(8,128)(2,1)}, bf16[4,3,160,960]{3,2,1,0:T(8,128)(2,1)}) custom-call(s32[2]{0:T(128)S(1)} %pad_add_fusion.1.refs_0_, bf16[512,960]{1,0:T(8,128)(2,1)S(1)} %multiply_convert_fusion.refs_1_, bf16[512,960]{1,0:T(8,128)(2,1)S(1)} %convert_element_type.441.refs_2_, ...), custom_call_target="tpu_custom_call" | custom-call | flops 11324620800 | bytes 14745600 | tf_op jit(solution)/shard_map/pallas_call | solution.py:1008
  298.3 5.1 fusion.47
  309.8 22.9 %shard_map.157 = (bf16[960,256]{1,0:T(8,128)(2,1)S(1)}, bf16[2,5,2,128,128]{4,3,2,1,0:T(8,128)(2,1)S(1)}, bf16[2,5,2,128,128]{4,3,2,1,0:T(8,128)(2,1)S(1)}, bf16[4,5,2,128,128]{4,3,2,1,0:T(8,128)(2,1)}) custom-call(s32[8]{0:T(128)S(1)} %compare_convert_fusion.refs_0_, bf16[960,512]{1,0:T(8,128)(2,1)S(1)} %bitcast.174, ...), custom_call_target="tpu_custom_call" | custom-call | flops 251658240 | bytes 1048576 | tf_op jit(solution)/shard_map/pallas_call | solution.py:772
  333.8 23.0 %shard_map.158 = (bf16[960,256]{1,0:T(8,128)(2,1)S(1)}, bf16[2,5,2,128,128]{4,3,2,1,0:T(8,128)(2,1)S(1)}, bf16[2,5,2,128,128]{4,3,2,1,0:T(8,128)(2,1)S(1)}, bf16[4,5,2,128,128]{4,3,2,1,0:T(8,128)(2,1)}) custom-call(s32[8]{0:T(128)S(1)} %compare_convert_fusion.refs_0_, bf16[960,512]{1,0:T(8,128)(2,1)S(1)} %bitcast.175, bf16[1,640,256]{2,1,0:T(8,128)(2,1)S(1)} %bitcast.179, ...), custom_call_target="tpu_custom_call" | custom-call | flops 251658240 | bytes 1048576 | tf_op jit(solution)/shard_map/pallas_call | solution.py:772
  361.8 4.8 add_convert_fusion
  369.3 24.1 %collective-permute-done.39 = bf16[4,5,2,128,128]{4,3,2,1,0:T(8,128)(2,1)S(1)} collective-permute-done((bf16[4,5,2,128,128]{4,3,2,1,0:T(8,128)(2,1)}, bf16[4,5,2,128,128]{4,3,2,1,0:T(8,128)(2,1)S(1)}, u32[]{:S(2)}, u32[]{:S(2)}) %collective-permute-start.39) | collective-permute-done | bytes 1310752 | tf_op jit(solution)/shard_map/ppermute | solution.py:106
  397.8 7.5 %collective-permute-done.42 = bf16[4,3,80,960]{3,2,1,0:T(8,128)(2,1)S(1)} collective-permute-done((bf16[4,3,80,960]{3,2,1,0:T(8,128)(2,1)S(1)}, bf16[4,3,80,960]{3,2,1,0:T(8,128)(2,1)S(1)}, u32[]{:S(2)}, u32[]{:S(2)}) %collective-permute-start.42) | collective-permute-done | bytes 1843232 | tf_op jit(solution)/shard_map/ppermute | solution.py:106
  405.3 9.9 %collective-permute-done.40 = bf16[2,5,2,128,128]{4,3,2,1,0:T(8,128)(2,1)S(1)} collective-permute-done((bf16[2,5,2,128,128]{4,3,2,1,0:T(8,128)(2,1)S(1)}, bf16[2,5,2,128,128]{4,3,2,1,0:T(8,128)(2,1)S(1)}, u32[]{:S(2)}, u32[]{:S(2)}) %collective-permute-start.40) | collective-permute-done | bytes 655392 | tf_op jit(solution)/shard_map/ppermute | solution.py:106
  418.7 15.8 %collective-permute-done.44 = bf16[4,3,80,960]{3,2,1,0:T(8,128)(2,1)} collective-permute-done((bf16[4,3,80,960]{3,2,1,0:T(8,128)(2,1)}, bf16[4,3,80,960]{3,2,1,0:T(8,128)(2,1)}, u32[]{:S(2)}, u32[]{:S(2)}) %collective-permute-start.44) | collective-permute-done | bytes 1843232 | tf_op jit(solution)/shard_map/ppermute | solution.py:106
  447.9 7.0 %shard_map.159 = (bf16[8,1,160,960]{3,2,1,0:T(8,128)(2,1)}, bf16[8,1,160,960]{3,2,1,0:T(8,128)(2,1)}) custom-call(s32[2]{0:T(128)S(1)} %pad_add_fusion.me_ref, bf16[1600,512]{1,0:T(8,128)(2,1)S(1)} %pad_maximum_fusion.qkv_ref, bf16[960,512]{1,0:T(8,128)(2,1)S(1)} %copy-done.9, bf16[512,960]{1,0:T(8,128)(2,1)S(1)} %copy-done, ...), custom_call_target="tpu_custom_call" | custom-call | flops 2516582400 | bytes 4915200 | tf_op jit(solution)/shard_map/pallas_call | solution.py:1052
  454.9 10.4 %collective-permute-done.45 = bf16[2,3,80,960]{3,2,1,0:T(8,128)(2,1)} collective-permute-done((bf16[2,3,80,960]{3,2,1,0:T(8,128)(2,1)}, bf16[2,3,80,960]{3,2,1,0:T(8,128)(2,1)}, u32[]{:S(2)}, u32[]{:S(2)}) %collective-permute-start.45) | collective-permute-done | bytes 921632 | tf_op jit(solution)/shard_map/ppermute | solution.py:106
  470.6 4.6 multiply_reduce_fusion.1
  486.4 24.5 %collective-permute-done.51 = bf16[2,2,80,960]{3,2,1,0:T(8,128)(2,1)S(1)} collective-permute-done((bf16[2,2,80,960]{3,2,1,0:T(8,128)(2,1)S(1)}, bf16[2,2,80,960]{3,2,1,0:T(8,128)(2,1)S(1)}, u32[]{:S(2)}, u32[]{:S(2)}) %collective-permute-start.51) | collective-permute-done | bytes 614432 | tf_op jit(solution)/shard_map/ppermute | solution.py:106
  516.3 11.8 %collective-permute-done.52 = bf16[2,80,960]{2,1,0:T(8,128)(2,1)S(1)} collective-permute-done((bf16[2,80,960]{2,1,0:T(8,128)(2,1)S(1)}, bf16[2,80,960]{2,1,0:T(8,128)(2,1)S(1)}, u32[]{:S(2)}, u32[]{:S(2)}) %collective-permute-start.52) | collective-permute-done | bytes 307232 | tf_op jit(solution)/shard_map/ppermute | solution.py:106
  534.4 5.8 %collective-permute-done.50 = bf16[96,960]{1,0:T(8,128)(2,1)S(1)} collective-permute-done((bf16[96,960]{1,0:T(8,128)(2,1)S(1)}, bf16[96,960]{1,0:T(8,128)(2,1)S(1)}, u32[]{:S(2)}, u32[]{:S(2)}) %collective-permute-start.50) | collective-permute-done | bytes 184352 | tf_op jit(solution)/shard_map/ppermute | solution.py:106
  542.3 9.5 %collective-permute-done.55 = bf16[176,960]{1,0:T(8,128)(2,1)S(1)} collective-permute-done((bf16[176,960]{1,0:T(8,128)(2,1)S(1)}, bf16[176,960]{1,0:T(8,128)(2,1)S(1)}, u32[]{:S(2)}, u32[]{:S(2)}) %collective-permute-start.55) | collective-permute-done | bytes 337952 | tf_op jit(solution)/shard_map/ppermute | solution.py:106
  (362 shorter events, 188.3 us)
Async XLA Ops:
  28.9 21.1 %collective-permute-start.4 = (bf16[320,960]{1,0:T(8,128)(2,1)S(1)}, bf16[320,960]{1,0:T(8,128)(2,1)}, u32[]{:S(2)}, u32[]{:S(2)}) collective-permute-start(bf16[320,960]{1,0:T(8,128)(2,1)S(1)} %copy-done.20), channel_id=1, source_target_pairs={{16,0},{8,24},{24,8},{17,1},{9,25},{25,9},{18,2},{10,26},{26,10},{... | collective-permute-start | bytes 1843208 | tf_op jit(solution)/shard_map/ppermute | solution.py:352
  79.7 24.8 %collective-permute-start.12 = (bf16[1,3,80,960]{3,2,1,0:T(8,128)(2,1)S(1)}, bf16[1,3,80,960]{3,2,1,0:T(8,128)(2,1)}, u32[]{:S(2)}, u32[]{:S(2)}) collective-permute-start(bf16[1,3,80,960]{3,2,1,0:T(8,128)(2,1)S(1)} %bitcast.239), channel_id=1, source_target_pairs={{0,4},{1,5},{2,6},{3,7},{4,0},{5,1},{6,2},{7,3},{8,12},{9,13},{10,... | collective-permute-start | bytes 1382408 | tf_op jit(solution)/shard_map/ppermute | solution.py:106
  118.6 30.4 %collective-permute-start.17 = (bf16[2,3,80,960]{3,2,1,0:T(8,128)(2,1)S(1)}, bf16[2,3,80,960]{3,2,1,0:T(8,128)(2,1)S(1)}, u32[]{:S(2)}, u32[]{:S(2)}) collective-permute-start(bf16[2,3,80,960]{3,2,1,0:T(8,128)(2,1)S(1)} %pad_maximum_fusion.5), channel_id=1, source_target_pairs={{0,16},{16,0},{1,17},{17,1},{2,18},{18,2},{3,19},{19,3},{4,20},{20... | collective-permute-start | bytes 2764808 | tf_op jit(solution)/shard_map/ppermute | solution.py:106
  118.7 30.3 %collective-permute-start.16 = (bf16[2,3,80,960]{3,2,1,0:T(8,128)(2,1)S(1)}, bf16[2,3,80,960]{3,2,1,0:T(8,128)(2,1)S(1)}, u32[]{:S(2)}, u32[]{:S(2)}) collective-permute-start(bf16[2,3,80,960]{3,2,1,0:T(8,128)(2,1)S(1)} %pad_maximum_fusion.5), channel_id=1, source_target_pairs={{0,1},{1,0},{2,3},{3,2},{4,5},{5,4},{6,7},{7,6},{8,9},{9,8},{10,11... | collective-permute-start | bytes 2764808 | tf_op jit(solution)/shard_map/ppermute | solution.py:106
  119.8 30.5 %collective-permute-start.15 = (bf16[2,3,80,960]{3,2,1,0:T(8,128)(2,1)S(1)}, bf16[2,3,80,960]{3,2,1,0:T(8,128)(2,1)}, u32[]{:S(2)}, u32[]{:S(2)}) collective-permute-start(bf16[2,3,80,960]{3,2,1,0:T(8,128)(2,1)S(1)} %pad_maximum_fusion.5), channel_id=1, source_target_pairs={{0,2},{1,3},{2,0},{3,1},{4,6},{5,7},{6,4},{7,5},{8,10},{9,11},{10,... | collective-permute-start | bytes 2764808 | tf_op jit(solution)/shard_map/ppermute | solution.py:106
  119.8 28.2 %collective-permute-start.13 = (bf16[640,256]{1,0:T(8,128)(2,1)S(1)}, bf16[640,256]{1,0:T(8,128)(2,1)S(1)}, u32[]{:S(2)}, u32[]{:S(2)}) collective-permute-start(bf16[640,256]{1,0:T(8,128)(2,1)S(1)} %get-tuple-element.239), channel_id=1, source_target_pairs={{0,4},{1,5},{2,6},{3,7},{4,0},{5,1},{6,2},{7,3},{8,12},{9,13},{10,... | collective-permute-start | bytes 983048 | tf_op jit(solution)/shard_map/ppermute | solution.py:106
  122.8 26.2 %collective-permute-start.14 = (bf16[640,256]{1,0:T(8,128)(2,1)S(1)}, bf16[640,256]{1,0:T(8,128)(2,1)S(1)}, u32[]{:S(2)}, u32[]{:S(2)}) collective-permute-start(bf16[640,256]{1,0:T(8,128)(2,1)S(1)} %get-tuple-element.239), channel_id=1, source_target_pairs={{0,1},{1,0},{2,3},{3,2},{4,5},{5,4},{6,7},{7,6},{8,9},{9,8},{10,11... | collective-permute-start | bytes 983048 | tf_op jit(solution)/shard_map/ppermute | solution.py:106
  150.3 24.1 %collective-permute-start.22 = (bf16[2,3,80,960]{3,2,1,0:T(8,128)(2,1)}, bf16[2,3,80,960]{3,2,1,0:T(8,128)(2,1)S(1)}, u32[]{:S(2)}, u32[]{:S(2)}) collective-permute-start(bf16[2,3,80,960]{3,2,1,0:T(8,128)(2,1)} %collective-permute-done.15), channel_id=1, source_target_pairs={{0,16},{16,0},{1,17},{17,1},{2,18},{18,2},{3,19},{19,3},{4,20},{20... | collective-permute-start | bytes 2764808 | tf_op jit(solution)/shard_map/ppermute | solution.py:106
  152.0 22.4 %collective-permute-start.18 = (bf16[2,640,256]{2,1,0:T(8,128)(2,1)S(1)}, bf16[2,640,256]{2,1,0:T(8,128)(2,1)S(1)}, u32[]{:S(2)}, u32[]{:S(2)}) collective-permute-start(bf16[2,640,256]{2,1,0:T(8,128)(2,1)S(1)} %pad_maximum_fusion.12), channel_id=1, source_target_pairs={{0,2},{1,3},{2,0},{3,1},{4,6},{5,7},{6,4},{7,5},{8,10},{9,11},{10,... | collective-permute-start | bytes 1966088 | tf_op jit(solution)/shard_map/ppermute | solution.py:106
  174.4 23.0 %collective-permute-start.26 = (bf16[2,3,80,960]{3,2,1,0:T(8,128)(2,1)S(1)}, bf16[2,3,80,960]{3,2,1,0:T(8,128)(2,1)S(1)}, u32[]{:S(2)}, u32[]{:S(2)}) collective-permute-start(bf16[2,3,80,960]{3,2,1,0:T(8,128)(2,1)S(1)} %collective-permute-done.16), channel_id=1, source_target_pairs={{0,16},{16,0},{1,17},{17,1},{2,18},{18,2},{3,19},{19,3},{4,20},{20... | collective-permute-start | bytes 2764808 | tf_op jit(solution)/shard_map/ppermute | solution.py:106
  174.9 22.5 %collective-permute-start.24 = (bf16[2,640,256]{2,1,0:T(8,128)(2,1)S(1)}, bf16[2,640,256]{2,1,0:T(8,128)(2,1)S(1)}, u32[]{:S(2)}, u32[]{:S(2)}) collective-permute-start(bf16[2,640,256]{2,1,0:T(8,128)(2,1)S(1)} %pad_maximum_fusion.13), channel_id=1, source_target_pairs={{0,2},{1,3},{2,0},{3,1},{4,6},{5,7},{6,4},{7,5},{8,10},{9,11},{10,... | collective-permute-start | bytes 1966088 | tf_op jit(solution)/shard_map/ppermute | solution.py:106
  176.3 21.1 %collective-permute-start.23 = (bf16[2,640,256]{2,1,0:T(8,128)(2,1)S(1)}, bf16[2,640,256]{2,1,0:T(8,128)(2,1)S(1)}, u32[]{:S(2)}, u32[]{:S(2)}) collective-permute-start(bf16[2,640,256]{2,1,0:T(8,128)(2,1)S(1)} %collective-permute-done.18.refs_4_.refs_5_.refs_12_.refs_13_), channel_id=1, source_target_pairs={{0,1},{1,0},{2,3},{3,2},{4,5},{5,4},{6,7},{7,6},{8,9},{9,8},{10,11... | collective-permute-start | bytes 1966088 | tf_op jit(solution)/shard_map/ppermute | solution.py:106
  178.9 18.6 %collective-permute-start.25 = (bf16[640,256]{1,0:T(8,128)(2,1)S(1)}, bf16[640,256]{1,0:T(8,128)(2,1)S(1)}, u32[]{:S(2)}, u32[]{:S(2)}) collective-permute-start(bf16[640,256]{1,0:T(8,128)(2,1)S(1)} %collective-permute-done.20), channel_id=1, source_target_pairs={{0,1},{1,0},{2,3},{3,2},{4,5},{5,4},{6,7},{7,6},{8,9},{9,8},{10,11... | collective-permute-start | bytes 983048 | tf_op jit(solution)/shard_map/ppermute | solution.py:106
  199.9 41.6 %collective-permute-start.30 = (bf16[4,3,80,960]{3,2,1,0:T(8,128)(2,1)S(1)}, bf16[4,3,80,960]{3,2,1,0:T(8,128)(2,1)}, u32[]{:S(2)}, u32[]{:S(2)}) collective-permute-start(bf16[4,3,80,960]{3,2,1,0:T(8,128)(2,1)S(1)} %constant_dynamic-update-slice_fusion.4.refs_4_), channel_id=1, source_target_pairs={{0,8},{8,0},{1,9},{9,1},{2,10},{10,2},{3,11},{11,3},{4,12},{12,4},... | collective-permute-start | bytes 5529608 | tf_op jit(solution)/shard_map/ppermute | solution.py:106
  202.3 39.2 %collective-permute-start.29 = (bf16[4,3,80,960]{3,2,1,0:T(8,128)(2,1)S(1)}, bf16[4,3,80,960]{3,2,1,0:T(8,128)(2,1)}, u32[]{:S(2)}, u32[]{:S(2)}) collective-permute-start(bf16[4,3,80,960]{3,2,1,0:T(8,128)(2,1)S(1)} %constant_dynamic-update-slice_fusion.2.refs_3_), channel_id=1, source_target_pairs={{0,8},{8,0},{1,9},{9,1},{2,10},{10,2},{3,11},{11,3},{4,12},{12,4},... | collective-permute-start | bytes 5529608 | tf_op jit(solution)/shard_map/ppermute | solution.py:106
  211.3 24.1 %collective-permute-start.28 = (bf16[2,3,80,960]{3,2,1,0:T(8,128)(2,1)}, bf16[2,3,80,960]{3,2,1,0:T(8,128)(2,1)}, u32[]{:S(2)}, u32[]{:S(2)}) collective-permute-start(bf16[2,3,80,960]{3,2,1,0:T(8,128)(2,1)} %collective-permute-done.15), channel_id=1, source_target_pairs={{0,1},{1,0},{2,3},{3,2},{4,5},{5,4},{6,7},{7,6},{8,9},{9,8},{10,11... | collective-permute-start | bytes 2764808 | tf_op jit(solution)/shard_map/ppermute | solution.py:106
  237.6 25.7 %collective-permute-start.32 = (bf16[4,3,80,960]{3,2,1,0:T(8,128)(2,1)}, bf16[4,3,80,960]{3,2,1,0:T(8,128)(2,1)}, u32[]{:S(2)}, u32[]{:S(2)}) collective-permute-start(bf16[4,3,80,960]{3,2,1,0:T(8,128)(2,1)} %constant_dynamic-update-slice_fusion.6.refs_5_), channel_id=1, source_target_pairs={{0,8},{8,0},{1,9},{9,1},{2,10},{10,2},{3,11},{11,3},{4,12},{12,4},... | collective-permute-start | bytes 5529608 | tf_op jit(solution)/shard_map/ppermute | solution.py:106
  239.9 23.4 %collective-permute-start.31 = (bf16[2,3,80,960]{3,2,1,0:T(8,128)(2,1)}, bf16[2,3,80,960]{3,2,1,0:T(8,128)(2,1)S(1)}, u32[]{:S(2)}, u32[]{:S(2)}) collective-permute-start(bf16[2,3,80,960]{3,2,1,0:T(8,128)(2,1)} %collective-permute-done.28), channel_id=1, source_target_pairs={{0,16},{16,0},{1,17},{17,1},{2,18},{18,2},{3,19},{19,3},{4,20},{20... | collective-permute-start | bytes 2764808 | tf_op jit(solution)/shard_map/ppermute | solution.py:106
  294.3 64.3 %collective-permute-start.41 = (bf16[4,3,160,960]{3,2,1,0:T(8,128)(2,1)}, bf16[4,3,160,960]{3,2,1,0:T(8,128)(2,1)}, u32[]{:S(2)}, u32[]{:S(2)}) collective-permute-start(bf16[4,3,160,960]{3,2,1,0:T(8,128)(2,1)} %get-tuple-element.161), channel_id=1, source_target_pairs={{0,8},{8,0},{1,9},{9,1},{2,10},{10,2},{3,11},{11,3},{4,12},{12,4},... | collective-permute-start | bytes 11059208 | tf_op jit(solution)/shard_map/ppermute | solution.py:106
  308.3 48.6 %collective-permute-start.38 = (bf16[4,3,80,960]{3,2,1,0:T(8,128)(2,1)}, bf16[4,3,80,960]{3,2,1,0:T(8,128)(2,1)}, u32[]{:S(2)}, u32[]{:S(2)}) collective-permute-start(bf16[4,3,80,960]{3,2,1,0:T(8,128)(2,1)} %add_convert_fusion.2), channel_id=1, source_target_pairs={{0,16},{16,0},{1,17},{17,1},{2,18},{18,2},{3,19},{19,3},{4,20},{20... | collective-permute-start | bytes 5529608 | tf_op jit(solution)/shard_map/ppermute | solution.py:106
  333.5 33.8 %collective-permute-start.35 = (bf16[4,5,2,128,128]{4,3,2,1,0:T(8,128)(2,1)}, bf16[4,5,2,128,128]{4,3,2,1,0:T(8,128)(2,1)}, u32[]{:S(2)}, u32[]{:S(2)}) collective-permute-start(bf16[4,5,2,128,128]{4,3,2,1,0:T(8,128)(2,1)} %get-tuple-element.151), channel_id=1, source_target_pairs={{0,1},{1,0},{2,3},{3,2},{4,5},{5,4},{6,7},{7,6},{8,9},{9,8},{10,11... | collective-permute-start | bytes 3932168 | tf_op jit(solution)/shard_map/ppermute | solution.py:106
  356.9 36.5 %collective-permute-start.39 = (bf16[4,5,2,128,128]{4,3,2,1,0:T(8,128)(2,1)}, bf16[4,5,2,128,128]{4,3,2,1,0:T(8,128)(2,1)S(1)}, u32[]{:S(2)}, u32[]{:S(2)}) collective-permute-start(bf16[4,5,2,128,128]{4,3,2,1,0:T(8,128)(2,1)} %get-tuple-element.158), channel_id=1, source_target_pairs={{0,1},{1,0},{2,3},{3,2},{4,5},{5,4},{6,7},{7,6},{8,9},{9,8},{10,11... | collective-permute-start | bytes 3932168 | tf_op jit(solution)/shard_map/ppermute | solution.py:106
  361.2 44.1 %collective-permute-start.42 = (bf16[4,3,80,960]{3,2,1,0:T(8,128)(2,1)S(1)}, bf16[4,3,80,960]{3,2,1,0:T(8,128)(2,1)S(1)}, u32[]{:S(2)}, u32[]{:S(2)}) collective-permute-start(bf16[4,3,80,960]{3,2,1,0:T(8,128)(2,1)S(1)} %add_convert_fusion.1), channel_id=1, source_target_pairs={{0,16},{16,0},{1,17},{17,1},{2,18},{18,2},{3,19},{19,3},{4,20},{20... | collective-permute-start | bytes 5529608 | tf_op jit(solution)/shard_map/ppermute | solution.py:106
  366.6 68.0 %collective-permute-start.44 = (bf16[4,3,80,960]{3,2,1,0:T(8,128)(2,1)}, bf16[4,3,80,960]{3,2,1,0:T(8,128)(2,1)}, u32[]{:S(2)}, u32[]{:S(2)}) collective-permute-start(bf16[4,3,80,960]{3,2,1,0:T(8,128)(2,1)} %add_convert_fusion), channel_id=1, source_target_pairs={{0,1},{1,0},{2,3},{3,2},{4,5},{5,4},{6,7},{7,6},{8,9},{9,8},{10,11... | collective-permute-start | bytes 5529608 | tf_op jit(solution)/shard_map/ppermute | solution.py:106
  368.6 25.5 %collective-permute-start.36 = (bf16[2,5,2,128,128]{4,3,2,1,0:T(8,128)(2,1)S(1)}, bf16[2,5,2,128,128]{4,3,2,1,0:T(8,128)(2,1)S(1)}, u32[]{:S(2)}, u32[]{:S(2)}) collective-permute-start(bf16[2,5,2,128,128]{4,3,2,1,0:T(8,128)(2,1)S(1)} %add_convert_fusion.8), channel_id=1, source_target_pairs={{0,2},{1,3},{2,0},{3,1},{4,6},{5,7},{6,4},{7,5},{8,10},{9,11},{10,... | collective-permute-start | bytes 1966088 | tf_op jit(solution)/shard_map/ppermute | solution.py:106
  393.6 21.6 %collective-permute-start.40 = (bf16[2,5,2,128,128]{4,3,2,1,0:T(8,128)(2,1)S(1)}, bf16[2,5,2,128,128]{4,3,2,1,0:T(8,128)(2,1)S(1)}, u32[]{:S(2)}, u32[]{:S(2)}) collective-permute-start(bf16[2,5,2,128,128]{4,3,2,1,0:T(8,128)(2,1)S(1)} %add_convert_fusion.7), channel_id=1, source_target_pairs={{0,2},{1,3},{2,0},{3,1},{4,6},{5,7},{6,4},{7,5},{8,10},{9,11},{10,... | collective-permute-start | bytes 1966088 | tf_op jit(solution)/shard_map/ppermute | solution.py:106
  395.4 21.9 %collective-permute-start.37 = (bf16[5,2,128,128]{3,2,1,0:T(8,128)(2,1)S(1)}, bf16[5,2,128,128]{3,2,1,0:T(8,128)(2,1)}, u32[]{:S(2)}, u32[]{:S(2)}) collective-permute-start(bf16[5,2,128,128]{3,2,1,0:T(8,128)(2,1)S(1)} %fusion.12), channel_id=1, source_target_pairs={{0,4},{1,5},{2,6},{3,7},{4,0},{5,1},{6,2},{7,3},{8,12},{9,13},{10,... | collective-permute-start | bytes 983048 | tf_op jit(solution)/shard_map/ppermute | solution.py:106
  442.3 23.0 %collective-permute-start.45 = (bf16[2,3,80,960]{3,2,1,0:T(8,128)(2,1)}, bf16[2,3,80,960]{3,2,1,0:T(8,128)(2,1)}, u32[]{:S(2)}, u32[]{:S(2)}) collective-permute-start(bf16[2,3,80,960]{3,2,1,0:T(8,128)(2,1)} %add_convert_fusion.3), channel_id=1, source_target_pairs={{0,2},{1,3},{2,0},{3,1},{4,6},{5,7},{6,4},{7,5},{8,10},{9,11},{10,... | collective-permute-start | bytes 2764808 | tf_op jit(solution)/shard_map/ppermute | solution.py:106
  481.5 29.8 %collective-permute-start.48 = (bf16[3,80,960]{2,1,0:T(8,128)(2,1)S(1)}, bf16[3,80,960]{2,1,0:T(8,128)(2,1)S(1)}, u32[]{:S(2)}, u32[]{:S(2)}) collective-permute-start(bf16[3,80,960]{2,1,0:T(8,128)(2,1)S(1)} %fusion.11), channel_id=1, source_target_pairs={{0,4},{1,5},{2,6},{3,7},{4,0},{5,1},{6,2},{7,3},{8,12},{9,13},{10,... | collective-permute-start | bytes 1382408 | tf_op jit(solution)/shard_map/ppermute | solution.py:106
  483.6 27.4 %collective-permute-start.51 = (bf16[2,2,80,960]{3,2,1,0:T(8,128)(2,1)S(1)}, bf16[2,2,80,960]{3,2,1,0:T(8,128)(2,1)S(1)}, u32[]{:S(2)}, u32[]{:S(2)}) collective-permute-start(bf16[2,2,80,960]{3,2,1,0:T(8,128)(2,1)S(1)} %fusion.5), channel_id=1, source_target_pairs={{0,2},{1,3},{2,0},{3,1},{4,6},{5,7},{6,4},{7,5},{8,10},{9,11},{10,... | collective-permute-start | bytes 1843208 | tf_op jit(solution)/shard_map/ppermute | solution.py:106
  484.7 26.5 %collective-permute-start.47 = (bf16[336,960]{1,0:T(8,128)(2,1)S(1)}, bf16[336,960]{1,0:T(8,128)(2,1)S(1)}, u32[]{:S(2)}, u32[]{:S(2)}) collective-permute-start(bf16[336,960]{1,0:T(8,128)(2,1)S(1)} %pad_maximum_fusion.6), channel_id=1, source_target_pairs={{0,1},{1,0},{2,3},{3,2},{4,5},{5,4},{6,7},{7,6},{8,9},{9,8},{10,11... | collective-permute-start | bytes 1935368 | tf_op jit(solution)/shard_map/ppermute | solution.py:106
  515.3 26.0 %collective-permute-start.54 = (bf16[2,80,960]{2,1,0:T(8,128)(2,1)S(1)}, bf16[2,80,960]{2,1,0:T(8,128)(2,1)S(1)}, u32[]{:S(2)}, u32[]{:S(2)}) collective-permute-start(bf16[2,80,960]{2,1,0:T(8,128)(2,1)S(1)} %fusion.7), channel_id=1, source_target_pairs={{0,16},{16,0},{1,17},{17,1},{2,18},{18,2},{3,19},{19,3},{4,20},{20... | collective-permute-start | bytes 921608 | tf_op jit(solution)/shard_map/ppermute | solution.py:106
  (86 other events, 751.7 us)

commit v12 on v11

--- a/solution.py
+++ b/solution.py
@@ -1098,6 +1098,8 @@
     cosine, sine_part = angle_tables(pos_here, 1.0)
     turn = (jnp.tile(cosine, (1, seqs)), jnp.tile(sine_part, (1, seqs)))
 
+    turn_back = (turn[0], -turn[1])
+
     def pack(flat):
         if aligned:
             return flat
@@ -1134,6 +1136,11 @@
     query_pos = by_columns(pos_here[None, :])
     packed_tables = (by_columns(cosine), by_columns(sine_part))
 
+    tokens_in, cot_in = lax.optimization_barrier(
+        (inputs.reshape(tokens, model_width), cotangent.reshape(tokens, model_width))
+    )
+    dy_low = cot_in.astype(jnp.bfloat16)
+    a_one = (normalize(tokens_in) * gains[0]).astype(jnp.bfloat16)
     if split:
         first_half, first_far_x = gather_first(weights)
         cuts = row_cuts(weight_rows // 2)
@@ -1146,13 +1153,10 @@
             (weights, first_far_x, first_own)
         )
         feed_quarter = gather_quarters(later_weights, first_far_x)
-        for position in (1, 2):
-            first_own = [
-                double(part, order[position]) for part, order in zip(first_own, backward)
-            ]
-        feed_quarter, first_own, packed_tables, flags, turn = lax.optimization_barrier(
-            (feed_quarter, first_own, packed_tables, flags, turn)
-        )
+        first_own = [double(part, order[1]) for part, order in zip(first_own, backward)]
+        first_own, a_one = lax.optimization_barrier((first_own, a_one))
+        first_own = [double(part, order[2]) for part, order in zip(first_own, backward)]
+        feed_quarter, first_own = lax.optimization_barrier((feed_quarter, first_own))
         feed_far_z = swap(feed_quarter[None], slots[0])
         first_far = [swap(part, ("core", 0)) for part in first_own]
         first_rows = place_rows(first_own, first_far)
@@ -1167,11 +1171,6 @@
         first_rows = jnp.concatenate(sides).reshape(-1, model_width)
     qkv_rows, o_rows = first_rows[:cut_o], first_rows[cut_o : cut_o + q_cols]
 
-    tokens_in, cot_in = lax.optimization_barrier(
-        (inputs.reshape(tokens, model_width), cotangent.reshape(tokens, model_width))
-    )
-    dy_low = cot_in.astype(jnp.bfloat16)
-    a_one = (normalize(tokens_in) * gains[0]).astype(jnp.bfloat16)
     pair_rows = matmul_t(qkv_rows[q_cols:], a_one)
     if split:
         pair_rows, feed_far_z = lax.optimization_barrier((pair_rows, feed_far_z))
@@ -1323,7 +1322,7 @@
     d_qkv = jnp.concatenate(
         [
             jnp.concatenate(d_q, axis=1),
-            rotate(d_own[:, :HD].reshape(kv_cols, tokens), (turn[0], -turn[1])).astype(jnp.bfloat16),
+            rotate(d_own[:, :HD].reshape(kv_cols, tokens), turn_back).astype(jnp.bfloat16),
             d_own[:, HD:].reshape(kv_cols, tokens).astype(jnp.bfloat16),
         ],
         axis=0,

time: 569 us -> 555 us (0.975)
  other arithmetic: 71.1 us -> 60.2 us
  local copies, waits for them, and re-layouts: 51.4 us -> 42.7 us
    unnamed x133 -> x169, local copies, waits for them, and re-layouts: 28.6 us -> 24.1 us
  transfers between devices with their start and end apart: 57 -> 57, of which waited for: 30 -> 32; matrix products, arithmetic and copies ran while one was open for 16% -> 15% of each run, Pallas kernels for 18% -> 18%
where the time goes in v12:
time: 555 us; the launch traced here: 549 us
  waiting for transfers between devices  252 us (45%)
  Pallas kernels  123 us (22%)
  other arithmetic  60.2 us (11%)
  starting transfers between devices  57.1 us (10%)
  local copies, waits for them, and re-layouts  42.7 us (8%)
  matrix products  12.2 us (2%)
    ppermute x55, waiting for transfers between devices, swap_by(): return lax.ppermute(values, axis, [(i, i ^ offset) for i in range(size)])  244 us
    ppermute x55, starting transfers between devices, swap_by(): return lax.ppermute(values, axis, [(i, i ^ offset) for i in range(size)])  50.9 us
    pallas_call x2, Pallas kernels, attend_slots_back(): pl.pallas_call(lambda *refs: attend_slots_back_body(count, *refs), grid=(...  46 us
    pallas_call x2, Pallas kernels, feed_forward(): pl.pallas_call(lambda *refs: feed_body(parts, split, bool(before), *refs)...  45.2 us
    unnamed x169, local copies, waits for them, and re-layouts  24.1 us
    convert_element_type x13, other arithmetic, total_low(): return total.astype(jnp.bfloat16)  20.9 us
    pallas_call x2, Pallas kernels, attend_slots(): pl.pallas_call(lambda *refs: attend_slots_body(count, *refs), grid=(KV,),...  16.9 us
  transfers between devices with their start and end apart: 57, of which 32 were waited for; matrix products, arithmetic and copies ran while one was open for 15% of the time, Pallas kernels for 18%

profile of v12, /device:TPU:0, one launch (start us, length us, event | category | flops | bytes accessed | tf_op | source)
XLA Modules:
  0.0 549.5 jit_solution(15181222104777355090)
XLA Ops:
  0.6 4.9 collective-permute-start
  5.5 8.4 %collective-permute-done = bf16[320,960]{1,0:T(8,128)(2,1)S(1)} collective-permute-done((bf16[320,960]{1,0:T(8,128)(2,1)}, bf16[320,960]{1,0:T(8,128)(2,1)S(1)}, u32[]{:S(2)}, u32[]{:S(2)}) %collective-permute-start) | collective-permute-done | bytes 614432 | tf_op jit(solution)/shard_map/ppermute | solution.py:343
  28.9 5.4 collective-permute-done.2
  41.9 7.7 %collective-permute-done.6 = bf16[2,80,960]{2,1,0:T(8,128)(2,1)} collective-permute-done((bf16[2,80,960]{2,1,0:T(8,128)(2,1)}, bf16[2,80,960]{2,1,0:T(8,128)(2,1)}, u32[]{:S(2)}, u32[]{:S(2)}) %collective-permute-start.6) | collective-permute-done | bytes 307232 | tf_op jit(solution)/shard_map/ppermute | solution.py:106
  50.8 5.0 collective-permute-done.7
  58.3 14.9 %collective-permute-done.8 = bf16[4,80,960]{2,1,0:T(8,128)(2,1)S(1)} collective-permute-done((bf16[4,80,960]{2,1,0:T(8,128)(2,1)S(1)}, bf16[4,80,960]{2,1,0:T(8,128)(2,1)S(1)}, u32[]{:S(2)}, u32[]{:S(2)}) %collective-permute-start.8) | collective-permute-done | bytes 614432 | tf_op jit(solution)/shard_map/ppermute | solution.py:106
  79.3 7.4 %shard_map.152 = bf16[8,320,960]{2,1,0:T(8,128)(2,1)} custom-call(s32[2]{0:T(128)S(1)} %pad_add_fusion.me_ref, bf16[8,80,960]{2,1,0:T(8,128)(2,1)S(1)} %pad_maximum_fusion.1.refs_0_, bf16[8,80,960]{2,1,0:T(8,128)(2,1)S(1)} %pad_maximum_fusion.2.refs_1_, bf16[8,80,960]{2,1,0:T(8,128)(2,1)} %collective-permute-done.10.refs_2_, ...), custom_call_target="tpu_custom_call" | custom-call | bytes 9830400 | tf_op jit(solution)/shard_map/pallas_call | solution.py:387
  89.3 10.1 %collective-permute-done.12 = bf16[1,3,80,960]{3,2,1,0:T(8,128)(2,1)} collective-permute-done((bf16[1,3,80,960]{3,2,1,0:T(8,128)(2,1)S(1)}, bf16[1,3,80,960]{3,2,1,0:T(8,128)(2,1)}, u32[]{:S(2)}, u32[]{:S(2)}) %collective-permute-start.12) | collective-permute-done | bytes 460832 | tf_op jit(solution)/shard_map/ppermute | solution.py:106
  110.0 24.7 %collective-permute-done.13 = bf16[640,256]{1,0:T(8,128)(2,1)S(1)} collective-permute-done((bf16[640,256]{1,0:T(8,128)(2,1)S(1)}, bf16[640,256]{1,0:T(8,128)(2,1)S(1)}, u32[]{:S(2)}, u32[]{:S(2)}) %collective-permute-start.13) | collective-permute-done | bytes 327712 | tf_op jit(solution)/shard_map/ppermute | solution.py:106
  150.8 4.3 collective-permute-done.21
  155.1 4.7 collective-permute-done.20
  167.1 17.8 %collective-permute-done.25 = bf16[640,256]{1,0:T(8,128)(2,1)S(1)} collective-permute-done((bf16[640,256]{1,0:T(8,128)(2,1)S(1)}, bf16[640,256]{1,0:T(8,128)(2,1)S(1)}, u32[]{:S(2)}, u32[]{:S(2)}) %collective-permute-start.25) | collective-permute-done | bytes 327712 | tf_op jit(solution)/shard_map/ppermute | solution.py:106
  186.7 8.4 %shard_map.153 = (bf16[960,256]{1,0:T(8,128)(2,1)S(1)}, f32[1,5,1,768]{3,2,1,0:T(1,128)S(1)}) custom-call(s32[8]{0:T(128)S(1)} %compare_convert_fusion.refs_0_, bf16[960,512]{1,0:T(8,128)(2,1)S(1)} %bitcast.172, bf16[1,640,256]{2,1,0:T(8,128)(2,1)S(1)} %get-tuple-element.234.refs_2_.refs_10_, bf16[1,640,256]{2,1,0:T(8,128)(2,1)S(1)} %bitcast.182, ...), custom_call_target="tpu_custom_call" | custom-call | flops 251658240 | bytes 1048576 | tf_op jit(solution)/shard_map/pallas_call | solution.py:737
  198.5 8.4 %shard_map.154 = (bf16[960,256]{1,0:T(8,128)(2,1)S(1)}, f32[1,5,1,768]{3,2,1,0:T(1,128)S(1)}) custom-call(s32[8]{0:T(128)S(1)} %compare_convert_fusion.refs_0_, bf16[960,512]{1,0:T(8,128)(2,1)S(1)} %bitcast.173, bf16[1,640,256]{2,1,0:T(8,128)(2,1)S(1)} %bitcast.177, bf16[1,640,256]{2,1,0:T(8,128)(2,1)S(1)} %bitcast.187, ...), custom_call_target="tpu_custom_call" | custom-call | flops 251658240 | bytes 1048576 | tf_op jit(solution)/shard_map/pallas_call | solution.py:737
  210.7 8.7 %collective-permute-done.28 = bf16[2,3,80,960]{3,2,1,0:T(8,128)(2,1)} collective-permute-done((bf16[2,3,80,960]{3,2,1,0:T(8,128)(2,1)S(1)}, bf16[2,3,80,960]{3,2,1,0:T(8,128)(2,1)}, u32[]{:S(2)}, u32[]{:S(2)}) %collective-permute-start.28) | collective-permute-done | bytes 921632 | tf_op jit(solution)/shard_map/ppermute | solution.py:106
  223.2 21.8 %shard_map.155 = (f32[512,960]{1,0:T(8,128)}, f32[512,960]{1,0:T(8,128)}, bf16[4,3,160,960]{3,2,1,0:T(8,128)(2,1)}, bf16[4,3,160,960]{3,2,1,0:T(8,128)(2,1)}) custom-call(s32[2]{0:T(128)S(1)} %pad_add_fusion.1.refs_0_, bf16[512,960]{1,0:T(8,128)(2,1)S(1)} %multiply_convert_fusion.refs_1_, bf16[512,960]{1,0:T(8,128)(2,1)S(1)} %convert_element_type.440.refs_2_, ...), custom_call_target="tpu_custom_call" | custom-call | flops 11324620800 | bytes 14745600 | tf_op jit(solution)/shard_map/pallas_call | solution.py:1008
  251.0 23.4 %shard_map.156 = (f32[512,960]{1,0:T(8,128)}, f32[512,960]{1,0:T(8,128)}, bf16[4,3,160,960]{3,2,1,0:T(8,128)(2,1)}, bf16[4,3,160,960]{3,2,1,0:T(8,128)(2,1)}) custom-call(s32[2]{0:T(128)S(1)} %pad_add_fusion.1.refs_0_, bf16[512,960]{1,0:T(8,128)(2,1)S(1)} %multiply_convert_fusion.refs_1_, bf16[512,960]{1,0:T(8,128)(2,1)S(1)} %convert_element_type.440.refs_2_, ...), custom_call_target="tpu_custom_call" | custom-call | flops 11324620800 | bytes 14745600 | tf_op jit(solution)/shard_map/pallas_call | solution.py:1008
  277.9 4.3 fusion.47
  298.4 23.0 %shard_map.157 = (bf16[960,256]{1,0:T(8,128)(2,1)S(1)}, bf16[2,5,2,128,128]{4,3,2,1,0:T(8,128)(2,1)S(1)}, bf16[2,5,2,128,128]{4,3,2,1,0:T(8,128)(2,1)S(1)}, bf16[4,5,2,128,128]{4,3,2,1,0:T(8,128)(2,1)}) custom-call(s32[8]{0:T(128)S(1)} %compare_convert_fusion.refs_0_, bf16[960,512]{1,0:T(8,128)(2,1)S(1)} %bitcast.174, ...), custom_call_target="tpu_custom_call" | custom-call | flops 251658240 | bytes 1048576 | tf_op jit(solution)/shard_map/pallas_call | solution.py:772
  323.6 23.0 %shard_map.158 = (bf16[960,256]{1,0:T(8,128)(2,1)S(1)}, bf16[2,5,2,128,128]{4,3,2,1,0:T(8,128)(2,1)S(1)}, bf16[2,5,2,128,128]{4,3,2,1,0:T(8,128)(2,1)S(1)}, bf16[4,5,2,128,128]{4,3,2,1,0:T(8,128)(2,1)}) custom-call(s32[8]{0:T(128)S(1)} %compare_convert_fusion.refs_0_, bf16[960,512]{1,0:T(8,128)(2,1)S(1)} %bitcast.175, bf16[1,640,256]{2,1,0:T(8,128)(2,1)S(1)} %bitcast.179, ...), custom_call_target="tpu_custom_call" | custom-call | flops 251658240 | bytes 1048576 | tf_op jit(solution)/shard_map/pallas_call | solution.py:772
  351.0 4.8 add_convert_fusion
  358.7 23.5 %collective-permute-done.39 = bf16[4,5,2,128,128]{4,3,2,1,0:T(8,128)(2,1)S(1)} collective-permute-done((bf16[4,5,2,128,128]{4,3,2,1,0:T(8,128)(2,1)}, bf16[4,5,2,128,128]{4,3,2,1,0:T(8,128)(2,1)S(1)}, u32[]{:S(2)}, u32[]{:S(2)}) %collective-permute-start.39) | collective-permute-done | bytes 1310752 | tf_op jit(solution)/shard_map/ppermute | solution.py:106
  386.4 7.8 %collective-permute-done.42 = bf16[4,3,80,960]{3,2,1,0:T(8,128)(2,1)} collective-permute-done((bf16[4,3,80,960]{3,2,1,0:T(8,128)(2,1)S(1)}, bf16[4,3,80,960]{3,2,1,0:T(8,128)(2,1)}, u32[]{:S(2)}, u32[]{:S(2)}) %collective-permute-start.42) | collective-permute-done | bytes 1843232 | tf_op jit(solution)/shard_map/ppermute | solution.py:106
  394.2 9.8 %collective-permute-done.40 = bf16[2,5,2,128,128]{4,3,2,1,0:T(8,128)(2,1)S(1)} collective-permute-done((bf16[2,5,2,128,128]{4,3,2,1,0:T(8,128)(2,1)S(1)}, bf16[2,5,2,128,128]{4,3,2,1,0:T(8,128)(2,1)S(1)}, u32[]{:S(2)}, u32[]{:S(2)}) %collective-permute-start.40) | collective-permute-done | bytes 655392 | tf_op jit(solution)/shard_map/ppermute | solution.py:106
  406.6 16.7 %collective-permute-done.44 = bf16[4,3,80,960]{3,2,1,0:T(8,128)(2,1)} collective-permute-done((bf16[4,3,80,960]{3,2,1,0:T(8,128)(2,1)}, bf16[4,3,80,960]{3,2,1,0:T(8,128)(2,1)}, u32[]{:S(2)}, u32[]{:S(2)}) %collective-permute-start.44) | collective-permute-done | bytes 1843232 | tf_op jit(solution)/shard_map/ppermute | solution.py:106
  435.2 7.1 %shard_map.159 = (bf16[8,1,160,960]{3,2,1,0:T(8,128)(2,1)}, bf16[8,1,160,960]{3,2,1,0:T(8,128)(2,1)}) custom-call(s32[2]{0:T(128)S(1)} %pad_add_fusion.me_ref, bf16[1600,512]{1,0:T(8,128)(2,1)S(1)} %pad_maximum_fusion.qkv_ref, bf16[960,512]{1,0:T(8,128)(2,1)S(1)} %copy-done.30, bf16[512,960]{1,0:T(8,128)(2,1)S(1)} %copy-done.22, bf16[512,960]{1,0:T(8,128)(2,1)S(1)} %copy-done.19), custom_call_target="tpu_custom_call" | custom-call | flops 2516582400 | bytes 4915200 | tf_op jit(solution)/shard_map/pallas_call | solution.py:1052
  442.3 9.9 %collective-permute-done.45 = bf16[2,3,80,960]{3,2,1,0:T(8,128)(2,1)} collective-permute-done((bf16[2,3,80,960]{3,2,1,0:T(8,128)(2,1)}, bf16[2,3,80,960]{3,2,1,0:T(8,128)(2,1)}, u32[]{:S(2)}, u32[]{:S(2)}) %collective-permute-start.45) | collective-permute-done | bytes 921632 | tf_op jit(solution)/shard_map/ppermute | solution.py:106
  457.7 4.6 multiply_reduce_fusion.1
  473.2 23.2 %collective-permute-done.51 = bf16[2,2,80,960]{3,2,1,0:T(8,128)(2,1)S(1)} collective-permute-done((bf16[2,2,80,960]{3,2,1,0:T(8,128)(2,1)S(1)}, bf16[2,2,80,960]{3,2,1,0:T(8,128)(2,1)S(1)}, u32[]{:S(2)}, u32[]{:S(2)}) %collective-permute-start.51) | collective-permute-done | bytes 614432 | tf_op jit(solution)/shard_map/ppermute | solution.py:106
  502.3 11.3 %collective-permute-done.52 = bf16[2,80,960]{2,1,0:T(8,128)(2,1)S(1)} collective-permute-done((bf16[2,80,960]{2,1,0:T(8,128)(2,1)S(1)}, bf16[2,80,960]{2,1,0:T(8,128)(2,1)S(1)}, u32[]{:S(2)}, u32[]{:S(2)}) %collective-permute-start.52) | collective-permute-done | bytes 307232 | tf_op jit(solution)/shard_map/ppermute | solution.py:106
  520.0 6.8 %collective-permute-done.50 = bf16[96,960]{1,0:T(8,128)(2,1)S(1)} collective-permute-done((bf16[96,960]{1,0:T(8,128)(2,1)S(1)}, bf16[96,960]{1,0:T(8,128)(2,1)S(1)}, u32[]{:S(2)}, u32[]{:S(2)}) %collective-permute-start.50) | collective-permute-done | bytes 184352 | tf_op jit(solution)/shard_map/ppermute | solution.py:106
  528.6 9.8 %collective-permute-done.55 = bf16[176,960]{1,0:T(8,128)(2,1)S(1)} collective-permute-done((bf16[176,960]{1,0:T(8,128)(2,1)S(1)}, bf16[176,960]{1,0:T(8,128)(2,1)S(1)}, u32[]{:S(2)}, u32[]{:S(2)}) %collective-permute-start.55) | collective-permute-done | bytes 337952 | tf_op jit(solution)/shard_map/ppermute | solution.py:106
  (398 shorter events, 175.4 us)
Async XLA Ops:
  35.9 20.5 %collective-permute-start.4 = (bf16[320,960]{1,0:T(8,128)(2,1)S(1)}, bf16[320,960]{1,0:T(8,128)(2,1)}, u32[]{:S(2)}, u32[]{:S(2)}) collective-permute-start(bf16[320,960]{1,0:T(8,128)(2,1)S(1)} %copy-done.40), channel_id=1, source_target_pairs={{16,0},{8,24},{24,8},{17,1},{9,25},{25,9},{18,2},{10,26},{26,10},{... | collective-permute-start | bytes 1843208 | tf_op jit(solution)/shard_map/ppermute | solution.py:352
  74.9 24.5 %collective-permute-start.12 = (bf16[1,3,80,960]{3,2,1,0:T(8,128)(2,1)S(1)}, bf16[1,3,80,960]{3,2,1,0:T(8,128)(2,1)}, u32[]{:S(2)}, u32[]{:S(2)}) collective-permute-start(bf16[1,3,80,960]{3,2,1,0:T(8,128)(2,1)S(1)} %bitcast.239), channel_id=1, source_target_pairs={{0,4},{1,5},{2,6},{3,7},{4,0},{5,1},{6,2},{7,3},{8,12},{9,13},{10,... | collective-permute-start | bytes 1382408 | tf_op jit(solution)/shard_map/ppermute | solution.py:106
  104.9 30.7 %collective-permute-start.17 = (bf16[2,3,80,960]{3,2,1,0:T(8,128)(2,1)S(1)}, bf16[2,3,80,960]{3,2,1,0:T(8,128)(2,1)S(1)}, u32[]{:S(2)}, u32[]{:S(2)}) collective-permute-start(bf16[2,3,80,960]{3,2,1,0:T(8,128)(2,1)S(1)} %copy-done.43), channel_id=1, source_target_pairs={{0,16},{16,0},{1,17},{17,1},{2,18},{18,2},{3,19},{19,3},{4,20},{20... | collective-permute-start | bytes 2764808 | tf_op jit(solution)/shard_map/ppermute | solution.py:106
  104.9 30.7 %collective-permute-start.16 = (bf16[2,3,80,960]{3,2,1,0:T(8,128)(2,1)S(1)}, bf16[2,3,80,960]{3,2,1,0:T(8,128)(2,1)S(1)}, u32[]{:S(2)}, u32[]{:S(2)}) collective-permute-start(bf16[2,3,80,960]{3,2,1,0:T(8,128)(2,1)S(1)} %copy-done.43), channel_id=1, source_target_pairs={{0,1},{1,0},{2,3},{3,2},{4,5},{5,4},{6,7},{7,6},{8,9},{9,8},{10,11... | collective-permute-start | bytes 2764808 | tf_op jit(solution)/shard_map/ppermute | solution.py:106
  106.5 30.4 %collective-permute-start.15 = (bf16[2,3,80,960]{3,2,1,0:T(8,128)(2,1)S(1)}, bf16[2,3,80,960]{3,2,1,0:T(8,128)(2,1)S(1)}, u32[]{:S(2)}, u32[]{:S(2)}) collective-permute-start(bf16[2,3,80,960]{3,2,1,0:T(8,128)(2,1)S(1)} %copy-done.43), channel_id=1, source_target_pairs={{0,2},{1,3},{2,0},{3,1},{4,6},{5,7},{6,4},{7,5},{8,10},{9,11},{10,... | collective-permute-start | bytes 2764808 | tf_op jit(solution)/shard_map/ppermute | solution.py:106
  106.5 28.2 %collective-permute-start.13 = (bf16[640,256]{1,0:T(8,128)(2,1)S(1)}, bf16[640,256]{1,0:T(8,128)(2,1)S(1)}, u32[]{:S(2)}, u32[]{:S(2)}) collective-permute-start(bf16[640,256]{1,0:T(8,128)(2,1)S(1)} %get-tuple-element.235), channel_id=1, source_target_pairs={{0,4},{1,5},{2,6},{3,7},{4,0},{5,1},{6,2},{7,3},{8,12},{9,13},{10,... | collective-permute-start | bytes 983048 | tf_op jit(solution)/shard_map/ppermute | solution.py:106
  109.5 26.1 %collective-permute-start.14 = (bf16[640,256]{1,0:T(8,128)(2,1)S(1)}, bf16[640,256]{1,0:T(8,128)(2,1)S(1)}, u32[]{:S(2)}, u32[]{:S(2)}) collective-permute-start(bf16[640,256]{1,0:T(8,128)(2,1)S(1)} %get-tuple-element.235), channel_id=1, source_target_pairs={{0,1},{1,0},{2,3},{3,2},{4,5},{5,4},{6,7},{7,6},{8,9},{9,8},{10,11... | collective-permute-start | bytes 983048 | tf_op jit(solution)/shard_map/ppermute | solution.py:106
  136.9 24.2 %collective-permute-start.22 = (bf16[2,3,80,960]{3,2,1,0:T(8,128)(2,1)S(1)}, bf16[2,3,80,960]{3,2,1,0:T(8,128)(2,1)S(1)}, u32[]{:S(2)}, u32[]{:S(2)}) collective-permute-start(bf16[2,3,80,960]{3,2,1,0:T(8,128)(2,1)S(1)} %collective-permute-done.15), channel_id=1, source_target_pairs={{0,16},{16,0},{1,17},{17,1},{2,18},{18,2},{3,19},{19,3},{4,20},{20... | collective-permute-start | bytes 2764808 | tf_op jit(solution)/shard_map/ppermute | solution.py:106
  138.7 22.4 %collective-permute-start.18 = (bf16[2,640,256]{2,1,0:T(8,128)(2,1)S(1)}, bf16[2,640,256]{2,1,0:T(8,128)(2,1)S(1)}, u32[]{:S(2)}, u32[]{:S(2)}) collective-permute-start(bf16[2,640,256]{2,1,0:T(8,128)(2,1)S(1)} %pad_maximum_fusion.12), channel_id=1, source_target_pairs={{0,2},{1,3},{2,0},{3,1},{4,6},{5,7},{6,4},{7,5},{8,10},{9,11},{10,... | collective-permute-start | bytes 1966088 | tf_op jit(solution)/shard_map/ppermute | solution.py:106
  161.1 23.9 %collective-permute-start.26 = (bf16[2,3,80,960]{3,2,1,0:T(8,128)(2,1)S(1)}, bf16[2,3,80,960]{3,2,1,0:T(8,128)(2,1)S(1)}, u32[]{:S(2)}, u32[]{:S(2)}) collective-permute-start(bf16[2,3,80,960]{3,2,1,0:T(8,128)(2,1)S(1)} %collective-permute-done.16), channel_id=1, source_target_pairs={{0,16},{16,0},{1,17},{17,1},{2,18},{18,2},{3,19},{19,3},{4,20},{20... | collective-permute-start | bytes 2764808 | tf_op jit(solution)/shard_map/ppermute | solution.py:106
  161.4 23.5 %collective-permute-start.24 = (bf16[2,640,256]{2,1,0:T(8,128)(2,1)S(1)}, bf16[2,640,256]{2,1,0:T(8,128)(2,1)S(1)}, u32[]{:S(2)}, u32[]{:S(2)}) collective-permute-start(bf16[2,640,256]{2,1,0:T(8,128)(2,1)S(1)} %pad_maximum_fusion.13), channel_id=1, source_target_pairs={{0,2},{1,3},{2,0},{3,1},{4,6},{5,7},{6,4},{7,5},{8,10},{9,11},{10,... | collective-permute-start | bytes 1966088 | tf_op jit(solution)/shard_map/ppermute | solution.py:106
  163.1 21.8 %collective-permute-start.23 = (bf16[2,640,256]{2,1,0:T(8,128)(2,1)S(1)}, bf16[2,640,256]{2,1,0:T(8,128)(2,1)S(1)}, u32[]{:S(2)}, u32[]{:S(2)}) collective-permute-start(bf16[2,640,256]{2,1,0:T(8,128)(2,1)S(1)} %collective-permute-done.18.refs_4_.refs_5_.refs_12_.refs_13_), channel_id=1, source_target_pairs={{0,1},{1,0},{2,3},{3,2},{4,5},{5,4},{6,7},{7,6},{8,9},{9,8},{10,11... | collective-permute-start | bytes 1966088 | tf_op jit(solution)/shard_map/ppermute | solution.py:106
  164.8 20.1 %collective-permute-start.25 = (bf16[640,256]{1,0:T(8,128)(2,1)S(1)}, bf16[640,256]{1,0:T(8,128)(2,1)S(1)}, u32[]{:S(2)}, u32[]{:S(2)}) collective-permute-start(bf16[640,256]{1,0:T(8,128)(2,1)S(1)} %collective-permute-done.20), channel_id=1, source_target_pairs={{0,1},{1,0},{2,3},{3,2},{4,5},{5,4},{6,7},{7,6},{8,9},{9,8},{10,11... | collective-permute-start | bytes 983048 | tf_op jit(solution)/shard_map/ppermute | solution.py:106
  185.9 37.3 %collective-permute-start.30 = (bf16[4,3,80,960]{3,2,1,0:T(8,128)(2,1)S(1)}, bf16[4,3,80,960]{3,2,1,0:T(8,128)(2,1)}, u32[]{:S(2)}, u32[]{:S(2)}) collective-permute-start(bf16[4,3,80,960]{3,2,1,0:T(8,128)(2,1)S(1)} %constant_dynamic-update-slice_fusion.4.refs_4_), channel_id=1, source_target_pairs={{0,8},{8,0},{1,9},{9,1},{2,10},{10,2},{3,11},{11,3},{4,12},{12,4},... | collective-permute-start | bytes 5529608 | tf_op jit(solution)/shard_map/ppermute | solution.py:106
  186.2 37.0 %collective-permute-start.29 = (bf16[4,3,80,960]{3,2,1,0:T(8,128)(2,1)S(1)}, bf16[4,3,80,960]{3,2,1,0:T(8,128)(2,1)}, u32[]{:S(2)}, u32[]{:S(2)}) collective-permute-start(bf16[4,3,80,960]{3,2,1,0:T(8,128)(2,1)S(1)} %constant_dynamic-update-slice_fusion.2.refs_3_), channel_id=1, source_target_pairs={{0,8},{8,0},{1,9},{9,1},{2,10},{10,2},{3,11},{11,3},{4,12},{12,4},... | collective-permute-start | bytes 5529608 | tf_op jit(solution)/shard_map/ppermute | solution.py:106
  195.2 24.2 %collective-permute-start.28 = (bf16[2,3,80,960]{3,2,1,0:T(8,128)(2,1)S(1)}, bf16[2,3,80,960]{3,2,1,0:T(8,128)(2,1)}, u32[]{:S(2)}, u32[]{:S(2)}) collective-permute-start(bf16[2,3,80,960]{3,2,1,0:T(8,128)(2,1)S(1)} %collective-permute-done.15), channel_id=1, source_target_pairs={{0,1},{1,0},{2,3},{3,2},{4,5},{5,4},{6,7},{7,6},{8,9},{9,8},{10,11... | collective-permute-start | bytes 2764808 | tf_op jit(solution)/shard_map/ppermute | solution.py:106
  220.7 24.9 %collective-permute-start.32 = (bf16[4,3,80,960]{3,2,1,0:T(8,128)(2,1)S(1)}, bf16[4,3,80,960]{3,2,1,0:T(8,128)(2,1)}, u32[]{:S(2)}, u32[]{:S(2)}) collective-permute-start(bf16[4,3,80,960]{3,2,1,0:T(8,128)(2,1)S(1)} %constant_dynamic-update-slice_fusion.6.refs_5_), channel_id=1, source_target_pairs={{0,8},{8,0},{1,9},{9,1},{2,10},{10,2},{3,11},{11,3},{4,12},{12,4},... | collective-permute-start | bytes 5529608 | tf_op jit(solution)/shard_map/ppermute | solution.py:106
  222.0 23.6 %collective-permute-start.31 = (bf16[2,3,80,960]{3,2,1,0:T(8,128)(2,1)}, bf16[2,3,80,960]{3,2,1,0:T(8,128)(2,1)S(1)}, u32[]{:S(2)}, u32[]{:S(2)}) collective-permute-start(bf16[2,3,80,960]{3,2,1,0:T(8,128)(2,1)} %collective-permute-done.28), channel_id=1, source_target_pairs={{0,16},{16,0},{1,17},{17,1},{2,18},{18,2},{3,19},{19,3},{4,20},{20... | collective-permute-start | bytes 2764808 | tf_op jit(solution)/shard_map/ppermute | solution.py:106
  274.5 72.8 %collective-permute-start.41 = (bf16[4,3,160,960]{3,2,1,0:T(8,128)(2,1)}, bf16[4,3,160,960]{3,2,1,0:T(8,128)(2,1)}, u32[]{:S(2)}, u32[]{:S(2)}) collective-permute-start(bf16[4,3,160,960]{3,2,1,0:T(8,128)(2,1)} %get-tuple-element.157), channel_id=1, source_target_pairs={{0,8},{8,0},{1,9},{9,1},{2,10},{10,2},{3,11},{11,3},{4,12},{12,4},... | collective-permute-start | bytes 11059208 | tf_op jit(solution)/shard_map/ppermute | solution.py:106
  288.5 58.1 %collective-permute-start.38 = (bf16[4,3,80,960]{3,2,1,0:T(8,128)(2,1)}, bf16[4,3,80,960]{3,2,1,0:T(8,128)(2,1)}, u32[]{:S(2)}, u32[]{:S(2)}) collective-permute-start(bf16[4,3,80,960]{3,2,1,0:T(8,128)(2,1)} %add_convert_fusion.2), channel_id=1, source_target_pairs={{0,16},{16,0},{1,17},{17,1},{2,18},{18,2},{3,19},{19,3},{4,20},{20... | collective-permute-start | bytes 5529608 | tf_op jit(solution)/shard_map/ppermute | solution.py:106
  322.2 34.7 %collective-permute-start.35 = (bf16[4,5,2,128,128]{4,3,2,1,0:T(8,128)(2,1)}, bf16[4,5,2,128,128]{4,3,2,1,0:T(8,128)(2,1)}, u32[]{:S(2)}, u32[]{:S(2)}) collective-permute-start(bf16[4,5,2,128,128]{4,3,2,1,0:T(8,128)(2,1)} %get-tuple-element.147), channel_id=1, source_target_pairs={{0,1},{1,0},{2,3},{3,2},{4,5},{5,4},{6,7},{7,6},{8,9},{9,8},{10,11... | collective-permute-start | bytes 3932168 | tf_op jit(solution)/shard_map/ppermute | solution.py:106
  346.6 35.6 %collective-permute-start.39 = (bf16[4,5,2,128,128]{4,3,2,1,0:T(8,128)(2,1)}, bf16[4,5,2,128,128]{4,3,2,1,0:T(8,128)(2,1)S(1)}, u32[]{:S(2)}, u32[]{:S(2)}) collective-permute-start(bf16[4,5,2,128,128]{4,3,2,1,0:T(8,128)(2,1)} %get-tuple-element.154), channel_id=1, source_target_pairs={{0,1},{1,0},{2,3},{3,2},{4,5},{5,4},{6,7},{7,6},{8,9},{9,8},{10,11... | collective-permute-start | bytes 3932168 | tf_op jit(solution)/shard_map/ppermute | solution.py:106
  350.0 44.2 %collective-permute-start.42 = (bf16[4,3,80,960]{3,2,1,0:T(8,128)(2,1)S(1)}, bf16[4,3,80,960]{3,2,1,0:T(8,128)(2,1)}, u32[]{:S(2)}, u32[]{:S(2)}) collective-permute-start(bf16[4,3,80,960]{3,2,1,0:T(8,128)(2,1)S(1)} %add_convert_fusion.1), channel_id=1, source_target_pairs={{0,16},{16,0},{1,17},{17,1},{2,18},{18,2},{3,19},{19,3},{4,20},{20... | collective-permute-start | bytes 5529608 | tf_op jit(solution)/shard_map/ppermute | solution.py:106
  355.8 67.5 %collective-permute-start.44 = (bf16[4,3,80,960]{3,2,1,0:T(8,128)(2,1)}, bf16[4,3,80,960]{3,2,1,0:T(8,128)(2,1)}, u32[]{:S(2)}, u32[]{:S(2)}) collective-permute-start(bf16[4,3,80,960]{3,2,1,0:T(8,128)(2,1)} %add_convert_fusion), channel_id=1, source_target_pairs={{0,1},{1,0},{2,3},{3,2},{4,5},{5,4},{6,7},{7,6},{8,9},{9,8},{10,11... | collective-permute-start | bytes 5529608 | tf_op jit(solution)/shard_map/ppermute | solution.py:106
  358.2 24.9 %collective-permute-start.36 = (bf16[2,5,2,128,128]{4,3,2,1,0:T(8,128)(2,1)S(1)}, bf16[2,5,2,128,128]{4,3,2,1,0:T(8,128)(2,1)S(1)}, u32[]{:S(2)}, u32[]{:S(2)}) collective-permute-start(bf16[2,5,2,128,128]{4,3,2,1,0:T(8,128)(2,1)S(1)} %add_convert_fusion.8), channel_id=1, source_target_pairs={{0,2},{1,3},{2,0},{3,1},{4,6},{5,7},{6,4},{7,5},{8,10},{9,11},{10,... | collective-permute-start | bytes 1966088 | tf_op jit(solution)/shard_map/ppermute | solution.py:106
  382.3 21.7 %collective-permute-start.40 = (bf16[2,5,2,128,128]{4,3,2,1,0:T(8,128)(2,1)S(1)}, bf16[2,5,2,128,128]{4,3,2,1,0:T(8,128)(2,1)S(1)}, u32[]{:S(2)}, u32[]{:S(2)}) collective-permute-start(bf16[2,5,2,128,128]{4,3,2,1,0:T(8,128)(2,1)S(1)} %add_convert_fusion.7), channel_id=1, source_target_pairs={{0,2},{1,3},{2,0},{3,1},{4,6},{5,7},{6,4},{7,5},{8,10},{9,11},{10,... | collective-permute-start | bytes 1966088 | tf_op jit(solution)/shard_map/ppermute | solution.py:106
  384.3 21.1 %collective-permute-start.37 = (bf16[5,2,128,128]{3,2,1,0:T(8,128)(2,1)S(1)}, bf16[5,2,128,128]{3,2,1,0:T(8,128)(2,1)}, u32[]{:S(2)}, u32[]{:S(2)}) collective-permute-start(bf16[5,2,128,128]{3,2,1,0:T(8,128)(2,1)S(1)} %fusion.12), channel_id=1, source_target_pairs={{0,4},{1,5},{2,6},{3,7},{4,0},{5,1},{6,2},{7,3},{8,12},{9,13},{10,... | collective-permute-start | bytes 983048 | tf_op jit(solution)/shard_map/ppermute | solution.py:106
  429.2 23.0 %collective-permute-start.45 = (bf16[2,3,80,960]{3,2,1,0:T(8,128)(2,1)}, bf16[2,3,80,960]{3,2,1,0:T(8,128)(2,1)}, u32[]{:S(2)}, u32[]{:S(2)}) collective-permute-start(bf16[2,3,80,960]{3,2,1,0:T(8,128)(2,1)} %add_convert_fusion.3), channel_id=1, source_target_pairs={{0,2},{1,3},{2,0},{3,1},{4,6},{5,7},{6,4},{7,5},{8,10},{9,11},{10,... | collective-permute-start | bytes 2764808 | tf_op jit(solution)/shard_map/ppermute | solution.py:106
  467.4 29.7 %collective-permute-start.48 = (bf16[3,80,960]{2,1,0:T(8,128)(2,1)S(1)}, bf16[3,80,960]{2,1,0:T(8,128)(2,1)S(1)}, u32[]{:S(2)}, u32[]{:S(2)}) collective-permute-start(bf16[3,80,960]{2,1,0:T(8,128)(2,1)S(1)} %fusion.11), channel_id=1, source_target_pairs={{0,4},{1,5},{2,6},{3,7},{4,0},{5,1},{6,2},{7,3},{8,12},{9,13},{10,... | collective-permute-start | bytes 1382408 | tf_op jit(solution)/shard_map/ppermute | solution.py:106
  469.2 27.2 %collective-permute-start.51 = (bf16[2,2,80,960]{3,2,1,0:T(8,128)(2,1)S(1)}, bf16[2,2,80,960]{3,2,1,0:T(8,128)(2,1)S(1)}, u32[]{:S(2)}, u32[]{:S(2)}) collective-permute-start(bf16[2,2,80,960]{3,2,1,0:T(8,128)(2,1)S(1)} %fusion.5), channel_id=1, source_target_pairs={{0,2},{1,3},{2,0},{3,1},{4,6},{5,7},{6,4},{7,5},{8,10},{9,11},{10,... | collective-permute-start | bytes 1843208 | tf_op jit(solution)/shard_map/ppermute | solution.py:106
  470.6 26.3 %collective-permute-start.47 = (bf16[336,960]{1,0:T(8,128)(2,1)S(1)}, bf16[336,960]{1,0:T(8,128)(2,1)S(1)}, u32[]{:S(2)}, u32[]{:S(2)}) collective-permute-start(bf16[336,960]{1,0:T(8,128)(2,1)S(1)} %pad_maximum_fusion.6), channel_id=1, source_target_pairs={{0,1},{1,0},{2,3},{3,2},{4,5},{5,4},{6,7},{7,6},{8,9},{9,8},{10,11... | collective-permute-start | bytes 1935368 | tf_op jit(solution)/shard_map/ppermute | solution.py:106
  501.6 26.3 %collective-permute-start.54 = (bf16[2,80,960]{2,1,0:T(8,128)(2,1)S(1)}, bf16[2,80,960]{2,1,0:T(8,128)(2,1)S(1)}, u32[]{:S(2)}, u32[]{:S(2)}) collective-permute-start(bf16[2,80,960]{2,1,0:T(8,128)(2,1)S(1)} %fusion.7), channel_id=1, source_target_pairs={{0,16},{16,0},{1,17},{17,1},{2,18},{18,2},{3,19},{19,3},{4,20},{20... | collective-permute-start | bytes 921608 | tf_op jit(solution)/shard_map/ppermute | solution.py:106
  (104 other events, 1307.1 us)

commit v13 on v12

--- a/solution.py
+++ b/solution.py
@@ -267,7 +267,7 @@
 
 
 def row_cuts(rows):
-    first = -(-rows // 32) * 16
+    first = -(-rows * 3 // 80) * 16
     return [(0, first), (first, rows)]
 
 

time: 555 us -> 560 us (level)
  waiting for transfers between devices: 252 us -> 261 us
    ppermute x55, waiting for transfers between devices: 244 us -> 252 us  [swap_by(): return lax.ppermute(values, axis, [(i, i ^ offset) for i in range(size)])]
    unnamed x169 -> x171, local copies, waits for them, and re-layouts: 24.1 us -> 24.2 us
  transfers between devices with their start and end apart: 57 -> 57, of which waited for: 32 -> 31; matrix products, arithmetic and copies ran while one was open for 15% -> 15% of each run, Pallas kernels for 18% -> 18%
where the time goes in v13:
time: 560 us; the launch traced here: 555 us
  waiting for transfers between devices  261 us (47%)
  Pallas kernels  123 us (22%)
  other arithmetic  59.3 us (11%)
  starting transfers between devices  55.2 us (10%)
  local copies, waits for them, and re-layouts  42.7 us (8%)
  matrix products  12.2 us (2%)
    ppermute x55, waiting for transfers between devices, swap_by(): return lax.ppermute(values, axis, [(i, i ^ offset) for i in range(size)])  252 us
    ppermute x55, starting transfers between devices, swap_by(): return lax.ppermute(values, axis, [(i, i ^ offset) for i in range(size)])  49 us
    pallas_call x2, Pallas kernels, attend_slots_back(): pl.pallas_call(lambda *refs: attend_slots_back_body(count, *refs), grid=(...  46 us
    pallas_call x2, Pallas kernels, feed_forward(): pl.pallas_call(lambda *refs: feed_body(parts, split, bool(before), *refs)...  45.2 us
    unnamed x171, local copies, waits for them, and re-layouts  24.2 us
    convert_element_type x13, other arithmetic, total_low(): return total.astype(jnp.bfloat16)  21 us
    pallas_call x2, Pallas kernels, attend_slots(): pl.pallas_call(lambda *refs: attend_slots_body(count, *refs), grid=(KV,),...  16.9 us
  transfers between devices with their start and end apart: 57, of which 31 were waited for; matrix products, arithmetic and copies ran while one was open for 15% of the time, Pallas kernels for 18%

profile of v13, /device:TPU:0, one launch (start us, length us, event | category | flops | bytes accessed | tf_op | source)
XLA Modules:
  0.0 554.8 jit_solution(16740399478919315993)
XLA Ops:
  0.6 4.9 collective-permute-start
  5.5 8.4 %collective-permute-done = bf16[320,960]{1,0:T(8,128)(2,1)S(1)} collective-permute-done((bf16[320,960]{1,0:T(8,128)(2,1)}, bf16[320,960]{1,0:T(8,128)(2,1)S(1)}, u32[]{:S(2)}, u32[]{:S(2)}) %collective-permute-start) | collective-permute-done | bytes 614432 | tf_op jit(solution)/shard_map/ppermute | solution.py:343
  28.2 7.5 %collective-permute-done.2 = bf16[1,96,960]{2,1,0:T(8,128)(2,1)S(1)} collective-permute-done((bf16[1,96,960]{2,1,0:T(8,128)(2,1)S(1)}, bf16[1,96,960]{2,1,0:T(8,128)(2,1)S(1)}, u32[]{:S(2)}, u32[]{:S(2)}) %collective-permute-start.2) | collective-permute-done | bytes 184352 | tf_op jit(solution)/shard_map/ppermute | solution.py:106
  43.4 9.8 %collective-permute-done.7 = bf16[2,64,960]{2,1,0:T(8,128)(2,1)S(1)} collective-permute-done((bf16[2,64,960]{2,1,0:T(8,128)(2,1)}, bf16[2,64,960]{2,1,0:T(8,128)(2,1)S(1)}, u32[]{:S(2)}, u32[]{:S(2)}) %collective-permute-start.7) | collective-permute-done | bytes 245792 | tf_op jit(solution)/shard_map/ppermute | solution.py:106
  58.9 12.0 %collective-permute-done.9 = bf16[4,64,960]{2,1,0:T(8,128)(2,1)S(1)} collective-permute-done((bf16[4,64,960]{2,1,0:T(8,128)(2,1)S(1)}, bf16[4,64,960]{2,1,0:T(8,128)(2,1)S(1)}, u32[]{:S(2)}, u32[]{:S(2)}) %collective-permute-start.9) | collective-permute-done | bytes 491552 | tf_op jit(solution)/shard_map/ppermute | solution.py:106
  71.0 5.6 %collective-permute-done.8 = bf16[4,96,960]{2,1,0:T(8,128)(2,1)S(1)} collective-permute-done((bf16[4,96,960]{2,1,0:T(8,128)(2,1)S(1)}, bf16[4,96,960]{2,1,0:T(8,128)(2,1)S(1)}, u32[]{:S(2)}, u32[]{:S(2)}) %collective-permute-start.8) | collective-permute-done | bytes 737312 | tf_op jit(solution)/shard_map/ppermute | solution.py:106
  82.6 7.4 %shard_map.152 = bf16[8,320,960]{2,1,0:T(8,128)(2,1)} custom-call(s32[2]{0:T(128)S(1)} %pad_add_fusion.me_ref, bf16[8,96,960]{2,1,0:T(8,128)(2,1)S(1)} %pad_maximum_fusion.1.refs_0_, bf16[8,64,960]{2,1,0:T(8,128)(2,1)S(1)} %pad_maximum_fusion.3.refs_1_, bf16[8,96,960]{2,1,0:T(8,128)(2,1)} %collective-permute-done.10.refs_2_, ...), custom_call_target="tpu_custom_call" | custom-call | bytes 9830400 | tf_op jit(solution)/shard_map/pallas_call | solution.py:387
  92.5 10.4 %collective-permute-done.12 = bf16[1,3,80,960]{3,2,1,0:T(8,128)(2,1)} collective-permute-done((bf16[1,3,80,960]{3,2,1,0:T(8,128)(2,1)S(1)}, bf16[1,3,80,960]{3,2,1,0:T(8,128)(2,1)}, u32[]{:S(2)}, u32[]{:S(2)}) %collective-permute-start.12) | collective-permute-done | bytes 460832 | tf_op jit(solution)/shard_map/ppermute | solution.py:106
  113.5 22.8 %collective-permute-done.13 = bf16[640,256]{1,0:T(8,128)(2,1)S(1)} collective-permute-done((bf16[640,256]{1,0:T(8,128)(2,1)S(1)}, bf16[640,256]{1,0:T(8,128)(2,1)S(1)}, u32[]{:S(2)}, u32[]{:S(2)}) %collective-permute-start.13) | collective-permute-done | bytes 327712 | tf_op jit(solution)/shard_map/ppermute | solution.py:106
  156.0 4.7 collective-permute-done.20
  168.7 17.5 %collective-permute-done.25 = bf16[640,256]{1,0:T(8,128)(2,1)S(1)} collective-permute-done((bf16[640,256]{1,0:T(8,128)(2,1)S(1)}, bf16[640,256]{1,0:T(8,128)(2,1)S(1)}, u32[]{:S(2)}, u32[]{:S(2)}) %collective-permute-start.25) | collective-permute-done | bytes 327712 | tf_op jit(solution)/shard_map/ppermute | solution.py:106
  189.0 8.4 %shard_map.153 = (bf16[960,256]{1,0:T(8,128)(2,1)S(1)}, f32[1,5,1,768]{3,2,1,0:T(1,128)S(1)}) custom-call(s32[8]{0:T(128)S(1)} %compare_convert_fusion.refs_0_, bf16[960,512]{1,0:T(8,128)(2,1)S(1)} %bitcast.172, bf16[1,640,256]{2,1,0:T(8,128)(2,1)S(1)} %get-tuple-element.234.refs_2_.refs_10_, bf16[1,640,256]{2,1,0:T(8,128)(2,1)S(1)} %bitcast.182, ...), custom_call_target="tpu_custom_call" | custom-call | flops 251658240 | bytes 1048576 | tf_op jit(solution)/shard_map/pallas_call | solution.py:737
  199.3 8.4 %shard_map.154 = (bf16[960,256]{1,0:T(8,128)(2,1)S(1)}, f32[1,5,1,768]{3,2,1,0:T(1,128)S(1)}) custom-call(s32[8]{0:T(128)S(1)} %compare_convert_fusion.refs_0_, bf16[960,512]{1,0:T(8,128)(2,1)S(1)} %bitcast.173, bf16[1,640,256]{2,1,0:T(8,128)(2,1)S(1)} %bitcast.177, bf16[1,640,256]{2,1,0:T(8,128)(2,1)S(1)} %bitcast.187, ...), custom_call_target="tpu_custom_call" | custom-call | flops 251658240 | bytes 1048576 | tf_op jit(solution)/shard_map/pallas_call | solution.py:737
  211.5 9.8 %collective-permute-done.28 = bf16[2,3,80,960]{3,2,1,0:T(8,128)(2,1)} collective-permute-done((bf16[2,3,80,960]{3,2,1,0:T(8,128)(2,1)S(1)}, bf16[2,3,80,960]{3,2,1,0:T(8,128)(2,1)}, u32[]{:S(2)}, u32[]{:S(2)}) %collective-permute-start.28) | collective-permute-done | bytes 921632 | tf_op jit(solution)/shard_map/ppermute | solution.py:106
  225.7 21.8 %shard_map.155 = (f32[512,960]{1,0:T(8,128)}, f32[512,960]{1,0:T(8,128)}, bf16[4,3,160,960]{3,2,1,0:T(8,128)(2,1)}, bf16[4,3,160,960]{3,2,1,0:T(8,128)(2,1)}) custom-call(s32[2]{0:T(128)S(1)} %pad_add_fusion.1.refs_0_, bf16[512,960]{1,0:T(8,128)(2,1)S(1)} %multiply_convert_fusion.refs_1_, bf16[512,960]{1,0:T(8,128)(2,1)S(1)} %convert_element_type.440.refs_2_, ...), custom_call_target="tpu_custom_call" | custom-call | flops 11324620800 | bytes 14745600 | tf_op jit(solution)/shard_map/pallas_call | solution.py:1008
  253.0 23.4 %shard_map.156 = (f32[512,960]{1,0:T(8,128)}, f32[512,960]{1,0:T(8,128)}, bf16[4,3,160,960]{3,2,1,0:T(8,128)(2,1)}, bf16[4,3,160,960]{3,2,1,0:T(8,128)(2,1)}) custom-call(s32[2]{0:T(128)S(1)} %pad_add_fusion.1.refs_0_, bf16[512,960]{1,0:T(8,128)(2,1)S(1)} %multiply_convert_fusion.refs_1_, bf16[512,960]{1,0:T(8,128)(2,1)S(1)} %convert_element_type.440.refs_2_, ...), custom_call_target="tpu_custom_call" | custom-call | flops 11324620800 | bytes 14745600 | tf_op jit(solution)/shard_map/pallas_call | solution.py:1008
  279.9 4.3 fusion.47
  301.0 23.0 %shard_map.157 = (bf16[960,256]{1,0:T(8,128)(2,1)S(1)}, bf16[2,5,2,128,128]{4,3,2,1,0:T(8,128)(2,1)S(1)}, bf16[2,5,2,128,128]{4,3,2,1,0:T(8,128)(2,1)S(1)}, bf16[4,5,2,128,128]{4,3,2,1,0:T(8,128)(2,1)}) custom-call(s32[8]{0:T(128)S(1)} %compare_convert_fusion.refs_0_, bf16[960,512]{1,0:T(8,128)(2,1)S(1)} %bitcast.174, ...), custom_call_target="tpu_custom_call" | custom-call | flops 251658240 | bytes 1048576 | tf_op jit(solution)/shard_map/pallas_call | solution.py:772
  325.4 23.0 %shard_map.158 = (bf16[960,256]{1,0:T(8,128)(2,1)S(1)}, bf16[2,5,2,128,128]{4,3,2,1,0:T(8,128)(2,1)S(1)}, bf16[2,5,2,128,128]{4,3,2,1,0:T(8,128)(2,1)S(1)}, bf16[4,5,2,128,128]{4,3,2,1,0:T(8,128)(2,1)}) custom-call(s32[8]{0:T(128)S(1)} %compare_convert_fusion.refs_0_, bf16[960,512]{1,0:T(8,128)(2,1)S(1)} %bitcast.175, bf16[1,640,256]{2,1,0:T(8,128)(2,1)S(1)} %bitcast.179, ...), custom_call_target="tpu_custom_call" | custom-call | flops 251658240 | bytes 1048576 | tf_op jit(solution)/shard_map/pallas_call | solution.py:772
  352.9 4.8 add_convert_fusion
  360.4 24.3 %collective-permute-done.39 = bf16[4,5,2,128,128]{4,3,2,1,0:T(8,128)(2,1)S(1)} collective-permute-done((bf16[4,5,2,128,128]{4,3,2,1,0:T(8,128)(2,1)}, bf16[4,5,2,128,128]{4,3,2,1,0:T(8,128)(2,1)S(1)}, u32[]{:S(2)}, u32[]{:S(2)}) %collective-permute-start.39) | collective-permute-done | bytes 1310752 | tf_op jit(solution)/shard_map/ppermute | solution.py:106
  388.1 8.6 %collective-permute-done.42 = bf16[4,3,80,960]{3,2,1,0:T(8,128)(2,1)} collective-permute-done((bf16[4,3,80,960]{3,2,1,0:T(8,128)(2,1)S(1)}, bf16[4,3,80,960]{3,2,1,0:T(8,128)(2,1)}, u32[]{:S(2)}, u32[]{:S(2)}) %collective-permute-start.42) | collective-permute-done | bytes 1843232 | tf_op jit(solution)/shard_map/ppermute | solution.py:106
  396.7 9.8 %collective-permute-done.40 = bf16[2,5,2,128,128]{4,3,2,1,0:T(8,128)(2,1)S(1)} collective-permute-done((bf16[2,5,2,128,128]{4,3,2,1,0:T(8,128)(2,1)S(1)}, bf16[2,5,2,128,128]{4,3,2,1,0:T(8,128)(2,1)S(1)}, u32[]{:S(2)}, u32[]{:S(2)}) %collective-permute-start.40) | collective-permute-done | bytes 655392 | tf_op jit(solution)/shard_map/ppermute | solution.py:106
  408.8 16.9 %collective-permute-done.44 = bf16[4,3,80,960]{3,2,1,0:T(8,128)(2,1)} collective-permute-done((bf16[4,3,80,960]{3,2,1,0:T(8,128)(2,1)}, bf16[4,3,80,960]{3,2,1,0:T(8,128)(2,1)}, u32[]{:S(2)}, u32[]{:S(2)}) %collective-permute-start.44) | collective-permute-done | bytes 1843232 | tf_op jit(solution)/shard_map/ppermute | solution.py:106
  437.5 7.1 %shard_map.159 = (bf16[8,1,160,960]{3,2,1,0:T(8,128)(2,1)}, bf16[8,1,160,960]{3,2,1,0:T(8,128)(2,1)}) custom-call(s32[2]{0:T(128)S(1)} %pad_add_fusion.me_ref, bf16[1600,512]{1,0:T(8,128)(2,1)S(1)} %pad_maximum_fusion.qkv_ref, bf16[960,512]{1,0:T(8,128)(2,1)S(1)} %copy-done.30, bf16[512,960]{1,0:T(8,128)(2,1)S(1)} %copy-done.22, bf16[512,960]{1,0:T(8,128)(2,1)S(1)} %copy-done.19), custom_call_target="tpu_custom_call" | custom-call | flops 2516582400 | bytes 4915200 | tf_op jit(solution)/shard_map/pallas_call | solution.py:1052
  444.6 10.1 %collective-permute-done.45 = bf16[2,3,80,960]{3,2,1,0:T(8,128)(2,1)} collective-permute-done((bf16[2,3,80,960]{3,2,1,0:T(8,128)(2,1)}, bf16[2,3,80,960]{3,2,1,0:T(8,128)(2,1)}, u32[]{:S(2)}, u32[]{:S(2)}) %collective-permute-start.45) | collective-permute-done | bytes 921632 | tf_op jit(solution)/shard_map/ppermute | solution.py:106
  460.3 4.6 multiply_reduce_fusion.1
  473.2 18.7 %collective-permute-done.51 = bf16[2,2,64,960]{3,2,1,0:T(8,128)(2,1)S(1)} collective-permute-done((bf16[2,2,64,960]{3,2,1,0:T(8,128)(2,1)S(1)}, bf16[2,2,64,960]{3,2,1,0:T(8,128)(2,1)S(1)}, u32[]{:S(2)}, u32[]{:S(2)}) %collective-permute-start.51) | collective-permute-done | bytes 491552 | tf_op jit(solution)/shard_map/ppermute | solution.py:106
  493.2 14.2 %collective-permute-done.52 = bf16[2,64,960]{2,1,0:T(8,128)(2,1)S(1)} collective-permute-done((bf16[2,64,960]{2,1,0:T(8,128)(2,1)S(1)}, bf16[2,64,960]{2,1,0:T(8,128)(2,1)S(1)}, u32[]{:S(2)}, u32[]{:S(2)}) %collective-permute-start.52) | collective-permute-done | bytes 245792 | tf_op jit(solution)/shard_map/ppermute | solution.py:106
  512.1 7.8 %collective-permute-done.49 = bf16[208,960]{1,0:T(8,128)(2,1)S(1)} collective-permute-done((bf16[208,960]{1,0:T(8,128)(2,1)S(1)}, bf16[208,960]{1,0:T(8,128)(2,1)S(1)}, u32[]{:S(2)}, u32[]{:S(2)}) %collective-permute-start.49) | collective-permute-done | bytes 399392 | tf_op jit(solution)/shard_map/ppermute | solution.py:106
  522.4 9.9 %collective-permute-done.50 = bf16[112,960]{1,0:T(8,128)(2,1)S(1)} collective-permute-done((bf16[112,960]{1,0:T(8,128)(2,1)S(1)}, bf16[112,960]{1,0:T(8,128)(2,1)S(1)}, u32[]{:S(2)}, u32[]{:S(2)}) %collective-permute-start.50) | collective-permute-done | bytes 215072 | tf_op jit(solution)/shard_map/ppermute | solution.py:106
  534.3 9.6 %collective-permute-done.55 = bf16[176,960]{1,0:T(8,128)(2,1)S(1)} collective-permute-done((bf16[176,960]{1,0:T(8,128)(2,1)S(1)}, bf16[176,960]{1,0:T(8,128)(2,1)S(1)}, u32[]{:S(2)}, u32[]{:S(2)}) %collective-permute-start.55) | collective-permute-done | bytes 337952 | tf_op jit(solution)/shard_map/ppermute | solution.py:106
  (401 shorter events, 172.9 us)
Async XLA Ops:
  36.5 20.6 %collective-permute-start.4 = (bf16[320,960]{1,0:T(8,128)(2,1)S(1)}, bf16[320,960]{1,0:T(8,128)(2,1)}, u32[]{:S(2)}, u32[]{:S(2)}) collective-permute-start(bf16[320,960]{1,0:T(8,128)(2,1)S(1)} %copy-done.40), channel_id=1, source_target_pairs={{16,0},{8,24},{24,8},{17,1},{9,25},{25,9},{18,2},{10,26},{26,10},{... | collective-permute-start | bytes 1843208 | tf_op jit(solution)/shard_map/ppermute | solution.py:352
  56.5 20.1 %collective-permute-start.8 = (bf16[4,96,960]{2,1,0:T(8,128)(2,1)S(1)}, bf16[4,96,960]{2,1,0:T(8,128)(2,1)S(1)}, u32[]{:S(2)}, u32[]{:S(2)}) collective-permute-start(bf16[4,96,960]{2,1,0:T(8,128)(2,1)S(1)} %pad_maximum_fusion.7), channel_id=1, source_target_pairs={{0,1},{1,0},{2,3},{3,2},{4,5},{5,4},{6,7},{7,6},{8,9},{9,8},{10,11... | collective-permute-start | bytes 2211848 | tf_op jit(solution)/shard_map/ppermute | solution.py:106
  78.1 24.8 %collective-permute-start.12 = (bf16[1,3,80,960]{3,2,1,0:T(8,128)(2,1)S(1)}, bf16[1,3,80,960]{3,2,1,0:T(8,128)(2,1)}, u32[]{:S(2)}, u32[]{:S(2)}) collective-permute-start(bf16[1,3,80,960]{3,2,1,0:T(8,128)(2,1)S(1)} %bitcast.239), channel_id=1, source_target_pairs={{0,4},{1,5},{2,6},{3,7},{4,0},{5,1},{6,2},{7,3},{8,12},{9,13},{10,... | collective-permute-start | bytes 1382408 | tf_op jit(solution)/shard_map/ppermute | solution.py:106
  108.4 29.9 %collective-permute-start.17 = (bf16[2,3,80,960]{3,2,1,0:T(8,128)(2,1)S(1)}, bf16[2,3,80,960]{3,2,1,0:T(8,128)(2,1)S(1)}, u32[]{:S(2)}, u32[]{:S(2)}) collective-permute-start(bf16[2,3,80,960]{3,2,1,0:T(8,128)(2,1)S(1)} %copy-done.43), channel_id=1, source_target_pairs={{0,16},{16,0},{1,17},{17,1},{2,18},{18,2},{3,19},{19,3},{4,20},{20... | collective-permute-start | bytes 2764808 | tf_op jit(solution)/shard_map/ppermute | solution.py:106
  108.4 29.9 %collective-permute-start.16 = (bf16[2,3,80,960]{3,2,1,0:T(8,128)(2,1)S(1)}, bf16[2,3,80,960]{3,2,1,0:T(8,128)(2,1)S(1)}, u32[]{:S(2)}, u32[]{:S(2)}) collective-permute-start(bf16[2,3,80,960]{3,2,1,0:T(8,128)(2,1)S(1)} %copy-done.43), channel_id=1, source_target_pairs={{0,1},{1,0},{2,3},{3,2},{4,5},{5,4},{6,7},{7,6},{8,9},{9,8},{10,11... | collective-permute-start | bytes 2764808 | tf_op jit(solution)/shard_map/ppermute | solution.py:106
  108.9 29.6 %collective-permute-start.15 = (bf16[2,3,80,960]{3,2,1,0:T(8,128)(2,1)S(1)}, bf16[2,3,80,960]{3,2,1,0:T(8,128)(2,1)S(1)}, u32[]{:S(2)}, u32[]{:S(2)}) collective-permute-start(bf16[2,3,80,960]{3,2,1,0:T(8,128)(2,1)S(1)} %copy-done.43), channel_id=1, source_target_pairs={{0,2},{1,3},{2,0},{3,1},{4,6},{5,7},{6,4},{7,5},{8,10},{9,11},{10,... | collective-permute-start | bytes 2764808 | tf_op jit(solution)/shard_map/ppermute | solution.py:106
  109.0 27.4 %collective-permute-start.13 = (bf16[640,256]{1,0:T(8,128)(2,1)S(1)}, bf16[640,256]{1,0:T(8,128)(2,1)S(1)}, u32[]{:S(2)}, u32[]{:S(2)}) collective-permute-start(bf16[640,256]{1,0:T(8,128)(2,1)S(1)} %get-tuple-element.235), channel_id=1, source_target_pairs={{0,4},{1,5},{2,6},{3,7},{4,0},{5,1},{6,2},{7,3},{8,12},{9,13},{10,... | collective-permute-start | bytes 983048 | tf_op jit(solution)/shard_map/ppermute | solution.py:106
  112.0 26.3 %collective-permute-start.14 = (bf16[640,256]{1,0:T(8,128)(2,1)S(1)}, bf16[640,256]{1,0:T(8,128)(2,1)S(1)}, u32[]{:S(2)}, u32[]{:S(2)}) collective-permute-start(bf16[640,256]{1,0:T(8,128)(2,1)S(1)} %get-tuple-element.235), channel_id=1, source_target_pairs={{0,1},{1,0},{2,3},{3,2},{4,5},{5,4},{6,7},{7,6},{8,9},{9,8},{10,11... | collective-permute-start | bytes 983048 | tf_op jit(solution)/shard_map/ppermute | solution.py:106
  138.6 24.1 %collective-permute-start.22 = (bf16[2,3,80,960]{3,2,1,0:T(8,128)(2,1)S(1)}, bf16[2,3,80,960]{3,2,1,0:T(8,128)(2,1)S(1)}, u32[]{:S(2)}, u32[]{:S(2)}) collective-permute-start(bf16[2,3,80,960]{3,2,1,0:T(8,128)(2,1)S(1)} %collective-permute-done.15), channel_id=1, source_target_pairs={{0,16},{16,0},{1,17},{17,1},{2,18},{18,2},{3,19},{19,3},{4,20},{20... | collective-permute-start | bytes 2764808 | tf_op jit(solution)/shard_map/ppermute | solution.py:106
  140.4 22.3 %collective-permute-start.18 = (bf16[2,640,256]{2,1,0:T(8,128)(2,1)S(1)}, bf16[2,640,256]{2,1,0:T(8,128)(2,1)S(1)}, u32[]{:S(2)}, u32[]{:S(2)}) collective-permute-start(bf16[2,640,256]{2,1,0:T(8,128)(2,1)S(1)} %pad_maximum_fusion.11), channel_id=1, source_target_pairs={{0,2},{1,3},{2,0},{3,1},{4,6},{5,7},{6,4},{7,5},{8,10},{9,11},{10,... | collective-permute-start | bytes 1966088 | tf_op jit(solution)/shard_map/ppermute | solution.py:106
  162.7 23.6 %collective-permute-start.26 = (bf16[2,3,80,960]{3,2,1,0:T(8,128)(2,1)S(1)}, bf16[2,3,80,960]{3,2,1,0:T(8,128)(2,1)S(1)}, u32[]{:S(2)}, u32[]{:S(2)}) collective-permute-start(bf16[2,3,80,960]{3,2,1,0:T(8,128)(2,1)S(1)} %collective-permute-done.16), channel_id=1, source_target_pairs={{0,16},{16,0},{1,17},{17,1},{2,18},{18,2},{3,19},{19,3},{4,20},{20... | collective-permute-start | bytes 2764808 | tf_op jit(solution)/shard_map/ppermute | solution.py:106
  163.0 23.3 %collective-permute-start.24 = (bf16[2,640,256]{2,1,0:T(8,128)(2,1)S(1)}, bf16[2,640,256]{2,1,0:T(8,128)(2,1)S(1)}, u32[]{:S(2)}, u32[]{:S(2)}) collective-permute-start(bf16[2,640,256]{2,1,0:T(8,128)(2,1)S(1)} %pad_maximum_fusion.12), channel_id=1, source_target_pairs={{0,2},{1,3},{2,0},{3,1},{4,6},{5,7},{6,4},{7,5},{8,10},{9,11},{10,... | collective-permute-start | bytes 1966088 | tf_op jit(solution)/shard_map/ppermute | solution.py:106
  164.5 21.8 %collective-permute-start.23 = (bf16[2,640,256]{2,1,0:T(8,128)(2,1)S(1)}, bf16[2,640,256]{2,1,0:T(8,128)(2,1)S(1)}, u32[]{:S(2)}, u32[]{:S(2)}) collective-permute-start(bf16[2,640,256]{2,1,0:T(8,128)(2,1)S(1)} %collective-permute-done.18.refs_4_.refs_5_.refs_12_.refs_13_), channel_id=1, source_target_pairs={{0,1},{1,0},{2,3},{3,2},{4,5},{5,4},{6,7},{7,6},{8,9},{9,8},{10,11... | collective-permute-start | bytes 1966088 | tf_op jit(solution)/shard_map/ppermute | solution.py:106
  188.1 37.6 %collective-permute-start.30 = (bf16[4,3,80,960]{3,2,1,0:T(8,128)(2,1)S(1)}, bf16[4,3,80,960]{3,2,1,0:T(8,128)(2,1)}, u32[]{:S(2)}, u32[]{:S(2)}) collective-permute-start(bf16[4,3,80,960]{3,2,1,0:T(8,128)(2,1)S(1)} %constant_dynamic-update-slice_fusion.4.refs_4_), channel_id=1, source_target_pairs={{0,8},{8,0},{1,9},{9,1},{2,10},{10,2},{3,11},{11,3},{4,12},{12,4},... | collective-permute-start | bytes 5529608 | tf_op jit(solution)/shard_map/ppermute | solution.py:106
  188.4 37.3 %collective-permute-start.29 = (bf16[4,3,80,960]{3,2,1,0:T(8,128)(2,1)S(1)}, bf16[4,3,80,960]{3,2,1,0:T(8,128)(2,1)}, u32[]{:S(2)}, u32[]{:S(2)}) collective-permute-start(bf16[4,3,80,960]{3,2,1,0:T(8,128)(2,1)S(1)} %constant_dynamic-update-slice_fusion.2.refs_3_), channel_id=1, source_target_pairs={{0,8},{8,0},{1,9},{9,1},{2,10},{10,2},{3,11},{11,3},{4,12},{12,4},... | collective-permute-start | bytes 5529608 | tf_op jit(solution)/shard_map/ppermute | solution.py:106
  197.4 23.9 %collective-permute-start.28 = (bf16[2,3,80,960]{3,2,1,0:T(8,128)(2,1)S(1)}, bf16[2,3,80,960]{3,2,1,0:T(8,128)(2,1)}, u32[]{:S(2)}, u32[]{:S(2)}) collective-permute-start(bf16[2,3,80,960]{3,2,1,0:T(8,128)(2,1)S(1)} %collective-permute-done.15), channel_id=1, source_target_pairs={{0,1},{1,0},{2,3},{3,2},{4,5},{5,4},{6,7},{7,6},{8,9},{9,8},{10,11... | collective-permute-start | bytes 2764808 | tf_op jit(solution)/shard_map/ppermute | solution.py:106
  222.6 24.9 %collective-permute-start.32 = (bf16[4,3,80,960]{3,2,1,0:T(8,128)(2,1)S(1)}, bf16[4,3,80,960]{3,2,1,0:T(8,128)(2,1)}, u32[]{:S(2)}, u32[]{:S(2)}) collective-permute-start(bf16[4,3,80,960]{3,2,1,0:T(8,128)(2,1)S(1)} %constant_dynamic-update-slice_fusion.6.refs_5_), channel_id=1, source_target_pairs={{0,8},{8,0},{1,9},{9,1},{2,10},{10,2},{3,11},{11,3},{4,12},{12,4},... | collective-permute-start | bytes 5529608 | tf_op jit(solution)/shard_map/ppermute | solution.py:106
  223.9 23.6 %collective-permute-start.31 = (bf16[2,3,80,960]{3,2,1,0:T(8,128)(2,1)}, bf16[2,3,80,960]{3,2,1,0:T(8,128)(2,1)S(1)}, u32[]{:S(2)}, u32[]{:S(2)}) collective-permute-start(bf16[2,3,80,960]{3,2,1,0:T(8,128)(2,1)} %collective-permute-done.28), channel_id=1, source_target_pairs={{0,16},{16,0},{1,17},{17,1},{2,18},{18,2},{3,19},{19,3},{4,20},{20... | collective-permute-start | bytes 2764808 | tf_op jit(solution)/shard_map/ppermute | solution.py:106
  276.5 73.4 %collective-permute-start.41 = (bf16[4,3,160,960]{3,2,1,0:T(8,128)(2,1)}, bf16[4,3,160,960]{3,2,1,0:T(8,128)(2,1)}, u32[]{:S(2)}, u32[]{:S(2)}) collective-permute-start(bf16[4,3,160,960]{3,2,1,0:T(8,128)(2,1)} %get-tuple-element.157), channel_id=1, source_target_pairs={{0,8},{8,0},{1,9},{9,1},{2,10},{10,2},{3,11},{11,3},{4,12},{12,4},... | collective-permute-start | bytes 11059208 | tf_op jit(solution)/shard_map/ppermute | solution.py:106
  290.4 58.0 %collective-permute-start.38 = (bf16[4,3,80,960]{3,2,1,0:T(8,128)(2,1)}, bf16[4,3,80,960]{3,2,1,0:T(8,128)(2,1)}, u32[]{:S(2)}, u32[]{:S(2)}) collective-permute-start(bf16[4,3,80,960]{3,2,1,0:T(8,128)(2,1)} %add_convert_fusion.2), channel_id=1, source_target_pairs={{0,16},{16,0},{1,17},{17,1},{2,18},{18,2},{3,19},{19,3},{4,20},{20... | collective-permute-start | bytes 5529608 | tf_op jit(solution)/shard_map/ppermute | solution.py:106
  324.7 33.7 %collective-permute-start.35 = (bf16[4,5,2,128,128]{4,3,2,1,0:T(8,128)(2,1)}, bf16[4,5,2,128,128]{4,3,2,1,0:T(8,128)(2,1)}, u32[]{:S(2)}, u32[]{:S(2)}) collective-permute-start(bf16[4,5,2,128,128]{4,3,2,1,0:T(8,128)(2,1)} %get-tuple-element.147), channel_id=1, source_target_pairs={{0,1},{1,0},{2,3},{3,2},{4,5},{5,4},{6,7},{7,6},{8,9},{9,8},{10,11... | collective-permute-start | bytes 3932168 | tf_op jit(solution)/shard_map/ppermute | solution.py:106
  348.4 36.2 %collective-permute-start.39 = (bf16[4,5,2,128,128]{4,3,2,1,0:T(8,128)(2,1)}, bf16[4,5,2,128,128]{4,3,2,1,0:T(8,128)(2,1)S(1)}, u32[]{:S(2)}, u32[]{:S(2)}) collective-permute-start(bf16[4,5,2,128,128]{4,3,2,1,0:T(8,128)(2,1)} %get-tuple-element.154), channel_id=1, source_target_pairs={{0,1},{1,0},{2,3},{3,2},{4,5},{5,4},{6,7},{7,6},{8,9},{9,8},{10,11... | collective-permute-start | bytes 3932168 | tf_op jit(solution)/shard_map/ppermute | solution.py:106
  352.5 44.2 %collective-permute-start.42 = (bf16[4,3,80,960]{3,2,1,0:T(8,128)(2,1)S(1)}, bf16[4,3,80,960]{3,2,1,0:T(8,128)(2,1)}, u32[]{:S(2)}, u32[]{:S(2)}) collective-permute-start(bf16[4,3,80,960]{3,2,1,0:T(8,128)(2,1)S(1)} %add_convert_fusion.1), channel_id=1, source_target_pairs={{0,16},{16,0},{1,17},{17,1},{2,18},{18,2},{3,19},{19,3},{4,20},{20... | collective-permute-start | bytes 5529608 | tf_op jit(solution)/shard_map/ppermute | solution.py:106
  357.7 68.0 %collective-permute-start.44 = (bf16[4,3,80,960]{3,2,1,0:T(8,128)(2,1)}, bf16[4,3,80,960]{3,2,1,0:T(8,128)(2,1)}, u32[]{:S(2)}, u32[]{:S(2)}) collective-permute-start(bf16[4,3,80,960]{3,2,1,0:T(8,128)(2,1)} %add_convert_fusion), channel_id=1, source_target_pairs={{0,1},{1,0},{2,3},{3,2},{4,5},{5,4},{6,7},{7,6},{8,9},{9,8},{10,11... | collective-permute-start | bytes 5529608 | tf_op jit(solution)/shard_map/ppermute | solution.py:106
  359.7 25.8 %collective-permute-start.36 = (bf16[2,5,2,128,128]{4,3,2,1,0:T(8,128)(2,1)S(1)}, bf16[2,5,2,128,128]{4,3,2,1,0:T(8,128)(2,1)S(1)}, u32[]{:S(2)}, u32[]{:S(2)}) collective-permute-start(bf16[2,5,2,128,128]{4,3,2,1,0:T(8,128)(2,1)S(1)} %add_convert_fusion.7), channel_id=1, source_target_pairs={{0,2},{1,3},{2,0},{3,1},{4,6},{5,7},{6,4},{7,5},{8,10},{9,11},{10,... | collective-permute-start | bytes 1966088 | tf_op jit(solution)/shard_map/ppermute | solution.py:106
  384.9 21.7 %collective-permute-start.40 = (bf16[2,5,2,128,128]{4,3,2,1,0:T(8,128)(2,1)S(1)}, bf16[2,5,2,128,128]{4,3,2,1,0:T(8,128)(2,1)S(1)}, u32[]{:S(2)}, u32[]{:S(2)}) collective-permute-start(bf16[2,5,2,128,128]{4,3,2,1,0:T(8,128)(2,1)S(1)} %add_convert_fusion.6), channel_id=1, source_target_pairs={{0,2},{1,3},{2,0},{3,1},{4,6},{5,7},{6,4},{7,5},{8,10},{9,11},{10,... | collective-permute-start | bytes 1966088 | tf_op jit(solution)/shard_map/ppermute | solution.py:106
  386.6 21.0 %collective-permute-start.37 = (bf16[5,2,128,128]{3,2,1,0:T(8,128)(2,1)S(1)}, bf16[5,2,128,128]{3,2,1,0:T(8,128)(2,1)}, u32[]{:S(2)}, u32[]{:S(2)}) collective-permute-start(bf16[5,2,128,128]{3,2,1,0:T(8,128)(2,1)S(1)} %fusion.16), channel_id=1, source_target_pairs={{0,4},{1,5},{2,6},{3,7},{4,0},{5,1},{6,2},{7,3},{8,12},{9,13},{10,... | collective-permute-start | bytes 983048 | tf_op jit(solution)/shard_map/ppermute | solution.py:106
  431.7 23.0 %collective-permute-start.45 = (bf16[2,3,80,960]{3,2,1,0:T(8,128)(2,1)}, bf16[2,3,80,960]{3,2,1,0:T(8,128)(2,1)}, u32[]{:S(2)}, u32[]{:S(2)}) collective-permute-start(bf16[2,3,80,960]{3,2,1,0:T(8,128)(2,1)} %add_convert_fusion.3), channel_id=1, source_target_pairs={{0,2},{1,3},{2,0},{3,1},{4,6},{5,7},{6,4},{7,5},{8,10},{9,11},{10,... | collective-permute-start | bytes 2764808 | tf_op jit(solution)/shard_map/ppermute | solution.py:106
  468.6 23.3 %collective-permute-start.51 = (bf16[2,2,64,960]{3,2,1,0:T(8,128)(2,1)S(1)}, bf16[2,2,64,960]{3,2,1,0:T(8,128)(2,1)S(1)}, u32[]{:S(2)}, u32[]{:S(2)}) collective-permute-start(bf16[2,2,64,960]{3,2,1,0:T(8,128)(2,1)S(1)} %fusion.10), channel_id=1, source_target_pairs={{0,2},{1,3},{2,0},{3,1},{4,6},{5,7},{6,4},{7,5},{8,10},{9,11},{10,... | collective-permute-start | bytes 1474568 | tf_op jit(solution)/shard_map/ppermute | solution.py:106
  470.8 38.1 %collective-permute-start.47 = (bf16[400,960]{1,0:T(8,128)(2,1)S(1)}, bf16[400,960]{1,0:T(8,128)(2,1)S(1)}, u32[]{:S(2)}, u32[]{:S(2)}) collective-permute-start(bf16[400,960]{1,0:T(8,128)(2,1)S(1)} %pad_maximum_fusion.6), channel_id=1, source_target_pairs={{0,1},{1,0},{2,3},{3,2},{4,5},{5,4},{6,7},{7,6},{8,9},{9,8},{10,11... | collective-permute-start | bytes 2304008 | tf_op jit(solution)/shard_map/ppermute | solution.py:106
  471.6 37.4 %collective-permute-start.48 = (bf16[3,80,960]{2,1,0:T(8,128)(2,1)S(1)}, bf16[3,80,960]{2,1,0:T(8,128)(2,1)S(1)}, u32[]{:S(2)}, u32[]{:S(2)}) collective-permute-start(bf16[3,80,960]{2,1,0:T(8,128)(2,1)S(1)} %fusion.11), channel_id=1, source_target_pairs={{0,4},{1,5},{2,6},{3,7},{4,0},{5,1},{6,2},{7,3},{8,12},{9,13},{10,... | collective-permute-start | bytes 1382408 | tf_op jit(solution)/shard_map/ppermute | solution.py:106
  511.6 21.9 %collective-permute-start.54 = (bf16[2,80,960]{2,1,0:T(8,128)(2,1)S(1)}, bf16[2,80,960]{2,1,0:T(8,128)(2,1)S(1)}, u32[]{:S(2)}, u32[]{:S(2)}) collective-permute-start(bf16[2,80,960]{2,1,0:T(8,128)(2,1)S(1)} %fusion.7), channel_id=1, source_target_pairs={{0,16},{16,0},{1,17},{17,1},{2,18},{18,2},{3,19},{19,3},{4,20},{20... | collective-permute-start | bytes 921608 | tf_op jit(solution)/shard_map/ppermute | solution.py:106
  (105 other events, 1320.1 us)
